TPU v7x, 32 devices: a whole 2x2x4 slice. The times are simulated.
32 devices in a mesh: seq: 8 (over z, x), head: 4 (over y, core).
Axes of the slice: x: 2, y: 2, z: 4, core: 2. Of those that a mesh axis runs over, the one named last changes fastest.
Arguments:
- queries: bfloat16 [8192, 4096], P('seq', 'head'), may hold values from -6 to 6
- key_vectors: bfloat16 [8192, 4096], P('seq', 'head'), may hold values from -6 to 6
- value_vectors: bfloat16 [8192, 4096], P('seq', 'head'), may hold values from -6 to 6
- gate_input: bfloat16 [8192, 4096], P('seq', 'head'), may hold values from -6 to 6
- log_decay: float32 [8192, 32], P('seq', 'head'), may hold values from -1.5 to 0, as said below
- out_weight: bfloat16 [4096, 4096], P('head'), may hold values from -0.09375 to 0.09375
Outputs:
- projected: bfloat16 [8192, 4096], P(('seq', 'head'))
Inputs may be any that keep to these rules, and one draw needn't show every extreme that they name: `log_decay`: every entry is negative.
All inputs are finite; a program needn't handle non-finite values.
Results may differ from a plain program's by a relative error of at most 0.0054.
Values sent between devices are 32-bit elements; how exact they have to be, the bound alone decides.
No kernel may reach another device: no remote copies, remote signals or barrier semaphores. Data moves between devices by JAX's collectives and lax.ppermute only.
A program may use at most 128 MiB of HBM per device.

v0:
```python
import jax
import jax.numpy as jnp
from jax import lax
from jax.sharding import PartitionSpec as P

HEAD_DIM = 128
BLOCK_LEN = 256


def entering(value, axis, join, neutral):
    count, mine = (lax.axis_size(axis), lax.axis_index(axis))
    pieces = jax.tree.map(lambda part: lax.all_gather(part, axis), value)
    so_far = jax.tree.map(
        lambda part, zero: jnp.full_like(part, 0) + jnp.asarray(zero, part.dtype), value, neutral
    )

    def hop(position, so_far):
        longer = join(so_far, jax.tree.map(lambda part: part[position], pieces))
        return jax.tree.map(lambda new, old: jnp.where(position < mine, new, old), longer, so_far)

    return lax.fori_loop(0, count - 1, hop, so_far)


def per_device(queries, key_vectors, value_vectors, gate_input, log_decay, out_weight):
    token_count, feature_count = queries.shape
    local_heads = feature_count // HEAD_DIM
    block_count = token_count // BLOCK_LEN
    split_shape = (block_count, BLOCK_LEN, local_heads, HEAD_DIM)
    highest = lax.Precision.HIGHEST
    query_blocks = queries.reshape(split_shape)
    key_blocks = key_vectors.reshape(split_shape)
    value_blocks = value_vectors.reshape(split_shape)
    log_rates = log_decay.reshape(block_count, BLOCK_LEN, local_heads)
    running = jnp.cumsum(log_rates, axis=1)
    block_total = running[:, -1, :]
    scores = jnp.einsum(
        "cihd,cjhd->chij", query_blocks, key_blocks, preferred_element_type=jnp.float32
    )
    token_places = lax.iota(jnp.int32, BLOCK_LEN)
    causal = token_places[:, None] >= token_places[None, :]
    by_head = jnp.transpose(running, (0, 2, 1))
    spread = by_head[:, :, :, None] - by_head[:, :, None, :]
    decay = jnp.exp(jnp.where(causal, spread, -1e30))
    weights = (scores * decay).astype(jnp.bfloat16)
    inside = jnp.einsum(
        "chij,cjhd->cihd", weights, value_blocks, preferred_element_type=jnp.float32
    )
    query_scaled = query_blocks.astype(jnp.float32) * jnp.exp(running)[..., None]
    key_scaled = (
        key_blocks.astype(jnp.float32) * jnp.exp(block_total[:, None, :] - running)[..., None]
    )
    contribution = jnp.einsum(
        "cjhd,cjhe->chde", key_scaled, value_blocks.astype(jnp.float32), precision=highest
    )
    block_decay = jnp.exp(block_total)
    lead_decay = jnp.exp(jnp.cumsum(block_total, axis=0) - block_total)
    start_list = []
    running_state = jnp.zeros((local_heads, HEAD_DIM, HEAD_DIM), jnp.float32)
    for block_index in range(block_count):
        start_list.append(running_state)
        running_state = (
            block_decay[block_index][:, None, None] * running_state + contribution[block_index]
        )
    start_states = jnp.stack(start_list)
    through = jnp.exp(jnp.sum(block_total, axis=0))

    def combine_states(earlier, later):
        return (earlier[0] * later[0], later[0][:, None, None] * earlier[1] + later[1])

    identity = (jnp.ones_like(through), jnp.zeros_like(running_state))
    _, incoming = entering((through, running_state), "seq", combine_states, identity)
    combined = start_states + lead_decay[:, :, None, None] * incoming[None]
    carried = jnp.einsum("cihd,chde->cihe", query_scaled, combined, precision=highest)
    attended = (inside + carried).reshape(token_count, local_heads, HEAD_DIM)
    inverse_rms = lax.rsqrt(jnp.mean(attended * attended, axis=-1, keepdims=True) + 1e-06)
    normed = (attended * inverse_rms).reshape(token_count, feature_count)
    hidden = (normed * jax.nn.silu(gate_input.astype(jnp.float32))).astype(jnp.bfloat16)
    return lax.psum_scatter(
        jnp.dot(hidden, out_weight, preferred_element_type=jnp.float32),
        "head",
        scatter_dimension=0,
        tiled=True,
    ).astype(jnp.bfloat16)


def solution(mesh):
    placed = (
        P("seq", "head"),
        P("seq", "head"),
        P("seq", "head"),
        P("seq", "head"),
        P("seq", "head"),
        P("head", None),
    )
    return jax.shard_map(
        per_device, mesh=mesh, in_specs=placed, out_specs=P(("seq", "head"), None), check_vma=False
    )
```

profile of v0, /device:TPU:24, one launch (start us, length us, event | category | flops | bytes accessed | tf_op | source)
XLA Modules:
  0.0 275.3 jit_solution(11796352794879571358)
XLA Ops:
  6.5 4.1 %reduce-window.6 = f32[4,8,2,128]{3,1,2,0:T(8,128)S(1)} reduce-window(f32[4,8,2,128]{3,1,2,0:T(8,128)} %bitcast.76, f32[]{:T(128)} %constant.42.clone.1), window={size=1x1x1x128 pad=0_0x0_0x0_0x127_0}, to_apply=%region_0.0 | reduce-window | flops 1040384 | bytes 65540 | tf_op jit(solution)/shard_map/reduce-window
  10.7 0.1 copy.48
  10.9 0.1 fusion.45
  11.0 0.2 slice_reduce_fusion
  11.2 0.1 subtract_exponential_fusion
  11.3 3.5 %copy.59 = bf16[128,8,8,128]{3,2,1,0:T(8,128)(2,1)} copy(bf16[128,8,8,128]{3,1,2,0:T(8,128)(2,1)} %bitcast.72) | data formatting | bytes 4194304
  14.9 3.0 %copy.51 = bf16[4,256,8,128]{1,3,2,0:T(8,128)(2,1)S(1)} copy(bf16[4,256,8,128]{3,2,1,0:T(8,128)(2,1)} %bitcast.67) | data formatting | bytes 4194304 | tf_op jit(solution)/shard_map/reshape | solution.py:31
  17.9 2.2 copy.60
  20.1 2.6 fusion.9
  22.8 1.3 slice_add_fusion
  24.2 0.6 dynamic-slice
  25.4 0.1 exponential_dynamic-update-slice_fusion
  25.5 17.2 %all-reduce = f32[64]{0:T(128)S(1)} all-reduce(f32[64]{0:T(128)S(1)} %exponential_dynamic-update-slice_fusion), channel_id=2, replica_groups=mesh['seq'=8,'head'=4] {'seq'}, use_global_device_ids=true, to_apply=%add | all-reduce | flops 64 | bytes 512
  42.8 3.6 %copy.58 = bf16[128,8,8,128]{3,2,1,0:T(8,128)(2,1)} copy(bf16[128,8,8,128]{3,1,2,0:T(8,128)(2,1)} %bitcast.74) | data formatting | bytes 4194304
  46.5 6.6 %fusion.5 = f32[4,8,256,128]{2,3,1,0:T(8,128)} fusion(f32[4,8,256]{2,1,0:T(8,128)S(1)} %add_bitcast_fusion.1, pred[256,256]{1,0:T(8,128)(4,1)S(1)} %iota_compare_fusion, bf16[4,256,8,128]{1,3,2,0:T(8,128)(2,1)S(1)} %copy.51, bf16[4,256,8,128]{3,2,1,0:T(8,128)(2,1)} %bitcast.66, bf16[4,256,8,128]{3,2,1,0:T(8,128)(2,1)} %bitcast.68), kind=kOutput, calls=%fused_computation.10 | convolution fusion | flops 1082130432 | bytes 10584064 | tf_op jit(solution)/shard_map/chij,cjhd->cihd/dot_general | solution.py:45
  53.1 43.9 %all-gather.3.cloned.1.call-done = f32[8,8,128,128]{3,2,1,0:T(8,128)} async-done(((f32[1,8,128,128]{3,2,1,0:T(8,128)}), f32[8,8,128,128]{3,2,1,0:T(8,128)}) %all-gather.3.cloned.1.call-update) | async-done | bytes 4194320 | tf_op jit(solution)/shard_map/all_gather | solution.py:12
  97.0 8.5 %while.14 = (s32[]{:T(128)}, f32[8,128,128]{2,1,0:T(8,128)S(1)}, s32[]{:T(128)}, f32[8,8]{1,0:T(8,128)S(1)}, f32[8,8,128,128]{3,2,1,0:T(8,128)}, /*index=5*/s32[]{:T(128)}, s32[]{:T(128)}) while((s32[]{:T(128)}, f32[8,128,128]{2,1,0:T(8,128)S(1)}, s32[]{:T(128)}, f32[8,8]{1,0:T(8,128)S(1)}, f32[8,8,128,128]{3,2,1,0:T(8,128)}, ...), condition=%wide.region_5.6_spmd.clone, body=%wide.region_4.5_spmd.clone.sunk | while | flops 524292 | bytes 1573073 | solution.py:21
  97.0 1.2 fusion.49
  98.2 1.2 fusion.49
  99.4 1.2 fusion.49
  100.7 1.2 fusion.49
  101.9 1.2 fusion.49
  103.1 1.2 fusion.49
  104.3 1.2 fusion.49
  105.5 9.2 %multiply_reduce_fusion = (f32[4,256,8]{1,2,0:T(8,128)S(1)}, f32[4,256,8,128]{1,3,2,0:T(8,128)}) fusion(f32[4,256,8]{1,2,0:T(8,128)S(1)} %get-tuple-element.134, bf16[4,256,8,128]{3,2,1,0:T(8,128)(2,1)} %bitcast.69, f32[1,8,128,128]{3,2,1,0:T(8,128)S(1)} %get-tuple-element.131, f32[1,8,128,128]{3,2,1,0:T(8,128)S(1)} %copy-done.2, ...), kind=kOutput, calls=%fused_computation.13 | convolution fusion | flops 1618468864 | bytes 12648592 | tf_op jit(solution)/shard_map/cihd,chde->cihe/dot_general | solution.py:73
  114.8 0.2 copy.56
  115.0 5.4 %copy.55 = f32[4,256,8,128]{3,2,1,0:T(8,128)} copy(f32[4,256,8,128]{1,3,2,0:T(8,128)} %get-tuple-element.143) | data formatting | bytes 8388608 | tf_op jit(solution)/shard_map/add | solution.py:74
  120.4 1.1 mul.147
  121.5 1.0 copy-done.1
  122.5 15.8 %fusion.21 = f32[1024,4096]{1,0:T(8,128)} fusion(bf16[1024,4096]{1,0:T(8,128)(2,1)} %param.13, bf16[1024,1024]{1,0:T(8,128)(2,1)S(1)} %copy-done.4, f32[128,8,8,128]{3,2,1,0:T(8,128)S(1)} %bitcast.70, f32[128,8,8,128]{3,2,1,0:T(8,128)S(1)} %bitcast.71), kind=kOutput, calls=%fused_computation.26 | convolution fusion | flops 8598323200 | bytes 35651584 | tf_op jit(solution)/shard_map/dot_general | solution.py:79
  138.4 126.3 %reduce-scatter.2.cloned.1.call-done = f32[256,4096]{1,0:T(8,128)} async-done(((f32[1024,4096]{1,0:T(8,128)}), f32[256,4096]{1,0:T(8,128)}) %reduce-scatter.2.cloned.1.call-update) | async-done | bytes 4194320 | tf_op jit(solution)/shard_map/reduce_scatter | solution.py:78
  264.7 3.8 %convert_element_type.24 = bf16[256,4096]{1,0:T(8,128)(2,1)} convert(f32[256,4096]{1,0:T(8,128)} %reduce-scatter.2.cloned.1.call-done) | non-fusion elementwise | flops 1048576 | bytes 6291456 | tf_op jit(solution)/shard_map/convert_element_type | solution.py:83
  (36 shorter events, 0.5 us)
Async XLA Ops:
  6.5 90.5 %all-gather.3.cloned.1.call-start = ((), (), s32[]{:S(2)}) async-start(), calls=%async_computation.1 | async-start | bytes 4718592 | tf_op jit(solution)/shard_map/all_gather | solution.py:12
  20.1 3.9 %copy-start = (bf16[128,8,8,128]{3,2,1,0:T(8,128)(2,1)}, bf16[128,8,8,128]{3,2,1,0:T(8,128)(2,1)S(1)}, u32[]{:S(2)}) copy-start(bf16[128,8,8,128]{3,2,1,0:T(8,128)(2,1)S(1)} %copy.60) | copy-start | bytes 6291460
  20.1 4.0 %copy-start.5 = (u32[32]{0:T(128)S(1)}, u32[32]{0:T(128)}, u32[]{:S(2)}) copy-start(u32[32]{0:T(128)} %constant.52) | copy-start | bytes 388
  24.1 240.6 %reduce-scatter.2.cloned.1.call-start = ((), (), s32[]{:S(2)}) async-start(), calls=%async_computation.2 | async-start | bytes 20971520 | tf_op jit(solution)/shard_map/reduce_scatter | solution.py:78
  53.1 52.4 %copy-start.2 = (f32[1,8,128,128]{3,2,1,0:T(8,128)S(1)}, f32[1,8,128,128]{3,2,1,0:T(8,128)}, u32[]{:S(2)}) copy-start(f32[1,8,128,128]{3,2,1,0:T(8,128)} %get-tuple-element.132) | copy-start | bytes 1572868
  53.1 52.4 %copy-start.3 = (f32[1,8,128,128]{3,2,1,0:T(8,128)S(1)}, f32[1,8,128,128]{3,2,1,0:T(8,128)}, u32[]{:S(2)}) copy-start(f32[1,8,128,128]{3,2,1,0:T(8,128)} %get-tuple-element.133) | copy-start | bytes 1572868
  115.0 6.5 %copy-start.4 = (bf16[1024,1024]{1,0:T(8,128)(2,1)S(1)}, bf16[1024,1024]{1,0:T(8,128)(2,1)}, u32[]{:S(2)}) copy-start(bf16[1024,1024]{1,0:T(8,128)(2,1)} %param.11) | copy-start | bytes 6291460
  120.4 2.2 copy-start.1
Sparse Core Ops, SparseCore 0:
  24.2 72.7 all-gather.2
  138.5 126.1 reduce-scatter.1
where the time goes:
time: 278 us; the launch traced here: 275 us
  waiting for transfers between devices  170 us (61%)
  matrix products  34.3 us (12%)
  local copies, waits for them, and re-layouts  21.1 us (8%)
  other arithmetic  18 us (6%)
  blocking collectives  17.2 us (6%)
  between operations  14.2 us (5%)
    reduce_scatter x1, waiting for transfers between devices, per_device(): lax.psum_scatter(jnp.dot(hidden, out_weight, preferred_element_type=jnp.f...  126 us
    all_gather x1, waiting for transfers between devices, entering(): pieces = jax.tree.map(lambda part: lax.all_gather(part, axis), value)  43.9 us
    unnamed x1, blocking collectives  17.2 us
    dot_general x1, matrix products, per_device(): jnp.dot(hidden, out_weight, preferred_element_type=jnp.float32)  15.8 us
    unnamed x18, local copies, waits for them, and re-layouts  11.1 us
    dot_general x1, matrix products, per_device(): jnp.einsum('cihd,chde->cihe', query_scaled, combined, precision=highest)  9.22 us
    select_n x7, other arithmetic, hop(): jnp.where(position < mine, new, old)  8.22 us
    dot_general x1, matrix products, per_device(): jnp.einsum('chij,cjhd->cihd', weights, value_blocks, preferred_element_ty...  6.58 us
  transfers between devices with their start and end apart: 2, of which 2 were waited for; matrix products, arithmetic and copies ran while one was open for 4% of the time, Pallas kernels for 0%

commit v1 on v0

v1 whole, which is shorter than its diff:
```python
import functools

import jax
import jax.numpy as jnp
from jax import lax
from jax.experimental import pallas as pl
from jax.experimental.pallas import tpu as pltpu
from jax.sharding import PartitionSpec as P

HEAD_DIM = 128
VMEM_LIMIT = 32 * 1024 * 1024
ROW_GROUPS = 4
CHAIN_PARTS = 2
F32 = jnp.float32
BF16 = jnp.bfloat16


def head_columns(head):
    return slice(head * HEAD_DIM, (head + 1) * HEAD_DIM)


def split_pair(value):
    high = value.astype(BF16)
    low = (value - high.astype(F32)).astype(BF16)
    return jnp.concatenate([high, low], axis=1)


def fold_pair(value):
    return value[:, :HEAD_DIM] + value[:, HEAD_DIM:]


def lower_triangle(size):
    rows = lax.broadcasted_iota(jnp.int32, (size, size), 0)
    columns = lax.broadcasted_iota(jnp.int32, (size, size), 1)
    return rows >= columns


def running_sum(log_rates):
    ones = lower_triangle(log_rates.shape[0]).astype(F32)
    return jnp.dot(ones, log_rates, precision=lax.Precision.HIGHEST, preferred_element_type=F32)


def running_sum_rows(log_rates):
    ones = lower_triangle(log_rates.shape[0]).astype(F32)
    return lax.dot_general(
        log_rates, ones, (((0,), (1,)), ((), ())),
        precision=lax.Precision.HIGHEST, preferred_element_type=F32,
    )


def params():
    return pltpu.CompilerParams(vmem_limit_bytes=VMEM_LIMIT)


def states_kernel(odd_ref, rate_ref, key_ref, value_ref, keep_ref, send_ref, start_ref, lead_ref,
                  state, lead):
    block, blocks = pl.program_id(0), pl.num_programs(0)
    heads = rate_ref.shape[1]
    half = heads // 2

    @pl.when(block == 0)
    def _():
        state[...] = jnp.zeros_like(state)
        lead[...] = jnp.zeros_like(lead)

    running = running_sum(rate_ref[...])
    total = running[-1:, :]
    fade = jnp.exp(total - running)
    block_decay = jnp.exp(total)
    lead_ref[...] = jnp.exp(running + lead[...])
    lead[...] = lead[...] + total
    for head in range(heads):
        at = head_columns(head)
        scaled = value_ref[:, at].astype(F32) * fade[:, head:head + 1]
        gained = fold_pair(lax.dot_general(
            key_ref[:, at], split_pair(scaled), (((0,), (0,)), ((), ())), preferred_element_type=F32
        ))
        before = state[head]
        start_ref[0, head] = before
        state[head] = block_decay[:, head:head + 1] * before + gained

    @pl.when(block == blocks - 1)
    def _():
        through = jnp.exp(lead[...])
        for head in range(heads):
            side, place = head // half, head % half
            decay = jnp.broadcast_to(through[:, head:head + 1], (8, HEAD_DIM))

            @pl.when(odd_ref[0] == side)
            def _():
                keep_ref[place, :HEAD_DIM] = state[head]
                keep_ref[place, HEAD_DIM:] = decay

            @pl.when(odd_ref[0] != side)
            def _():
                send_ref[place, :HEAD_DIM] = state[head]
                send_ref[place, HEAD_DIM:] = decay


def local_states(odd, log_decay, key_vectors, value_vectors, block_len):
    tokens, features = key_vectors.shape
    heads = features // HEAD_DIM
    blocks = tokens // block_len
    message = jax.ShapeDtypeStruct((heads // 2, HEAD_DIM + 8, HEAD_DIM), F32)
    whole = pl.BlockSpec(message.shape, lambda b, odd: (0, 0, 0))
    rows = pl.BlockSpec((block_len, features), lambda b, odd: (b, 0))
    rates = pl.BlockSpec((block_len, heads), lambda b, odd: (b, 0))
    return pl.pallas_call(
        states_kernel,
        grid_spec=pltpu.PrefetchScalarGridSpec(
            num_scalar_prefetch=1,
            grid=(blocks,),
            in_specs=[rates, rows, rows],
            out_specs=[
                whole, whole,
                pl.BlockSpec((1, heads, HEAD_DIM, HEAD_DIM), lambda b, odd: (b, 0, 0, 0)),
                rates,
            ],
            scratch_shapes=[
                pltpu.VMEM((heads, HEAD_DIM, HEAD_DIM), F32), pltpu.VMEM((1, heads), F32)
            ],
        ),
        out_shape=[
            message, message,
            jax.ShapeDtypeStruct((blocks, heads, HEAD_DIM, HEAD_DIM), F32),
            jax.ShapeDtypeStruct((tokens, heads), F32),
        ],
        compiler_params=params(),
        cost_estimate=pl.CostEstimate(
            flops=4 * tokens * features * HEAD_DIM, bytes_accessed=8 * tokens * features,
            transcendentals=0),
    )(odd, log_decay, key_vectors, value_vectors)


def inside_kernel(first_ref, rate_ref, query_ref, key_ref, value_ref, start_ref, part_ref):
    heads = rate_ref.shape[1]
    size = rate_ref.shape[0]
    running = running_sum(rate_ref[...])
    running_rows = running_sum_rows(rate_ref[...])
    fade = jnp.exp(running)
    causal = lower_triangle(size)
    for head in range(heads):
        at = head_columns(head)
        queries = query_ref[:, at]
        scores = lax.dot_general(
            queries, key_ref[:, at], (((1,), (1,)), ((), ())), preferred_element_type=F32
        )
        spread = running[:, head:head + 1] - running_rows[head:head + 1, :]
        decay = jnp.exp(jnp.where(causal, spread, -1e30))
        weights = (scores * decay).astype(BF16)
        inside = jnp.dot(weights, value_ref[:, at], preferred_element_type=F32)
        carried = fold_pair(
            jnp.dot(queries, split_pair(start_ref[0, head]), preferred_element_type=F32)
        )
        part_ref[:, at] = inside + carried * fade[:, head:head + 1]


def inside_part(first, log_decay, queries, key_vectors, value_vectors, starts, block_len, count):
    tokens, features = queries.shape
    heads = features // HEAD_DIM
    rows = pl.BlockSpec((block_len, features), lambda b, first: (first[0] + b, 0))
    return pl.pallas_call(
        inside_kernel,
        grid_spec=pltpu.PrefetchScalarGridSpec(
            num_scalar_prefetch=1,
            grid=(count,),
            in_specs=[
                pl.BlockSpec((block_len, heads), lambda b, first: (first[0] + b, 0)),
                rows, rows, rows,
                pl.BlockSpec((1, heads, HEAD_DIM, HEAD_DIM), lambda b, first: (first[0] + b, 0, 0, 0)),
            ],
            out_specs=pl.BlockSpec((block_len, features), lambda b, first: (b, 0)),
        ),
        out_shape=jax.ShapeDtypeStruct((count * block_len, features), F32),
        compiler_params=params(),
        cost_estimate=pl.CostEstimate(
            flops=count * block_len * features * (4 * block_len + 4 * HEAD_DIM),
            bytes_accessed=count * block_len * features * 10,
            transcendentals=count * block_len * block_len * heads),
    )(first, log_decay, queries, key_vectors, value_vectors, starts)


def project_kernel(place_ref, *refs):
    sides = (refs[0:4], refs[4:8])
    keep_ref, got_ref, weight_ref = refs[8:11]
    outs, hidden = refs[11:13], refs[13]
    heads = keep_ref.shape[0] * 2
    half = heads // 2
    rows = outs[0].shape[0]

    @pl.when(pl.program_id(0) == 0)
    def _():
        is_odd = place_ref[2] == 1
        for head in range(heads):
            at = head_columns(head)
            side, place = head // half, head % half
            kept, got = keep_ref[place], got_ref[place]
            incoming = jnp.where(is_odd, kept, got) if side else jnp.where(is_odd, got, kept)
            pair = split_pair(incoming)
            for which, (query_ref, part_ref, gate_ref, lead_ref) in enumerate(sides):
                carried = fold_pair(jnp.dot(query_ref[:, at], pair, preferred_element_type=F32))
                attended = part_ref[:, at] + carried * lead_ref[:, head:head + 1]
                mean = jnp.mean(attended * attended, axis=1, keepdims=True)
                gate = gate_ref[:, at].astype(F32)
                normed = attended * lax.rsqrt(mean + 1e-6)
                hidden[which * rows:(which + 1) * rows, at] = (
                    normed * (gate / (1.0 + jnp.exp(-gate)))
                ).astype(BF16)

    result = jnp.dot(hidden[...], weight_ref[...], preferred_element_type=F32)
    outs[0][...] = result[:rows]
    outs[1][...] = result[rows:]


def project_rows(place, rows, row_group, block_len, queries, part, gate_input, lead, kept, got,
                 out_weight):
    tokens, features = queries.shape
    heads = features // HEAD_DIM
    width = out_weight.shape[1]
    tile = min(512, width)
    per_block = block_len // rows

    def side(which):
        def global_row(j, place):
            return (place[which] * per_block + row_group, 0)

        def group_row(j, place):
            core = place[3]
            local = core if which == 1 else 1 - core
            return (local * per_block + row_group, 0)

        return [
            pl.BlockSpec((rows, features), global_row),
            pl.BlockSpec((rows, features), group_row),
            pl.BlockSpec((rows, features), global_row),
            pl.BlockSpec((rows, heads), global_row),
        ]

    states = pl.BlockSpec((heads // 2, HEAD_DIM, HEAD_DIM), lambda j, place: (0, 0, 0))
    out = pl.BlockSpec((rows, tile), lambda j, place: (0, j))
    shape = jax.ShapeDtypeStruct((rows, width), F32)
    return pl.pallas_call(
        project_kernel,
        grid_spec=pltpu.PrefetchScalarGridSpec(
            num_scalar_prefetch=1,
            grid=(width // tile,),
            in_specs=side(0) + side(1) + [
                states, states, pl.BlockSpec((features, tile), lambda j, place: (0, j))
            ],
            out_specs=[out, out],
            scratch_shapes=[pltpu.VMEM((2 * rows, features), BF16)],
        ),
        out_shape=[shape, shape],
        compiler_params=params(),
        cost_estimate=pl.CostEstimate(
            flops=4 * rows * features * width, bytes_accessed=2 * features * width + 8 * rows * width,
            transcendentals=2 * rows * features),
    )(place, queries, part, gate_input, lead, queries, part, gate_input, lead, kept, got, out_weight)


def finish_kernel(*refs):
    out_ref = refs[-1]
    total = refs[0][...]
    for ref in refs[1:]:
        if ref is not out_ref and ref.dtype == F32:
            total = total + ref[...]
    out_ref[...] = total.astype(out_ref.dtype)


def finish_rows(group, arrived, own, sibling, result):
    rows, width = arrived[0].shape
    block_len = own.shape[0]
    here = pl.BlockSpec((rows, width), lambda i: (group, 0))
    plain = pl.BlockSpec((rows, width), lambda i: (0, 0))
    operands = [own, sibling, *arrived]
    specs = [here, here] + [plain] * len(arrived)
    aliases = {}
    if result is not None:
        aliases = {len(operands): 0}
        operands.append(result)
        specs.append(pl.BlockSpec(memory_space=pl.ANY))
    return pl.pallas_call(
        finish_kernel if result is None else lambda *refs: finish_kernel(*refs[:-2], refs[-1]),
        grid=(1,),
        in_specs=specs,
        out_specs=here,
        out_shape=jax.ShapeDtypeStruct((block_len, width), BF16),
        input_output_aliases=aliases,
        compiler_params=params(),
        cost_estimate=pl.CostEstimate(
            flops=rows * width, bytes_accessed=14 * rows * width, transcendentals=0),
    )(*operands)


def incoming_states(odd, kept, sent):
    count = lax.axis_size("seq")
    swap = [(i, i ^ 1) for i in range(count)]
    is_odd = odd == 1
    size = kept.shape[0] // CHAIN_PARTS
    pieces = [slice(i * size, (i + 1) * size) for i in range(CHAIN_PARTS)]
    got = [lax.ppermute(sent[at], "seq", swap) for at in pieces]
    first, first_decay, pair, pair_decay = [], [], [], []
    for at, other in zip(pieces, got):
        mine = kept[at]
        early = jnp.where(is_odd, other, mine)
        late = jnp.where(is_odd, mine, other)
        early_decay, late_decay = early[:, HEAD_DIM:HEAD_DIM + 1], late[:, HEAD_DIM:HEAD_DIM + 1]
        first.append(early[:, :HEAD_DIM])
        first_decay.append(early_decay)
        pair.append(late_decay * early[:, :HEAD_DIM] + late[:, :HEAD_DIM])
        pair_decay.append(late_decay * early_decay)
    entering = [None] * CHAIN_PARTS
    for hop in range(count // 2 - 1):
        along = [(2 * hop, 2 * hop + 2), (2 * hop + 1, 2 * hop + 3)]
        for i in range(CHAIN_PARTS):
            value = pair[i] if entering[i] is None else pair_decay[i] * entering[i] + pair[i]
            landed = lax.ppermute(value, "seq", along)
            entering[i] = landed if entering[i] is None else entering[i] + landed
    keep, back = [], []
    for i in range(CHAIN_PARTS):
        before = entering[i]
        after = first_decay[i] * before + first[i]
        keep.append(jnp.where(is_odd, after, before))
        back.append(lax.ppermute(jnp.where(is_odd, before, after), "seq", swap))
    return jnp.concatenate(keep), jnp.concatenate(back)


def per_device(queries, key_vectors, value_vectors, gate_input, log_decay, out_weight):
    tokens, features = queries.shape
    count = lax.axis_size("head")
    chips = count // 2
    block_len = tokens // count
    rows = block_len // ROW_GROUPS
    index = lax.axis_index("head")
    chip, core = index // 2, index % 2
    odd = lax.axis_index("seq") % 2
    odd_1 = odd.reshape(1).astype(jnp.int32)

    kept, sent, starts, lead = local_states(odd_1, log_decay, key_vectors, value_vectors, block_len)

    def part_of(target):
        return inside_part(
            (2 * target).reshape(1).astype(jnp.int32), log_decay, queries, key_vectors,
            value_vectors, starts, block_len, 2)

    def project(target, part, group, size):
        place = jnp.stack([2 * target + 1 - core, 2 * target + core, odd, core]).astype(jnp.int32)
        return project_rows(place, size, group, block_len, queries, part, gate_input, lead, keep, got,
                            out_weight)

    cores = [(i, i ^ 1) for i in range(count)]
    targets = [(chip + step) % chips for step in range(1, chips)]
    parts = [part_of(target) for target in targets]
    keep, got = incoming_states(odd, kept, sent)
    arrived = [[] for _ in range(ROW_GROUPS)]
    for step, (target, part) in enumerate(zip(targets, parts), 1):
        across = [(i, ((i // 2 + step) % chips) * 2 + i % 2) for i in range(count)]
        for group in range(ROW_GROUPS):
            theirs, mine = project(target, part, group, rows)
            total = mine + lax.ppermute(theirs, "head", cores)
            arrived[group].append(lax.ppermute(total, "head", across))
    theirs, mine = project(chip, part_of(chip), 0, block_len)
    sibling = lax.ppermute(theirs, "head", cores)
    result = None
    for group in range(ROW_GROUPS):
        result = finish_rows(group, arrived[group], mine, sibling, result)
    return result


def solution(mesh):
    placed = (
        P("seq", "head"),
        P("seq", "head"),
        P("seq", "head"),
        P("seq", "head"),
        P("seq", "head"),
        P("head", None),
    )
    return jax.shard_map(
        per_device, mesh=mesh, in_specs=placed, out_specs=P(("seq", "head"), None), check_vma=False
    )
```

time: 278 us -> 184 us (0.66)
  waiting for transfers between devices: 170 us -> 97.3 us
  Pallas kernels: 0 us -> 55.5 us
  matrix products: 34.3 us -> 0 us
  blocking collectives: 17.2 us -> 0 us
  starting transfers between devices: 0.04 us -> 16.2 us
  other arithmetic: 18 us -> 1.85 us
  between operations: 14.2 us -> 0.38 us
  local copies, waits for them, and re-layouts: 21.1 us -> 12.4 us
    reduce_scatter x1 -> x0, waiting for transfers between devices: 126 us -> none  [per_device(): lax.psum_scatter(jnp.dot(hidden, out_weight, preferred_element_type=jnp.f...]
    ppermute x0 -> x19, waiting for transfers between devices: none -> 97.3 us  [the longest x4 81.8 us: per_device(): arrived[group].append(lax.ppermute(total, 'head', across))]
    pallas_call x0 -> x12, Pallas kernels: none -> 55.5 us  [the longest x5 35.5 us: project_rows(): pl.pallas_call(project_kernel, grid_spec=pltpu.PrefetchScalarGridSpec(num...]
    all_gather x1 -> x0, waiting for transfers between devices: 43.9 us -> none  [entering(): pieces = jax.tree.map(lambda part: lax.all_gather(part, axis), value)]
    dot_general x4 -> x0, matrix products: 34.3 us -> none  [the longest x1 15.8 us: per_device(): jnp.dot(hidden, out_weight, preferred_element_type=jnp.float32)]
    unnamed x1 -> x0, blocking collectives: 17.2 us -> none
    ppermute x0 -> x19, starting transfers between devices: none -> 16.2 us  [the longest x6 5.7 us: incoming_states(): landed = lax.ppermute(value, 'seq', along)]
    select_n x7 -> x3, other arithmetic: 8.22 us -> 1.08 us  [the longest x1 1.02 us: incoming_states(): late = jnp.where(is_odd, mine, other)]
  transfers between devices with their start and end apart: 2 -> 19, of which waited for: 2 -> 7; matrix products, arithmetic and copies ran while one was open for 4% -> 0% of each run, Pallas kernels for 0% -> 19%
where the time goes in v1:
time: 184 us
  waiting for transfers between devices  97.3 us (53%)
  Pallas kernels  55.5 us (30%)
  starting transfers between devices  16.2 us (9%)
  local copies, waits for them, and re-layouts  12.4 us (7%)
  other arithmetic  1.85 us (1%)
    ppermute x4, waiting for transfers between devices, per_device(): arrived[group].append(lax.ppermute(total, 'head', across))  81.8 us
    pallas_call x5, Pallas kernels, project_rows(): pl.pallas_call(project_kernel, grid_spec=pltpu.PrefetchScalarGridSpec(num...  35.5 us
    ppermute x6, waiting for transfers between devices, incoming_states(): landed = lax.ppermute(value, 'seq', along)  11.9 us
    unnamed x36, local copies, waits for them, and re-layouts  11.6 us
    pallas_call x4, Pallas kernels, finish_rows(): pl.pallas_call(finish_kernel if result is None else lambda *refs: finish_...  8.62 us
    pallas_call x2, Pallas kernels, inside_part(): pl.pallas_call(inside_kernel, grid_spec=pltpu.PrefetchScalarGridSpec(num_...  6.6 us
    ppermute x6, starting transfers between devices, incoming_states(): landed = lax.ppermute(value, 'seq', along)  5.7 us
    pallas_call x1, Pallas kernels, local_states(): pl.pallas_call(states_kernel, grid_spec=pltpu.PrefetchScalarGridSpec(num_...  4.76 us
  transfers between devices with their start and end apart: 19, of which 7 were waited for; matrix products, arithmetic and copies ran while one was open for 0% of the time, Pallas kernels for 19%

profile of v1, /device:TPU:24, one launch (start us, length us, event | category | flops | bytes accessed | tf_op | source)
XLA Modules:
  0.0 183.6 jit_solution(3626019997073620235)
XLA Ops:
  1.0 1.6 copy-done.6
  2.6 1.6 copy-done.9
  4.2 4.8 %shard_map.64 = (f32[4,136,128]{2,1,0:T(8,128)S(1)}, f32[4,136,128]{2,1,0:T(8,128)S(1)}, f32[4,8,128,128]{3,2,1,0:T(8,128)S(1)}, f32[1024,8]{1,0:T(8,128)S(1)}) custom-call(s32[1]{0:T(128)} %bitcast.2.odd_ref, f32[1024,8]{1,0:T(8,128)S(1)} %copy.11.rate_ref, bf16[1024,1024]{1,0:T(8,128)(2,1)S(1)} %copy-done.6, bf16[1024,1024]{1,0:T(8,128)(2,1)S(1)} %copy-done.9), custom_call_target="tpu_custom_call" | custom-call | flops 536870912 | bytes 8388608 | tf_op jit(solution)/shard_map/pallas_call | solution.py:108
  8.9 1.3 copy-done.12
  11.0 1.5 collective-permute-start
  13.0 1.6 copy-done.7
  14.6 1.6 copy-done.10
  16.2 1.6 copy-done.13
  17.8 3.3 %shard_map.65.refs_1_.refs_5_ = f32[512,1024]{1,0:T(8,128)S(1)} custom-call(s32[1]{0:T(128)} %bitcast.4.first_ref, f32[1024,8]{1,0:T(8,128)S(1)} %copy.11.rate_ref, bf16[1024,1024]{1,0:T(8,128)(2,1)S(1)} %copy-done, bf16[1024,1024]{1,0:T(8,128)(2,1)S(1)} %copy-done.7, bf16[1024,1024]{1,0:T(8,128)(2,1)S(1)} %copy-done.10, f32[4,8,128,128]{3,2,1,0:T(8,128)S(1)} %copy-done.13), custom_call_target="tpu_custom_call" | custom-call | flops 805306368 | bytes 5242880 | tf_op jit(solution)/shard_map/pallas_call | solution.py:162
  21.1 1.3 copy-done.4
  28.1 1.5 collective-permute-start.7
  29.5 11.9 %collective-permute-done.3 = f32[2,128,128]{2,1,0:T(8,128)S(1)} collective-permute-done((f32[2,128,128]{2,1,0:T(8,128)S(1)}, f32[2,128,128]{2,1,0:T(8,128)S(1)}, u32[]{:S(2)}, u32[]{:S(2)}) %collective-permute-start.3) | collective-permute-done | bytes 131104 | tf_op jit(solution)/shard_map/ppermute | solution.py:317
  41.4 1.6 collective-permute-start.8
  43.0 1.4 collective-permute-start.9
  44.4 2.0 %collective-permute-done.8 = f32[2,128,128]{2,1,0:T(8,128)S(1)} collective-permute-done((f32[2,128,128]{2,1,0:T(8,128)S(1)}, f32[2,128,128]{2,1,0:T(8,128)S(1)}, u32[]{:S(2)}, u32[]{:S(2)}) %collective-permute-start.8) | collective-permute-done | bytes 131104 | tf_op jit(solution)/shard_map/ppermute | solution.py:324
  46.5 1.6 collective-permute-done.9
  48.2 13.2 %shard_map.66 = (f32[256,4096]{1,0:T(8,128)}, f32[256,4096]{1,0:T(8,128)S(1)}) custom-call(s32[4]{0:T(128)S(1)} %get-tuple-element.55.place_ref, bf16[1024,1024]{1,0:T(8,128)(2,1)S(1)} %copy-done, f32[512,1024]{1,0:T(8,128)S(1)} %copy-done.5, bf16[1024,1024]{1,0:T(8,128)(2,1)S(1)} %copy-done.1, f32[1024,8]{1,0:T(8,128)S(1)} %get-tuple-element.20.refs_3_.refs_7_, ...), custom_call_target="tpu_custom_call" | custom-call | flops 4294967296 | bytes 16777216 | tf_op jit(solution)/shard_map/pallas_call | solution.py:242
  61.4 3.3 %shard_map.67.refs_1_.refs_5_ = f32[512,1024]{1,0:T(8,128)S(1)} custom-call(s32[1]{0:T(128)} %bitcast.13.first_ref, f32[1024,8]{1,0:T(8,128)S(1)} %copy.11.rate_ref, bf16[1024,1024]{1,0:T(8,128)(2,1)S(1)} %copy-done, bf16[1024,1024]{1,0:T(8,128)(2,1)S(1)} %copy-done.8, bf16[1024,1024]{1,0:T(8,128)(2,1)S(1)} %copy-done.11, f32[4,8,128,128]{3,2,1,0:T(8,128)S(1)} %copy-done.14), custom_call_target="tpu_custom_call" | custom-call | flops 805306368 | bytes 5242880 | tf_op jit(solution)/shard_map/pallas_call | solution.py:162
  64.8 5.6 %shard_map.71 = (f32[64,4096]{1,0:T(8,128)S(1)}, f32[64,4096]{1,0:T(8,128)S(1)}) custom-call(s32[4]{0:T(128)S(1)} %get-tuple-element.56.place_ref, bf16[1024,1024]{1,0:T(8,128)(2,1)S(1)} %copy-done, f32[512,1024]{1,0:T(8,128)S(1)} %shard_map.67.refs_1_.refs_5_, bf16[1024,1024]{1,0:T(8,128)(2,1)S(1)} %copy-done.1, ...), custom_call_target="tpu_custom_call" | custom-call | flops 1073741824 | bytes 10485760 | tf_op jit(solution)/shard_map/pallas_call | solution.py:242
  70.9 5.6 %shard_map.70 = (f32[64,4096]{1,0:T(8,128)S(1)}, f32[64,4096]{1,0:T(8,128)S(1)}) custom-call(s32[4]{0:T(128)S(1)} %get-tuple-element.56.place_ref, bf16[1024,1024]{1,0:T(8,128)(2,1)S(1)} %copy-done, f32[512,1024]{1,0:T(8,128)S(1)} %shard_map.67.refs_1_.refs_5_, bf16[1024,1024]{1,0:T(8,128)(2,1)S(1)} %copy-done.1, ...), custom_call_target="tpu_custom_call" | custom-call | flops 1073741824 | bytes 10485760 | tf_op jit(solution)/shard_map/pallas_call | solution.py:242
  76.6 5.6 %shard_map.69 = (f32[64,4096]{1,0:T(8,128)S(1)}, f32[64,4096]{1,0:T(8,128)S(1)}) custom-call(s32[4]{0:T(128)S(1)} %get-tuple-element.56.place_ref, bf16[1024,1024]{1,0:T(8,128)(2,1)S(1)} %copy-done, f32[512,1024]{1,0:T(8,128)S(1)} %shard_map.67.refs_1_.refs_5_, bf16[1024,1024]{1,0:T(8,128)(2,1)S(1)} %copy-done.1, ...), custom_call_target="tpu_custom_call" | custom-call | flops 1073741824 | bytes 10485760 | tf_op jit(solution)/shard_map/pallas_call | solution.py:242
  82.7 5.6 %shard_map.68 = (f32[64,4096]{1,0:T(8,128)S(1)}, f32[64,4096]{1,0:T(8,128)S(1)}) custom-call(s32[4]{0:T(128)S(1)} %get-tuple-element.56.place_ref, bf16[1024,1024]{1,0:T(8,128)(2,1)S(1)} %copy-done, f32[512,1024]{1,0:T(8,128)S(1)} %shard_map.67.refs_1_.refs_5_, bf16[1024,1024]{1,0:T(8,128)(2,1)S(1)} %copy-done.1, ...), custom_call_target="tpu_custom_call" | custom-call | flops 1073741824 | bytes 10485760 | tf_op jit(solution)/shard_map/pallas_call | solution.py:242
  88.5 1.6 collective-permute-start.18
  90.9 1.6 collective-permute-start.14
  93.2 21.3 %collective-permute-done.18.refs_2_ = f32[64,4096]{1,0:T(8,128)S(1)} collective-permute-done((f32[64,4096]{1,0:T(8,128)S(1)}, f32[64,4096]{1,0:T(8,128)S(1)}, u32[]{:S(2)}, u32[]{:S(2)}) %collective-permute-start.18) | collective-permute-done | bytes 1048608 | tf_op jit(solution)/shard_map/ppermute | solution.py:361
  114.5 2.2 %shard_map.72.refs_3_ = bf16[256,4096]{1,0:T(8,128)(2,1)} custom-call(f32[256,4096]{1,0:T(8,128)S(1)} %copy-done.3, f32[256,4096]{1,0:T(8,128)} %collective-permute-done.10.refs_1_, f32[64,4096]{1,0:T(8,128)S(1)} %collective-permute-done.18.refs_2_), custom_call_target="tpu_custom_call" | custom-call | flops 262144 | bytes 3670016 | tf_op jit(solution)/shard_map/pallas_call | solution.py:282
  116.6 20.3 %collective-permute-done.16.refs_2_ = f32[64,4096]{1,0:T(8,128)S(1)} collective-permute-done((f32[64,4096]{1,0:T(8,128)S(1)}, f32[64,4096]{1,0:T(8,128)S(1)}, u32[]{:S(2)}, u32[]{:S(2)}) %collective-permute-start.16) | collective-permute-done | bytes 1048608 | tf_op jit(solution)/shard_map/ppermute | solution.py:361
  137.0 2.2 %shard_map.73.refs_3_ = bf16[256,4096]{1,0:T(8,128)(2,1)} custom-call(f32[256,4096]{1,0:T(8,128)S(1)} %copy-done.3, f32[256,4096]{1,0:T(8,128)} %collective-permute-done.10.refs_1_, f32[64,4096]{1,0:T(8,128)S(1)} %collective-permute-done.16.refs_2_, bf16[256,4096]{1,0:T(8,128)(2,1)} %shard_map.72.refs_3_), custom_call_target="tpu_custom_call", output_to_operand_aliasing={{}: (3, {})} | custom-call | flops 262144 | bytes 3670016 | tf_op jit(solution)/shard_map/pallas_call | solution.py:282
  139.1 20.3 %collective-permute-done.14.refs_2_ = f32[64,4096]{1,0:T(8,128)S(1)} collective-permute-done((f32[64,4096]{1,0:T(8,128)S(1)}, f32[64,4096]{1,0:T(8,128)S(1)}, u32[]{:S(2)}, u32[]{:S(2)}) %collective-permute-start.14) | collective-permute-done | bytes 1048608 | tf_op jit(solution)/shard_map/ppermute | solution.py:361
  159.4 2.2 %shard_map.74.refs_3_ = bf16[256,4096]{1,0:T(8,128)(2,1)} custom-call(f32[256,4096]{1,0:T(8,128)S(1)} %copy-done.3, f32[256,4096]{1,0:T(8,128)} %collective-permute-done.10.refs_1_, f32[64,4096]{1,0:T(8,128)S(1)} %collective-permute-done.14.refs_2_, bf16[256,4096]{1,0:T(8,128)(2,1)} %shard_map.73.refs_3_), custom_call_target="tpu_custom_call", output_to_operand_aliasing={{}: (3, {})} | custom-call | flops 262144 | bytes 3670016 | tf_op jit(solution)/shard_map/pallas_call | solution.py:282
  161.6 19.9 %collective-permute-done.12.refs_2_ = f32[64,4096]{1,0:T(8,128)S(1)} collective-permute-done((f32[64,4096]{1,0:T(8,128)S(1)}, f32[64,4096]{1,0:T(8,128)S(1)}, u32[]{:S(2)}, u32[]{:S(2)}) %collective-permute-start.12) | collective-permute-done | bytes 1048608 | tf_op jit(solution)/shard_map/ppermute | solution.py:361
  181.5 2.2 %shard_map.75 = bf16[256,4096]{1,0:T(8,128)(2,1)} custom-call(f32[256,4096]{1,0:T(8,128)S(1)} %copy-done.3, f32[256,4096]{1,0:T(8,128)} %collective-permute-done.10.refs_1_, f32[64,4096]{1,0:T(8,128)S(1)} %collective-permute-done.12.refs_2_, bf16[256,4096]{1,0:T(8,128)(2,1)} %shard_map.74.refs_3_), custom_call_target="tpu_custom_call", output_to_operand_aliasing={{}: (3, {})} | custom-call | flops 262144 | bytes 3670016 | tf_op jit(solution)/shard_map/pallas_call | solution.py:282
  (74 shorter events, 10.8 us)
Async XLA Ops:
  1.0 1.6 copy-start.6
  2.6 1.6 copy-start.9
  4.2 8.9 %copy-start = (bf16[1024,1024]{1,0:T(8,128)(2,1)S(1)}, bf16[1024,1024]{1,0:T(8,128)(2,1)}, u32[]{:S(2)}) copy-start(bf16[1024,1024]{1,0:T(8,128)(2,1)} %refs_4_.9) | copy-start | bytes 6291460
  11.0 11.5 %collective-permute-start = (f32[2,136,128]{2,1,0:T(8,128)}, f32[2,136,128]{2,1,0:T(8,128)}, u32[]{:S(2)}, u32[]{:S(2)}) collective-permute-start(f32[2,136,128]{2,1,0:T(8,128)} %get-tuple-element.47), channel_id=1, source_target_pairs={{0,4},{4,0},{8,12},{12,8},{16,20},{20,16},{24,28},{28,24},{1,5},{5... | collective-permute-start | bytes 417800 | tf_op jit(solution)/shard_map/ppermute | solution.py:301
  12.5 10.0 %collective-permute-start.4 = (f32[2,136,128]{2,1,0:T(8,128)}, f32[2,136,128]{2,1,0:T(8,128)}, u32[]{:S(2)}, u32[]{:S(2)}) collective-permute-start(f32[2,136,128]{2,1,0:T(8,128)} %get-tuple-element.48), channel_id=1, source_target_pairs={{0,4},{4,0},{8,12},{12,8},{16,20},{20,16},{24,28},{28,24},{1,5},{5... | collective-permute-start | bytes 417800 | tf_op jit(solution)/shard_map/ppermute | solution.py:301
  13.0 1.6 copy-start.7
  23.6 1.4 collective-permute-start.1
  24.3 1.5 collective-permute-start.5
  25.0 23.1 %copy-start.5 = (f32[512,1024]{1,0:T(8,128)S(1)}, f32[512,1024]{1,0:T(8,128)}, u32[]{:S(2)}) copy-start(f32[512,1024]{1,0:T(8,128)} %copy-done.4) | copy-start | bytes 6291460
  25.0 23.1 %copy-start.1 = (bf16[1024,1024]{1,0:T(8,128)(2,1)S(1)}, bf16[1024,1024]{1,0:T(8,128)(2,1)}, u32[]{:S(2)}) copy-start(bf16[1024,1024]{1,0:T(8,128)(2,1)} %refs_6_.9) | copy-start | bytes 6291460
  25.0 1.7 collective-permute-start.2
  25.9 2.2 %collective-permute-start.6 = (f32[2,128,128]{2,1,0:T(8,128)S(1)}, f32[2,128,128]{2,1,0:T(8,128)S(1)}, u32[]{:S(2)}, u32[]{:S(2)}) collective-permute-start(f32[2,128,128]{2,1,0:T(8,128)S(1)} %multiply_add_fusion.2), channel_id=1, source_target_pairs={{8,16},{12,20},{9,17},{13,21},{10,18},{14,22},{11,19},{15,23}} | collective-permute-start | bytes 393224 | tf_op jit(solution)/shard_map/ppermute | solution.py:317
  26.7 14.7 %collective-permute-start.3 = (f32[2,128,128]{2,1,0:T(8,128)S(1)}, f32[2,128,128]{2,1,0:T(8,128)S(1)}, u32[]{:S(2)}, u32[]{:S(2)}) collective-permute-start(f32[2,128,128]{2,1,0:T(8,128)S(1)} %get-tuple-element.33), channel_id=1, source_target_pairs={{16,24},{20,28},{17,25},{21,29},{18,26},{22,30},{19,27},{23,31}} | collective-permute-start | bytes 393224 | tf_op jit(solution)/shard_map/ppermute | solution.py:317
  28.1 14.9 %collective-permute-start.7 = (f32[2,128,128]{2,1,0:T(8,128)S(1)}, f32[2,128,128]{2,1,0:T(8,128)S(1)}, u32[]{:S(2)}, u32[]{:S(2)}) collective-permute-start(f32[2,128,128]{2,1,0:T(8,128)S(1)} %get-tuple-element.35), channel_id=1, source_target_pairs={{16,24},{20,28},{17,25},{21,29},{18,26},{22,30},{19,27},{23,31}} | collective-permute-start | bytes 393224 | tf_op jit(solution)/shard_map/ppermute | solution.py:317
  41.4 5.0 %collective-permute-start.8 = (f32[2,128,128]{2,1,0:T(8,128)S(1)}, f32[2,128,128]{2,1,0:T(8,128)S(1)}, u32[]{:S(2)}, u32[]{:S(2)}) collective-permute-start(f32[2,128,128]{2,1,0:T(8,128)S(1)} %get-tuple-element.43), channel_id=1, source_target_pairs={{0,4},{4,0},{8,12},{12,8},{16,20},{20,16},{24,28},{28,24},{1,5},{5... | collective-permute-start | bytes 393224 | tf_op jit(solution)/shard_map/ppermute | solution.py:324
  43.0 5.0 %collective-permute-start.9 = (f32[2,128,128]{2,1,0:T(8,128)S(1)}, f32[2,128,128]{2,1,0:T(8,128)S(1)}, u32[]{:S(2)}, u32[]{:S(2)}) collective-permute-start(f32[2,128,128]{2,1,0:T(8,128)S(1)} %get-tuple-element.41), channel_id=1, source_target_pairs={{0,4},{4,0},{8,12},{12,8},{16,20},{20,16},{24,28},{28,24},{1,5},{5... | collective-permute-start | bytes 393224 | tf_op jit(solution)/shard_map/ppermute | solution.py:324
  44.4 20.3 %slice-start = ((s8[8388608]{0:T(1024)(128)(4,1)}), s8[4194304]{0:T(1024)(128)(4,1)S(1)}, s32[]{:S(2)}) async-start(s8[8388608]{0:T(1024)(128)(4,1)} %bitcast.14), calls=%async_computation | async-start | bytes 8388608
  48.1 13.3 %copy-start.8 = (bf16[1024,1024]{1,0:T(8,128)(2,1)S(1)}, bf16[1024,1024]{1,0:T(8,128)(2,1)}, u32[]{:S(2)}) copy-start(bf16[1024,1024]{1,0:T(8,128)(2,1)} %key_ref.5) | copy-start | bytes 6291460
  48.1 13.3 %copy-start.11 = (bf16[1024,1024]{1,0:T(8,128)(2,1)S(1)}, bf16[1024,1024]{1,0:T(8,128)(2,1)}, u32[]{:S(2)}) copy-start(bf16[1024,1024]{1,0:T(8,128)(2,1)} %value_ref.5) | copy-start | bytes 6291460
  48.1 13.3 %copy-start.14 = (f32[4,8,128,128]{3,2,1,0:T(8,128)S(1)}, f32[4,8,128,128]{3,2,1,0:T(8,128)}, u32[]{:S(2)}) copy-start(f32[4,8,128,128]{3,2,1,0:T(8,128)} %copy-done.12) | copy-start | bytes 6291460
  48.1 16.6 %slice-start.1 = ((s8[8388608]{0:T(1024)(128)(4,1)}), s8[4194304]{0:T(1024)(128)(4,1)S(1)}, s32[]{:S(2)}) async-start(s8[8388608]{0:T(1024)(128)(4,1)} %bitcast.14), calls=%async_computation.1 | async-start | bytes 8388608
  61.4 3.4 %copy-start.2 = (f32[256,4096]{1,0:T(8,128)}, f32[256,4096]{1,0:T(8,128)S(1)}, u32[]{:S(2)}) copy-start(f32[256,4096]{1,0:T(8,128)S(1)} %get-tuple-element.23.refs_0_) | copy-start | bytes 12582916
  61.4 53.1 %collective-permute-start.10 = (f32[256,4096]{1,0:T(8,128)}, f32[256,4096]{1,0:T(8,128)}, u32[]{:S(2)}, u32[]{:S(2)}) collective-permute-start(f32[256,4096]{1,0:T(8,128)} %get-tuple-element.24), channel_id=1, source_target_pairs={{0,1},{1,0},{2,3},{3,2},{4,5},{5,4},{6,7},{7,6},{8,9},{9,8},{10,11... | collective-permute-start | bytes 12582920 | tf_op jit(solution)/shard_map/ppermute | solution.py:363
  70.3 18.0 %collective-permute-start.17 = (f32[64,4096]{1,0:T(8,128)S(1)}, f32[64,4096]{1,0:T(8,128)S(1)}, u32[]{:S(2)}, u32[]{:S(2)}) collective-permute-start(f32[64,4096]{1,0:T(8,128)S(1)} %get-tuple-element.32), channel_id=1, source_target_pairs={{0,1},{1,0},{2,3},{3,2},{4,5},{5,4},{6,7},{7,6},{8,9},{9,8},{10,11... | collective-permute-start | bytes 3145736 | tf_op jit(solution)/shard_map/ppermute | solution.py:360
  76.5 13.6 %collective-permute-start.15 = (f32[64,4096]{1,0:T(8,128)S(1)}, f32[64,4096]{1,0:T(8,128)S(1)}, u32[]{:S(2)}, u32[]{:S(2)}) collective-permute-start(f32[64,4096]{1,0:T(8,128)S(1)} %get-tuple-element.30), channel_id=1, source_target_pairs={{0,1},{1,0},{2,3},{3,2},{4,5},{5,4},{6,7},{7,6},{8,9},{9,8},{10,11... | collective-permute-start | bytes 3145736 | tf_op jit(solution)/shard_map/ppermute | solution.py:360
  82.1 8.6 %collective-permute-start.13 = (f32[64,4096]{1,0:T(8,128)S(1)}, f32[64,4096]{1,0:T(8,128)S(1)}, u32[]{:S(2)}, u32[]{:S(2)}) collective-permute-start(f32[64,4096]{1,0:T(8,128)S(1)} %get-tuple-element.28), channel_id=1, source_target_pairs={{0,1},{1,0},{2,3},{3,2},{4,5},{5,4},{6,7},{7,6},{8,9},{9,8},{10,11... | collective-permute-start | bytes 3145736 | tf_op jit(solution)/shard_map/ppermute | solution.py:360
  88.3 4.2 %collective-permute-start.11 = (f32[64,4096]{1,0:T(8,128)S(1)}, f32[64,4096]{1,0:T(8,128)S(1)}, u32[]{:S(2)}, u32[]{:S(2)}) collective-permute-start(f32[64,4096]{1,0:T(8,128)S(1)} %get-tuple-element.26), channel_id=1, source_target_pairs={{0,1},{1,0},{2,3},{3,2},{4,5},{5,4},{6,7},{7,6},{8,9},{9,8},{10,11... | collective-permute-start | bytes 3145736 | tf_op jit(solution)/shard_map/ppermute | solution.py:360
  88.5 26.0 %collective-permute-start.18 = (f32[64,4096]{1,0:T(8,128)S(1)}, f32[64,4096]{1,0:T(8,128)S(1)}, u32[]{:S(2)}, u32[]{:S(2)}) collective-permute-start(f32[64,4096]{1,0:T(8,128)S(1)} %add.103), channel_id=1, source_target_pairs={{0,2},{1,3},{2,0},{3,1},{4,6},{5,7},{6,4},{7,5},{8,10},{9,11},{10,... | collective-permute-start | bytes 3145736 | tf_op jit(solution)/shard_map/ppermute | solution.py:361
  90.2 46.8 %collective-permute-start.16 = (f32[64,4096]{1,0:T(8,128)S(1)}, f32[64,4096]{1,0:T(8,128)S(1)}, u32[]{:S(2)}, u32[]{:S(2)}) collective-permute-start(f32[64,4096]{1,0:T(8,128)S(1)} %add.102), channel_id=1, source_target_pairs={{0,2},{1,3},{2,0},{3,1},{4,6},{5,7},{6,4},{7,5},{8,10},{9,11},{10,... | collective-permute-start | bytes 3145736 | tf_op jit(solution)/shard_map/ppermute | solution.py:361
  90.7 23.7 %copy-start.3 = (f32[256,4096]{1,0:T(8,128)S(1)}, f32[256,4096]{1,0:T(8,128)}, u32[]{:S(2)}) copy-start(f32[256,4096]{1,0:T(8,128)} %copy-done.2) | copy-start | bytes 12582916
  90.9 68.5 %collective-permute-start.14 = (f32[64,4096]{1,0:T(8,128)S(1)}, f32[64,4096]{1,0:T(8,128)S(1)}, u32[]{:S(2)}, u32[]{:S(2)}) collective-permute-start(f32[64,4096]{1,0:T(8,128)S(1)} %add.101), channel_id=1, source_target_pairs={{0,2},{1,3},{2,0},{3,1},{4,6},{5,7},{6,4},{7,5},{8,10},{9,11},{10,... | collective-permute-start | bytes 3145736 | tf_op jit(solution)/shard_map/ppermute | solution.py:361
  92.6 88.8 %collective-permute-start.12 = (f32[64,4096]{1,0:T(8,128)S(1)}, f32[64,4096]{1,0:T(8,128)S(1)}, u32[]{:S(2)}, u32[]{:S(2)}) collective-permute-start(f32[64,4096]{1,0:T(8,128)S(1)} %add.100), channel_id=1, source_target_pairs={{0,2},{1,3},{2,0},{3,1},{4,6},{5,7},{6,4},{7,5},{8,10},{9,11},{10,... | collective-permute-start | bytes 3145736 | tf_op jit(solution)/shard_map/ppermute | solution.py:361
  (4 other events, 5.8 us)

commit v2 on v1

--- a/solution.py
+++ b/solution.py
@@ -11,6 +11,10 @@
 VMEM_LIMIT = 32 * 1024 * 1024
 ROW_GROUPS = 4
 CHAIN_PARTS = 2
+CORE_PIECES = 4
+OWN_PIECES = 2
+DEPTH = 2
+SHORT = pl.CostEstimate(flops=1, bytes_accessed=1, transcendentals=0)
 F32 = jnp.float32
 BF16 = jnp.bfloat16
 
@@ -126,13 +130,12 @@
             jax.ShapeDtypeStruct((tokens, heads), F32),
         ],
         compiler_params=params(),
-        cost_estimate=pl.CostEstimate(
-            flops=4 * tokens * features * HEAD_DIM, bytes_accessed=8 * tokens * features,
-            transcendentals=0),
+        cost_estimate=SHORT,
     )(odd, log_decay, key_vectors, value_vectors)
 
 
-def inside_kernel(first_ref, rate_ref, query_ref, key_ref, value_ref, start_ref, part_ref):
+def inside_kernel(first_ref, rate_ref, query_ref, key_ref, value_ref, start_ref, after_ref, part_ref):
+    del after_ref
     heads = rate_ref.shape[1]
     size = rate_ref.shape[0]
     running = running_sum(rate_ref[...])
@@ -155,7 +158,7 @@
         part_ref[:, at] = inside + carried * fade[:, head:head + 1]
 
 
-def inside_part(first, log_decay, queries, key_vectors, value_vectors, starts, block_len, count):
+def inside_part(first, log_decay, queries, key_vectors, value_vectors, starts, block_len, count, after):
     tokens, features = queries.shape
     heads = features // HEAD_DIM
     rows = pl.BlockSpec((block_len, features), lambda b, first: (first[0] + b, 0))
@@ -168,25 +171,24 @@
                 pl.BlockSpec((block_len, heads), lambda b, first: (first[0] + b, 0)),
                 rows, rows, rows,
                 pl.BlockSpec((1, heads, HEAD_DIM, HEAD_DIM), lambda b, first: (first[0] + b, 0, 0, 0)),
+                pl.BlockSpec(memory_space=pl.ANY),
             ],
             out_specs=pl.BlockSpec((block_len, features), lambda b, first: (b, 0)),
         ),
         out_shape=jax.ShapeDtypeStruct((count * block_len, features), F32),
         compiler_params=params(),
-        cost_estimate=pl.CostEstimate(
-            flops=count * block_len * features * (4 * block_len + 4 * HEAD_DIM),
-            bytes_accessed=count * block_len * features * 10,
-            transcendentals=count * block_len * block_len * heads),
-    )(first, log_decay, queries, key_vectors, value_vectors, starts)
+        cost_estimate=SHORT,
+    )(first, log_decay, queries, key_vectors, value_vectors, starts, after)
 
 
 def project_kernel(place_ref, *refs):
     sides = (refs[0:4], refs[4:8])
     keep_ref, got_ref, weight_ref = refs[8:11]
-    outs, hidden = refs[11:13], refs[13]
+    outs, hidden = refs[12:-1], refs[-1]
     heads = keep_ref.shape[0] * 2
     half = heads // 2
-    rows = outs[0].shape[0]
+    rows = outs[-1].shape[0]
+    piece = outs[0].shape[0]
 
     @pl.when(pl.program_id(0) == 0)
     def _():
@@ -208,12 +210,13 @@
                 ).astype(BF16)
 
     result = jnp.dot(hidden[...], weight_ref[...], preferred_element_type=F32)
-    outs[0][...] = result[:rows]
-    outs[1][...] = result[rows:]
+    for i, out_ref in enumerate(outs[:-1]):
+        out_ref[...] = result[i * piece:(i + 1) * piece]
+    outs[-1][...] = result[rows:]
 
 
 def project_rows(place, rows, row_group, block_len, queries, part, gate_input, lead, kept, got,
-                 out_weight):
+                 out_weight, after, pieces):
     tokens, features = queries.shape
     heads = features // HEAD_DIM
     width = out_weight.shape[1]
@@ -237,59 +240,81 @@
         ]
 
     states = pl.BlockSpec((heads // 2, HEAD_DIM, HEAD_DIM), lambda j, place: (0, 0, 0))
-    out = pl.BlockSpec((rows, tile), lambda j, place: (0, j))
-    shape = jax.ShapeDtypeStruct((rows, width), F32)
+    sizes = [rows // pieces] * pieces + [rows]
     return pl.pallas_call(
         project_kernel,
         grid_spec=pltpu.PrefetchScalarGridSpec(
             num_scalar_prefetch=1,
             grid=(width // tile,),
             in_specs=side(0) + side(1) + [
-                states, states, pl.BlockSpec((features, tile), lambda j, place: (0, j))
+                states, states, pl.BlockSpec((features, tile), lambda j, place: (0, j)),
+                pl.BlockSpec(memory_space=pl.ANY),
             ],
-            out_specs=[out, out],
+            out_specs=[pl.BlockSpec((size, tile), lambda j, place: (0, j)) for size in sizes],
             scratch_shapes=[pltpu.VMEM((2 * rows, features), BF16)],
         ),
-        out_shape=[shape, shape],
+        out_shape=[jax.ShapeDtypeStruct((size, width), F32) for size in sizes],
         compiler_params=params(),
-        cost_estimate=pl.CostEstimate(
-            flops=4 * rows * features * width, bytes_accessed=2 * features * width + 8 * rows * width,
-            transcendentals=2 * rows * features),
-    )(place, queries, part, gate_input, lead, queries, part, gate_input, lead, kept, got, out_weight)
-
-
-def finish_kernel(*refs):
+        cost_estimate=SHORT,
+    )(place, queries, part, gate_input, lead, queries, part, gate_input, lead, kept, got, out_weight,
+      after)
+
+
+def add_kernel(own_ref, *refs):
+    pieces, out_ref = refs[:-2], refs[-1]
+    at = 0
+    for ref in pieces:
+        size = ref.shape[0]
+        out_ref[at:at + size] = own_ref[at:at + size] + ref[...]
+        at += size
+
+
+def add_pieces(own, pieces, after):
+    whole = pl.BlockSpec(own.shape, lambda: (0, 0))
+    return pl.pallas_call(
+        add_kernel,
+        in_specs=[whole] + [pl.BlockSpec(piece.shape, lambda: (0, 0)) for piece in pieces]
+        + [pl.BlockSpec(memory_space=pl.ANY)],
+        out_specs=whole,
+        out_shape=jax.ShapeDtypeStruct(own.shape, F32),
+        compiler_params=params(),
+        cost_estimate=SHORT,
+    )(own, *pieces, after)
+
+
+def finish_kernel(arrivals, own_ref, *refs):
     out_ref = refs[-1]
-    total = refs[0][...]
-    for ref in refs[1:]:
-        if ref is not out_ref and ref.dtype == F32:
-            total = total + ref[...]
-    out_ref[...] = total.astype(out_ref.dtype)
-
-
-def finish_rows(group, arrived, own, sibling, result):
-    rows, width = arrived[0].shape
-    block_len = own.shape[0]
-    here = pl.BlockSpec((rows, width), lambda i: (group, 0))
-    plain = pl.BlockSpec((rows, width), lambda i: (0, 0))
-    operands = [own, sibling, *arrived]
-    specs = [here, here] + [plain] * len(arrived)
-    aliases = {}
-    if result is not None:
-        aliases = {len(operands): 0}
-        operands.append(result)
-        specs.append(pl.BlockSpec(memory_space=pl.ANY))
+    arrived, pieces = refs[:arrivals], refs[arrivals:-2]
+    at = 0
+    for ref in pieces:
+        size = ref.shape[0]
+        total = own_ref[at:at + size] + ref[...]
+        for other in arrived:
+            total = total + other[at:at + size]
+        out_ref[at:at + size] = total.astype(out_ref.dtype)
+        at += size
+
+
+def finish_rows(group, arrived, own, pieces, result, block_len):
+    rows, width = own.shape
+    whole = pl.BlockSpec((rows, width), lambda i: (0, 0))
+    alias = {}
+    if result is None:
+        result = own
+    else:
+        alias = {1 + len(arrived) + len(pieces): 0}
     return pl.pallas_call(
-        finish_kernel if result is None else lambda *refs: finish_kernel(*refs[:-2], refs[-1]),
+        functools.partial(finish_kernel, len(arrived)),
         grid=(1,),
-        in_specs=specs,
-        out_specs=here,
+        in_specs=[whole] * (1 + len(arrived))
+        + [pl.BlockSpec(piece.shape, lambda i: (0, 0)) for piece in pieces]
+        + [pl.BlockSpec(memory_space=pl.ANY)],
+        out_specs=pl.BlockSpec((rows, width), lambda i: (group, 0)),
         out_shape=jax.ShapeDtypeStruct((block_len, width), BF16),
-        input_output_aliases=aliases,
+        input_output_aliases=alias,
         compiler_params=params(),
-        cost_estimate=pl.CostEstimate(
-            flops=rows * width, bytes_accessed=14 * rows * width, transcendentals=0),
-    )(*operands)
+        cost_estimate=SHORT,
+    )(own, *arrived, *pieces, result)
 
 
 def incoming_states(odd, kept, sent):
@@ -338,32 +363,39 @@
 
     kept, sent, starts, lead = local_states(odd_1, log_decay, key_vectors, value_vectors, block_len)
 
-    def part_of(target):
+    def part_of(target, after):
         return inside_part(
             (2 * target).reshape(1).astype(jnp.int32), log_decay, queries, key_vectors,
-            value_vectors, starts, block_len, 2)
-
-    def project(target, part, group, size):
+            value_vectors, starts, block_len, 2, after)
+
+    def project(target, part, group, after, pieces):
         place = jnp.stack([2 * target + 1 - core, 2 * target + core, odd, core]).astype(jnp.int32)
-        return project_rows(place, size, group, block_len, queries, part, gate_input, lead, keep, got,
-                            out_weight)
+        *theirs, mine = project_rows(
+            place, rows, group, block_len, queries, part, gate_input, lead, keep, got, out_weight,
+            after, pieces)
+        return mine, [lax.ppermute(piece, "head", cores) for piece in theirs]
 
     cores = [(i, i ^ 1) for i in range(count)]
     targets = [(chip + step) % chips for step in range(1, chips)]
-    parts = [part_of(target) for target in targets]
+    parts = [part_of(target, sent) for target in targets]
     keep, got = incoming_states(odd, kept, sent)
+    landed, last, own, result = [sent, sent], sent, [], None
     arrived = [[] for _ in range(ROW_GROUPS)]
-    for step, (target, part) in enumerate(zip(targets, parts), 1):
-        across = [(i, ((i // 2 + step) % chips) * 2 + i % 2) for i in range(count)]
-        for group in range(ROW_GROUPS):
-            theirs, mine = project(target, part, group, rows)
-            total = mine + lax.ppermute(theirs, "head", cores)
-            arrived[group].append(lax.ppermute(total, "head", across))
-    theirs, mine = project(chip, part_of(chip), 0, block_len)
-    sibling = lax.ppermute(theirs, "head", cores)
-    result = None
     for group in range(ROW_GROUPS):
-        result = finish_rows(group, arrived[group], mine, sibling, result)
+        for step, (target, part) in enumerate(zip(targets, parts), 1):
+            across = [(i, ((i // 2 + step) % chips) * 2 + i % 2) for i in range(count)]
+            mine, pieces = project(target, part, group, last, CORE_PIECES)
+            last = add_pieces(mine, pieces, landed[-DEPTH])
+            landed.append(lax.ppermute(last, "head", across))
+            arrived[group].append(landed[-1])
+    own_part = part_of(chip, last)
+    for group in range(ROW_GROUPS):
+        if group == ROW_GROUPS - 1:
+            last = landed[-2]
+        own.append(project(chip, own_part, group, last, OWN_PIECES))
+        last = own[-1][0]
+    for group in range(ROW_GROUPS):
+        result = finish_rows(group, arrived[group], *own[group], result, block_len)
     return result
 
 

time: 184 us -> 155 us (0.84)
  waiting for transfers between devices: 97.3 us -> 34.1 us
  local copies, waits for them, and re-layouts: 12.4 us -> 28.3 us
  Pallas kernels: 55.5 us -> 67.7 us
  starting transfers between devices: 16.2 us -> 22.5 us
    ppermute x9 -> x28, waiting for transfers between devices: 81.8 us -> 18.6 us  [the longest x4 11.2 us: per_device(): landed.append(lax.ppermute(last, 'head', across))]
    unnamed x36 -> x52, local copies, waits for them, and re-layouts: 11.6 us -> 27.5 us
    pallas_call x5 -> x8, Pallas kernels: 35.5 us -> 46.4 us  [project_rows(): pl.pallas_call(project_kernel, grid_spec=pltpu.PrefetchScalarGridSpec(num...]
    ppermute x9 -> x28, starting transfers between devices: 5.6 us -> 11.9 us  [the longest x24 6.12 us: project(): return (mine, [lax.ppermute(piece, 'head', cores) for piece in theirs])]
    pallas_call x4 -> x8, Pallas kernels: 8.62 us -> 9.96 us  [the longest x4 6.18 us: finish_rows(): pl.pallas_call(functools.partial(finish_kernel, len(arrived)), grid=(1,),...]
  transfers between devices with their start and end apart: 19 -> 38, of which waited for: 7 -> 21; matrix products, arithmetic and copies ran while one was open for 0% -> 0% of each run, Pallas kernels for 19% -> 36%
where the time goes in v2:
time: 155 us
  Pallas kernels  67.7 us (44%)
  waiting for transfers between devices  34.1 us (22%)
  local copies, waits for them, and re-layouts  28.3 us (18%)
  starting transfers between devices  22.5 us (15%)
    pallas_call x8, Pallas kernels, project_rows(): pl.pallas_call(project_kernel, grid_spec=pltpu.PrefetchScalarGridSpec(num...  46.4 us
    unnamed x52, local copies, waits for them, and re-layouts  27.5 us
    ppermute x6, waiting for transfers between devices, incoming_states(): landed = lax.ppermute(value, 'seq', along)  11.9 us
    ppermute x4, waiting for transfers between devices, per_device(): landed.append(lax.ppermute(last, 'head', across))  11.2 us
    ppermute x24, waiting for transfers between devices, project(): return (mine, [lax.ppermute(piece, 'head', cores) for piece in theirs])  7.45 us
    pallas_call x2, Pallas kernels, inside_part(): pl.pallas_call(inside_kernel, grid_spec=pltpu.PrefetchScalarGridSpec(num_...  6.57 us
    pallas_call x4, Pallas kernels, finish_rows(): pl.pallas_call(functools.partial(finish_kernel, len(arrived)), grid=(1,),...  6.18 us
    ppermute x24, starting transfers between devices, project(): return (mine, [lax.ppermute(piece, 'head', cores) for piece in theirs])  6.12 us
  transfers between devices with their start and end apart: 38, of which 21 were waited for; matrix products, arithmetic and copies ran while one was open for 0% of the time, Pallas kernels for 36%

profile of v2, /device:TPU:24, one launch (start us, length us, event | category | flops | bytes accessed | tf_op | source)
XLA Modules:
  0.0 154.6 jit_solution(5888333399947233742)
XLA Ops:
  1.0 1.8 %copy-done.7 = bf16[1024,1024]{1,0:T(8,128)(2,1)S(1)} copy-done((bf16[1024,1024]{1,0:T(8,128)(2,1)S(1)}, bf16[1024,1024]{1,0:T(8,128)(2,1)}, u32[]{:S(2)}) %copy-start.7) | copy-done | bytes 2097176
  2.8 1.6 %copy-done.10 = bf16[1024,1024]{1,0:T(8,128)(2,1)S(1)} copy-done((bf16[1024,1024]{1,0:T(8,128)(2,1)S(1)}, bf16[1024,1024]{1,0:T(8,128)(2,1)}, u32[]{:S(2)}) %copy-start.10) | copy-done | bytes 2097176
  4.4 4.7 %shard_map.64 = (f32[4,136,128]{2,1,0:T(8,128)S(1)}, f32[4,136,128]{2,1,0:T(8,128)S(1)}, f32[4,8,128,128]{3,2,1,0:T(8,128)S(1)}, f32[1024,8]{1,0:T(8,128)S(1)}) custom-call(s32[1]{0:T(128)} %bitcast.2.odd_ref, f32[1024,8]{1,0:T(8,128)S(1)} %copy.12.rate_ref, bf16[1024,1024]{1,0:T(8,128)(2,1)S(1)} %copy-done.7, bf16[1024,1024]{1,0:T(8,128)(2,1)S(1)} %copy-done.10), custom_call_target="tpu_custom_call" | custom-call | flops 1 | bytes 1 | tf_op jit(solution)/shard_map/pallas_call | solution.py:112
  13.9 1.6 %copy-done.8 = bf16[1024,1024]{1,0:T(8,128)(2,1)S(1)} copy-done((bf16[1024,1024]{1,0:T(8,128)(2,1)S(1)}, bf16[1024,1024]{1,0:T(8,128)(2,1)}, u32[]{:S(2)}) %copy-start.8) | copy-done | bytes 2097176
  15.5 1.6 %copy-done.11 = bf16[1024,1024]{1,0:T(8,128)(2,1)S(1)} copy-done((bf16[1024,1024]{1,0:T(8,128)(2,1)S(1)}, bf16[1024,1024]{1,0:T(8,128)(2,1)}, u32[]{:S(2)}) %copy-start.11) | copy-done | bytes 2097176
  17.1 1.6 %copy-done.16 = f32[4,8,128,128]{3,2,1,0:T(8,128)S(1)} copy-done((f32[4,8,128,128]{3,2,1,0:T(8,128)S(1)}, f32[4,8,128,128]{3,2,1,0:T(8,128)}, u32[]{:S(2)}) %copy-start.16) | copy-done | bytes 2097176
  18.6 3.3 %shard_map.65.refs_1_.refs_5_ = f32[512,1024]{1,0:T(8,128)S(1)} custom-call(s32[1]{0:T(128)} %bitcast.7.first_ref, f32[1024,8]{1,0:T(8,128)S(1)} %copy.12.rate_ref, bf16[1024,1024]{1,0:T(8,128)(2,1)S(1)} %copy-done, bf16[1024,1024]{1,0:T(8,128)(2,1)S(1)} %copy-done.8, bf16[1024,1024]{1,0:T(8,128)(2,1)S(1)} %copy-done.11, f32[4,8,128,128]{3,2,1,0:T(8,128)S(1)} %copy-done.16, ...), custom_call_target="tpu_custom_call" | custom-call | flops 1 | bytes 1 | tf_op jit(solution)/shard_map/pallas_call | solution.py:165
  30.5 11.9 %collective-permute-done.3 = f32[2,128,128]{2,1,0:T(8,128)S(1)} collective-permute-done((f32[2,128,128]{2,1,0:T(8,128)S(1)}, f32[2,128,128]{2,1,0:T(8,128)S(1)}, u32[]{:S(2)}, u32[]{:S(2)}) %collective-permute-start.3) | collective-permute-done | bytes 131104 | tf_op jit(solution)/shard_map/ppermute | solution.py:342
  42.4 1.6 %collective-permute-start.8 = (f32[2,128,128]{2,1,0:T(8,128)S(1)}, f32[2,128,128]{2,1,0:T(8,128)S(1)}, u32[]{:S(2)}, u32[]{:S(2)}) collective-permute-start(f32[2,128,128]{2,1,0:T(8,128)S(1)} %get-tuple-element.87), channel_id=1, source_target_pairs={{0,4},{4,0},{8,12},{12,8},{16,20},{20,16},{24,28},{28,24},{1,5},{5... | collective-permute-start | bytes 393224 | tf_op jit(solution)/shard_map/ppermute | solution.py:349
  45.4 2.0 %collective-permute-done.8 = f32[2,128,128]{2,1,0:T(8,128)S(1)} collective-permute-done((f32[2,128,128]{2,1,0:T(8,128)S(1)}, f32[2,128,128]{2,1,0:T(8,128)S(1)}, u32[]{:S(2)}, u32[]{:S(2)}) %collective-permute-start.8) | collective-permute-done | bytes 131104 | tf_op jit(solution)/shard_map/ppermute | solution.py:349
  47.4 1.6 %collective-permute-done.9 = f32[2,128,128]{2,1,0:T(8,128)S(1)} collective-permute-done((f32[2,128,128]{2,1,0:T(8,128)S(1)}, f32[2,128,128]{2,1,0:T(8,128)S(1)}, u32[]{:S(2)}, u32[]{:S(2)}) %collective-permute-start.9) | collective-permute-done | bytes 131104 | tf_op jit(solution)/shard_map/ppermute | solution.py:349
  49.1 3.4 %copy-done.1 = bf16[1024,4096]{1,0:T(8,128)(2,1)S(1)} copy-done((bf16[1024,4096]{1,0:T(8,128)(2,1)S(1)}, bf16[1024,4096]{1,0:T(8,128)(2,1)}, u32[]{:S(2)}) %copy-start.1) | copy-done | bytes 8388632
  52.5 5.7 %shard_map.66 = (f32[16,4096]{1,0:T(8,128)S(1)}, f32[16,4096]{1,0:T(8,128)S(1)}, f32[16,4096]{1,0:T(8,128)S(1)}, f32[16,4096]{1,0:T(8,128)S(1)}, f32[64,4096]{1,0:T(8,128)S(1)}) custom-call(s32[4]{0:T(128)S(1)} %add_add_fusion.1.place_ref, bf16[1024,1024]{1,0:T(8,128)(2,1)S(1)} %copy-done, f32[512,1024]{1,0:T(8,128)S(1)} %copy-done.6, ...), custom_call_target="tpu_custom_call" | custom-call | flops 1 | bytes 1 | tf_op jit(solution)/shard_map/pallas_call | solution.py:244
  61.0 1.6 %collective-permute-start.22 = (f32[64,4096]{1,0:T(8,128)S(1)}, f32[64,4096]{1,0:T(8,128)S(1)}, u32[]{:S(2)}, u32[]{:S(2)}) collective-permute-start(f32[64,4096]{1,0:T(8,128)S(1)} %shard_map.67.refs_11_), channel_id=1, source_target_pairs={{0,2},{1,3},{2,0},{3,1},{4,6},{5,7},{6,4},{7,5},{8,10},{9,11},{10,... | collective-permute-start | bytes 3145736 | tf_op jit(solution)/shard_map/ppermute | solution.py:389
  62.5 3.4 %copy-done.2 = bf16[1024,4096]{1,0:T(8,128)(2,1)S(1)} copy-done((bf16[1024,4096]{1,0:T(8,128)(2,1)S(1)}, bf16[1024,4096]{1,0:T(8,128)(2,1)}, u32[]{:S(2)}) %copy-start.2) | copy-done | bytes 8388632
  65.9 5.7 %shard_map.68 = (f32[16,4096]{1,0:T(8,128)S(1)}, f32[16,4096]{1,0:T(8,128)S(1)}, f32[16,4096]{1,0:T(8,128)S(1)}, f32[16,4096]{1,0:T(8,128)S(1)}, f32[64,4096]{1,0:T(8,128)S(1)}) custom-call(s32[4]{0:T(128)S(1)} %add_add_fusion.1.place_ref, bf16[1024,1024]{1,0:T(8,128)(2,1)S(1)} %copy-done, f32[512,1024]{1,0:T(8,128)S(1)} %copy-done.6, ...), custom_call_target="tpu_custom_call" | custom-call | flops 1 | bytes 1 | tf_op jit(solution)/shard_map/pallas_call | solution.py:244
  75.4 5.7 %shard_map.70 = (f32[16,4096]{1,0:T(8,128)S(1)}, f32[16,4096]{1,0:T(8,128)S(1)}, f32[16,4096]{1,0:T(8,128)S(1)}, f32[16,4096]{1,0:T(8,128)S(1)}, f32[64,4096]{1,0:T(8,128)S(1)}) custom-call(s32[4]{0:T(128)S(1)} %add_add_fusion.1.place_ref, bf16[1024,1024]{1,0:T(8,128)(2,1)S(1)} %copy-done, f32[512,1024]{1,0:T(8,128)S(1)} %copy-done.6, ...), custom_call_target="tpu_custom_call" | custom-call | flops 1 | bytes 1 | tf_op jit(solution)/shard_map/pallas_call | solution.py:244
  83.8 2.9 %collective-permute-done.22.refs_4_.refs_0_ = f32[64,4096]{1,0:T(8,128)S(1)} collective-permute-done((f32[64,4096]{1,0:T(8,128)S(1)}, f32[64,4096]{1,0:T(8,128)S(1)}, u32[]{:S(2)}, u32[]{:S(2)}) %collective-permute-start.22) | collective-permute-done | bytes 1048608 | tf_op jit(solution)/shard_map/ppermute | solution.py:389
  88.1 1.8 %collective-permute-start.28 = (f32[64,4096]{1,0:T(8,128)}, f32[64,4096]{1,0:T(8,128)}, u32[]{:S(2)}, u32[]{:S(2)}) collective-permute-start(f32[64,4096]{1,0:T(8,128)} %shard_map.71.refs_11_), channel_id=1, source_target_pairs={{0,2},{1,3},{2,0},{3,1},{4,6},{5,7},{6,4},{7,5},{8,10},{9,11},{10,... | collective-permute-start | bytes 3145736 | tf_op jit(solution)/shard_map/ppermute | solution.py:389
  89.9 6.8 %shard_map.72 = (f32[16,4096]{1,0:T(8,128)S(1)}, f32[16,4096]{1,0:T(8,128)}, f32[16,4096]{1,0:T(8,128)}, f32[16,4096]{1,0:T(8,128)}, f32[64,4096]{1,0:T(8,128)S(1)}) custom-call(s32[4]{0:T(128)S(1)} %add_add_fusion.1.place_ref, bf16[1024,1024]{1,0:T(8,128)(2,1)S(1)} %copy-done, f32[512,1024]{1,0:T(8,128)S(1)} %copy-done.6, bf16[1024,1024]{1,0:T(8,128)(2,1)S(1)} %copy-done.3, ...), custom_call_target="tpu_custom_call" | custom-call | flops 1 | bytes 1 | tf_op jit(solution)/shard_map/pallas_call | solution.py:244
  101.5 7.8 %collective-permute-done.27.refs_4_.refs_0_ = f32[64,4096]{1,0:T(8,128)} collective-permute-done((f32[64,4096]{1,0:T(8,128)}, f32[64,4096]{1,0:T(8,128)}, u32[]{:S(2)}, u32[]{:S(2)}) %collective-permute-start.27) | collective-permute-done | bytes 1048608 | tf_op jit(solution)/shard_map/ppermute | solution.py:389
  111.9 1.7 %copy-done.9 = bf16[1024,1024]{1,0:T(8,128)(2,1)S(1)} copy-done((bf16[1024,1024]{1,0:T(8,128)(2,1)S(1)}, bf16[1024,1024]{1,0:T(8,128)(2,1)}, u32[]{:S(2)}) %copy-start.9) | copy-done | bytes 2097176
  113.6 1.6 %copy-done.12 = bf16[1024,1024]{1,0:T(8,128)(2,1)S(1)} copy-done((bf16[1024,1024]{1,0:T(8,128)(2,1)S(1)}, bf16[1024,1024]{1,0:T(8,128)(2,1)}, u32[]{:S(2)}) %copy-start.12) | copy-done | bytes 2097176
  116.3 1.6 %copy-done.17 = f32[4,8,128,128]{3,2,1,0:T(8,128)S(1)} copy-done((f32[4,8,128,128]{3,2,1,0:T(8,128)S(1)}, f32[4,8,128,128]{3,2,1,0:T(8,128)}, u32[]{:S(2)}) %copy-start.17) | copy-done | bytes 2097176
  117.9 3.3 %shard_map.74.refs_1_.refs_5_ = f32[512,1024]{1,0:T(8,128)S(1)} custom-call(s32[1]{0:T(128)} %bitcast.4.first_ref, f32[1024,8]{1,0:T(8,128)S(1)} %copy-done.14, bf16[1024,1024]{1,0:T(8,128)(2,1)S(1)} %copy-done, bf16[1024,1024]{1,0:T(8,128)(2,1)S(1)} %copy-done.9, bf16[1024,1024]{1,0:T(8,128)(2,1)S(1)} %copy-done.12, f32[4,8,128,128]{3,2,1,0:T(8,128)S(1)} %copy-done.17, ...), custom_call_target="tpu_custom_call" | custom-call | flops 1 | bytes 1 | tf_op jit(solution)/shard_map/pallas_call | solution.py:165
  121.2 1.9 %collective-permute-start.29 = (f32[64,4096]{1,0:T(8,128)S(1)}, f32[64,4096]{1,0:T(8,128)S(1)}, u32[]{:S(2)}, u32[]{:S(2)}) collective-permute-start(f32[64,4096]{1,0:T(8,128)S(1)} %shard_map.73.after_ref.refs_11_), channel_id=1, source_target_pairs={{0,2},{1,3},{2,0},{3,1},{4,6},{5,7},{6,4},{7,5},{8,10},{9,11},{10,... | collective-permute-start | bytes 3145736 | tf_op jit(solution)/shard_map/ppermute | solution.py:389
  123.0 5.6 %shard_map.76 = (f32[32,4096]{1,0:T(8,128)S(1)}, f32[32,4096]{1,0:T(8,128)S(1)}, f32[64,4096]{1,0:T(8,128)S(1)}) custom-call(s32[4]{0:T(128)S(1)} %add_add_fusion.place_ref, bf16[1024,1024]{1,0:T(8,128)(2,1)S(1)} %copy-done, f32[512,1024]{1,0:T(8,128)S(1)} %shard_map.74.refs_1_.refs_5_, bf16[1024,1024]{1,0:T(8,128)(2,1)S(1)} %copy-done.4, ...), custom_call_target="tpu_custom_call" | custom-call | flops 1 | bytes 1 | tf_op jit(solution)/shard_map/pallas_call | solution.py:244
  129.2 5.6 %shard_map.77 = (f32[32,4096]{1,0:T(8,128)S(1)}, f32[32,4096]{1,0:T(8,128)S(1)}, f32[64,4096]{1,0:T(8,128)S(1)}) custom-call(s32[4]{0:T(128)S(1)} %add_add_fusion.place_ref, bf16[1024,1024]{1,0:T(8,128)(2,1)S(1)} %copy-done, f32[512,1024]{1,0:T(8,128)S(1)} %shard_map.74.refs_1_.refs_5_, bf16[1024,1024]{1,0:T(8,128)(2,1)S(1)} %copy-done.4, ...), custom_call_target="tpu_custom_call" | custom-call | flops 1 | bytes 1 | tf_op jit(solution)/shard_map/pallas_call | solution.py:244
  135.4 5.8 %shard_map.78 = (f32[32,4096]{1,0:T(8,128)S(1)}, f32[32,4096]{1,0:T(8,128)S(1)}, f32[64,4096]{1,0:T(8,128)S(1)}) custom-call(s32[4]{0:T(128)S(1)} %add_add_fusion.place_ref, bf16[1024,1024]{1,0:T(8,128)(2,1)S(1)} %copy-done, f32[512,1024]{1,0:T(8,128)S(1)} %shard_map.74.refs_1_.refs_5_, bf16[1024,1024]{1,0:T(8,128)(2,1)S(1)} %copy-done.4, ...), custom_call_target="tpu_custom_call" | custom-call | flops 1 | bytes 1 | tf_op jit(solution)/shard_map/pallas_call | solution.py:244
  141.2 5.6 %shard_map.75 = (f32[32,4096]{1,0:T(8,128)S(1)}, f32[32,4096]{1,0:T(8,128)S(1)}, f32[64,4096]{1,0:T(8,128)S(1)}) custom-call(s32[4]{0:T(128)S(1)} %add_add_fusion.place_ref, bf16[1024,1024]{1,0:T(8,128)(2,1)S(1)} %copy-done, f32[512,1024]{1,0:T(8,128)S(1)} %shard_map.74.refs_1_.refs_5_, bf16[1024,1024]{1,0:T(8,128)(2,1)S(1)} %copy-done.4, ...), custom_call_target="tpu_custom_call" | custom-call | flops 1 | bytes 1 | tf_op jit(solution)/shard_map/pallas_call | solution.py:244
  148.9 2.2 %shard_map.80.refs_3_ = bf16[256,4096]{1,0:T(8,128)(2,1)} custom-call(f32[64,4096]{1,0:T(8,128)S(1)} %get-tuple-element.69.refs_11_.own_ref, f32[64,4096]{1,0:T(8,128)} %collective-permute-done.27.refs_4_.refs_0_, f32[32,4096]{1,0:T(8,128)S(1)} %collective-permute-done.34.refs_1_, ...), custom_call_target="tpu_custom_call", output_to_operand_aliasing={{}: (4, {})} | custom-call | flops 1 | bytes 1 | tf_op jit(solution)/shard_map/pallas_call | solution.py:306
  151.1 2.2 %shard_map.81.refs_3_ = bf16[256,4096]{1,0:T(8,128)(2,1)} custom-call(f32[64,4096]{1,0:T(8,128)S(1)} %get-tuple-element.70.own_ref, f32[64,4096]{1,0:T(8,128)} %collective-permute-done.28.refs_11_.refs_0_, f32[32,4096]{1,0:T(8,128)S(1)} %collective-permute-done.32.refs_1_, ...), custom_call_target="tpu_custom_call", output_to_operand_aliasing={{}: (4, {})} | custom-call | flops 1 | bytes 1 | tf_op jit(solution)/shard_map/pallas_call | solution.py:306
  (132 shorter events, 39.3 us)
Async XLA Ops:
  11.8 11.5 %collective-permute-start = (f32[2,136,128]{2,1,0:T(8,128)}, f32[2,136,128]{2,1,0:T(8,128)}, u32[]{:S(2)}, u32[]{:S(2)}) collective-permute-start(f32[2,136,128]{2,1,0:T(8,128)} %get-tuple-element.91), channel_id=1, source_target_pairs={{0,4},{4,0},{8,12},{12,8},{16,20},{20,16},{24,28},{28,24},{1,5},{5... | collective-permute-start | bytes 417800 | tf_op jit(solution)/shard_map/ppermute | solution.py:326
  13.3 10.0 %collective-permute-start.4 = (f32[2,136,128]{2,1,0:T(8,128)}, f32[2,136,128]{2,1,0:T(8,128)}, u32[]{:S(2)}, u32[]{:S(2)}) collective-permute-start(f32[2,136,128]{2,1,0:T(8,128)} %get-tuple-element.92), channel_id=1, source_target_pairs={{0,4},{4,0},{8,12},{12,8},{16,20},{20,16},{24,28},{28,24},{1,5},{5... | collective-permute-start | bytes 417800 | tf_op jit(solution)/shard_map/ppermute | solution.py:326
  26.8 2.2 %collective-permute-start.6 = (f32[2,128,128]{2,1,0:T(8,128)S(1)}, f32[2,128,128]{2,1,0:T(8,128)S(1)}, u32[]{:S(2)}, u32[]{:S(2)}) collective-permute-start(f32[2,128,128]{2,1,0:T(8,128)S(1)} %multiply_add_fusion.2), channel_id=1, source_target_pairs={{8,16},{12,20},{9,17},{13,21},{10,18},{14,22},{11,19},{15,23}} | collective-permute-start | bytes 393224 | tf_op jit(solution)/shard_map/ppermute | solution.py:342
  27.7 14.7 %collective-permute-start.3 = (f32[2,128,128]{2,1,0:T(8,128)S(1)}, f32[2,128,128]{2,1,0:T(8,128)S(1)}, u32[]{:S(2)}, u32[]{:S(2)}) collective-permute-start(f32[2,128,128]{2,1,0:T(8,128)S(1)} %get-tuple-element.77), channel_id=1, source_target_pairs={{16,24},{20,28},{17,25},{21,29},{18,26},{22,30},{19,27},{23,31}} | collective-permute-start | bytes 393224 | tf_op jit(solution)/shard_map/ppermute | solution.py:342
  29.0 14.9 %collective-permute-start.7 = (f32[2,128,128]{2,1,0:T(8,128)S(1)}, f32[2,128,128]{2,1,0:T(8,128)S(1)}, u32[]{:S(2)}, u32[]{:S(2)}) collective-permute-start(f32[2,128,128]{2,1,0:T(8,128)S(1)} %get-tuple-element.79), channel_id=1, source_target_pairs={{16,24},{20,28},{17,25},{21,29},{18,26},{22,30},{19,27},{23,31}} | collective-permute-start | bytes 393224 | tf_op jit(solution)/shard_map/ppermute | solution.py:342
  42.4 5.0 %collective-permute-start.8 = (f32[2,128,128]{2,1,0:T(8,128)S(1)}, f32[2,128,128]{2,1,0:T(8,128)S(1)}, u32[]{:S(2)}, u32[]{:S(2)}) collective-permute-start(f32[2,128,128]{2,1,0:T(8,128)S(1)} %get-tuple-element.87), channel_id=1, source_target_pairs={{0,4},{4,0},{8,12},{12,8},{16,20},{20,16},{24,28},{28,24},{1,5},{5... | collective-permute-start | bytes 393224 | tf_op jit(solution)/shard_map/ppermute | solution.py:349
  44.0 5.0 %collective-permute-start.9 = (f32[2,128,128]{2,1,0:T(8,128)S(1)}, f32[2,128,128]{2,1,0:T(8,128)S(1)}, u32[]{:S(2)}, u32[]{:S(2)}) collective-permute-start(f32[2,128,128]{2,1,0:T(8,128)S(1)} %get-tuple-element.85), channel_id=1, source_target_pairs={{0,4},{4,0},{8,12},{12,8},{16,20},{20,16},{24,28},{28,24},{1,5},{5... | collective-permute-start | bytes 393224 | tf_op jit(solution)/shard_map/ppermute | solution.py:349
  58.2 1.9 %collective-permute-start.11 = (f32[16,4096]{1,0:T(8,128)S(1)}, f32[16,4096]{1,0:T(8,128)S(1)}, u32[]{:S(2)}, u32[]{:S(2)}) collective-permute-start(f32[16,4096]{1,0:T(8,128)S(1)} %get-tuple-element.47), channel_id=1, source_target_pairs={{0,1},{1,0},{2,3},{3,2},{4,5},{5,4},{6,7},{7,6},{8,9},{9,8},{10,11... | collective-permute-start | bytes 786440 | tf_op jit(solution)/shard_map/ppermute | solution.py:376
  58.7 1.8 %collective-permute-start.12 = (f32[16,4096]{1,0:T(8,128)S(1)}, f32[16,4096]{1,0:T(8,128)S(1)}, u32[]{:S(2)}, u32[]{:S(2)}) collective-permute-start(f32[16,4096]{1,0:T(8,128)S(1)} %get-tuple-element.48), channel_id=1, source_target_pairs={{0,1},{1,0},{2,3},{3,2},{4,5},{5,4},{6,7},{7,6},{8,9},{9,8},{10,11... | collective-permute-start | bytes 786440 | tf_op jit(solution)/shard_map/ppermute | solution.py:376
  58.8 2.1 %collective-permute-start.13 = (f32[16,4096]{1,0:T(8,128)S(1)}, f32[16,4096]{1,0:T(8,128)S(1)}, u32[]{:S(2)}, u32[]{:S(2)}) collective-permute-start(f32[16,4096]{1,0:T(8,128)S(1)} %get-tuple-element.49), channel_id=1, source_target_pairs={{0,1},{1,0},{2,3},{3,2},{4,5},{5,4},{6,7},{7,6},{8,9},{9,8},{10,11... | collective-permute-start | bytes 786440 | tf_op jit(solution)/shard_map/ppermute | solution.py:376
  61.0 25.8 %collective-permute-start.22 = (f32[64,4096]{1,0:T(8,128)S(1)}, f32[64,4096]{1,0:T(8,128)S(1)}, u32[]{:S(2)}, u32[]{:S(2)}) collective-permute-start(f32[64,4096]{1,0:T(8,128)S(1)} %shard_map.67.refs_11_), channel_id=1, source_target_pairs={{0,2},{1,3},{2,0},{3,1},{4,6},{5,7},{6,4},{7,5},{8,10},{9,11},{10,... | collective-permute-start | bytes 3145736 | tf_op jit(solution)/shard_map/ppermute | solution.py:389
  71.7 1.9 %collective-permute-start.15 = (f32[16,4096]{1,0:T(8,128)S(1)}, f32[16,4096]{1,0:T(8,128)S(1)}, u32[]{:S(2)}, u32[]{:S(2)}) collective-permute-start(f32[16,4096]{1,0:T(8,128)S(1)} %get-tuple-element.52), channel_id=1, source_target_pairs={{0,1},{1,0},{2,3},{3,2},{4,5},{5,4},{6,7},{7,6},{8,9},{9,8},{10,11... | collective-permute-start | bytes 786440 | tf_op jit(solution)/shard_map/ppermute | solution.py:376
  72.2 1.8 %collective-permute-start.16 = (f32[16,4096]{1,0:T(8,128)S(1)}, f32[16,4096]{1,0:T(8,128)S(1)}, u32[]{:S(2)}, u32[]{:S(2)}) collective-permute-start(f32[16,4096]{1,0:T(8,128)S(1)} %get-tuple-element.53), channel_id=1, source_target_pairs={{0,1},{1,0},{2,3},{3,2},{4,5},{5,4},{6,7},{7,6},{8,9},{9,8},{10,11... | collective-permute-start | bytes 786440 | tf_op jit(solution)/shard_map/ppermute | solution.py:376
  72.2 2.1 %collective-permute-start.17 = (f32[16,4096]{1,0:T(8,128)S(1)}, f32[16,4096]{1,0:T(8,128)S(1)}, u32[]{:S(2)}, u32[]{:S(2)}) collective-permute-start(f32[16,4096]{1,0:T(8,128)S(1)} %get-tuple-element.54), channel_id=1, source_target_pairs={{0,1},{1,0},{2,3},{3,2},{4,5},{5,4},{6,7},{7,6},{8,9},{9,8},{10,11... | collective-permute-start | bytes 786440 | tf_op jit(solution)/shard_map/ppermute | solution.py:376
  81.3 1.9 %collective-permute-start.19 = (f32[16,4096]{1,0:T(8,128)S(1)}, f32[16,4096]{1,0:T(8,128)S(1)}, u32[]{:S(2)}, u32[]{:S(2)}) collective-permute-start(f32[16,4096]{1,0:T(8,128)S(1)} %get-tuple-element.57), channel_id=1, source_target_pairs={{0,1},{1,0},{2,3},{3,2},{4,5},{5,4},{6,7},{7,6},{8,9},{9,8},{10,11... | collective-permute-start | bytes 786440 | tf_op jit(solution)/shard_map/ppermute | solution.py:376
  81.7 1.8 %collective-permute-start.20 = (f32[16,4096]{1,0:T(8,128)S(1)}, f32[16,4096]{1,0:T(8,128)S(1)}, u32[]{:S(2)}, u32[]{:S(2)}) collective-permute-start(f32[16,4096]{1,0:T(8,128)S(1)} %get-tuple-element.58), channel_id=1, source_target_pairs={{0,1},{1,0},{2,3},{3,2},{4,5},{5,4},{6,7},{7,6},{8,9},{9,8},{10,11... | collective-permute-start | bytes 786440 | tf_op jit(solution)/shard_map/ppermute | solution.py:376
  81.8 2.0 %collective-permute-start.21 = (f32[16,4096]{1,0:T(8,128)S(1)}, f32[16,4096]{1,0:T(8,128)S(1)}, u32[]{:S(2)}, u32[]{:S(2)}) collective-permute-start(f32[16,4096]{1,0:T(8,128)S(1)} %get-tuple-element.59), channel_id=1, source_target_pairs={{0,1},{1,0},{2,3},{3,2},{4,5},{5,4},{6,7},{7,6},{8,9},{9,8},{10,11... | collective-permute-start | bytes 786440 | tf_op jit(solution)/shard_map/ppermute | solution.py:376
  82.7 26.6 %collective-permute-start.27 = (f32[64,4096]{1,0:T(8,128)}, f32[64,4096]{1,0:T(8,128)}, u32[]{:S(2)}, u32[]{:S(2)}) collective-permute-start(f32[64,4096]{1,0:T(8,128)} %shard_map.69.refs_11_), channel_id=1, source_target_pairs={{0,2},{1,3},{2,0},{3,1},{4,6},{5,7},{6,4},{7,5},{8,10},{9,11},{10,... | collective-permute-start | bytes 3145736 | tf_op jit(solution)/shard_map/ppermute | solution.py:389
  88.1 46.9 %collective-permute-start.28 = (f32[64,4096]{1,0:T(8,128)}, f32[64,4096]{1,0:T(8,128)}, u32[]{:S(2)}, u32[]{:S(2)}) collective-permute-start(f32[64,4096]{1,0:T(8,128)} %shard_map.71.refs_11_), channel_id=1, source_target_pairs={{0,2},{1,3},{2,0},{3,1},{4,6},{5,7},{6,4},{7,5},{8,10},{9,11},{10,... | collective-permute-start | bytes 3145736 | tf_op jit(solution)/shard_map/ppermute | solution.py:389
  97.7 1.9 %collective-permute-start.23 = (f32[16,4096]{1,0:T(8,128)S(1)}, f32[16,4096]{1,0:T(8,128)S(1)}, u32[]{:S(2)}, u32[]{:S(2)}) collective-permute-start(f32[16,4096]{1,0:T(8,128)S(1)} %get-tuple-element.61), channel_id=1, source_target_pairs={{0,1},{1,0},{2,3},{3,2},{4,5},{5,4},{6,7},{7,6},{8,9},{9,8},{10,11... | collective-permute-start | bytes 786440 | tf_op jit(solution)/shard_map/ppermute | solution.py:376
  97.7 2.2 %collective-permute-start.24 = (f32[16,4096]{1,0:T(8,128)}, f32[16,4096]{1,0:T(8,128)}, u32[]{:S(2)}, u32[]{:S(2)}) collective-permute-start(f32[16,4096]{1,0:T(8,128)} %get-tuple-element.62), channel_id=1, source_target_pairs={{0,1},{1,0},{2,3},{3,2},{4,5},{5,4},{6,7},{7,6},{8,9},{9,8},{10,11... | collective-permute-start | bytes 786440 | tf_op jit(solution)/shard_map/ppermute | solution.py:376
  98.2 2.1 %collective-permute-start.25 = (f32[16,4096]{1,0:T(8,128)}, f32[16,4096]{1,0:T(8,128)}, u32[]{:S(2)}, u32[]{:S(2)}) collective-permute-start(f32[16,4096]{1,0:T(8,128)} %get-tuple-element.63), channel_id=1, source_target_pairs={{0,1},{1,0},{2,3},{3,2},{4,5},{5,4},{6,7},{7,6},{8,9},{9,8},{10,11... | collective-permute-start | bytes 786440 | tf_op jit(solution)/shard_map/ppermute | solution.py:376
  99.6 1.9 %collective-permute-start.26 = (f32[16,4096]{1,0:T(8,128)}, f32[16,4096]{1,0:T(8,128)}, u32[]{:S(2)}, u32[]{:S(2)}) collective-permute-start(f32[16,4096]{1,0:T(8,128)} %get-tuple-element.64), channel_id=1, source_target_pairs={{0,1},{1,0},{2,3},{3,2},{4,5},{5,4},{6,7},{7,6},{8,9},{9,8},{10,11... | collective-permute-start | bytes 786440 | tf_op jit(solution)/shard_map/ppermute | solution.py:376
  121.2 32.5 %collective-permute-start.29 = (f32[64,4096]{1,0:T(8,128)S(1)}, f32[64,4096]{1,0:T(8,128)S(1)}, u32[]{:S(2)}, u32[]{:S(2)}) collective-permute-start(f32[64,4096]{1,0:T(8,128)S(1)} %shard_map.73.after_ref.refs_11_), channel_id=1, source_target_pairs={{0,2},{1,3},{2,0},{3,1},{4,6},{5,7},{6,4},{7,5},{8,10},{9,11},{10,... | collective-permute-start | bytes 3145736 | tf_op jit(solution)/shard_map/ppermute | solution.py:389
  128.6 18.2 %collective-permute-start.36 = (f32[32,4096]{1,0:T(8,128)S(1)}, f32[32,4096]{1,0:T(8,128)S(1)}, u32[]{:S(2)}, u32[]{:S(2)}) collective-permute-start(f32[32,4096]{1,0:T(8,128)S(1)} %get-tuple-element.75), channel_id=1, source_target_pairs={{0,1},{1,0},{2,3},{3,2},{4,5},{5,4},{6,7},{7,6},{8,9},{9,8},{10,11... | collective-permute-start | bytes 1572872 | tf_op jit(solution)/shard_map/ppermute | solution.py:376
  128.7 18.3 %collective-permute-start.37 = (f32[32,4096]{1,0:T(8,128)S(1)}, f32[32,4096]{1,0:T(8,128)S(1)}, u32[]{:S(2)}, u32[]{:S(2)}) collective-permute-start(f32[32,4096]{1,0:T(8,128)S(1)} %get-tuple-element.76), channel_id=1, source_target_pairs={{0,1},{1,0},{2,3},{3,2},{4,5},{5,4},{6,7},{7,6},{8,9},{9,8},{10,11... | collective-permute-start | bytes 1572872 | tf_op jit(solution)/shard_map/ppermute | solution.py:376
  134.8 12.7 %collective-permute-start.34 = (f32[32,4096]{1,0:T(8,128)S(1)}, f32[32,4096]{1,0:T(8,128)S(1)}, u32[]{:S(2)}, u32[]{:S(2)}) collective-permute-start(f32[32,4096]{1,0:T(8,128)S(1)} %get-tuple-element.73), channel_id=1, source_target_pairs={{0,1},{1,0},{2,3},{3,2},{4,5},{5,4},{6,7},{7,6},{8,9},{9,8},{10,11... | collective-permute-start | bytes 1572872 | tf_op jit(solution)/shard_map/ppermute | solution.py:376
  135.0 12.6 %collective-permute-start.35 = (f32[32,4096]{1,0:T(8,128)S(1)}, f32[32,4096]{1,0:T(8,128)S(1)}, u32[]{:S(2)}, u32[]{:S(2)}) collective-permute-start(f32[32,4096]{1,0:T(8,128)S(1)} %get-tuple-element.74), channel_id=1, source_target_pairs={{0,1},{1,0},{2,3},{3,2},{4,5},{5,4},{6,7},{7,6},{8,9},{9,8},{10,11... | collective-permute-start | bytes 1572872 | tf_op jit(solution)/shard_map/ppermute | solution.py:376
  146.9 4.2 %collective-permute-start.32 = (f32[32,4096]{1,0:T(8,128)S(1)}, f32[32,4096]{1,0:T(8,128)S(1)}, u32[]{:S(2)}, u32[]{:S(2)}) collective-permute-start(f32[32,4096]{1,0:T(8,128)S(1)} %get-tuple-element.71), channel_id=1, source_target_pairs={{0,1},{1,0},{2,3},{3,2},{4,5},{5,4},{6,7},{7,6},{8,9},{9,8},{10,11... | collective-permute-start | bytes 1572872 | tf_op jit(solution)/shard_map/ppermute | solution.py:376
  147.0 4.1 %collective-permute-start.33 = (f32[32,4096]{1,0:T(8,128)S(1)}, f32[32,4096]{1,0:T(8,128)S(1)}, u32[]{:S(2)}, u32[]{:S(2)}) collective-permute-start(f32[32,4096]{1,0:T(8,128)S(1)} %get-tuple-element.72), channel_id=1, source_target_pairs={{0,1},{1,0},{2,3},{3,2},{4,5},{5,4},{6,7},{7,6},{8,9},{9,8},{10,11... | collective-permute-start | bytes 1572872 | tf_op jit(solution)/shard_map/ppermute | solution.py:376
  147.5 6.2 %collective-permute-start.30 = (f32[32,4096]{1,0:T(8,128)S(1)}, f32[32,4096]{1,0:T(8,128)S(1)}, u32[]{:S(2)}, u32[]{:S(2)}) collective-permute-start(f32[32,4096]{1,0:T(8,128)S(1)} %get-tuple-element.66), channel_id=1, source_target_pairs={{0,1},{1,0},{2,3},{3,2},{4,5},{5,4},{6,7},{7,6},{8,9},{9,8},{10,11... | collective-permute-start | bytes 1572872 | tf_op jit(solution)/shard_map/ppermute | solution.py:376
  147.6 6.1 %collective-permute-start.31 = (f32[32,4096]{1,0:T(8,128)S(1)}, f32[32,4096]{1,0:T(8,128)S(1)}, u32[]{:S(2)}, u32[]{:S(2)}) collective-permute-start(f32[32,4096]{1,0:T(8,128)S(1)} %get-tuple-element.67), channel_id=1, source_target_pairs={{0,1},{1,0},{2,3},{3,2},{4,5},{5,4},{6,7},{7,6},{8,9},{9,8},{10,11... | collective-permute-start | bytes 1572872 | tf_op jit(solution)/shard_map/ppermute | solution.py:376
  (31 other events, 135.4 us)

commit v3 on v0

v3 whole, which is shorter than its diff:
```python
import functools

import jax
import jax.numpy as jnp
from jax import lax
from jax.experimental import pallas as pl
from jax.experimental.pallas import tpu as pltpu
from jax.sharding import PartitionSpec as P

HEAD_DIM = 128
MIB = 1024 * 1024
ROW_GROUPS = 4
OWN_GROUPS = 2
CHAIN_PARTS = 2
CORE_PIECES = 4
OWN_PIECES = 2
DEPTH = 2
TILE = 1024
STREAM_MIB = 32
KERNEL_MIB = 32
SHORT = pl.CostEstimate(flops=1, bytes_accessed=1, transcendentals=0)
F32 = jnp.float32
BF16 = jnp.bfloat16


def head_columns(head):
    return slice(head * HEAD_DIM, (head + 1) * HEAD_DIM)


def split_pair(value):
    high = value.astype(BF16)
    low = (value - high.astype(F32)).astype(BF16)
    return jnp.concatenate([high, low], axis=1)


def fold_pair(value):
    return value[:, :HEAD_DIM] + value[:, HEAD_DIM:]


def lower_triangle(size):
    rows = lax.broadcasted_iota(jnp.int32, (size, size), 0)
    columns = lax.broadcasted_iota(jnp.int32, (size, size), 1)
    return rows >= columns


def split_three(value):
    high = value.astype(BF16).astype(F32)
    rest = value - high
    middle = rest.astype(BF16).astype(F32)
    return jnp.concatenate([high, middle, rest - middle], axis=0).astype(BF16)


def fold_three(value):
    count = value.shape[1] // 3
    return value[:, :count] + value[:, count:2 * count] + value[:, 2 * count:]


def running_sum(rates):
    ones = lower_triangle(rates.shape[1]).astype(F32).astype(BF16)
    return fold_three(lax.dot_general(
        ones, split_three(rates), (((1,), (1,)), ((), ())), preferred_element_type=F32
    ))


def running_sum_rows(rates):
    ones = lower_triangle(rates.shape[1]).astype(F32).astype(BF16)
    count = rates.shape[0]
    value = lax.dot_general(
        split_three(rates), ones, (((1,), (1,)), ((), ())), preferred_element_type=F32
    )
    return value[:count] + value[count:2 * count] + value[2 * count:]


def in_hbm(*arrays):
    return [pltpu.with_memory_space_constraint(array, pltpu.HBM) for array in arrays]


def params(mib=KERNEL_MIB):
    return pltpu.CompilerParams(vmem_limit_bytes=mib * MIB)


def states_kernel(side_ref, rate_ref, key_hbm, value_hbm, *refs):
    message_refs = refs[:CHAIN_PARTS]
    start_hbm, keys, values, starts, key_sem, value_sem, start_sem = refs[CHAIN_PARTS:]
    blocks, half = starts.shape[:2]
    width = keys.shape[1]
    size = keys.shape[0] // blocks
    per_part = half // CHAIN_PARTS
    columns = pl.ds(pl.multiple_of(side_ref[0] * width, width), width)
    rows = [slice(block * size, (block + 1) * size) for block in range(blocks)]
    loads = [
        (pltpu.make_async_copy(key_hbm.at[at, columns], keys.at[at], key_sem.at[block]),
         pltpu.make_async_copy(value_hbm.at[at, columns], values.at[at], value_sem.at[block]))
        for block, at in enumerate(rows)
    ]
    stores = [
        pltpu.make_async_copy(starts.at[block], start_hbm.at[block], start_sem.at[block])
        for block in range(blocks)
    ]
    for load in [load for pair in loads[:2] for load in pair]:
        load.start()
    starts[0] = jnp.zeros_like(starts[0])
    stores[0].start()
    rates = jnp.where(side_ref[0] == 1, rate_ref[half:, :], rate_ref[:half, :])
    lead = jnp.zeros((1, half), F32)
    for block, at in enumerate(rows):
        running = running_sum(rates[:, at])
        total = running[-1:, :]
        fade = jnp.exp(total - running)
        block_decay = jnp.exp(total)
        lead = lead + total
        for load in loads[block]:
            load.wait()
        for load in loads[block + 2] if block + 2 < blocks else ():
            load.start()
        for head in range(half):
            of_head = head_columns(head)
            scaled = values[at, of_head].astype(F32) * fade[:, head:head + 1]
            gained = fold_pair(lax.dot_general(
                keys[at, of_head], split_pair(scaled), (((0,), (0,)), ((), ())),
                preferred_element_type=F32
            ))
            state = block_decay[:, head:head + 1] * starts[block, head] + gained
            if block + 1 < blocks:
                starts[block + 1, head] = state
            else:
                message_refs[head // per_part][head % per_part, :HEAD_DIM] = state
        if block + 1 < blocks:
            stores[block + 1].start()
    through = jnp.exp(lead)
    for head in range(half):
        message_refs[head // per_part][head % per_part, HEAD_DIM:] = jnp.broadcast_to(
            through[:, head:head + 1], (8, HEAD_DIM))
    for store in stores:
        store.wait()


def local_states(side, rates, key_vectors, value_vectors, block_len):
    tokens, features = key_vectors.shape
    half = features // HEAD_DIM // 2
    blocks = tokens // block_len
    message = jax.ShapeDtypeStruct((half // CHAIN_PARTS, HEAD_DIM + 8, HEAD_DIM), F32)
    starts = pltpu.HBM((blocks, half, HEAD_DIM, HEAD_DIM), F32)
    vmem, far = pl.BlockSpec(memory_space=pltpu.VMEM), pl.BlockSpec(memory_space=pl.ANY)
    *messages, starts = pl.pallas_call(
        states_kernel,
        in_specs=[pl.BlockSpec(memory_space=pltpu.SMEM), vmem, far, far],
        out_specs=[vmem] * CHAIN_PARTS + [far],
        out_shape=[message] * CHAIN_PARTS + [starts],
        scratch_shapes=[
            pltpu.VMEM((tokens, features // 2), BF16),
            pltpu.VMEM((tokens, features // 2), BF16),
            pltpu.VMEM((blocks, half, HEAD_DIM, HEAD_DIM), F32),
        ] + [pltpu.SemaphoreType.DMA((blocks,))] * 3,
        compiler_params=params(STREAM_MIB),
        cost_estimate=SHORT,
    )(side, *in_hbm(rates, key_vectors, value_vectors))
    return messages, starts


def inside_kernel(place_ref, rate_ref, query_hbm, key_hbm, value_hbm, keep_hbm, send_hbm, after_ref,
                  *refs):
    del after_ref
    queries, keys, values, keeps, sends, parts, load_sem, store_sem = refs[-8:]
    outs = refs[:-8]
    heads, tokens = rate_ref.shape
    count, half = keeps.shape[:2]
    size = queries.shape[0] // count
    is_odd = place_ref[count] == 1
    rows = [slice(block * size, (block + 1) * size) for block in range(count)]
    loads = [[] for _ in rows]
    for block, at in enumerate(rows):
        place = place_ref[block]
        far = pl.ds(pl.multiple_of(place * size, size), size)
        pairs = [(query_hbm.at[far], queries.at[at]), (key_hbm.at[far], keys.at[at]),
                 (value_hbm.at[far], values.at[at]), (keep_hbm.at[place], keeps.at[block]),
                 (send_hbm.at[place], sends.at[block])]
        for i, (source, target) in enumerate(pairs):
            loads[block].append(pltpu.make_async_copy(source, target, load_sem.at[block, i]))
    for load in loads[0]:
        load.start()
    stores = [
        pltpu.make_async_copy(parts.at[at], outs[2 * block], store_sem.at[block])
        for block, at in enumerate(rows)
    ]
    causal = lower_triangle(size)
    for block, at in enumerate(rows):
        begin = place_ref[block] * size
        rates = rate_ref[:, pl.ds(pl.multiple_of(begin, size), size)]
        ahead = (lax.broadcasted_iota(jnp.int32, (8, tokens), 1) < begin).astype(F32)
        lead = fold_three(lax.dot_general(
            ahead.astype(BF16), split_three(rate_ref[...]), (((1,), (1,)), ((), ())),
            preferred_element_type=F32,
        ))
        running = running_sum(rates)
        running_rows = running_sum_rows(rates)
        fade = jnp.exp(running)
        outs[2 * block + 1][...] = jnp.exp(running + lead[:1])
        for load in loads[block]:
            load.wait()
        for load in loads[block + 1] if block + 1 < count else ():
            load.start()
        for head in range(heads):
            of_head = head_columns(head)
            side, slot = head // half, head % half
            kept, sent = keeps[block, slot], sends[block, slot]
            start = jnp.where(is_odd, kept, sent) if side else jnp.where(is_odd, sent, kept)
            query = queries[at, of_head]
            scores = lax.dot_general(
                query, keys[at, of_head], (((1,), (1,)), ((), ())), preferred_element_type=F32
            )
            spread = running[:, head:head + 1] - running_rows[head:head + 1, :]
            decay = jnp.exp(jnp.where(causal, spread, -1e30))
            weights = (scores * decay).astype(BF16)
            inside = jnp.dot(weights, values[at, of_head], preferred_element_type=F32)
            carried = fold_pair(jnp.dot(query, split_pair(start), preferred_element_type=F32))
            parts[at, of_head] = inside + carried * fade[:, head:head + 1]
        stores[block].start()
    for store in stores:
        store.wait()


def inside_part(place, rates, queries, key_vectors, value_vectors, starts, block_len, after):
    count = place.shape[0] - 1
    features = queries.shape[1]
    heads = features // HEAD_DIM
    vmem, far = pl.BlockSpec(memory_space=pltpu.VMEM), pl.BlockSpec(memory_space=pl.ANY)
    rows = pltpu.VMEM((count * block_len, features), BF16)
    state = pltpu.VMEM((count, heads // 2, HEAD_DIM, HEAD_DIM), F32)
    return pl.pallas_call(
        inside_kernel,
        in_specs=[pl.BlockSpec(memory_space=pltpu.SMEM), vmem] + [far] * 6,
        out_specs=[far, vmem] * count,
        out_shape=[
            pltpu.HBM((block_len, features), F32), pltpu.HBM((block_len, heads), F32),
        ] * count,
        scratch_shapes=[rows, rows, rows, state, state,
                        pltpu.VMEM((count * block_len, features), F32),
                        pltpu.SemaphoreType.DMA((count, 5)), pltpu.SemaphoreType.DMA((count,))],
        compiler_params=params(STREAM_MIB),
        cost_estimate=SHORT,
    )(place, *in_hbm(rates, queries, key_vectors, value_vectors, *starts, after))


def project_kernel(first_row, block_len, pieces, place_ref, query_hbm, gate_hbm, weight_hbm, part_0,
                   lead_0, part_1, lead_1, after_ref, *refs):
    del after_ref
    states, refs = refs[:2 * CHAIN_PARTS], refs[2 * CHAIN_PARTS:]
    outs, refs = refs[:pieces + 1], refs[pieces + 1:]
    queries, parts, gates, leads, incoming, weight, hidden, result = refs[:8]
    row_sem, state_sem, weight_sem, out_sem = refs[8:]
    rows, width = outs[-1].shape
    features = queries.shape[1]
    heads = features // HEAD_DIM
    half = heads // 2
    per_part = half // CHAIN_PARTS
    tile = width // weight_sem.shape[0]
    is_odd = place_ref[2] == 1

    loads = []
    for which, (part_hbm, lead_hbm) in enumerate(((part_0, lead_0), (part_1, lead_1))):
        whole = pl.ds(pl.multiple_of(place_ref[which] * block_len + first_row, rows), rows)
        group = slice(first_row, first_row + rows)
        at = slice(which * rows, (which + 1) * rows)
        pairs = [(query_hbm.at[whole], queries.at[at]), (part_hbm.at[group], parts.at[at]),
                 (gate_hbm.at[whole], gates.at[at]), (lead_hbm.at[group], leads.at[at])]
        loads += [pltpu.make_async_copy(source, target, row_sem.at[which, i])
                  for i, (source, target) in enumerate(pairs)]
    loads += [pltpu.make_async_copy(ref, incoming.at[i], state_sem.at[i])
              for i, ref in enumerate(states)]
    columns = [slice(at, at + tile) for at in range(0, width, tile)]
    weights = [
        pltpu.make_async_copy(weight_hbm.at[:, at], weight.at[:, at], weight_sem.at[i])
        for i, at in enumerate(columns)
    ]
    for load in loads + weights[:1]:
        load.start()
    for load in loads:
        load.wait()
    for load in weights[1:]:
        load.start()
    for head in range(heads):
        at = head_columns(head)
        side, place = head // half, head % half
        part, slot = place // per_part, place % per_part
        kept, got = incoming[part, slot], incoming[CHAIN_PARTS + part, slot]
        state = jnp.where(is_odd, kept, got) if side else jnp.where(is_odd, got, kept)
        carried = fold_pair(jnp.dot(queries[:, at], split_pair(state), preferred_element_type=F32))
        attended = parts[:, at] + carried * leads[:, head:head + 1]
        mean = jnp.mean(attended * attended, axis=1, keepdims=True)
        gate = gates[:, at].astype(F32)
        normed = attended * lax.rsqrt(mean + 1e-6)
        hidden[:, at] = (normed * (gate / (1.0 + jnp.exp(-gate)))).astype(BF16)
    stores = []
    for i, at in enumerate(columns):
        weights[i].wait()
        result[:, at] = jnp.dot(hidden[...], weight[:, at], preferred_element_type=F32)
        begin = 0
        for j, out in enumerate(outs):
            size = out.shape[0]
            store = pltpu.make_async_copy(
                result.at[begin:begin + size, at], out.at[:, at], out_sem.at[j, i])
            store.start()
            stores.append(store)
            begin += size
    for store in stores:
        store.wait()


def project_rows(place, rows, first_row, block_len, queries, parts, gate_input, kept, got,
                 out_weight, after, pieces):
    features = queries.shape[1]
    width = out_weight.shape[1]
    tiles = max(1, width // TILE)
    sizes = [rows // pieces] * pieces + [rows]
    far = pl.BlockSpec(memory_space=pl.ANY)
    dma = pltpu.SemaphoreType.DMA
    return pl.pallas_call(
        functools.partial(project_kernel, first_row, block_len, pieces),
        in_specs=[pl.BlockSpec(memory_space=pltpu.SMEM)] + [far] * (8 + 2 * CHAIN_PARTS),
        out_specs=[far] * len(sizes),
        out_shape=[jax.ShapeDtypeStruct((size, width), F32) for size in sizes],
        scratch_shapes=[
            pltpu.VMEM((2 * rows, features), BF16),
            pltpu.VMEM((2 * rows, features), F32),
            pltpu.VMEM((2 * rows, features), BF16),
            pltpu.VMEM((2 * rows, features // HEAD_DIM), F32),
            pltpu.VMEM((2 * CHAIN_PARTS, *kept[0].shape), F32),
            pltpu.VMEM(out_weight.shape, BF16),
            pltpu.VMEM((2 * rows, features), BF16),
            pltpu.VMEM((2 * rows, width), F32),
            dma((2, 4)), dma((2 * CHAIN_PARTS,)), dma((tiles,)), dma((len(sizes), tiles)),
        ],
        compiler_params=params(),
        cost_estimate=SHORT,
    )(place, *in_hbm(queries, gate_input, out_weight, *parts[0], *parts[1], after), *kept, *got)


def add_kernel(own_ref, *refs):
    pieces, out_ref = refs[:-2], refs[-1]
    at = 0
    for ref in pieces:
        size = ref.shape[0]
        out_ref[at:at + size] = own_ref[at:at + size] + ref[...]
        at += size


def add_pieces(own, pieces, after):
    whole = pl.BlockSpec(own.shape, lambda: (0, 0))
    return pl.pallas_call(
        add_kernel,
        in_specs=[whole] + [pl.BlockSpec(piece.shape, lambda: (0, 0)) for piece in pieces]
        + [pl.BlockSpec(memory_space=pl.ANY)],
        out_specs=whole,
        out_shape=jax.ShapeDtypeStruct(own.shape, F32),
        compiler_params=params(),
        cost_estimate=SHORT,
    )(own, *pieces, *in_hbm(after))


def finish_kernel(arrivals, own_ref, *refs):
    out_ref = refs[-1]
    arrived, pieces = refs[:arrivals], refs[arrivals:-2]
    at = 0
    for ref in pieces:
        size = ref.shape[0]
        total = own_ref[at:at + size] + ref[...]
        for other in arrived:
            total = total + other[at:at + size]
        out_ref[at:at + size] = total.astype(out_ref.dtype)
        at += size


def finish_rows(group, arrived, own, own_group, pieces, result, block_len):
    rows, width = arrived[0].shape
    whole = pl.BlockSpec((rows, width), lambda i: (0, 0))
    alias = {}
    if result is None:
        result = own
    else:
        alias = {1 + len(arrived) + len(pieces): 0}
    return pl.pallas_call(
        functools.partial(finish_kernel, len(arrived)),
        grid=(1,),
        in_specs=[pl.BlockSpec((rows, width), lambda i: (own_group, 0))] + [whole] * len(arrived)
        + [pl.BlockSpec(piece.shape, lambda i: (0, 0)) for piece in pieces]
        + [pl.BlockSpec(memory_space=pl.ANY)],
        out_specs=pl.BlockSpec((rows, width), lambda i: (group, 0)),
        out_shape=jax.ShapeDtypeStruct((block_len, width), BF16),
        input_output_aliases=alias,
        compiler_params=params(),
        cost_estimate=SHORT,
    )(own, *arrived, *pieces, result)


def hop_kernel(hops, odd_ref, *refs):
    landed, (kept_ref, got_ref, after_ref, value_ref) = refs[:hops], refs[hops:]
    del after_ref
    is_odd = odd_ref[0] == 1
    for slot in range(value_ref.shape[0]):
        kept, got = kept_ref[slot], got_ref[slot]
        early, late = jnp.where(is_odd, got, kept), jnp.where(is_odd, kept, got)
        late_decay = late[HEAD_DIM:HEAD_DIM + 1]
        value = early[:HEAD_DIM]
        if landed:
            before = landed[0][slot]
            for ref in landed[1:]:
                before = before + ref[slot]
            value = early[HEAD_DIM:HEAD_DIM + 1] * before + value
        value_ref[slot] = late_decay * value + late[:HEAD_DIM]


def hop_states(odd, landed, kept, got, after):
    vmem = pl.BlockSpec(memory_space=pltpu.VMEM)
    return pl.pallas_call(
        functools.partial(hop_kernel, len(landed)),
        in_specs=[pl.BlockSpec(memory_space=pltpu.SMEM)] + [vmem] * (len(landed) + 2)
        + [pl.BlockSpec(memory_space=pl.ANY)],
        out_specs=vmem,
        out_shape=jax.ShapeDtypeStruct((kept.shape[0], HEAD_DIM, HEAD_DIM), F32),
        compiler_params=params(),
        cost_estimate=SHORT,
    )(odd, *landed, kept, got, *in_hbm(after))


def entering_kernel(hops, odd_ref, *refs):
    landed, (kept_ref, got_ref, after_ref, keep_ref, back_ref) = refs[:hops], refs[hops:]
    del after_ref
    is_odd = odd_ref[0] == 1
    for slot in range(keep_ref.shape[0]):
        before = landed[0][slot]
        for ref in landed[1:]:
            before = before + ref[slot]
        first = jnp.where(is_odd, got_ref[slot], kept_ref[slot])
        after = first[HEAD_DIM:HEAD_DIM + 1] * before + first[:HEAD_DIM]
        keep_ref[slot] = jnp.where(is_odd, after, before)
        back_ref[slot] = jnp.where(is_odd, before, after)


def entering_states(odd, landed, kept, got, after):
    shape = jax.ShapeDtypeStruct(landed[0].shape, F32)
    vmem = pl.BlockSpec(memory_space=pltpu.VMEM)
    return pl.pallas_call(
        functools.partial(entering_kernel, len(landed)),
        in_specs=[pl.BlockSpec(memory_space=pltpu.SMEM)] + [vmem] * (len(landed) + 2)
        + [pl.BlockSpec(memory_space=pl.ANY)],
        out_specs=[vmem, vmem],
        out_shape=[shape, shape],
        compiler_params=params(),
        cost_estimate=SHORT,
    )(odd, *landed, kept, got, *in_hbm(after))


def incoming_states(odd, kept, got, after, meanwhile):
    count = lax.axis_size("seq")
    swap = [(i, i ^ 1) for i in range(count)]
    parts = range(CHAIN_PARTS)
    landed = [[] for _ in parts]
    for hop in range(count // 2 - 1):
        along = [(2 * hop, 2 * hop + 2), (2 * hop + 1, 2 * hop + 3)]
        for i in parts:
            value = hop_states(odd, landed[i], kept[i], got[i], after)
            landed[i].append(lax.ppermute(value, "seq", along))
        if hop == count // 2 - 3:
            for work in meanwhile:
                after = work(value)
    keep, back = [], []
    for i in parts:
        mine, other = entering_states(odd, landed[i], kept[i], got[i], after)
        keep.append(mine)
        back.append(lax.ppermute(other, "seq", swap))
    return keep, back


def per_device(queries, key_vectors, value_vectors, gate_input, log_decay, out_weight):
    tokens = queries.shape[0]
    count = lax.axis_size("head")
    chips = count // 2
    block_len = tokens // count
    sizes = [block_len // ROW_GROUPS] * ROW_GROUPS
    firsts = [sum(sizes[:i]) for i in range(len(sizes))]
    index = lax.axis_index("head")
    chip, core = index // 2, index % 2
    place_in_seq = lax.axis_index("seq")
    odd = (place_in_seq % 2).reshape(1).astype(jnp.int32)
    rates = log_decay.T
    swap = [(i, i ^ 1) for i in range(lax.axis_size("seq"))]

    sent, sent_starts = local_states(1 - odd, rates, key_vectors, value_vectors, block_len)
    met = [lax.ppermute(piece, "seq", swap) for piece in sent]
    kept, kept_starts = local_states(odd, rates, key_vectors, value_vectors, block_len)

    def parts_of(target, after):
        place = jnp.stack([2 * target + 1 - core, 2 * target + core, odd[0]]).astype(jnp.int32)
        outs = inside_part(place, rates, queries, key_vectors, value_vectors,
                           (kept_starts, sent_starts), block_len, after)
        return outs[:2], outs[2:]

    def project(target, parts, group, after, pieces):
        place = jnp.stack([2 * target + 1 - core, 2 * target + core, odd[0]]).astype(jnp.int32)
        *theirs, mine = project_rows(
            place, sizes[group], firsts[group], block_len, queries, parts, gate_input, keep, got,
            out_weight, after, pieces)
        return mine, [lax.ppermute(piece, "head", cores) for piece in theirs]

    cores = [(i, i ^ 1) for i in range(count)]
    targets = [(chip + step) % chips for step in range(1, chips)]
    parts = []

    def inside_of(target, after):
        parts.append(parts_of(target, after))
        return parts[-1][1][1]

    keep, got = incoming_states(
        odd, kept, met, kept_starts, [functools.partial(inside_of, target) for target in targets])
    last = keep[0]
    landed, own, result = [last, last], [], None
    arrived = [[] for _ in sizes]
    for group in range(len(sizes)):
        for step, target in enumerate(targets):
            across = [(i, ((i // 2 + step + 1) % chips) * 2 + i % 2) for i in range(count)]
            mine, pieces = project(target, parts[step], group, last, CORE_PIECES)
            last = add_pieces(mine, pieces, landed[-DEPTH])
            landed.append(lax.ppermute(last, "head", across))
            arrived[group].append(landed[-1])
    own_parts = parts_of(chip, last)
    ratio = ROW_GROUPS // OWN_GROUPS
    sizes = [block_len // OWN_GROUPS] * OWN_GROUPS
    firsts = [sum(sizes[:i]) for i in range(len(sizes))]
    for group in range(len(sizes)):
        if group == len(sizes) - 1:
            last = landed[-2]
        own.append(project(chip, own_parts, group, last, OWN_PIECES * ratio))
        last = own[-1][0]
    for group in range(len(arrived)):
        mine, pieces = own[group // ratio]
        place = group % ratio
        result = finish_rows(group, arrived[group], mine, place,
                             pieces[place * OWN_PIECES:(place + 1) * OWN_PIECES], result, block_len)
    return result


def solution(mesh):
    placed = (
        P("seq", "head"),
        P("seq", "head"),
        P("seq", "head"),
        P("seq", "head"),
        P("seq", "head"),
        P("head", None),
    )
    return jax.shard_map(
        per_device, mesh=mesh, in_specs=placed, out_specs=P(("seq", "head"), None), check_vma=False
    )
```

time: 278 us -> 141 us (0.51)
  waiting for transfers between devices: 170 us -> 42.6 us
  Pallas kernels: 0 us -> 67.7 us
  matrix products: 34.3 us -> 0 us
  starting transfers between devices: 0.04 us -> 21.5 us
  other arithmetic: 18 us -> 0.15 us
  blocking collectives: 17.2 us -> 0 us
  local copies, waits for them, and re-layouts: 21.1 us -> 6.87 us
  between operations: 14.2 us -> 0.41 us
    reduce_scatter x1 -> x0, waiting for transfers between devices: 126 us -> none  [per_device(): lax.psum_scatter(jnp.dot(hidden, out_weight, preferred_element_type=jnp.f...]
    pallas_call x0 -> x26, Pallas kernels: none -> 67.7 us  [the longest x6 39 us: project_rows(): pl.pallas_call(functools.partial(project_kernel, first_row, block_len, pi...]
    all_gather x1 -> x0, waiting for transfers between devices: 43.9 us -> none  [entering(): pieces = jax.tree.map(lambda part: lax.all_gather(part, axis), value)]
    ppermute x0 -> x38, waiting for transfers between devices: none -> 42.6 us  [the longest x4 25.6 us: per_device(): landed.append(lax.ppermute(last, 'head', across))]
    dot_general x4 -> x0, matrix products: 34.3 us -> none  [the longest x1 15.8 us: per_device(): jnp.dot(hidden, out_weight, preferred_element_type=jnp.float32)]
    ppermute x0 -> x38, starting transfers between devices: none -> 21.5 us  [the longest x4 5.59 us: per_device(): landed.append(lax.ppermute(last, 'head', across))]
    unnamed x1 -> x0, blocking collectives: 17.2 us -> none
    select_n x7 -> x0, other arithmetic: 8.22 us -> none  [hop(): jnp.where(position < mine, new, old)]
  transfers between devices with their start and end apart: 2 -> 38, of which waited for: 2 -> 22; matrix products, arithmetic and copies ran while one was open for 4% -> 0% of each run, Pallas kernels for 0% -> 41%
where the time goes in v3:
time: 141 us; the launch traced here: 139 us
  Pallas kernels  67.7 us (48%)
  waiting for transfers between devices  42.6 us (30%)
  starting transfers between devices  21.5 us (15%)
  local copies, waits for them, and re-layouts  6.87 us (5%)
    pallas_call x6, Pallas kernels, project_rows(): pl.pallas_call(functools.partial(project_kernel, first_row, block_len, pi...  39 us
    ppermute x4, waiting for transfers between devices, per_device(): landed.append(lax.ppermute(last, 'head', across))  25.6 us
    pallas_call x2, Pallas kernels, inside_part(): pl.pallas_call(inside_kernel, in_specs=[pl.BlockSpec(memory_space=pltpu.S...  13.6 us
    pallas_call x2, Pallas kernels, local_states(): pl.pallas_call(states_kernel, in_specs=[pl.BlockSpec(memory_space=pltpu.S...  8.23 us
    ppermute x24, waiting for transfers between devices, project(): return (mine, [lax.ppermute(piece, 'head', cores) for piece in theirs])  7.03 us
    unnamed x30, local copies, waits for them, and re-layouts  6.87 us
    ppermute x4, starting transfers between devices, per_device(): landed.append(lax.ppermute(last, 'head', across))  5.59 us
    ppermute x24, starting transfers between devices, project(): return (mine, [lax.ppermute(piece, 'head', cores) for piece in theirs])  5.54 us
  transfers between devices with their start and end apart: 38, of which 22 were waited for; matrix products, arithmetic and copies ran while one was open for 0% of the time, Pallas kernels for 41%

profile of v3, /device:TPU:24, one launch (start us, length us, event | category | flops | bytes accessed | tf_op | source)
XLA Modules:
  0.0 139.3 jit_solution(17463170703497258996)
XLA Ops:
  0.0 4.1 %shard_map.65 = (f32[2,136,128]{2,1,0:T(8,128)S(1)}, f32[2,136,128]{2,1,0:T(8,128)S(1)}, f32[4,4,128,128]{3,2,1,0:T(8,128)}) custom-call(s32[1]{0:T(128)S(6)} %sub.21.side_ref, f32[8,1024]{1,0:T(8,128)} %bitcast.6, bf16[1024,1024]{1,0:T(8,128)(2,1)} %key_hbm.7, bf16[1024,1024]{1,0:T(8,128)(2,1)} %value_hbm.7), custom_call_target="tpu_custom_call" | custom-call | flops 1 | bytes 1 | tf_op jit(solution)/shard_map/pallas_call | solution.py:145
  4.1 1.6 %collective-permute-start = (f32[2,136,128]{2,1,0:T(8,128)S(1)}, f32[2,136,128]{2,1,0:T(8,128)S(1)}, u32[]{:S(2)}, u32[]{:S(2)}) collective-permute-start(f32[2,136,128]{2,1,0:T(8,128)S(1)} %get-tuple-element.56), channel_id=1, source_target_pairs={{0,4},{4,0},{8,12},{12,8},{16,20},{20,16},{24,28},{28,24},{1,5},{5... | collective-permute-start | bytes 417800 | tf_op jit(solution)/shard_map/ppermute | solution.py:490
  6.2 4.1 %shard_map.64 = (f32[2,136,128]{2,1,0:T(8,128)S(1)}, f32[2,136,128]{2,1,0:T(8,128)S(1)}, f32[4,4,128,128]{3,2,1,0:T(8,128)}) custom-call(s32[1]{0:T(128)} %bitcast.2.side_ref.odd_ref, f32[8,1024]{1,0:T(8,128)} %bitcast.7, bf16[1024,1024]{1,0:T(8,128)(2,1)} %key_hbm.7, bf16[1024,1024]{1,0:T(8,128)(2,1)} %value_hbm.7), custom_call_target="tpu_custom_call" | custom-call | flops 1 | bytes 1 | tf_op jit(solution)/shard_map/pallas_call | solution.py:145
  11.5 1.1 collective-permute-done.2.refs_1_.refs_2_.refs_3_.refs_4_
  14.9 6.8 %shard_map.68 = (f32[256,1024]{1,0:T(8,128)}, f32[256,8]{1,0:T(8,128)}, f32[256,1024]{1,0:T(8,128)}, f32[256,8]{1,0:T(8,128)}) custom-call(s32[3]{0:T(128)S(1)} %add_add_fusion.1.place_ref, f32[8,1024]{1,0:T(8,128)} %bitcast.8, bf16[1024,1024]{1,0:T(8,128)(2,1)} %query_hbm.15, bf16[1024,1024]{1,0:T(8,128)(2,1)} %key_hbm.7, bf16[1024,1024]{1,0:T(8,128)(2,1)} %value_hbm.7, ...), custom_call_target="tpu_custom_call" | custom-call | flops 1 | bytes 1 | tf_op jit(solution)/shard_map/pallas_call | solution.py:230
  21.8 1.3 collective-permute-start.7
  23.1 1.5 %collective-permute-start.5 = (f32[2,128,128]{2,1,0:T(8,128)S(1)}, f32[2,128,128]{2,1,0:T(8,128)S(1)}, u32[]{:S(2)}, u32[]{:S(2)}) collective-permute-start(f32[2,128,128]{2,1,0:T(8,128)S(1)} %shard_map.71), channel_id=1, source_target_pairs={{16,24},{20,28},{17,25},{21,29},{18,26},{22,30},{19,27},{23,31}} | collective-permute-start | bytes 393224 | tf_op jit(solution)/shard_map/ppermute | solution.py:463
  24.6 4.8 %collective-permute-done.7.refs_2_ = f32[2,128,128]{2,1,0:T(8,128)S(1)} collective-permute-done((f32[2,128,128]{2,1,0:T(8,128)S(1)}, f32[2,128,128]{2,1,0:T(8,128)S(1)}, u32[]{:S(2)}, u32[]{:S(2)}) %collective-permute-start.7) | collective-permute-done | bytes 131104 | tf_op jit(solution)/shard_map/ppermute | solution.py:463
  29.5 1.6 %collective-permute-start.9 = (f32[2,128,128]{2,1,0:T(8,128)S(1)}, f32[2,128,128]{2,1,0:T(8,128)S(1)}, u32[]{:S(2)}, u32[]{:S(2)}) collective-permute-start(f32[2,128,128]{2,1,0:T(8,128)S(1)} %get-tuple-element.66), channel_id=1, source_target_pairs={{0,4},{4,0},{8,12},{12,8},{16,20},{20,16},{24,28},{28,24},{1,5},{5... | collective-permute-start | bytes 393224 | tf_op jit(solution)/shard_map/ppermute | solution.py:471
  31.8 1.3 collective-permute-start.8
  33.0 1.6 %collective-permute-done.9.refs_3_ = f32[2,128,128]{2,1,0:T(8,128)S(1)} collective-permute-done((f32[2,128,128]{2,1,0:T(8,128)S(1)}, f32[2,128,128]{2,1,0:T(8,128)S(1)}, u32[]{:S(2)}, u32[]{:S(2)}) %collective-permute-start.9) | collective-permute-done | bytes 131104 | tf_op jit(solution)/shard_map/ppermute | solution.py:471
  34.6 2.1 %collective-permute-done.8.refs_2_ = f32[2,128,128]{2,1,0:T(8,128)S(1)} collective-permute-done((f32[2,128,128]{2,1,0:T(8,128)S(1)}, f32[2,128,128]{2,1,0:T(8,128)S(1)}, u32[]{:S(2)}, u32[]{:S(2)}) %collective-permute-start.8) | collective-permute-done | bytes 131104 | tf_op jit(solution)/shard_map/ppermute | solution.py:471
  36.7 6.0 %shard_map.75 = (f32[16,4096]{1,0:T(8,128)S(1)}, f32[16,4096]{1,0:T(8,128)S(1)}, f32[16,4096]{1,0:T(8,128)S(1)}, f32[16,4096]{1,0:T(8,128)S(1)}, f32[64,4096]{1,0:T(8,128)S(1)}) custom-call(s32[3]{0:T(128)S(1)} %add_add_fusion.1.place_ref, bf16[1024,1024]{1,0:T(8,128)(2,1)} %query_hbm.15, bf16[1024,1024]{1,0:T(8,128)(2,1)} %gate_hbm.11, ...), custom_call_target="tpu_custom_call" | custom-call | flops 1 | bytes 1 | tf_op jit(solution)/shard_map/pallas_call | solution.py:318
  45.6 1.6 %collective-permute-start.22 = (f32[64,4096]{1,0:T(8,128)S(1)}, f32[64,4096]{1,0:T(8,128)S(1)}, u32[]{:S(2)}, u32[]{:S(2)}) collective-permute-start(f32[64,4096]{1,0:T(8,128)S(1)} %shard_map.76.after_ref), channel_id=1, source_target_pairs={{0,2},{1,3},{2,0},{3,1},{4,6},{5,7},{6,4},{7,5},{8,10},{9,11},{10,... | collective-permute-start | bytes 3145736 | tf_op jit(solution)/shard_map/ppermute | solution.py:524
  47.2 6.0 %shard_map.77 = (f32[16,4096]{1,0:T(8,128)S(1)}, f32[16,4096]{1,0:T(8,128)S(1)}, f32[16,4096]{1,0:T(8,128)S(1)}, f32[16,4096]{1,0:T(8,128)S(1)}, f32[64,4096]{1,0:T(8,128)S(1)}) custom-call(s32[3]{0:T(128)S(1)} %add_add_fusion.1.place_ref, bf16[1024,1024]{1,0:T(8,128)(2,1)} %query_hbm.15, bf16[1024,1024]{1,0:T(8,128)(2,1)} %gate_hbm.11, ...), custom_call_target="tpu_custom_call" | custom-call | flops 1 | bytes 1 | tf_op jit(solution)/shard_map/pallas_call | solution.py:318
  57.0 6.0 %shard_map.79 = (f32[16,4096]{1,0:T(8,128)S(1)}, f32[16,4096]{1,0:T(8,128)S(1)}, f32[16,4096]{1,0:T(8,128)S(1)}, f32[16,4096]{1,0:T(8,128)S(1)}, f32[64,4096]{1,0:T(8,128)S(1)}) custom-call(s32[3]{0:T(128)S(1)} %add_add_fusion.1.place_ref, bf16[1024,1024]{1,0:T(8,128)(2,1)} %query_hbm.15, bf16[1024,1024]{1,0:T(8,128)(2,1)} %gate_hbm.11, ...), custom_call_target="tpu_custom_call" | custom-call | flops 1 | bytes 1 | tf_op jit(solution)/shard_map/pallas_call | solution.py:318
  65.7 6.0 %collective-permute-done.22.refs_4_.refs_0_ = f32[64,4096]{1,0:T(8,128)S(1)} collective-permute-done((f32[64,4096]{1,0:T(8,128)S(1)}, f32[64,4096]{1,0:T(8,128)S(1)}, u32[]{:S(2)}, u32[]{:S(2)}) %collective-permute-start.22) | collective-permute-done | bytes 1048608 | tf_op jit(solution)/shard_map/ppermute | solution.py:524
  72.7 1.6 %collective-permute-start.28 = (f32[64,4096]{1,0:T(8,128)S(1)}, f32[64,4096]{1,0:T(8,128)S(1)}, u32[]{:S(2)}, u32[]{:S(2)}) collective-permute-start(f32[64,4096]{1,0:T(8,128)S(1)} %shard_map.80.after_ref), channel_id=1, source_target_pairs={{0,2},{1,3},{2,0},{3,1},{4,6},{5,7},{6,4},{7,5},{8,10},{9,11},{10,... | collective-permute-start | bytes 3145736 | tf_op jit(solution)/shard_map/ppermute | solution.py:524
  74.3 6.5 %shard_map.81 = (f32[16,4096]{1,0:T(8,128)S(1)}, f32[16,4096]{1,0:T(8,128)}, f32[16,4096]{1,0:T(8,128)}, f32[16,4096]{1,0:T(8,128)}, f32[64,4096]{1,0:T(8,128)S(1)}) custom-call(s32[3]{0:T(128)S(1)} %add_add_fusion.1.place_ref, bf16[1024,1024]{1,0:T(8,128)(2,1)} %query_hbm.15, bf16[1024,1024]{1,0:T(8,128)(2,1)} %gate_hbm.11, bf16[1024,4096]{1,0:T(8,128)(2,1)} %weight_hbm.11, ...), custom_call_target="tpu_custom_call" | custom-call | flops 1 | bytes 1 | tf_op jit(solution)/shard_map/pallas_call | solution.py:318
  82.3 1.4 collective-permute-done.23.refs_0_
  84.3 1.3 collective-permute-done.26.refs_3_
  85.6 8.7 %collective-permute-done.27.refs_4_.refs_0_ = f32[64,4096]{1,0:T(8,128)} collective-permute-done((f32[64,4096]{1,0:T(8,128)}, f32[64,4096]{1,0:T(8,128)}, u32[]{:S(2)}, u32[]{:S(2)}) %collective-permute-start.27) | collective-permute-done | bytes 1048608 | tf_op jit(solution)/shard_map/ppermute | solution.py:524
  94.2 1.2 copy-done.13
  95.4 1.1 shard_map.82.after_ref
  97.5 6.8 %shard_map.83 = (f32[256,1024]{1,0:T(8,128)}, f32[256,8]{1,0:T(8,128)}, f32[256,1024]{1,0:T(8,128)}, f32[256,8]{1,0:T(8,128)}) custom-call(s32[3]{0:T(128)S(1)} %add_add_fusion.place_ref, f32[8,1024]{1,0:T(8,128)} %bitcast.9, bf16[1024,1024]{1,0:T(8,128)(2,1)} %query_hbm.15, bf16[1024,1024]{1,0:T(8,128)(2,1)} %key_hbm.7, bf16[1024,1024]{1,0:T(8,128)(2,1)} %value_hbm.7, ...), custom_call_target="tpu_custom_call" | custom-call | flops 1 | bytes 1 | tf_op jit(solution)/shard_map/pallas_call | solution.py:230
  104.3 7.3 %shard_map.85 = (f32[32,4096]{1,0:T(8,128)S(1)}, f32[32,4096]{1,0:T(8,128)S(1)}, f32[32,4096]{1,0:T(8,128)S(1)}, f32[32,4096]{1,0:T(8,128)S(1)}, f32[128,4096]{1,0:T(8,128)S(1)}) custom-call(s32[3]{0:T(128)S(1)} %add_add_fusion.place_ref, bf16[1024,1024]{1,0:T(8,128)(2,1)} %query_hbm.15, bf16[1024,1024]{1,0:T(8,128)(2,1)} %gate_hbm.11, ...), custom_call_target="tpu_custom_call" | custom-call | flops 1 | bytes 1 | tf_op jit(solution)/shard_map/pallas_call | solution.py:318
  112.2 1.5 %collective-permute-start.29 = (f32[64,4096]{1,0:T(8,128)S(1)}, f32[64,4096]{1,0:T(8,128)S(1)}, u32[]{:S(2)}, u32[]{:S(2)}) collective-permute-start(f32[64,4096]{1,0:T(8,128)S(1)} %copy-done.4), channel_id=1, source_target_pairs={{0,2},{1,3},{2,0},{3,1},{4,6},{5,7},{6,4},{7,5},{8,10},{9,11},{10,... | collective-permute-start | bytes 3145736 | tf_op jit(solution)/shard_map/ppermute | solution.py:524
  113.7 2.9 %collective-permute-done.28.after_ref.refs_0_ = f32[64,4096]{1,0:T(8,128)S(1)} collective-permute-done((f32[64,4096]{1,0:T(8,128)S(1)}, f32[64,4096]{1,0:T(8,128)S(1)}, u32[]{:S(2)}, u32[]{:S(2)}) %collective-permute-start.28) | collective-permute-done | bytes 1048608 | tf_op jit(solution)/shard_map/ppermute | solution.py:524
  116.6 1.0 copy-done.8
  117.6 7.3 %shard_map.84 = (f32[32,4096]{1,0:T(8,128)S(1)}, f32[32,4096]{1,0:T(8,128)S(1)}, f32[32,4096]{1,0:T(8,128)S(1)}, f32[32,4096]{1,0:T(8,128)S(1)}, f32[128,4096]{1,0:T(8,128)S(1)}) custom-call(s32[3]{0:T(128)S(1)} %add_add_fusion.place_ref, bf16[1024,1024]{1,0:T(8,128)(2,1)} %query_hbm.15, bf16[1024,1024]{1,0:T(8,128)(2,1)} %gate_hbm.11, ...), custom_call_target="tpu_custom_call" | custom-call | flops 1 | bytes 1 | tf_op jit(solution)/shard_map/pallas_call | solution.py:318
  126.9 2.3 %shard_map.87.refs_3_ = bf16[256,4096]{1,0:T(8,128)(2,1)} custom-call(f32[128,4096]{1,0:T(8,128)S(1)} %get-tuple-element.96.own_ref.refs_3_, f32[64,4096]{1,0:T(8,128)} %collective-permute-done.27.refs_4_.refs_0_, f32[32,4096]{1,0:T(8,128)S(1)} %collective-permute-done.34.refs_1_, ...), custom_call_target="tpu_custom_call", output_to_operand_aliasing={{}: (4, {})} | custom-call | flops 1 | bytes 1 | tf_op jit(solution)/shard_map/pallas_call | solution.py:382
  130.2 8.0 %collective-permute-done.29.refs_0_ = f32[64,4096]{1,0:T(8,128)S(1)} collective-permute-done((f32[64,4096]{1,0:T(8,128)S(1)}, f32[64,4096]{1,0:T(8,128)S(1)}, u32[]{:S(2)}, u32[]{:S(2)}) %collective-permute-start.29) | collective-permute-done | bytes 1048608 | tf_op jit(solution)/shard_map/ppermute | solution.py:524
  (102 shorter events, 22.8 us)
Async XLA Ops:
  4.1 6.6 %collective-permute-start = (f32[2,136,128]{2,1,0:T(8,128)S(1)}, f32[2,136,128]{2,1,0:T(8,128)S(1)}, u32[]{:S(2)}, u32[]{:S(2)}) collective-permute-start(f32[2,136,128]{2,1,0:T(8,128)S(1)} %get-tuple-element.56), channel_id=1, source_target_pairs={{0,4},{4,0},{8,12},{12,8},{16,20},{20,16},{24,28},{28,24},{1,5},{5... | collective-permute-start | bytes 417800 | tf_op jit(solution)/shard_map/ppermute | solution.py:490
  5.7 6.9 %collective-permute-start.2 = (f32[2,136,128]{2,1,0:T(8,128)S(1)}, f32[2,136,128]{2,1,0:T(8,128)S(1)}, u32[]{:S(2)}, u32[]{:S(2)}) collective-permute-start(f32[2,136,128]{2,1,0:T(8,128)S(1)} %get-tuple-element.62), channel_id=1, source_target_pairs={{0,4},{4,0},{8,12},{12,8},{16,20},{20,16},{24,28},{28,24},{1,5},{5... | collective-permute-start | bytes 417800 | tf_op jit(solution)/shard_map/ppermute | solution.py:490
  10.8 2.5 %collective-permute-start.1 = (f32[2,128,128]{2,1,0:T(8,128)S(1)}, f32[2,128,128]{2,1,0:T(8,128)S(1)}, u32[]{:S(2)}, u32[]{:S(2)}) collective-permute-start(f32[2,128,128]{2,1,0:T(8,128)S(1)} %shard_map.66), channel_id=1, source_target_pairs={{0,8},{4,12},{1,9},{5,13},{2,10},{6,14},{3,11},{7,15}} | collective-permute-start | bytes 393224 | tf_op jit(solution)/shard_map/ppermute | solution.py:463
  13.4 8.3 %collective-permute-start.6 = (f32[2,128,128]{2,1,0:T(8,128)S(1)}, f32[2,128,128]{2,1,0:T(8,128)S(1)}, u32[]{:S(2)}, u32[]{:S(2)}) collective-permute-start(f32[2,128,128]{2,1,0:T(8,128)S(1)} %shard_map.67.after_ref), channel_id=1, source_target_pairs={{8,16},{12,20},{9,17},{13,21},{10,18},{14,22},{11,19},{15,23}} | collective-permute-start | bytes 393224 | tf_op jit(solution)/shard_map/ppermute | solution.py:463
  14.1 9.0 %collective-permute-start.4 = (f32[2,128,128]{2,1,0:T(8,128)S(1)}, f32[2,128,128]{2,1,0:T(8,128)S(1)}, u32[]{:S(2)}, u32[]{:S(2)}) collective-permute-start(f32[2,128,128]{2,1,0:T(8,128)S(1)} %shard_map.70), channel_id=1, source_target_pairs={{8,16},{12,20},{9,17},{13,21},{10,18},{14,22},{11,19},{15,23}} | collective-permute-start | bytes 393224 | tf_op jit(solution)/shard_map/ppermute | solution.py:463
  21.8 7.7 %collective-permute-start.7 = (f32[2,128,128]{2,1,0:T(8,128)S(1)}, f32[2,128,128]{2,1,0:T(8,128)S(1)}, u32[]{:S(2)}, u32[]{:S(2)}) collective-permute-start(f32[2,128,128]{2,1,0:T(8,128)S(1)} %shard_map.73), channel_id=1, source_target_pairs={{16,24},{20,28},{17,25},{21,29},{18,26},{22,30},{19,27},{23,31}} | collective-permute-start | bytes 393224 | tf_op jit(solution)/shard_map/ppermute | solution.py:463
  23.1 7.9 %collective-permute-start.5 = (f32[2,128,128]{2,1,0:T(8,128)S(1)}, f32[2,128,128]{2,1,0:T(8,128)S(1)}, u32[]{:S(2)}, u32[]{:S(2)}) collective-permute-start(f32[2,128,128]{2,1,0:T(8,128)S(1)} %shard_map.71), channel_id=1, source_target_pairs={{16,24},{20,28},{17,25},{21,29},{18,26},{22,30},{19,27},{23,31}} | collective-permute-start | bytes 393224 | tf_op jit(solution)/shard_map/ppermute | solution.py:463
  29.5 5.2 %collective-permute-start.9 = (f32[2,128,128]{2,1,0:T(8,128)S(1)}, f32[2,128,128]{2,1,0:T(8,128)S(1)}, u32[]{:S(2)}, u32[]{:S(2)}) collective-permute-start(f32[2,128,128]{2,1,0:T(8,128)S(1)} %get-tuple-element.66), channel_id=1, source_target_pairs={{0,4},{4,0},{8,12},{12,8},{16,20},{20,16},{24,28},{28,24},{1,5},{5... | collective-permute-start | bytes 393224 | tf_op jit(solution)/shard_map/ppermute | solution.py:471
  31.8 5.0 %collective-permute-start.8 = (f32[2,128,128]{2,1,0:T(8,128)S(1)}, f32[2,128,128]{2,1,0:T(8,128)S(1)}, u32[]{:S(2)}, u32[]{:S(2)}) collective-permute-start(f32[2,128,128]{2,1,0:T(8,128)S(1)} %get-tuple-element.65), channel_id=1, source_target_pairs={{0,4},{4,0},{8,12},{12,8},{16,20},{20,16},{24,28},{28,24},{1,5},{5... | collective-permute-start | bytes 393224 | tf_op jit(solution)/shard_map/ppermute | solution.py:471
  42.8 1.9 %collective-permute-start.11 = (f32[16,4096]{1,0:T(8,128)S(1)}, f32[16,4096]{1,0:T(8,128)S(1)}, u32[]{:S(2)}, u32[]{:S(2)}) collective-permute-start(f32[16,4096]{1,0:T(8,128)S(1)} %get-tuple-element.69), channel_id=1, source_target_pairs={{0,1},{1,0},{2,3},{3,2},{4,5},{5,4},{6,7},{7,6},{8,9},{9,8},{10,11... | collective-permute-start | bytes 786440 | tf_op jit(solution)/shard_map/ppermute | solution.py:504
  43.4 2.1 %collective-permute-start.13 = (f32[16,4096]{1,0:T(8,128)S(1)}, f32[16,4096]{1,0:T(8,128)S(1)}, u32[]{:S(2)}, u32[]{:S(2)}) collective-permute-start(f32[16,4096]{1,0:T(8,128)S(1)} %get-tuple-element.71), channel_id=1, source_target_pairs={{0,1},{1,0},{2,3},{3,2},{4,5},{5,4},{6,7},{7,6},{8,9},{9,8},{10,11... | collective-permute-start | bytes 786440 | tf_op jit(solution)/shard_map/ppermute | solution.py:504
  45.6 26.1 %collective-permute-start.22 = (f32[64,4096]{1,0:T(8,128)S(1)}, f32[64,4096]{1,0:T(8,128)S(1)}, u32[]{:S(2)}, u32[]{:S(2)}) collective-permute-start(f32[64,4096]{1,0:T(8,128)S(1)} %shard_map.76.after_ref), channel_id=1, source_target_pairs={{0,2},{1,3},{2,0},{3,1},{4,6},{5,7},{6,4},{7,5},{8,10},{9,11},{10,... | collective-permute-start | bytes 3145736 | tf_op jit(solution)/shard_map/ppermute | solution.py:524
  53.2 1.9 %collective-permute-start.15 = (f32[16,4096]{1,0:T(8,128)S(1)}, f32[16,4096]{1,0:T(8,128)S(1)}, u32[]{:S(2)}, u32[]{:S(2)}) collective-permute-start(f32[16,4096]{1,0:T(8,128)S(1)} %get-tuple-element.74), channel_id=1, source_target_pairs={{0,1},{1,0},{2,3},{3,2},{4,5},{5,4},{6,7},{7,6},{8,9},{9,8},{10,11... | collective-permute-start | bytes 786440 | tf_op jit(solution)/shard_map/ppermute | solution.py:504
  53.8 2.1 %collective-permute-start.17 = (f32[16,4096]{1,0:T(8,128)S(1)}, f32[16,4096]{1,0:T(8,128)S(1)}, u32[]{:S(2)}, u32[]{:S(2)}) collective-permute-start(f32[16,4096]{1,0:T(8,128)S(1)} %get-tuple-element.76), channel_id=1, source_target_pairs={{0,1},{1,0},{2,3},{3,2},{4,5},{5,4},{6,7},{7,6},{8,9},{9,8},{10,11... | collective-permute-start | bytes 786440 | tf_op jit(solution)/shard_map/ppermute | solution.py:504
  63.1 2.3 %collective-permute-start.19 = (f32[16,4096]{1,0:T(8,128)S(1)}, f32[16,4096]{1,0:T(8,128)S(1)}, u32[]{:S(2)}, u32[]{:S(2)}) collective-permute-start(f32[16,4096]{1,0:T(8,128)S(1)} %get-tuple-element.79), channel_id=1, source_target_pairs={{0,1},{1,0},{2,3},{3,2},{4,5},{5,4},{6,7},{7,6},{8,9},{9,8},{10,11... | collective-permute-start | bytes 786440 | tf_op jit(solution)/shard_map/ppermute | solution.py:504
  63.5 2.0 %collective-permute-start.20 = (f32[16,4096]{1,0:T(8,128)S(1)}, f32[16,4096]{1,0:T(8,128)S(1)}, u32[]{:S(2)}, u32[]{:S(2)}) collective-permute-start(f32[16,4096]{1,0:T(8,128)S(1)} %get-tuple-element.80), channel_id=1, source_target_pairs={{0,1},{1,0},{2,3},{3,2},{4,5},{5,4},{6,7},{7,6},{8,9},{9,8},{10,11... | collective-permute-start | bytes 786440 | tf_op jit(solution)/shard_map/ppermute | solution.py:504
  63.7 2.0 %collective-permute-start.21 = (f32[16,4096]{1,0:T(8,128)S(1)}, f32[16,4096]{1,0:T(8,128)S(1)}, u32[]{:S(2)}, u32[]{:S(2)}) collective-permute-start(f32[16,4096]{1,0:T(8,128)S(1)} %get-tuple-element.81), channel_id=1, source_target_pairs={{0,1},{1,0},{2,3},{3,2},{4,5},{5,4},{6,7},{7,6},{8,9},{9,8},{10,11... | collective-permute-start | bytes 786440 | tf_op jit(solution)/shard_map/ppermute | solution.py:504
  64.5 29.7 %collective-permute-start.27 = (f32[64,4096]{1,0:T(8,128)}, f32[64,4096]{1,0:T(8,128)}, u32[]{:S(2)}, u32[]{:S(2)}) collective-permute-start(f32[64,4096]{1,0:T(8,128)} %copy-done.5), channel_id=1, source_target_pairs={{0,2},{1,3},{2,0},{3,1},{4,6},{5,7},{6,4},{7,5},{8,10},{9,11},{10,... | collective-permute-start | bytes 3145736 | tf_op jit(solution)/shard_map/ppermute | solution.py:524
  72.7 43.8 %collective-permute-start.28 = (f32[64,4096]{1,0:T(8,128)S(1)}, f32[64,4096]{1,0:T(8,128)S(1)}, u32[]{:S(2)}, u32[]{:S(2)}) collective-permute-start(f32[64,4096]{1,0:T(8,128)S(1)} %shard_map.80.after_ref), channel_id=1, source_target_pairs={{0,2},{1,3},{2,0},{3,1},{4,6},{5,7},{6,4},{7,5},{8,10},{9,11},{10,... | collective-permute-start | bytes 3145736 | tf_op jit(solution)/shard_map/ppermute | solution.py:524
  81.8 1.9 %collective-permute-start.23 = (f32[16,4096]{1,0:T(8,128)S(1)}, f32[16,4096]{1,0:T(8,128)S(1)}, u32[]{:S(2)}, u32[]{:S(2)}) collective-permute-start(f32[16,4096]{1,0:T(8,128)S(1)} %get-tuple-element.83), channel_id=1, source_target_pairs={{0,1},{1,0},{2,3},{3,2},{4,5},{5,4},{6,7},{7,6},{8,9},{9,8},{10,11... | collective-permute-start | bytes 786440 | tf_op jit(solution)/shard_map/ppermute | solution.py:504
  81.8 2.1 %collective-permute-start.24 = (f32[16,4096]{1,0:T(8,128)}, f32[16,4096]{1,0:T(8,128)S(1)}, u32[]{:S(2)}, u32[]{:S(2)}) collective-permute-start(f32[16,4096]{1,0:T(8,128)} %get-tuple-element.84), channel_id=1, source_target_pairs={{0,1},{1,0},{2,3},{3,2},{4,5},{5,4},{6,7},{7,6},{8,9},{9,8},{10,11... | collective-permute-start | bytes 786440 | tf_op jit(solution)/shard_map/ppermute | solution.py:504
  82.3 2.0 %collective-permute-start.25 = (f32[16,4096]{1,0:T(8,128)}, f32[16,4096]{1,0:T(8,128)S(1)}, u32[]{:S(2)}, u32[]{:S(2)}) collective-permute-start(f32[16,4096]{1,0:T(8,128)} %get-tuple-element.85), channel_id=1, source_target_pairs={{0,1},{1,0},{2,3},{3,2},{4,5},{5,4},{6,7},{7,6},{8,9},{9,8},{10,11... | collective-permute-start | bytes 786440 | tf_op jit(solution)/shard_map/ppermute | solution.py:504
  83.7 1.9 %collective-permute-start.26 = (f32[16,4096]{1,0:T(8,128)}, f32[16,4096]{1,0:T(8,128)}, u32[]{:S(2)}, u32[]{:S(2)}) collective-permute-start(f32[16,4096]{1,0:T(8,128)} %get-tuple-element.86), channel_id=1, source_target_pairs={{0,1},{1,0},{2,3},{3,2},{4,5},{5,4},{6,7},{7,6},{8,9},{9,8},{10,11... | collective-permute-start | bytes 786440 | tf_op jit(solution)/shard_map/ppermute | solution.py:504
  111.6 13.3 %collective-permute-start.36 = (f32[32,4096]{1,0:T(8,128)S(1)}, f32[32,4096]{1,0:T(8,128)S(1)}, u32[]{:S(2)}, u32[]{:S(2)}) collective-permute-start(f32[32,4096]{1,0:T(8,128)S(1)} %get-tuple-element.99), channel_id=1, source_target_pairs={{0,1},{1,0},{2,3},{3,2},{4,5},{5,4},{6,7},{7,6},{8,9},{9,8},{10,11... | collective-permute-start | bytes 1572872 | tf_op jit(solution)/shard_map/ppermute | solution.py:504
  111.7 13.3 %collective-permute-start.37 = (f32[32,4096]{1,0:T(8,128)S(1)}, f32[32,4096]{1,0:T(8,128)S(1)}, u32[]{:S(2)}, u32[]{:S(2)}) collective-permute-start(f32[32,4096]{1,0:T(8,128)S(1)} %get-tuple-element.100), channel_id=1, source_target_pairs={{0,1},{1,0},{2,3},{3,2},{4,5},{5,4},{6,7},{7,6},{8,9},{9,8},{10,11... | collective-permute-start | bytes 1572872 | tf_op jit(solution)/shard_map/ppermute | solution.py:504
  112.2 26.1 %collective-permute-start.29 = (f32[64,4096]{1,0:T(8,128)S(1)}, f32[64,4096]{1,0:T(8,128)S(1)}, u32[]{:S(2)}, u32[]{:S(2)}) collective-permute-start(f32[64,4096]{1,0:T(8,128)S(1)} %copy-done.4), channel_id=1, source_target_pairs={{0,2},{1,3},{2,0},{3,1},{4,6},{5,7},{6,4},{7,5},{8,10},{9,11},{10,... | collective-permute-start | bytes 3145736 | tf_op jit(solution)/shard_map/ppermute | solution.py:524
  113.7 11.8 %collective-permute-start.34 = (f32[32,4096]{1,0:T(8,128)S(1)}, f32[32,4096]{1,0:T(8,128)S(1)}, u32[]{:S(2)}, u32[]{:S(2)}) collective-permute-start(f32[32,4096]{1,0:T(8,128)S(1)} %get-tuple-element.97), channel_id=1, source_target_pairs={{0,1},{1,0},{2,3},{3,2},{4,5},{5,4},{6,7},{7,6},{8,9},{9,8},{10,11... | collective-permute-start | bytes 1572872 | tf_op jit(solution)/shard_map/ppermute | solution.py:504
  116.6 9.0 %collective-permute-start.35 = (f32[32,4096]{1,0:T(8,128)S(1)}, f32[32,4096]{1,0:T(8,128)S(1)}, u32[]{:S(2)}, u32[]{:S(2)}) collective-permute-start(f32[32,4096]{1,0:T(8,128)S(1)} %get-tuple-element.98), channel_id=1, source_target_pairs={{0,1},{1,0},{2,3},{3,2},{4,5},{5,4},{6,7},{7,6},{8,9},{9,8},{10,11... | collective-permute-start | bytes 1572872 | tf_op jit(solution)/shard_map/ppermute | solution.py:504
  124.9 4.3 %collective-permute-start.32 = (f32[32,4096]{1,0:T(8,128)S(1)}, f32[32,4096]{1,0:T(8,128)S(1)}, u32[]{:S(2)}, u32[]{:S(2)}) collective-permute-start(f32[32,4096]{1,0:T(8,128)S(1)} %get-tuple-element.94), channel_id=1, source_target_pairs={{0,1},{1,0},{2,3},{3,2},{4,5},{5,4},{6,7},{7,6},{8,9},{9,8},{10,11... | collective-permute-start | bytes 1572872 | tf_op jit(solution)/shard_map/ppermute | solution.py:504
  125.0 4.3 %collective-permute-start.33 = (f32[32,4096]{1,0:T(8,128)S(1)}, f32[32,4096]{1,0:T(8,128)S(1)}, u32[]{:S(2)}, u32[]{:S(2)}) collective-permute-start(f32[32,4096]{1,0:T(8,128)S(1)} %get-tuple-element.95), channel_id=1, source_target_pairs={{0,1},{1,0},{2,3},{3,2},{4,5},{5,4},{6,7},{7,6},{8,9},{9,8},{10,11... | collective-permute-start | bytes 1572872 | tf_op jit(solution)/shard_map/ppermute | solution.py:504
  125.5 12.8 %collective-permute-start.30 = (f32[32,4096]{1,0:T(8,128)S(1)}, f32[32,4096]{1,0:T(8,128)S(1)}, u32[]{:S(2)}, u32[]{:S(2)}) collective-permute-start(f32[32,4096]{1,0:T(8,128)S(1)} %get-tuple-element.92), channel_id=1, source_target_pairs={{0,1},{1,0},{2,3},{3,2},{4,5},{5,4},{6,7},{7,6},{8,9},{9,8},{10,11... | collective-permute-start | bytes 1572872 | tf_op jit(solution)/shard_map/ppermute | solution.py:504
  125.6 12.7 %collective-permute-start.31 = (f32[32,4096]{1,0:T(8,128)S(1)}, f32[32,4096]{1,0:T(8,128)S(1)}, u32[]{:S(2)}, u32[]{:S(2)}) collective-permute-start(f32[32,4096]{1,0:T(8,128)S(1)} %get-tuple-element.93), channel_id=1, source_target_pairs={{0,1},{1,0},{2,3},{3,2},{4,5},{5,4},{6,7},{7,6},{8,9},{9,8},{10,11... | collective-permute-start | bytes 1572872 | tf_op jit(solution)/shard_map/ppermute | solution.py:504
  (21 other events, 49.3 us)

commit v4 on v3

--- a/solution.py
+++ b/solution.py
@@ -9,11 +9,10 @@
 
 HEAD_DIM = 128
 MIB = 1024 * 1024
-ROW_GROUPS = 4
+ROW_SHARES = (4, 4, 4, 4)
 OWN_GROUPS = 2
 CHAIN_PARTS = 2
 CORE_PIECES = 4
-OWN_PIECES = 2
 DEPTH = 2
 TILE = 1024
 STREAM_MIB = 32
@@ -79,9 +78,9 @@
     return pltpu.CompilerParams(vmem_limit_bytes=mib * MIB)
 
 
-def states_kernel(side_ref, rate_ref, key_hbm, value_hbm, *refs):
+def states_kernel(side_ref, rate_hbm, key_hbm, value_hbm, *refs):
     message_refs = refs[:CHAIN_PARTS]
-    start_hbm, keys, values, starts, key_sem, value_sem, start_sem = refs[CHAIN_PARTS:]
+    start_hbm, rate_ref, keys, values, starts, rate_sem, key_sem, value_sem, start_sem = refs[CHAIN_PARTS:]
     blocks, half = starts.shape[:2]
     width = keys.shape[1]
     size = keys.shape[0] // blocks
@@ -97,10 +96,13 @@
         pltpu.make_async_copy(starts.at[block], start_hbm.at[block], start_sem.at[block])
         for block in range(blocks)
     ]
+    rate_load = pltpu.make_async_copy(rate_hbm, rate_ref, rate_sem)
+    rate_load.start()
     for load in [load for pair in loads[:2] for load in pair]:
         load.start()
     starts[0] = jnp.zeros_like(starts[0])
     stores[0].start()
+    rate_load.wait()
     rates = jnp.where(side_ref[0] == 1, rate_ref[half:, :], rate_ref[:half, :])
     lead = jnp.zeros((1, half), F32)
     for block, at in enumerate(rows):
@@ -144,13 +146,15 @@
     vmem, far = pl.BlockSpec(memory_space=pltpu.VMEM), pl.BlockSpec(memory_space=pl.ANY)
     *messages, starts = pl.pallas_call(
         states_kernel,
-        in_specs=[pl.BlockSpec(memory_space=pltpu.SMEM), vmem, far, far],
+        in_specs=[pl.BlockSpec(memory_space=pltpu.SMEM), far, far, far],
         out_specs=[vmem] * CHAIN_PARTS + [far],
         out_shape=[message] * CHAIN_PARTS + [starts],
         scratch_shapes=[
+            pltpu.VMEM(rates.shape, F32),
             pltpu.VMEM((tokens, features // 2), BF16),
             pltpu.VMEM((tokens, features // 2), BF16),
             pltpu.VMEM((blocks, half, HEAD_DIM, HEAD_DIM), F32),
+            pltpu.SemaphoreType.DMA,
         ] + [pltpu.SemaphoreType.DMA((blocks,))] * 3,
         compiler_params=params(STREAM_MIB),
         cost_estimate=SHORT,
@@ -158,11 +162,11 @@
     return messages, starts
 
 
-def inside_kernel(place_ref, rate_ref, query_hbm, key_hbm, value_hbm, keep_hbm, send_hbm, after_ref,
+def inside_kernel(place_ref, rate_hbm, query_hbm, key_hbm, value_hbm, keep_hbm, send_hbm, after_ref,
                   *refs):
     del after_ref
-    queries, keys, values, keeps, sends, parts, load_sem, store_sem = refs[-8:]
-    outs = refs[:-8]
+    rate_ref, queries, keys, values, keeps, sends, parts, rate_sem, load_sem, store_sem = refs[-10:]
+    outs = refs[:-10]
     heads, tokens = rate_ref.shape
     count, half = keeps.shape[:2]
     size = queries.shape[0] // count
@@ -177,8 +181,10 @@
                  (send_hbm.at[place], sends.at[block])]
         for i, (source, target) in enumerate(pairs):
             loads[block].append(pltpu.make_async_copy(source, target, load_sem.at[block, i]))
-    for load in loads[0]:
+    rate_load = pltpu.make_async_copy(rate_hbm, rate_ref, rate_sem)
+    for load in [rate_load] + loads[0]:
         load.start()
+    rate_load.wait()
     stores = [
         pltpu.make_async_copy(parts.at[at], outs[2 * block], store_sem.at[block])
         for block, at in enumerate(rows)
@@ -229,50 +235,94 @@
     state = pltpu.VMEM((count, heads // 2, HEAD_DIM, HEAD_DIM), F32)
     return pl.pallas_call(
         inside_kernel,
-        in_specs=[pl.BlockSpec(memory_space=pltpu.SMEM), vmem] + [far] * 6,
+        in_specs=[pl.BlockSpec(memory_space=pltpu.SMEM)] + [far] * 7,
         out_specs=[far, vmem] * count,
         out_shape=[
             pltpu.HBM((block_len, features), F32), pltpu.HBM((block_len, heads), F32),
         ] * count,
-        scratch_shapes=[rows, rows, rows, state, state,
-                        pltpu.VMEM((count * block_len, features), F32),
+        scratch_shapes=[pltpu.VMEM(rates.shape, F32), rows, rows, rows, state, state,
+                        pltpu.VMEM((count * block_len, features), F32), pltpu.SemaphoreType.DMA,
                         pltpu.SemaphoreType.DMA((count, 5)), pltpu.SemaphoreType.DMA((count,))],
         compiler_params=params(STREAM_MIB),
         cost_estimate=SHORT,
-    )(place, *in_hbm(rates, queries, key_vectors, value_vectors, *starts, after))
-
-
-def project_kernel(first_row, block_len, pieces, place_ref, query_hbm, gate_hbm, weight_hbm, part_0,
-                   lead_0, part_1, lead_1, after_ref, *refs):
-    del after_ref
-    states, refs = refs[:2 * CHAIN_PARTS], refs[2 * CHAIN_PARTS:]
-    outs, refs = refs[:pieces + 1], refs[pieces + 1:]
-    queries, parts, gates, leads, incoming, weight, hidden, result = refs[:8]
-    row_sem, state_sem, weight_sem, out_sem = refs[8:]
-    rows, width = outs[-1].shape
-    features = queries.shape[1]
-    heads = features // HEAD_DIM
-    half = heads // 2
-    per_part = half // CHAIN_PARTS
-    tile = width // weight_sem.shape[0]
-    is_odd = place_ref[2] == 1
-
+    )(place, *in_hbm(rates, queries, key_vectors, value_vectors, *starts), after)
+
+
+def row_loads(first_row, block_len, place_ref, query_hbm, gate_hbm, parts_hbm, queries, gates, parts,
+              leads, sem):
+    rows = queries.shape[0] // 2
     loads = []
-    for which, (part_hbm, lead_hbm) in enumerate(((part_0, lead_0), (part_1, lead_1))):
+    for which, (part_hbm, lead_hbm) in enumerate(parts_hbm):
         whole = pl.ds(pl.multiple_of(place_ref[which] * block_len + first_row, rows), rows)
         group = slice(first_row, first_row + rows)
         at = slice(which * rows, (which + 1) * rows)
         pairs = [(query_hbm.at[whole], queries.at[at]), (part_hbm.at[group], parts.at[at]),
                  (gate_hbm.at[whole], gates.at[at]), (lead_hbm.at[group], leads.at[at])]
-        loads += [pltpu.make_async_copy(source, target, row_sem.at[which, i])
+        loads += [pltpu.make_async_copy(source, target, sem.at[which, i])
                   for i, (source, target) in enumerate(pairs)]
-    loads += [pltpu.make_async_copy(ref, incoming.at[i], state_sem.at[i])
-              for i, ref in enumerate(states)]
+    return loads
+
+
+def bring_kernel(first_row, block_len, place_ref, query_hbm, gate_hbm, weight_hbm, part_0, lead_0,
+                 part_1, lead_1, after_ref, queries, gates, parts, leads, weight, row_sem, weight_sem):
+    del after_ref
+    loads = row_loads(first_row, block_len, place_ref, query_hbm, gate_hbm,
+                      ((part_0, lead_0), (part_1, lead_1)), queries, gates, parts, leads, row_sem)
+    loads.append(pltpu.make_async_copy(weight_hbm.at[:, :weight.shape[1]], weight, weight_sem))
+    for load in loads:
+        load.start()
+    for load in loads:
+        load.wait()
+
+
+def row_shapes(rows, features):
+    return [((2 * rows, features), BF16), ((2 * rows, features), BF16), ((2 * rows, features), F32),
+            ((2 * rows, features // HEAD_DIM), F32)]
+
+
+def bring_rows(place, rows, first_row, block_len, queries, parts, gate_input, out_weight, after):
+    features, width = out_weight.shape
+    shapes = row_shapes(rows, features) + [((features, width // TILE // 2 * TILE), BF16)]
+    return pl.pallas_call(
+        functools.partial(bring_kernel, first_row, block_len),
+        in_specs=[pl.BlockSpec(memory_space=pltpu.SMEM)] + [pl.BlockSpec(memory_space=pl.ANY)] * 8,
+        out_specs=[pl.BlockSpec(memory_space=pltpu.VMEM)] * len(shapes),
+        out_shape=[pltpu.VMEM(*shape) for shape in shapes],
+        scratch_shapes=[pltpu.SemaphoreType.DMA((2, 4)), pltpu.SemaphoreType.DMA],
+        compiler_params=params(),
+        cost_estimate=SHORT,
+    )(place, *in_hbm(queries, gate_input, out_weight, *parts[0], *parts[1]), after)
+
+
+def project_kernel(first_row, block_len, pieces, brought, place_ref, *refs):
+    states, refs = refs[:2 * CHAIN_PARTS], refs[2 * CHAIN_PARTS:]
+    if brought:
+        queries, gates, parts, leads, early, weight_hbm, after_ref, *refs = refs
+    else:
+        query_hbm, gate_hbm, weight_hbm, part_0, lead_0, part_1, lead_1, after_ref, *refs = refs
+    del after_ref
+    outs, refs = refs[:pieces + 1], refs[pieces + 1:]
+    incoming, hidden, result, weight, state_sem, out_sem, weight_sem, *refs = refs
+    rows, width = outs[-1].shape
+    tiles = weight_sem.shape[0]
+    tile = width // tiles
+    is_odd = place_ref[2] == 1
     columns = [slice(at, at + tile) for at in range(0, width, tile)]
+    loads = [pltpu.make_async_copy(ref, incoming.at[i], state_sem.at[i])
+             for i, ref in enumerate(states)]
+    skipped = early.shape[1] if brought else 0
     weights = [
-        pltpu.make_async_copy(weight_hbm.at[:, at], weight.at[:, at], weight_sem.at[i])
-        for i, at in enumerate(columns)
+        pltpu.make_async_copy(
+            weight_hbm.at[:, at], weight.at[:, at.start - skipped:at.stop - skipped], weight_sem.at[i])
+        for i, at in enumerate(columns) if at.start >= skipped
     ]
+    if not brought:
+        queries, gates, parts, leads, row_sem = refs
+        loads += row_loads(first_row, block_len, place_ref, query_hbm, gate_hbm,
+                           ((part_0, lead_0), (part_1, lead_1)), queries, gates, parts, leads, row_sem)
+    heads = queries.shape[1] // HEAD_DIM
+    half = heads // 2
+    per_part = half // CHAIN_PARTS
     for load in loads + weights[:1]:
         load.start()
     for load in loads:
@@ -293,47 +343,56 @@
         hidden[:, at] = (normed * (gate / (1.0 + jnp.exp(-gate)))).astype(BF16)
     stores = []
     for i, at in enumerate(columns):
-        weights[i].wait()
-        result[:, at] = jnp.dot(hidden[...], weight[:, at], preferred_element_type=F32)
-        begin = 0
-        for j, out in enumerate(outs):
-            size = out.shape[0]
-            store = pltpu.make_async_copy(
-                result.at[begin:begin + size, at], out.at[:, at], out_sem.at[j, i])
-            store.start()
-            stores.append(store)
-            begin += size
+        if at.start < skipped:
+            tile_weight = early[:, at]
+        else:
+            weights[i - skipped // tile].wait()
+            tile_weight = weight[:, at.start - skipped:at.stop - skipped]
+        result[:, at] = jnp.dot(hidden[...], tile_weight, preferred_element_type=F32)
+    begin = 0
+    for j, out in enumerate(outs):
+        size = out.shape[0]
+        store = pltpu.make_async_copy(result.at[begin:begin + size], out, out_sem.at[j])
+        store.start()
+        stores.append(store)
+        begin += size
     for store in stores:
         store.wait()
 
 
 def project_rows(place, rows, first_row, block_len, queries, parts, gate_input, kept, got,
-                 out_weight, after, pieces):
+                 out_weight, after, pieces, brought=None):
     features = queries.shape[1]
     width = out_weight.shape[1]
     tiles = max(1, width // TILE)
     sizes = [rows // pieces] * pieces + [rows]
-    far = pl.BlockSpec(memory_space=pl.ANY)
+    far, vmem = pl.BlockSpec(memory_space=pl.ANY), pl.BlockSpec(memory_space=pltpu.VMEM)
     dma = pltpu.SemaphoreType.DMA
+    scratch = [
+        pltpu.VMEM((2 * CHAIN_PARTS, *kept[0].shape), F32),
+        pltpu.VMEM((2 * rows, features), BF16),
+        pltpu.VMEM((2 * rows, width), F32),
+        pltpu.VMEM((features, width if brought is None else width - brought[-1].shape[1]), BF16),
+        dma((2 * CHAIN_PARTS,)), dma((len(sizes),)), dma((tiles,)),
+    ]
+    if brought is not None:
+        operands = [pltpu.with_memory_space_constraint(value, pltpu.VMEM) for value in brought]
+        specs = [vmem] * len(operands) + [far]
+        operands += in_hbm(out_weight)
+    else:
+        operands = in_hbm(queries, gate_input, out_weight, *parts[0], *parts[1])
+        specs = [far] * len(operands)
+        scratch += [pltpu.VMEM(*shape) for shape in row_shapes(rows, features)]
+        scratch += [dma((2, 4))]
     return pl.pallas_call(
-        functools.partial(project_kernel, first_row, block_len, pieces),
-        in_specs=[pl.BlockSpec(memory_space=pltpu.SMEM)] + [far] * (8 + 2 * CHAIN_PARTS),
+        functools.partial(project_kernel, first_row, block_len, pieces, brought is not None),
+        in_specs=[pl.BlockSpec(memory_space=pltpu.SMEM)] + [far] * 2 * CHAIN_PARTS + specs + [far],
         out_specs=[far] * len(sizes),
         out_shape=[jax.ShapeDtypeStruct((size, width), F32) for size in sizes],
-        scratch_shapes=[
-            pltpu.VMEM((2 * rows, features), BF16),
-            pltpu.VMEM((2 * rows, features), F32),
-            pltpu.VMEM((2 * rows, features), BF16),
-            pltpu.VMEM((2 * rows, features // HEAD_DIM), F32),
-            pltpu.VMEM((2 * CHAIN_PARTS, *kept[0].shape), F32),
-            pltpu.VMEM(out_weight.shape, BF16),
-            pltpu.VMEM((2 * rows, features), BF16),
-            pltpu.VMEM((2 * rows, width), F32),
-            dma((2, 4)), dma((2 * CHAIN_PARTS,)), dma((tiles,)), dma((len(sizes), tiles)),
-        ],
+        scratch_shapes=scratch,
         compiler_params=params(),
         cost_estimate=SHORT,
-    )(place, *in_hbm(queries, gate_input, out_weight, *parts[0], *parts[1], after), *kept, *got)
+    )(place, *kept, *got, *operands, after)
 
 
 def add_kernel(own_ref, *refs):
@@ -355,7 +414,7 @@
         out_shape=jax.ShapeDtypeStruct(own.shape, F32),
         compiler_params=params(),
         cost_estimate=SHORT,
-    )(own, *pieces, *in_hbm(after))
+    )(own, *pieces, after)
 
 
 def finish_kernel(arrivals, own_ref, *refs):
@@ -477,7 +536,7 @@
     count = lax.axis_size("head")
     chips = count // 2
     block_len = tokens // count
-    sizes = [block_len // ROW_GROUPS] * ROW_GROUPS
+    sizes = [block_len // share for share in ROW_SHARES]
     firsts = [sum(sizes[:i]) for i in range(len(sizes))]
     index = lax.axis_index("head")
     chip, core = index // 2, index % 2
@@ -490,17 +549,18 @@
     met = [lax.ppermute(piece, "seq", swap) for piece in sent]
     kept, kept_starts = local_states(odd, rates, key_vectors, value_vectors, block_len)
 
+    def place_of(target):
+        return jnp.stack([2 * target + 1 - core, 2 * target + core, odd[0]]).astype(jnp.int32)
+
     def parts_of(target, after):
-        place = jnp.stack([2 * target + 1 - core, 2 * target + core, odd[0]]).astype(jnp.int32)
-        outs = inside_part(place, rates, queries, key_vectors, value_vectors,
+        outs = inside_part(place_of(target), rates, queries, key_vectors, value_vectors,
                            (kept_starts, sent_starts), block_len, after)
         return outs[:2], outs[2:]
 
-    def project(target, parts, group, after, pieces):
-        place = jnp.stack([2 * target + 1 - core, 2 * target + core, odd[0]]).astype(jnp.int32)
+    def project(target, parts, group, after, pieces, brought=None):
         *theirs, mine = project_rows(
-            place, sizes[group], firsts[group], block_len, queries, parts, gate_input, keep, got,
-            out_weight, after, pieces)
+            place_of(target), sizes[group], firsts[group], block_len, queries, parts, gate_input, keep,
+            got, out_weight, after, pieces, brought)
         return mine, [lax.ppermute(piece, "head", cores) for piece in theirs]
 
     cores = [(i, i ^ 1) for i in range(count)]
@@ -513,30 +573,34 @@
 
     keep, got = incoming_states(
         odd, kept, met, kept_starts, [functools.partial(inside_of, target) for target in targets])
-    last = keep[0]
+    last = keep[-1]
+    brought = bring_rows(place_of(targets[0]), sizes[0], firsts[0], block_len, queries, parts[0],
+                         gate_input, out_weight, last)
     landed, own, result = [last, last], [], None
     arrived = [[] for _ in sizes]
     for group in range(len(sizes)):
         for step, target in enumerate(targets):
             across = [(i, ((i // 2 + step + 1) % chips) * 2 + i % 2) for i in range(count)]
-            mine, pieces = project(target, parts[step], group, last, CORE_PIECES)
+            mine, pieces = project(target, parts[step], group, last, CORE_PIECES, brought)
+            brought = None
             last = add_pieces(mine, pieces, landed[-DEPTH])
             landed.append(lax.ppermute(last, "head", across))
             arrived[group].append(landed[-1])
     own_parts = parts_of(chip, last)
-    ratio = ROW_GROUPS // OWN_GROUPS
-    sizes = [block_len // OWN_GROUPS] * OWN_GROUPS
-    firsts = [sum(sizes[:i]) for i in range(len(sizes))]
+    groups = list(zip(firsts, sizes))
+    own_rows, piece = block_len // OWN_GROUPS, block_len // 8
+    sizes = [own_rows] * OWN_GROUPS
+    firsts = [own_rows * i for i in range(OWN_GROUPS)]
     for group in range(len(sizes)):
         if group == len(sizes) - 1:
             last = landed[-2]
-        own.append(project(chip, own_parts, group, last, OWN_PIECES * ratio))
+        own.append(project(chip, own_parts, group, last, own_rows // piece))
         last = own[-1][0]
-    for group in range(len(arrived)):
-        mine, pieces = own[group // ratio]
-        place = group % ratio
-        result = finish_rows(group, arrived[group], mine, place,
-                             pieces[place * OWN_PIECES:(place + 1) * OWN_PIECES], result, block_len)
+    for group, (first, size) in enumerate(groups):
+        mine, pieces = own[first // own_rows]
+        at = first % own_rows
+        result = finish_rows(first // size, arrived[group], mine, at // size,
+                             pieces[at // piece:(at + size) // piece], result, block_len)
     return result
 
 

time: 141 us -> 138 us (0.979)
  local copies, waits for them, and re-layouts: 6.87 us -> 3.08 us
  Pallas kernels: 67.7 us -> 70.2 us
    unnamed x30 -> x8, local copies, waits for them, and re-layouts: 6.87 us -> 3.08 us
    ppermute x2, waiting for transfers between devices: 3.68 us -> 0.44 us  [incoming_states(): back.append(lax.ppermute(other, 'seq', swap))]
    pallas_call x0 -> x1, Pallas kernels: none -> 3.22 us  [bring_rows(): pl.pallas_call(functools.partial(bring_kernel, first_row, block_len), in_...]
  transfers between devices with their start and end apart: 38 -> 38, of which waited for: 22 -> 22; matrix products, arithmetic and copies ran while one was open for 0% -> 0% of each run, Pallas kernels for 41% -> 45%
where the time goes in v4:
time: 138 us; the launch traced here: 136 us
  Pallas kernels  70.2 us (51%)
  waiting for transfers between devices  41.4 us (30%)
  starting transfers between devices  21.2 us (15%)
  local copies, waits for them, and re-layouts  3.08 us (2%)
    pallas_call x6, Pallas kernels, project_rows(): pl.pallas_call(functools.partial(project_kernel, first_row, block_len, pi...  38.4 us
    ppermute x4, waiting for transfers between devices, per_device(): landed.append(lax.ppermute(last, 'head', across))  26.6 us
    pallas_call x2, Pallas kernels, inside_part(): pl.pallas_call(inside_kernel, in_specs=[pl.BlockSpec(memory_space=pltpu.S...  13.3 us
    ppermute x24, waiting for transfers between devices, project(): return (mine, [lax.ppermute(piece, 'head', cores) for piece in theirs])  7.45 us
    pallas_call x2, Pallas kernels, local_states(): pl.pallas_call(states_kernel, in_specs=[pl.BlockSpec(memory_space=pltpu.S...  7.2 us
    pallas_call x4, Pallas kernels, finish_rows(): pl.pallas_call(functools.partial(finish_kernel, len(arrived)), grid=(1,),...  6.31 us
    ppermute x24, starting transfers between devices, project(): return (mine, [lax.ppermute(piece, 'head', cores) for piece in theirs])  5.63 us
    ppermute x6, starting transfers between devices, incoming_states(): landed[i].append(lax.ppermute(value, 'seq', along))  5.44 us
  transfers between devices with their start and end apart: 38, of which 22 were waited for; matrix products, arithmetic and copies ran while one was open for 0% of the time, Pallas kernels for 45%

profile of v4, /device:TPU:24, one launch (start us, length us, event | category | flops | bytes accessed | tf_op | source)
XLA Modules:
  0.0 136.4 jit_solution(7533657747455669621)
XLA Ops:
  0.0 3.6 %shard_map.65 = (f32[2,136,128]{2,1,0:T(8,128)S(1)}, f32[2,136,128]{2,1,0:T(8,128)S(1)}, f32[4,4,128,128]{3,2,1,0:T(8,128)}) custom-call(s32[1]{0:T(128)S(6)} %sub.22.side_ref, f32[8,1024]{1,0:T(8,128)} %bitcast.6, bf16[1024,1024]{1,0:T(8,128)(2,1)} %key_hbm.7, bf16[1024,1024]{1,0:T(8,128)(2,1)} %value_hbm.7), custom_call_target="tpu_custom_call" | custom-call | flops 1 | bytes 1 | tf_op jit(solution)/shard_map/pallas_call | solution.py:147
  3.6 1.6 %collective-permute-start.3 = (f32[2,136,128]{2,1,0:T(8,128)S(1)}, f32[2,136,128]{2,1,0:T(8,128)S(1)}, u32[]{:S(2)}, u32[]{:S(2)}) collective-permute-start(f32[2,136,128]{2,1,0:T(8,128)S(1)} %get-tuple-element.63), channel_id=1, source_target_pairs={{0,4},{4,0},{8,12},{12,8},{16,20},{20,16},{24,28},{28,24},{1,5},{5... | collective-permute-start | bytes 417800 | tf_op jit(solution)/shard_map/ppermute | solution.py:549
  5.7 3.6 %shard_map.64 = (f32[2,136,128]{2,1,0:T(8,128)S(1)}, f32[2,136,128]{2,1,0:T(8,128)S(1)}, f32[4,4,128,128]{3,2,1,0:T(8,128)}) custom-call(s32[1]{0:T(128)} %bitcast.2.side_ref.odd_ref, f32[8,1024]{1,0:T(8,128)} %bitcast.7, bf16[1024,1024]{1,0:T(8,128)(2,1)} %key_hbm.7, bf16[1024,1024]{1,0:T(8,128)(2,1)} %value_hbm.7), custom_call_target="tpu_custom_call" | custom-call | flops 1 | bytes 1 | tf_op jit(solution)/shard_map/pallas_call | solution.py:147
  10.9 1.1 collective-permute-done.refs_1_.refs_2_.refs_3_.refs_4_
  14.4 6.7 %shard_map.70 = (f32[256,1024]{1,0:T(8,128)}, f32[256,8]{1,0:T(8,128)}, f32[256,1024]{1,0:T(8,128)}, f32[256,8]{1,0:T(8,128)}) custom-call(s32[3]{0:T(128)S(1)} %add_add_fusion.1.place_ref, f32[8,1024]{1,0:T(8,128)} %bitcast.8, bf16[1024,1024]{1,0:T(8,128)(2,1)} %refs_4_.9, bf16[1024,1024]{1,0:T(8,128)(2,1)} %key_hbm.7, bf16[1024,1024]{1,0:T(8,128)(2,1)} %value_hbm.7, ...), custom_call_target="tpu_custom_call" | custom-call | flops 1 | bytes 1 | tf_op jit(solution)/shard_map/pallas_call | solution.py:236
  21.1 1.3 collective-permute-start.7
  22.5 1.5 %collective-permute-start.5 = (f32[2,128,128]{2,1,0:T(8,128)S(1)}, f32[2,128,128]{2,1,0:T(8,128)S(1)}, u32[]{:S(2)}, u32[]{:S(2)}) collective-permute-start(f32[2,128,128]{2,1,0:T(8,128)S(1)} %shard_map.71), channel_id=1, source_target_pairs={{16,24},{20,28},{17,25},{21,29},{18,26},{22,30},{19,27},{23,31}} | collective-permute-start | bytes 393224 | tf_op jit(solution)/shard_map/ppermute | solution.py:522
  23.9 4.8 %collective-permute-done.7.refs_2_ = f32[2,128,128]{2,1,0:T(8,128)S(1)} collective-permute-done((f32[2,128,128]{2,1,0:T(8,128)S(1)}, f32[2,128,128]{2,1,0:T(8,128)S(1)}, u32[]{:S(2)}, u32[]{:S(2)}) %collective-permute-start.7) | collective-permute-done | bytes 131104 | tf_op jit(solution)/shard_map/ppermute | solution.py:522
  28.8 1.6 %collective-permute-start.9 = (f32[2,128,128]{2,1,0:T(8,128)S(1)}, f32[2,128,128]{2,1,0:T(8,128)S(1)}, u32[]{:S(2)}, u32[]{:S(2)}) collective-permute-start(f32[2,128,128]{2,1,0:T(8,128)S(1)} %get-tuple-element.68), channel_id=1, source_target_pairs={{0,4},{4,0},{8,12},{12,8},{16,20},{20,16},{24,28},{28,24},{1,5},{5... | collective-permute-start | bytes 393224 | tf_op jit(solution)/shard_map/ppermute | solution.py:530
  30.4 1.3 collective-permute-start.8
  31.8 3.2 %shard_map.75 = (bf16[128,1024]{1,0:T(8,128)(2,1)S(1)}, bf16[128,1024]{1,0:T(8,128)(2,1)S(1)}, f32[128,1024]{1,0:T(8,128)S(1)}, f32[128,8]{1,0:T(8,128)S(1)}, bf16[1024,2048]{1,0:T(8,128)(2,1)S(1)}) custom-call(s32[3]{0:T(128)S(1)} %add_add_fusion.1.place_ref, bf16[1024,1024]{1,0:T(8,128)(2,1)} %refs_4_.9, bf16[1024,1024]{1,0:T(8,128)(2,1)} %refs_5_.9, ...), custom_call_target="tpu_custom_call" | custom-call | flops 1 | bytes 1 | tf_op jit(solution)/shard_map/pallas_call | solution.py:286
  35.5 4.5 %shard_map.76 = (f32[16,4096]{1,0:T(8,128)S(1)}, f32[16,4096]{1,0:T(8,128)S(1)}, f32[16,4096]{1,0:T(8,128)S(1)}, f32[16,4096]{1,0:T(8,128)S(1)}, f32[64,4096]{1,0:T(8,128)S(1)}) custom-call(s32[3]{0:T(128)S(1)} %add_add_fusion.1.place_ref, f32[2,128,128]{2,1,0:T(8,128)S(1)} %get-tuple-element.65.refs_0_, ...), custom_call_target="tpu_custom_call" | custom-call | flops 1 | bytes 1 | tf_op jit(solution)/shard_map/pallas_call | solution.py:387
  42.8 1.6 %collective-permute-start.22 = (f32[64,4096]{1,0:T(8,128)S(1)}, f32[64,4096]{1,0:T(8,128)S(1)}, u32[]{:S(2)}, u32[]{:S(2)}) collective-permute-start(f32[64,4096]{1,0:T(8,128)S(1)} %shard_map.77.refs_11_), channel_id=1, source_target_pairs={{0,2},{1,3},{2,0},{3,1},{4,6},{5,7},{6,4},{7,5},{8,10},{9,11},{10,... | collective-permute-start | bytes 3145736 | tf_op jit(solution)/shard_map/ppermute | solution.py:587
  44.3 6.3 %shard_map.78 = (f32[16,4096]{1,0:T(8,128)S(1)}, f32[16,4096]{1,0:T(8,128)S(1)}, f32[16,4096]{1,0:T(8,128)S(1)}, f32[16,4096]{1,0:T(8,128)S(1)}, f32[64,4096]{1,0:T(8,128)S(1)}) custom-call(s32[3]{0:T(128)S(1)} %add_add_fusion.1.place_ref, f32[2,128,128]{2,1,0:T(8,128)S(1)} %get-tuple-element.65.refs_0_, ...), custom_call_target="tpu_custom_call" | custom-call | flops 1 | bytes 1 | tf_op jit(solution)/shard_map/pallas_call | solution.py:387
  53.5 6.3 %shard_map.80 = (f32[16,4096]{1,0:T(8,128)S(1)}, f32[16,4096]{1,0:T(8,128)S(1)}, f32[16,4096]{1,0:T(8,128)S(1)}, f32[16,4096]{1,0:T(8,128)S(1)}, f32[64,4096]{1,0:T(8,128)S(1)}) custom-call(s32[3]{0:T(128)S(1)} %add_add_fusion.1.place_ref, f32[2,128,128]{2,1,0:T(8,128)S(1)} %get-tuple-element.65.refs_0_, ...), custom_call_target="tpu_custom_call" | custom-call | flops 1 | bytes 1 | tf_op jit(solution)/shard_map/pallas_call | solution.py:387
  62.5 6.3 %collective-permute-done.22.refs_4_.refs_0_ = f32[64,4096]{1,0:T(8,128)S(1)} collective-permute-done((f32[64,4096]{1,0:T(8,128)S(1)}, f32[64,4096]{1,0:T(8,128)S(1)}, u32[]{:S(2)}, u32[]{:S(2)}) %collective-permute-start.22) | collective-permute-done | bytes 1048608 | tf_op jit(solution)/shard_map/ppermute | solution.py:587
  69.8 1.5 %collective-permute-start.28 = (f32[64,4096]{1,0:T(8,128)S(1)}, f32[64,4096]{1,0:T(8,128)}, u32[]{:S(2)}, u32[]{:S(2)}) collective-permute-start(f32[64,4096]{1,0:T(8,128)S(1)} %shard_map.81.refs_11_), channel_id=1, source_target_pairs={{0,2},{1,3},{2,0},{3,1},{4,6},{5,7},{6,4},{7,5},{8,10},{9,11},{10,... | collective-permute-start | bytes 3145736 | tf_op jit(solution)/shard_map/ppermute | solution.py:587
  71.3 7.0 %shard_map.82 = (f32[16,4096]{1,0:T(8,128)S(1)}, f32[16,4096]{1,0:T(8,128)}, f32[16,4096]{1,0:T(8,128)}, f32[16,4096]{1,0:T(8,128)}, f32[64,4096]{1,0:T(8,128)S(1)}) custom-call(s32[3]{0:T(128)S(1)} %add_add_fusion.1.place_ref, f32[2,128,128]{2,1,0:T(8,128)S(1)} %get-tuple-element.65.refs_0_, ...), custom_call_target="tpu_custom_call" | custom-call | flops 1 | bytes 1 | tf_op jit(solution)/shard_map/pallas_call | solution.py:387
  78.4 1.0 copy-done.2
  79.9 1.4 %collective-permute-done.23.refs_0_ = f32[16,4096]{1,0:T(8,128)S(1)} collective-permute-done((f32[16,4096]{1,0:T(8,128)S(1)}, f32[16,4096]{1,0:T(8,128)S(1)}, u32[]{:S(2)}, u32[]{:S(2)}) %collective-permute-start.23) | collective-permute-done | bytes 262176 | tf_op jit(solution)/shard_map/ppermute | solution.py:564
  81.9 1.3 collective-permute-done.26.refs_3_
  83.1 8.3 %collective-permute-done.27.refs_4_.refs_0_ = f32[64,4096]{1,0:T(8,128)} collective-permute-done((f32[64,4096]{1,0:T(8,128)S(1)}, f32[64,4096]{1,0:T(8,128)}, u32[]{:S(2)}, u32[]{:S(2)}) %collective-permute-start.27) | collective-permute-done | bytes 1048608 | tf_op jit(solution)/shard_map/ppermute | solution.py:587
  91.4 1.2 copy-done.3
  92.6 1.1 shard_map.83.after_ref.refs_11_
  93.7 6.7 %shard_map.84 = (f32[256,1024]{1,0:T(8,128)}, f32[256,8]{1,0:T(8,128)}, f32[256,1024]{1,0:T(8,128)}, f32[256,8]{1,0:T(8,128)}) custom-call(s32[3]{0:T(128)S(1)} %add_add_fusion.place_ref, f32[8,1024]{1,0:T(8,128)} %bitcast.9, bf16[1024,1024]{1,0:T(8,128)(2,1)} %refs_4_.9, bf16[1024,1024]{1,0:T(8,128)(2,1)} %key_hbm.7, bf16[1024,1024]{1,0:T(8,128)(2,1)} %value_hbm.7, ...), custom_call_target="tpu_custom_call" | custom-call | flops 1 | bytes 1 | tf_op jit(solution)/shard_map/pallas_call | solution.py:236
  100.4 7.2 %shard_map.86 = (f32[32,4096]{1,0:T(8,128)S(1)}, f32[32,4096]{1,0:T(8,128)S(1)}, f32[32,4096]{1,0:T(8,128)S(1)}, f32[32,4096]{1,0:T(8,128)S(1)}, f32[128,4096]{1,0:T(8,128)S(1)}) custom-call(s32[3]{0:T(128)S(1)} %add_add_fusion.place_ref, f32[2,128,128]{2,1,0:T(8,128)S(1)} %get-tuple-element.65.refs_0_, ...), custom_call_target="tpu_custom_call" | custom-call | flops 1 | bytes 1 | tf_op jit(solution)/shard_map/pallas_call | solution.py:387
  108.1 1.5 %collective-permute-start.29 = (f32[64,4096]{1,0:T(8,128)S(1)}, f32[64,4096]{1,0:T(8,128)S(1)}, u32[]{:S(2)}, u32[]{:S(2)}) collective-permute-start(f32[64,4096]{1,0:T(8,128)S(1)} %shard_map.83.after_ref.refs_11_), channel_id=1, source_target_pairs={{0,2},{1,3},{2,0},{3,1},{4,6},{5,7},{6,4},{7,5},{8,10},{9,11},{10,... | collective-permute-start | bytes 3145736 | tf_op jit(solution)/shard_map/ppermute | solution.py:587
  109.7 4.2 %collective-permute-done.28.refs_11_.refs_0_ = f32[64,4096]{1,0:T(8,128)} collective-permute-done((f32[64,4096]{1,0:T(8,128)S(1)}, f32[64,4096]{1,0:T(8,128)}, u32[]{:S(2)}, u32[]{:S(2)}) %collective-permute-start.28) | collective-permute-done | bytes 1048608 | tf_op jit(solution)/shard_map/ppermute | solution.py:587
  113.9 7.2 %shard_map.85 = (f32[32,4096]{1,0:T(8,128)S(1)}, f32[32,4096]{1,0:T(8,128)S(1)}, f32[32,4096]{1,0:T(8,128)S(1)}, f32[32,4096]{1,0:T(8,128)S(1)}, f32[128,4096]{1,0:T(8,128)S(1)}) custom-call(s32[3]{0:T(128)S(1)} %add_add_fusion.place_ref, f32[2,128,128]{2,1,0:T(8,128)S(1)} %get-tuple-element.65.refs_0_, ...), custom_call_target="tpu_custom_call" | custom-call | flops 1 | bytes 1 | tf_op jit(solution)/shard_map/pallas_call | solution.py:387
  123.2 2.2 %shard_map.88.refs_3_ = bf16[256,4096]{1,0:T(8,128)(2,1)} custom-call(f32[128,4096]{1,0:T(8,128)S(1)} %get-tuple-element.106.own_ref.refs_3_, f32[64,4096]{1,0:T(8,128)} %collective-permute-done.27.refs_4_.refs_0_, f32[32,4096]{1,0:T(8,128)S(1)} %collective-permute-done.34.refs_1_, ...), custom_call_target="tpu_custom_call", output_to_operand_aliasing={{}: (4, {})} | custom-call | flops 1 | bytes 1 | tf_op jit(solution)/shard_map/pallas_call | solution.py:441
  125.4 2.2 %shard_map.89.refs_3_ = bf16[256,4096]{1,0:T(8,128)(2,1)} custom-call(f32[128,4096]{1,0:T(8,128)S(1)} %get-tuple-element.101.own_ref, f32[64,4096]{1,0:T(8,128)} %collective-permute-done.28.refs_11_.refs_0_, f32[32,4096]{1,0:T(8,128)S(1)} %collective-permute-done.32.refs_1_, ...), custom_call_target="tpu_custom_call", output_to_operand_aliasing={{}: (4, {})} | custom-call | flops 1 | bytes 1 | tf_op jit(solution)/shard_map/pallas_call | solution.py:441
  127.6 7.8 %collective-permute-done.29.refs_0_ = f32[64,4096]{1,0:T(8,128)S(1)} collective-permute-done((f32[64,4096]{1,0:T(8,128)S(1)}, f32[64,4096]{1,0:T(8,128)S(1)}, u32[]{:S(2)}, u32[]{:S(2)}) %collective-permute-start.29) | collective-permute-done | bytes 1048608 | tf_op jit(solution)/shard_map/ppermute | solution.py:587
  (81 shorter events, 19.1 us)
Async XLA Ops:
  3.6 6.6 %collective-permute-start.3 = (f32[2,136,128]{2,1,0:T(8,128)S(1)}, f32[2,136,128]{2,1,0:T(8,128)S(1)}, u32[]{:S(2)}, u32[]{:S(2)}) collective-permute-start(f32[2,136,128]{2,1,0:T(8,128)S(1)} %get-tuple-element.63), channel_id=1, source_target_pairs={{0,4},{4,0},{8,12},{12,8},{16,20},{20,16},{24,28},{28,24},{1,5},{5... | collective-permute-start | bytes 417800 | tf_op jit(solution)/shard_map/ppermute | solution.py:549
  5.2 6.9 %collective-permute-start = (f32[2,136,128]{2,1,0:T(8,128)S(1)}, f32[2,136,128]{2,1,0:T(8,128)S(1)}, u32[]{:S(2)}, u32[]{:S(2)}) collective-permute-start(f32[2,136,128]{2,1,0:T(8,128)S(1)} %get-tuple-element.59), channel_id=1, source_target_pairs={{0,4},{4,0},{8,12},{12,8},{16,20},{20,16},{24,28},{28,24},{1,5},{5... | collective-permute-start | bytes 417800 | tf_op jit(solution)/shard_map/ppermute | solution.py:549
  10.3 2.5 %collective-permute-start.4 = (f32[2,128,128]{2,1,0:T(8,128)S(1)}, f32[2,128,128]{2,1,0:T(8,128)S(1)}, u32[]{:S(2)}, u32[]{:S(2)}) collective-permute-start(f32[2,128,128]{2,1,0:T(8,128)S(1)} %shard_map.68), channel_id=1, source_target_pairs={{0,8},{4,12},{1,9},{5,13},{2,10},{6,14},{3,11},{7,15}} | collective-permute-start | bytes 393224 | tf_op jit(solution)/shard_map/ppermute | solution.py:522
  12.8 8.2 %collective-permute-start.6 = (f32[2,128,128]{2,1,0:T(8,128)S(1)}, f32[2,128,128]{2,1,0:T(8,128)S(1)}, u32[]{:S(2)}, u32[]{:S(2)}) collective-permute-start(f32[2,128,128]{2,1,0:T(8,128)S(1)} %shard_map.69.after_ref), channel_id=1, source_target_pairs={{8,16},{12,20},{9,17},{13,21},{10,18},{14,22},{11,19},{15,23}} | collective-permute-start | bytes 393224 | tf_op jit(solution)/shard_map/ppermute | solution.py:522
  13.6 8.8 %collective-permute-start.2 = (f32[2,128,128]{2,1,0:T(8,128)S(1)}, f32[2,128,128]{2,1,0:T(8,128)S(1)}, u32[]{:S(2)}, u32[]{:S(2)}) collective-permute-start(f32[2,128,128]{2,1,0:T(8,128)S(1)} %shard_map.67), channel_id=1, source_target_pairs={{8,16},{12,20},{9,17},{13,21},{10,18},{14,22},{11,19},{15,23}} | collective-permute-start | bytes 393224 | tf_op jit(solution)/shard_map/ppermute | solution.py:522
  21.1 7.7 %collective-permute-start.7 = (f32[2,128,128]{2,1,0:T(8,128)S(1)}, f32[2,128,128]{2,1,0:T(8,128)S(1)}, u32[]{:S(2)}, u32[]{:S(2)}) collective-permute-start(f32[2,128,128]{2,1,0:T(8,128)S(1)} %shard_map.73), channel_id=1, source_target_pairs={{16,24},{20,28},{17,25},{21,29},{18,26},{22,30},{19,27},{23,31}} | collective-permute-start | bytes 393224 | tf_op jit(solution)/shard_map/ppermute | solution.py:522
  22.5 7.9 %collective-permute-start.5 = (f32[2,128,128]{2,1,0:T(8,128)S(1)}, f32[2,128,128]{2,1,0:T(8,128)S(1)}, u32[]{:S(2)}, u32[]{:S(2)}) collective-permute-start(f32[2,128,128]{2,1,0:T(8,128)S(1)} %shard_map.71), channel_id=1, source_target_pairs={{16,24},{20,28},{17,25},{21,29},{18,26},{22,30},{19,27},{23,31}} | collective-permute-start | bytes 393224 | tf_op jit(solution)/shard_map/ppermute | solution.py:522
  28.8 6.2 %collective-permute-start.9 = (f32[2,128,128]{2,1,0:T(8,128)S(1)}, f32[2,128,128]{2,1,0:T(8,128)S(1)}, u32[]{:S(2)}, u32[]{:S(2)}) collective-permute-start(f32[2,128,128]{2,1,0:T(8,128)S(1)} %get-tuple-element.68), channel_id=1, source_target_pairs={{0,4},{4,0},{8,12},{12,8},{16,20},{20,16},{24,28},{28,24},{1,5},{5... | collective-permute-start | bytes 393224 | tf_op jit(solution)/shard_map/ppermute | solution.py:530
  30.4 5.0 %collective-permute-start.8 = (f32[2,128,128]{2,1,0:T(8,128)S(1)}, f32[2,128,128]{2,1,0:T(8,128)S(1)}, u32[]{:S(2)}, u32[]{:S(2)}) collective-permute-start(f32[2,128,128]{2,1,0:T(8,128)S(1)} %get-tuple-element.67), channel_id=1, source_target_pairs={{0,4},{4,0},{8,12},{12,8},{16,20},{20,16},{24,28},{28,24},{1,5},{5... | collective-permute-start | bytes 393224 | tf_op jit(solution)/shard_map/ppermute | solution.py:530
  40.0 1.9 %collective-permute-start.11 = (f32[16,4096]{1,0:T(8,128)S(1)}, f32[16,4096]{1,0:T(8,128)S(1)}, u32[]{:S(2)}, u32[]{:S(2)}) collective-permute-start(f32[16,4096]{1,0:T(8,128)S(1)} %get-tuple-element.79), channel_id=1, source_target_pairs={{0,1},{1,0},{2,3},{3,2},{4,5},{5,4},{6,7},{7,6},{8,9},{9,8},{10,11... | collective-permute-start | bytes 786440 | tf_op jit(solution)/shard_map/ppermute | solution.py:564
  40.5 1.8 %collective-permute-start.12 = (f32[16,4096]{1,0:T(8,128)S(1)}, f32[16,4096]{1,0:T(8,128)S(1)}, u32[]{:S(2)}, u32[]{:S(2)}) collective-permute-start(f32[16,4096]{1,0:T(8,128)S(1)} %get-tuple-element.80), channel_id=1, source_target_pairs={{0,1},{1,0},{2,3},{3,2},{4,5},{5,4},{6,7},{7,6},{8,9},{9,8},{10,11... | collective-permute-start | bytes 786440 | tf_op jit(solution)/shard_map/ppermute | solution.py:564
  40.6 2.1 %collective-permute-start.13 = (f32[16,4096]{1,0:T(8,128)S(1)}, f32[16,4096]{1,0:T(8,128)S(1)}, u32[]{:S(2)}, u32[]{:S(2)}) collective-permute-start(f32[16,4096]{1,0:T(8,128)S(1)} %get-tuple-element.81), channel_id=1, source_target_pairs={{0,1},{1,0},{2,3},{3,2},{4,5},{5,4},{6,7},{7,6},{8,9},{9,8},{10,11... | collective-permute-start | bytes 786440 | tf_op jit(solution)/shard_map/ppermute | solution.py:564
  42.8 26.1 %collective-permute-start.22 = (f32[64,4096]{1,0:T(8,128)S(1)}, f32[64,4096]{1,0:T(8,128)S(1)}, u32[]{:S(2)}, u32[]{:S(2)}) collective-permute-start(f32[64,4096]{1,0:T(8,128)S(1)} %shard_map.77.refs_11_), channel_id=1, source_target_pairs={{0,2},{1,3},{2,0},{3,1},{4,6},{5,7},{6,4},{7,5},{8,10},{9,11},{10,... | collective-permute-start | bytes 3145736 | tf_op jit(solution)/shard_map/ppermute | solution.py:587
  50.7 1.9 %collective-permute-start.15 = (f32[16,4096]{1,0:T(8,128)S(1)}, f32[16,4096]{1,0:T(8,128)S(1)}, u32[]{:S(2)}, u32[]{:S(2)}) collective-permute-start(f32[16,4096]{1,0:T(8,128)S(1)} %get-tuple-element.84), channel_id=1, source_target_pairs={{0,1},{1,0},{2,3},{3,2},{4,5},{5,4},{6,7},{7,6},{8,9},{9,8},{10,11... | collective-permute-start | bytes 786440 | tf_op jit(solution)/shard_map/ppermute | solution.py:564
  51.3 2.1 %collective-permute-start.17 = (f32[16,4096]{1,0:T(8,128)S(1)}, f32[16,4096]{1,0:T(8,128)S(1)}, u32[]{:S(2)}, u32[]{:S(2)}) collective-permute-start(f32[16,4096]{1,0:T(8,128)S(1)} %get-tuple-element.86), channel_id=1, source_target_pairs={{0,1},{1,0},{2,3},{3,2},{4,5},{5,4},{6,7},{7,6},{8,9},{9,8},{10,11... | collective-permute-start | bytes 786440 | tf_op jit(solution)/shard_map/ppermute | solution.py:564
  60.0 1.9 %collective-permute-start.19 = (f32[16,4096]{1,0:T(8,128)S(1)}, f32[16,4096]{1,0:T(8,128)S(1)}, u32[]{:S(2)}, u32[]{:S(2)}) collective-permute-start(f32[16,4096]{1,0:T(8,128)S(1)} %get-tuple-element.89), channel_id=1, source_target_pairs={{0,1},{1,0},{2,3},{3,2},{4,5},{5,4},{6,7},{7,6},{8,9},{9,8},{10,11... | collective-permute-start | bytes 786440 | tf_op jit(solution)/shard_map/ppermute | solution.py:564
  60.5 2.0 %collective-permute-start.21 = (f32[16,4096]{1,0:T(8,128)S(1)}, f32[16,4096]{1,0:T(8,128)S(1)}, u32[]{:S(2)}, u32[]{:S(2)}) collective-permute-start(f32[16,4096]{1,0:T(8,128)S(1)} %get-tuple-element.91), channel_id=1, source_target_pairs={{0,1},{1,0},{2,3},{3,2},{4,5},{5,4},{6,7},{7,6},{8,9},{9,8},{10,11... | collective-permute-start | bytes 786440 | tf_op jit(solution)/shard_map/ppermute | solution.py:564
  61.4 30.0 %collective-permute-start.27 = (f32[64,4096]{1,0:T(8,128)S(1)}, f32[64,4096]{1,0:T(8,128)}, u32[]{:S(2)}, u32[]{:S(2)}) collective-permute-start(f32[64,4096]{1,0:T(8,128)S(1)} %shard_map.79.refs_11_), channel_id=1, source_target_pairs={{0,2},{1,3},{2,0},{3,1},{4,6},{5,7},{6,4},{7,5},{8,10},{9,11},{10,... | collective-permute-start | bytes 3145736 | tf_op jit(solution)/shard_map/ppermute | solution.py:587
  69.8 44.1 %collective-permute-start.28 = (f32[64,4096]{1,0:T(8,128)S(1)}, f32[64,4096]{1,0:T(8,128)}, u32[]{:S(2)}, u32[]{:S(2)}) collective-permute-start(f32[64,4096]{1,0:T(8,128)S(1)} %shard_map.81.refs_11_), channel_id=1, source_target_pairs={{0,2},{1,3},{2,0},{3,1},{4,6},{5,7},{6,4},{7,5},{8,10},{9,11},{10,... | collective-permute-start | bytes 3145736 | tf_op jit(solution)/shard_map/ppermute | solution.py:587
  79.4 1.9 %collective-permute-start.23 = (f32[16,4096]{1,0:T(8,128)S(1)}, f32[16,4096]{1,0:T(8,128)S(1)}, u32[]{:S(2)}, u32[]{:S(2)}) collective-permute-start(f32[16,4096]{1,0:T(8,128)S(1)} %get-tuple-element.93), channel_id=1, source_target_pairs={{0,1},{1,0},{2,3},{3,2},{4,5},{5,4},{6,7},{7,6},{8,9},{9,8},{10,11... | collective-permute-start | bytes 786440 | tf_op jit(solution)/shard_map/ppermute | solution.py:564
  79.4 2.1 %collective-permute-start.24 = (f32[16,4096]{1,0:T(8,128)}, f32[16,4096]{1,0:T(8,128)S(1)}, u32[]{:S(2)}, u32[]{:S(2)}) collective-permute-start(f32[16,4096]{1,0:T(8,128)} %get-tuple-element.94), channel_id=1, source_target_pairs={{0,1},{1,0},{2,3},{3,2},{4,5},{5,4},{6,7},{7,6},{8,9},{9,8},{10,11... | collective-permute-start | bytes 786440 | tf_op jit(solution)/shard_map/ppermute | solution.py:564
  79.9 2.0 %collective-permute-start.25 = (f32[16,4096]{1,0:T(8,128)}, f32[16,4096]{1,0:T(8,128)S(1)}, u32[]{:S(2)}, u32[]{:S(2)}) collective-permute-start(f32[16,4096]{1,0:T(8,128)} %get-tuple-element.95), channel_id=1, source_target_pairs={{0,1},{1,0},{2,3},{3,2},{4,5},{5,4},{6,7},{7,6},{8,9},{9,8},{10,11... | collective-permute-start | bytes 786440 | tf_op jit(solution)/shard_map/ppermute | solution.py:564
  81.2 1.9 %collective-permute-start.26 = (f32[16,4096]{1,0:T(8,128)}, f32[16,4096]{1,0:T(8,128)}, u32[]{:S(2)}, u32[]{:S(2)}) collective-permute-start(f32[16,4096]{1,0:T(8,128)} %get-tuple-element.96), channel_id=1, source_target_pairs={{0,1},{1,0},{2,3},{3,2},{4,5},{5,4},{6,7},{7,6},{8,9},{9,8},{10,11... | collective-permute-start | bytes 786440 | tf_op jit(solution)/shard_map/ppermute | solution.py:564
  107.6 13.5 %collective-permute-start.36 = (f32[32,4096]{1,0:T(8,128)S(1)}, f32[32,4096]{1,0:T(8,128)S(1)}, u32[]{:S(2)}, u32[]{:S(2)}) collective-permute-start(f32[32,4096]{1,0:T(8,128)S(1)} %get-tuple-element.109), channel_id=1, source_target_pairs={{0,1},{1,0},{2,3},{3,2},{4,5},{5,4},{6,7},{7,6},{8,9},{9,8},{10,11... | collective-permute-start | bytes 1572872 | tf_op jit(solution)/shard_map/ppermute | solution.py:564
  107.6 14.0 %collective-permute-start.37 = (f32[32,4096]{1,0:T(8,128)S(1)}, f32[32,4096]{1,0:T(8,128)S(1)}, u32[]{:S(2)}, u32[]{:S(2)}) collective-permute-start(f32[32,4096]{1,0:T(8,128)S(1)} %get-tuple-element.110), channel_id=1, source_target_pairs={{0,1},{1,0},{2,3},{3,2},{4,5},{5,4},{6,7},{7,6},{8,9},{9,8},{10,11... | collective-permute-start | bytes 1572872 | tf_op jit(solution)/shard_map/ppermute | solution.py:564
  108.1 27.3 %collective-permute-start.29 = (f32[64,4096]{1,0:T(8,128)S(1)}, f32[64,4096]{1,0:T(8,128)S(1)}, u32[]{:S(2)}, u32[]{:S(2)}) collective-permute-start(f32[64,4096]{1,0:T(8,128)S(1)} %shard_map.83.after_ref.refs_11_), channel_id=1, source_target_pairs={{0,2},{1,3},{2,0},{3,1},{4,6},{5,7},{6,4},{7,5},{8,10},{9,11},{10,... | collective-permute-start | bytes 3145736 | tf_op jit(solution)/shard_map/ppermute | solution.py:587
  109.7 12.1 %collective-permute-start.34 = (f32[32,4096]{1,0:T(8,128)S(1)}, f32[32,4096]{1,0:T(8,128)S(1)}, u32[]{:S(2)}, u32[]{:S(2)}) collective-permute-start(f32[32,4096]{1,0:T(8,128)S(1)} %get-tuple-element.107), channel_id=1, source_target_pairs={{0,1},{1,0},{2,3},{3,2},{4,5},{5,4},{6,7},{7,6},{8,9},{9,8},{10,11... | collective-permute-start | bytes 1572872 | tf_op jit(solution)/shard_map/ppermute | solution.py:564
  113.9 8.3 %collective-permute-start.35 = (f32[32,4096]{1,0:T(8,128)S(1)}, f32[32,4096]{1,0:T(8,128)S(1)}, u32[]{:S(2)}, u32[]{:S(2)}) collective-permute-start(f32[32,4096]{1,0:T(8,128)S(1)} %get-tuple-element.108), channel_id=1, source_target_pairs={{0,1},{1,0},{2,3},{3,2},{4,5},{5,4},{6,7},{7,6},{8,9},{9,8},{10,11... | collective-permute-start | bytes 1572872 | tf_op jit(solution)/shard_map/ppermute | solution.py:564
  121.1 4.3 %collective-permute-start.32 = (f32[32,4096]{1,0:T(8,128)S(1)}, f32[32,4096]{1,0:T(8,128)S(1)}, u32[]{:S(2)}, u32[]{:S(2)}) collective-permute-start(f32[32,4096]{1,0:T(8,128)S(1)} %get-tuple-element.104), channel_id=1, source_target_pairs={{0,1},{1,0},{2,3},{3,2},{4,5},{5,4},{6,7},{7,6},{8,9},{9,8},{10,11... | collective-permute-start | bytes 1572872 | tf_op jit(solution)/shard_map/ppermute | solution.py:564
  121.6 3.8 %collective-permute-start.33 = (f32[32,4096]{1,0:T(8,128)S(1)}, f32[32,4096]{1,0:T(8,128)S(1)}, u32[]{:S(2)}, u32[]{:S(2)}) collective-permute-start(f32[32,4096]{1,0:T(8,128)S(1)} %get-tuple-element.105), channel_id=1, source_target_pairs={{0,1},{1,0},{2,3},{3,2},{4,5},{5,4},{6,7},{7,6},{8,9},{9,8},{10,11... | collective-permute-start | bytes 1572872 | tf_op jit(solution)/shard_map/ppermute | solution.py:564
  121.7 13.7 %collective-permute-start.30 = (f32[32,4096]{1,0:T(8,128)S(1)}, f32[32,4096]{1,0:T(8,128)S(1)}, u32[]{:S(2)}, u32[]{:S(2)}) collective-permute-start(f32[32,4096]{1,0:T(8,128)S(1)} %get-tuple-element.102), channel_id=1, source_target_pairs={{0,1},{1,0},{2,3},{3,2},{4,5},{5,4},{6,7},{7,6},{8,9},{9,8},{10,11... | collective-permute-start | bytes 1572872 | tf_op jit(solution)/shard_map/ppermute | solution.py:564
  122.2 13.3 %collective-permute-start.31 = (f32[32,4096]{1,0:T(8,128)S(1)}, f32[32,4096]{1,0:T(8,128)S(1)}, u32[]{:S(2)}, u32[]{:S(2)}) collective-permute-start(f32[32,4096]{1,0:T(8,128)S(1)} %get-tuple-element.103), channel_id=1, source_target_pairs={{0,1},{1,0},{2,3},{3,2},{4,5},{5,4},{6,7},{7,6},{8,9},{9,8},{10,11... | collective-permute-start | bytes 1572872 | tf_op jit(solution)/shard_map/ppermute | solution.py:564
  (10 other events, 21.3 us)

commit v5 on v4

--- a/solution.py
+++ b/solution.py
@@ -11,6 +11,7 @@
 MIB = 1024 * 1024
 ROW_SHARES = (4, 4, 4, 4)
 OWN_GROUPS = 2
+EARLY_GROUPS = 3
 CHAIN_PARTS = 2
 CORE_PIECES = 4
 DEPTH = 2
@@ -32,6 +33,12 @@
     return jnp.concatenate([high, low], axis=1)
 
 
+def split_rows(value):
+    high = value.astype(BF16)
+    low = (value - high.astype(F32)).astype(BF16)
+    return jnp.concatenate([high, low], axis=0)
+
+
 def fold_pair(value):
     return value[:, :HEAD_DIM] + value[:, HEAD_DIM:]
 
@@ -49,19 +56,7 @@
     return jnp.concatenate([high, middle, rest - middle], axis=0).astype(BF16)
 
 
-def fold_three(value):
-    count = value.shape[1] // 3
-    return value[:, :count] + value[:, count:2 * count] + value[:, 2 * count:]
-
-
 def running_sum(rates):
-    ones = lower_triangle(rates.shape[1]).astype(F32).astype(BF16)
-    return fold_three(lax.dot_general(
-        ones, split_three(rates), (((1,), (1,)), ((), ())), preferred_element_type=F32
-    ))
-
-
-def running_sum_rows(rates):
     ones = lower_triangle(rates.shape[1]).astype(F32).astype(BF16)
     count = rates.shape[0]
     value = lax.dot_general(
@@ -78,9 +73,16 @@
     return pltpu.CompilerParams(vmem_limit_bytes=mib * MIB)
 
 
-def states_kernel(side_ref, rate_hbm, key_hbm, value_hbm, *refs):
-    message_refs = refs[:CHAIN_PARTS]
-    start_hbm, rate_ref, keys, values, starts, rate_sem, key_sem, value_sem, start_sem = refs[CHAIN_PARTS:]
+def states_kernel(half_done, side_ref, rate_hbm, key_hbm, value_hbm, *refs):
+    if half_done:
+        other, *refs = refs
+    message_refs, refs = refs[:CHAIN_PARTS], refs[CHAIN_PARTS:]
+    if half_done:
+        start_hbm, other_hbm, rate_ref, keys, values, rate_sem, key_sem, value_sem, starts, start_sem = refs
+        stores = [pltpu.make_async_copy(starts, start_hbm, start_sem.at[0]),
+                  pltpu.make_async_copy(other, other_hbm, start_sem.at[1])]
+    else:
+        starts, rate_ref, keys, values, rate_sem, key_sem, value_sem = refs
     blocks, half = starts.shape[:2]
     width = keys.shape[1]
     size = keys.shape[0] // blocks
@@ -92,22 +94,17 @@
          pltpu.make_async_copy(value_hbm.at[at, columns], values.at[at], value_sem.at[block]))
         for block, at in enumerate(rows)
     ]
-    stores = [
-        pltpu.make_async_copy(starts.at[block], start_hbm.at[block], start_sem.at[block])
-        for block in range(blocks)
-    ]
     rate_load = pltpu.make_async_copy(rate_hbm, rate_ref, rate_sem)
     rate_load.start()
     for load in [load for pair in loads[:2] for load in pair]:
         load.start()
     starts[0] = jnp.zeros_like(starts[0])
-    stores[0].start()
     rate_load.wait()
     rates = jnp.where(side_ref[0] == 1, rate_ref[half:, :], rate_ref[:half, :])
-    lead = jnp.zeros((1, half), F32)
+    lead = jnp.zeros((half, 1), F32)
     for block, at in enumerate(rows):
         running = running_sum(rates[:, at])
-        total = running[-1:, :]
+        total = running[:, -1:]
         fade = jnp.exp(total - running)
         block_decay = jnp.exp(total)
         lead = lead + total
@@ -115,93 +112,93 @@
             load.wait()
         for load in loads[block + 2] if block + 2 < blocks else ():
             load.start()
+        if half_done and block == 0:
+            stores[1].start()
         for head in range(half):
             of_head = head_columns(head)
-            scaled = values[at, of_head].astype(F32) * fade[:, head:head + 1]
-            gained = fold_pair(lax.dot_general(
-                keys[at, of_head], split_pair(scaled), (((0,), (0,)), ((), ())),
-                preferred_element_type=F32
-            ))
-            state = block_decay[:, head:head + 1] * starts[block, head] + gained
+            scaled = keys[at, of_head].T.astype(F32) * fade[head:head + 1]
+            gained = jnp.dot(split_rows(scaled), values[at, of_head], preferred_element_type=F32)
+            gained = gained[:HEAD_DIM] + gained[HEAD_DIM:]
+            state = block_decay[head:head + 1] * starts[block, head] + gained
             if block + 1 < blocks:
                 starts[block + 1, head] = state
             else:
                 message_refs[head // per_part][head % per_part, :HEAD_DIM] = state
-        if block + 1 < blocks:
-            stores[block + 1].start()
+    if half_done:
+        stores[0].start()
     through = jnp.exp(lead)
     for head in range(half):
         message_refs[head // per_part][head % per_part, HEAD_DIM:] = jnp.broadcast_to(
-            through[:, head:head + 1], (8, HEAD_DIM))
-    for store in stores:
-        store.wait()
-
-
-def local_states(side, rates, key_vectors, value_vectors, block_len):
+            through[head:head + 1], (8, HEAD_DIM))
+    if half_done:
+        for store in stores:
+            store.wait()
+
+
+def local_states(side, rates, key_vectors, value_vectors, block_len, other=None):
     tokens, features = key_vectors.shape
     half = features // HEAD_DIM // 2
     blocks = tokens // block_len
     message = jax.ShapeDtypeStruct((half // CHAIN_PARTS, HEAD_DIM + 8, HEAD_DIM), F32)
-    starts = pltpu.HBM((blocks, half, HEAD_DIM, HEAD_DIM), F32)
+    starts = ((blocks, half, HEAD_DIM, HEAD_DIM), F32)
     vmem, far = pl.BlockSpec(memory_space=pltpu.VMEM), pl.BlockSpec(memory_space=pl.ANY)
-    *messages, starts = pl.pallas_call(
-        states_kernel,
-        in_specs=[pl.BlockSpec(memory_space=pltpu.SMEM), far, far, far],
-        out_specs=[vmem] * CHAIN_PARTS + [far],
-        out_shape=[message] * CHAIN_PARTS + [starts],
-        scratch_shapes=[
-            pltpu.VMEM(rates.shape, F32),
-            pltpu.VMEM((tokens, features // 2), BF16),
-            pltpu.VMEM((tokens, features // 2), BF16),
-            pltpu.VMEM((blocks, half, HEAD_DIM, HEAD_DIM), F32),
-            pltpu.SemaphoreType.DMA,
-        ] + [pltpu.SemaphoreType.DMA((blocks,))] * 3,
+    dma = pltpu.SemaphoreType.DMA
+    rows = pltpu.VMEM((tokens, features // 2), BF16)
+    scratch = [pltpu.VMEM(rates.shape, F32), rows, rows, dma, dma((blocks,)), dma((blocks,))]
+    if other is None:
+        others, start_specs, start_shapes = [], [vmem], [jax.ShapeDtypeStruct(*starts)]
+    else:
+        others, start_specs, start_shapes = [other], [far] * 2, [pltpu.HBM(*starts)] * 2
+        scratch += [pltpu.VMEM(*starts), dma((2,))]
+    outs = pl.pallas_call(
+        functools.partial(states_kernel, other is not None),
+        in_specs=[pl.BlockSpec(memory_space=pltpu.SMEM), far, far, far] + [far] * len(others),
+        out_specs=[vmem] * CHAIN_PARTS + start_specs,
+        out_shape=[message] * CHAIN_PARTS + start_shapes,
+        scratch_shapes=scratch,
         compiler_params=params(STREAM_MIB),
         cost_estimate=SHORT,
-    )(side, *in_hbm(rates, key_vectors, value_vectors))
-    return messages, starts
-
-
-def inside_kernel(place_ref, rate_hbm, query_hbm, key_hbm, value_hbm, keep_hbm, send_hbm, after_ref,
-                  *refs):
+    )(side, *in_hbm(rates, key_vectors, value_vectors), *others)
+    return outs[:CHAIN_PARTS], outs[CHAIN_PARTS:]
+
+
+def inside_kernel(begin, end, place_ref, rate_hbm, query_hbm, key_hbm, value_hbm, keep_hbm, send_hbm,
+                  after_ref, *refs):
     del after_ref
     rate_ref, queries, keys, values, keeps, sends, parts, rate_sem, load_sem, store_sem = refs[-10:]
     outs = refs[:-10]
     heads, tokens = rate_ref.shape
     count, half = keeps.shape[:2]
-    size = queries.shape[0] // count
+    size = tokens // keep_hbm.shape[0]
     is_odd = place_ref[count] == 1
-    rows = [slice(block * size, (block + 1) * size) for block in range(count)]
-    loads = [[] for _ in rows]
-    for block, at in enumerate(rows):
+    loads = []
+    for block in range(count):
         place = place_ref[block]
-        far = pl.ds(pl.multiple_of(place * size, size), size)
-        pairs = [(query_hbm.at[far], queries.at[at]), (key_hbm.at[far], keys.at[at]),
-                 (value_hbm.at[far], values.at[at]), (keep_hbm.at[place], keeps.at[block]),
-                 (send_hbm.at[place], sends.at[block])]
-        for i, (source, target) in enumerate(pairs):
-            loads[block].append(pltpu.make_async_copy(source, target, load_sem.at[block, i]))
+        far = pl.ds(pl.multiple_of(place * size + begin, 16), end - begin)
+        until = pl.ds(pl.multiple_of(place * size, size), end)
+        pairs = [(query_hbm.at[far], queries), (key_hbm.at[until], keys), (value_hbm.at[until], values),
+                 (keep_hbm.at[place], keeps), (send_hbm.at[place], sends)]
+        loads.append([pltpu.make_async_copy(source, target.at[block], load_sem.at[block, i])
+                      for i, (source, target) in enumerate(pairs)])
     rate_load = pltpu.make_async_copy(rate_hbm, rate_ref, rate_sem)
     for load in [rate_load] + loads[0]:
         load.start()
     rate_load.wait()
     stores = [
-        pltpu.make_async_copy(parts.at[at], outs[2 * block], store_sem.at[block])
-        for block, at in enumerate(rows)
+        pltpu.make_async_copy(parts.at[block], outs[2 * block], store_sem.at[block])
+        for block in range(count)
     ]
-    causal = lower_triangle(size)
-    for block, at in enumerate(rows):
-        begin = place_ref[block] * size
-        rates = rate_ref[:, pl.ds(pl.multiple_of(begin, size), size)]
-        ahead = (lax.broadcasted_iota(jnp.int32, (8, tokens), 1) < begin).astype(F32)
-        lead = fold_three(lax.dot_general(
-            ahead.astype(BF16), split_three(rate_ref[...]), (((1,), (1,)), ((), ())),
-            preferred_element_type=F32,
-        ))
-        running = running_sum(rates)
-        running_rows = running_sum_rows(rates)
+    causal = lower_triangle(size)[begin:end, :end]
+    for block in range(count):
+        first = place_ref[block] * size
+        rates = rate_ref[:, pl.ds(pl.multiple_of(first, size), size)]
+        ahead = lax.broadcasted_iota(jnp.int32, (heads, tokens), 1) < first
+        lead = jnp.sum(jnp.where(ahead, rate_ref[...], 0.0), axis=1, keepdims=True)
+        running_rows = running_sum(rates)
+        running = running_rows.T[begin:end]
         fade = jnp.exp(running)
-        outs[2 * block + 1][...] = jnp.exp(running + lead[:1])
+        outs[2 * block + 1][...] = jnp.exp(running_rows + lead).T[begin:end]
+        running_rows = running_rows[:, :end]
         for load in loads[block]:
             load.wait()
         for load in loads[block + 1] if block + 1 < count else ():
@@ -211,50 +208,50 @@
             side, slot = head // half, head % half
             kept, sent = keeps[block, slot], sends[block, slot]
             start = jnp.where(is_odd, kept, sent) if side else jnp.where(is_odd, sent, kept)
-            query = queries[at, of_head]
+            query = queries[block, :, of_head]
             scores = lax.dot_general(
-                query, keys[at, of_head], (((1,), (1,)), ((), ())), preferred_element_type=F32
+                query, keys[block, :, of_head], (((1,), (1,)), ((), ())), preferred_element_type=F32
             )
             spread = running[:, head:head + 1] - running_rows[head:head + 1, :]
             decay = jnp.exp(jnp.where(causal, spread, -1e30))
             weights = (scores * decay).astype(BF16)
-            inside = jnp.dot(weights, values[at, of_head], preferred_element_type=F32)
+            inside = jnp.dot(weights, values[block, :, of_head], preferred_element_type=F32)
             carried = fold_pair(jnp.dot(query, split_pair(start), preferred_element_type=F32))
-            parts[at, of_head] = inside + carried * fade[:, head:head + 1]
+            parts[block, :, of_head] = inside + carried * fade[:, head:head + 1]
         stores[block].start()
     for store in stores:
         store.wait()
 
 
-def inside_part(place, rates, queries, key_vectors, value_vectors, starts, block_len, after):
+def inside_part(place, begin, end, rates, queries, key_vectors, value_vectors, starts, block_len, after):
     count = place.shape[0] - 1
     features = queries.shape[1]
     heads = features // HEAD_DIM
+    rows = end - begin
     vmem, far = pl.BlockSpec(memory_space=pltpu.VMEM), pl.BlockSpec(memory_space=pl.ANY)
-    rows = pltpu.VMEM((count * block_len, features), BF16)
+    keys = pltpu.VMEM((count, end, features), BF16)
     state = pltpu.VMEM((count, heads // 2, HEAD_DIM, HEAD_DIM), F32)
     return pl.pallas_call(
-        inside_kernel,
+        functools.partial(inside_kernel, begin, end),
         in_specs=[pl.BlockSpec(memory_space=pltpu.SMEM)] + [far] * 7,
         out_specs=[far, vmem] * count,
-        out_shape=[
-            pltpu.HBM((block_len, features), F32), pltpu.HBM((block_len, heads), F32),
-        ] * count,
-        scratch_shapes=[pltpu.VMEM(rates.shape, F32), rows, rows, rows, state, state,
-                        pltpu.VMEM((count * block_len, features), F32), pltpu.SemaphoreType.DMA,
-                        pltpu.SemaphoreType.DMA((count, 5)), pltpu.SemaphoreType.DMA((count,))],
+        out_shape=[pltpu.HBM((rows, features), F32), pltpu.HBM((rows, heads), F32)] * count,
+        scratch_shapes=[pltpu.VMEM(rates.shape, F32), pltpu.VMEM((count, rows, features), BF16), keys, keys,
+                        state, state, pltpu.VMEM((count, rows, features), F32),
+                        pltpu.SemaphoreType.DMA, pltpu.SemaphoreType.DMA((count, 5)),
+                        pltpu.SemaphoreType.DMA((count,))],
         compiler_params=params(STREAM_MIB),
         cost_estimate=SHORT,
     )(place, *in_hbm(rates, queries, key_vectors, value_vectors, *starts), after)
 
 
-def row_loads(first_row, block_len, place_ref, query_hbm, gate_hbm, parts_hbm, queries, gates, parts,
+def row_loads(first_row, part_row, block_len, place_ref, query_hbm, gate_hbm, parts_hbm, queries, gates, parts,
               leads, sem):
     rows = queries.shape[0] // 2
     loads = []
     for which, (part_hbm, lead_hbm) in enumerate(parts_hbm):
         whole = pl.ds(pl.multiple_of(place_ref[which] * block_len + first_row, rows), rows)
-        group = slice(first_row, first_row + rows)
+        group = slice(part_row, part_row + rows)
         at = slice(which * rows, (which + 1) * rows)
         pairs = [(query_hbm.at[whole], queries.at[at]), (part_hbm.at[group], parts.at[at]),
                  (gate_hbm.at[whole], gates.at[at]), (lead_hbm.at[group], leads.at[at])]
@@ -263,10 +260,10 @@
     return loads
 
 
-def bring_kernel(first_row, block_len, place_ref, query_hbm, gate_hbm, weight_hbm, part_0, lead_0,
+def bring_kernel(first_row, part_row, block_len, place_ref, query_hbm, gate_hbm, weight_hbm, part_0, lead_0,
                  part_1, lead_1, after_ref, queries, gates, parts, leads, weight, row_sem, weight_sem):
     del after_ref
-    loads = row_loads(first_row, block_len, place_ref, query_hbm, gate_hbm,
+    loads = row_loads(first_row, part_row, block_len, place_ref, query_hbm, gate_hbm,
                       ((part_0, lead_0), (part_1, lead_1)), queries, gates, parts, leads, row_sem)
     loads.append(pltpu.make_async_copy(weight_hbm.at[:, :weight.shape[1]], weight, weight_sem))
     for load in loads:
@@ -280,11 +277,11 @@
             ((2 * rows, features // HEAD_DIM), F32)]
 
 
-def bring_rows(place, rows, first_row, block_len, queries, parts, gate_input, out_weight, after):
+def bring_rows(place, rows, first_row, part_row, block_len, queries, parts, gate_input, out_weight, after):
     features, width = out_weight.shape
     shapes = row_shapes(rows, features) + [((features, width // TILE // 2 * TILE), BF16)]
     return pl.pallas_call(
-        functools.partial(bring_kernel, first_row, block_len),
+        functools.partial(bring_kernel, first_row, part_row, block_len),
         in_specs=[pl.BlockSpec(memory_space=pltpu.SMEM)] + [pl.BlockSpec(memory_space=pl.ANY)] * 8,
         out_specs=[pl.BlockSpec(memory_space=pltpu.VMEM)] * len(shapes),
         out_shape=[pltpu.VMEM(*shape) for shape in shapes],
@@ -294,7 +291,7 @@
     )(place, *in_hbm(queries, gate_input, out_weight, *parts[0], *parts[1]), after)
 
 
-def project_kernel(first_row, block_len, pieces, brought, place_ref, *refs):
+def project_kernel(first_row, part_row, block_len, pieces, brought, place_ref, *refs):
     states, refs = refs[:2 * CHAIN_PARTS], refs[2 * CHAIN_PARTS:]
     if brought:
         queries, gates, parts, leads, early, weight_hbm, after_ref, *refs = refs
@@ -318,7 +315,7 @@
     ]
     if not brought:
         queries, gates, parts, leads, row_sem = refs
-        loads += row_loads(first_row, block_len, place_ref, query_hbm, gate_hbm,
+        loads += row_loads(first_row, part_row, block_len, place_ref, query_hbm, gate_hbm,
                            ((part_0, lead_0), (part_1, lead_1)), queries, gates, parts, leads, row_sem)
     heads = queries.shape[1] // HEAD_DIM
     half = heads // 2
@@ -360,7 +357,7 @@
         store.wait()
 
 
-def project_rows(place, rows, first_row, block_len, queries, parts, gate_input, kept, got,
+def project_rows(place, rows, first_row, part_row, block_len, queries, parts, gate_input, kept, got,
                  out_weight, after, pieces, brought=None):
     features = queries.shape[1]
     width = out_weight.shape[1]
@@ -385,7 +382,7 @@
         scratch += [pltpu.VMEM(*shape) for shape in row_shapes(rows, features)]
         scratch += [dma((2, 4))]
     return pl.pallas_call(
-        functools.partial(project_kernel, first_row, block_len, pieces, brought is not None),
+        functools.partial(project_kernel, first_row, part_row, block_len, pieces, brought is not None),
         in_specs=[pl.BlockSpec(memory_space=pltpu.SMEM)] + [far] * 2 * CHAIN_PARTS + specs + [far],
         out_specs=[far] * len(sizes),
         out_shape=[jax.ShapeDtypeStruct((size, width), F32) for size in sizes],
@@ -545,21 +542,22 @@
     rates = log_decay.T
     swap = [(i, i ^ 1) for i in range(lax.axis_size("seq"))]
 
-    sent, sent_starts = local_states(1 - odd, rates, key_vectors, value_vectors, block_len)
+    sent, (sent_starts,) = local_states(1 - odd, rates, key_vectors, value_vectors, block_len)
     met = [lax.ppermute(piece, "seq", swap) for piece in sent]
-    kept, kept_starts = local_states(odd, rates, key_vectors, value_vectors, block_len)
+    kept, starts = local_states(odd, rates, key_vectors, value_vectors, block_len, sent_starts)
 
     def place_of(target):
         return jnp.stack([2 * target + 1 - core, 2 * target + core, odd[0]]).astype(jnp.int32)
 
-    def parts_of(target, after):
-        outs = inside_part(place_of(target), rates, queries, key_vectors, value_vectors,
-                           (kept_starts, sent_starts), block_len, after)
+    def parts_of(target, begin, end, after):
+        outs = inside_part(place_of(target), begin, end, rates, queries, key_vectors, value_vectors,
+                           starts, block_len, after)
         return outs[:2], outs[2:]
 
-    def project(target, parts, group, after, pieces, brought=None):
+    def project(target, parts, part_begin, group, after, pieces, brought=None):
+        first = firsts[group]
         *theirs, mine = project_rows(
-            place_of(target), sizes[group], firsts[group], block_len, queries, parts, gate_input, keep,
+            place_of(target), sizes[group], first, first - part_begin, block_len, queries, parts, gate_input, keep,
             got, out_weight, after, pieces, brought)
         return mine, [lax.ppermute(piece, "head", cores) for piece in theirs]
 
@@ -568,25 +566,28 @@
     parts = []
 
     def inside_of(target, after):
-        parts.append(parts_of(target, after))
+        parts.append(parts_of(target, 0, firsts[EARLY_GROUPS], after))
         return parts[-1][1][1]
 
     keep, got = incoming_states(
-        odd, kept, met, kept_starts, [functools.partial(inside_of, target) for target in targets])
+        odd, kept, met, starts[0], [functools.partial(inside_of, target) for target in targets])
     last = keep[-1]
-    brought = bring_rows(place_of(targets[0]), sizes[0], firsts[0], block_len, queries, parts[0],
+    brought = bring_rows(place_of(targets[0]), sizes[0], 0, 0, block_len, queries, parts[0],
                          gate_input, out_weight, last)
     landed, own, result = [last, last], [], None
     arrived = [[] for _ in sizes]
     for group in range(len(sizes)):
         for step, target in enumerate(targets):
             across = [(i, ((i // 2 + step + 1) % chips) * 2 + i % 2) for i in range(count)]
-            mine, pieces = project(target, parts[step], group, last, CORE_PIECES, brought)
+            mine, pieces = project(
+                target, parts[step], firsts[EARLY_GROUPS] if group >= EARLY_GROUPS else 0, group, last, CORE_PIECES, brought)
             brought = None
             last = add_pieces(mine, pieces, landed[-DEPTH])
             landed.append(lax.ppermute(last, "head", across))
             arrived[group].append(landed[-1])
-    own_parts = parts_of(chip, last)
+        if group == EARLY_GROUPS - 1:
+            parts = [parts_of(target, firsts[EARLY_GROUPS], block_len, last) for target in targets]
+    own_parts = parts_of(chip, 0, block_len, last)
     groups = list(zip(firsts, sizes))
     own_rows, piece = block_len // OWN_GROUPS, block_len // 8
     sizes = [own_rows] * OWN_GROUPS
@@ -594,7 +595,7 @@
     for group in range(len(sizes)):
         if group == len(sizes) - 1:
             last = landed[-2]
-        own.append(project(chip, own_parts, group, last, own_rows // piece))
+        own.append(project(chip, own_parts, 0, group, last, own_rows // piece))
         last = own[-1][0]
     for group, (first, size) in enumerate(groups):
         mine, pieces = own[first // own_rows]

time: 138 us -> 137 us (level)
  waiting for transfers between devices: 41.4 us -> 35.7 us
  Pallas kernels: 70.2 us -> 75.1 us
    ppermute x4, waiting for transfers between devices: 26.6 us -> 21.2 us  [per_device(): landed.append(lax.ppermute(last, 'head', across))]
    pallas_call x11 -> x12, Pallas kernels: 62.2 us -> 67.1 us  [the longest x6 38.5 us: project_rows(): pl.pallas_call(functools.partial(project_kernel, first_row, part_row, blo...]
  transfers between devices with their start and end apart: 38 -> 38, of which waited for: 22 -> 22; matrix products, arithmetic and copies ran while one was open for 0% -> 0% of each run, Pallas kernels for 45% -> 49%
where the time goes in v5:
time: 137 us; the launch traced here: 136 us
  Pallas kernels  75.1 us (55%)
  waiting for transfers between devices  35.7 us (26%)
  starting transfers between devices  21.2 us (15%)
  local copies, waits for them, and re-layouts  3.08 us (2%)
    pallas_call x6, Pallas kernels, project_rows(): pl.pallas_call(functools.partial(project_kernel, first_row, part_row, blo...  38.5 us
    ppermute x4, waiting for transfers between devices, per_device(): landed.append(lax.ppermute(last, 'head', across))  21.2 us
    pallas_call x3, Pallas kernels, inside_part(): pl.pallas_call(functools.partial(inside_kernel, begin, end), in_specs=[pl...  18.4 us
    ppermute x24, waiting for transfers between devices, project(): return (mine, [lax.ppermute(piece, 'head', cores) for piece in theirs])  7.43 us
    pallas_call x2, Pallas kernels, local_states(): pl.pallas_call(functools.partial(states_kernel, other is not None), in_sp...  7.01 us
    pallas_call x4, Pallas kernels, finish_rows(): pl.pallas_call(functools.partial(finish_kernel, len(arrived)), grid=(1,),...  6.31 us
    ppermute x24, starting transfers between devices, project(): return (mine, [lax.ppermute(piece, 'head', cores) for piece in theirs])  5.63 us
    ppermute x6, starting transfers between devices, incoming_states(): landed[i].append(lax.ppermute(value, 'seq', along))  5.44 us
  transfers between devices with their start and end apart: 38, of which 22 were waited for; matrix products, arithmetic and copies ran while one was open for 0% of the time, Pallas kernels for 49%

profile of v5, /device:TPU:24, one launch (start us, length us, event | category | flops | bytes accessed | tf_op | source)
XLA Modules:
  0.0 135.6 jit_solution(14294076019827684262)
XLA Ops:
  0.0 3.0 %shard_map.64 = (f32[2,136,128]{2,1,0:T(8,128)S(1)}, f32[2,136,128]{2,1,0:T(8,128)S(1)}, f32[4,4,128,128]{3,2,1,0:T(8,128)S(1)}) custom-call(s32[1]{0:T(128)S(6)} %sub.12.side_ref, f32[8,1024]{1,0:T(8,128)} %bitcast.6, bf16[1024,1024]{1,0:T(8,128)(2,1)} %key_hbm.9, bf16[1024,1024]{1,0:T(8,128)(2,1)} %value_hbm.9), custom_call_target="tpu_custom_call" | custom-call | flops 1 | bytes 1 | tf_op jit(solution)/shard_map/pallas_call | solution.py:153
  3.0 1.6 %collective-permute-start = (f32[2,136,128]{2,1,0:T(8,128)S(1)}, f32[2,136,128]{2,1,0:T(8,128)S(1)}, u32[]{:S(2)}, u32[]{:S(2)}) collective-permute-start(f32[2,136,128]{2,1,0:T(8,128)S(1)} %get-tuple-element.65), channel_id=1, source_target_pairs={{0,4},{4,0},{8,12},{12,8},{16,20},{20,16},{24,28},{28,24},{1,5},{5... | collective-permute-start | bytes 417800 | tf_op jit(solution)/shard_map/ppermute | solution.py:546
  5.1 4.0 %shard_map.65 = (f32[2,136,128]{2,1,0:T(8,128)S(1)}, f32[2,136,128]{2,1,0:T(8,128)S(1)}, f32[4,4,128,128]{3,2,1,0:T(8,128)}, f32[4,4,128,128]{3,2,1,0:T(8,128)}) custom-call(s32[1]{0:T(128)} %bitcast.2.side_ref.odd_ref, f32[8,1024]{1,0:T(8,128)} %bitcast.7, bf16[1024,1024]{1,0:T(8,128)(2,1)} %key_hbm.9, bf16[1024,1024]{1,0:T(8,128)(2,1)} %value_hbm.9, ...), custom_call_target="tpu_custom_call" | custom-call | flops 1 | bytes 1 | tf_op jit(solution)/shard_map/pallas_call | solution.py:153
  10.3 1.1 collective-permute-done.3.refs_1_.refs_2_.refs_3_.refs_4_
  13.7 6.2 %shard_map.70 = (f32[192,1024]{1,0:T(8,128)}, f32[192,8]{1,0:T(8,128)}, f32[192,1024]{1,0:T(8,128)}, f32[192,8]{1,0:T(8,128)}) custom-call(s32[3]{0:T(128)S(1)} %add_add_fusion.1.place_ref, f32[8,1024]{1,0:T(8,128)} %bitcast.8, bf16[1024,1024]{1,0:T(8,128)(2,1)} %refs_4_.9, bf16[1024,1024]{1,0:T(8,128)(2,1)} %key_hbm.9, bf16[1024,1024]{1,0:T(8,128)(2,1)} %value_hbm.9, ...), custom_call_target="tpu_custom_call" | custom-call | flops 1 | bytes 1 | tf_op jit(solution)/shard_map/pallas_call | solution.py:234
  20.0 1.3 collective-permute-start.5
  21.4 1.5 %collective-permute-start.7 = (f32[2,128,128]{2,1,0:T(8,128)S(1)}, f32[2,128,128]{2,1,0:T(8,128)S(1)}, u32[]{:S(2)}, u32[]{:S(2)}) collective-permute-start(f32[2,128,128]{2,1,0:T(8,128)S(1)} %shard_map.73), channel_id=1, source_target_pairs={{16,24},{20,28},{17,25},{21,29},{18,26},{22,30},{19,27},{23,31}} | collective-permute-start | bytes 393224 | tf_op jit(solution)/shard_map/ppermute | solution.py:519
  22.9 5.0 %collective-permute-done.5.refs_2_ = f32[2,128,128]{2,1,0:T(8,128)S(1)} collective-permute-done((f32[2,128,128]{2,1,0:T(8,128)S(1)}, f32[2,128,128]{2,1,0:T(8,128)S(1)}, u32[]{:S(2)}, u32[]{:S(2)}) %collective-permute-start.5) | collective-permute-done | bytes 131104 | tf_op jit(solution)/shard_map/ppermute | solution.py:519
  27.9 1.6 %collective-permute-start.8 = (f32[2,128,128]{2,1,0:T(8,128)S(1)}, f32[2,128,128]{2,1,0:T(8,128)S(1)}, u32[]{:S(2)}, u32[]{:S(2)}) collective-permute-start(f32[2,128,128]{2,1,0:T(8,128)S(1)} %get-tuple-element.73), channel_id=1, source_target_pairs={{0,4},{4,0},{8,12},{12,8},{16,20},{20,16},{24,28},{28,24},{1,5},{5... | collective-permute-start | bytes 393224 | tf_op jit(solution)/shard_map/ppermute | solution.py:527
  29.6 1.4 collective-permute-start.9
  31.0 3.2 %shard_map.75 = (bf16[128,1024]{1,0:T(8,128)(2,1)S(1)}, bf16[128,1024]{1,0:T(8,128)(2,1)S(1)}, f32[128,1024]{1,0:T(8,128)S(1)}, f32[128,8]{1,0:T(8,128)S(1)}, bf16[1024,2048]{1,0:T(8,128)(2,1)S(1)}) custom-call(s32[3]{0:T(128)S(1)} %add_add_fusion.1.place_ref, bf16[1024,1024]{1,0:T(8,128)(2,1)} %refs_4_.9, bf16[1024,1024]{1,0:T(8,128)(2,1)} %refs_5_.9, ...), custom_call_target="tpu_custom_call" | custom-call | flops 1 | bytes 1 | tf_op jit(solution)/shard_map/pallas_call | solution.py:283
  34.6 4.5 %shard_map.76 = (f32[16,4096]{1,0:T(8,128)S(1)}, f32[16,4096]{1,0:T(8,128)S(1)}, f32[16,4096]{1,0:T(8,128)S(1)}, f32[16,4096]{1,0:T(8,128)S(1)}, f32[64,4096]{1,0:T(8,128)S(1)}) custom-call(s32[3]{0:T(128)S(1)} %add_add_fusion.1.place_ref, f32[2,128,128]{2,1,0:T(8,128)S(1)} %get-tuple-element.71.refs_0_, ...), custom_call_target="tpu_custom_call" | custom-call | flops 1 | bytes 1 | tf_op jit(solution)/shard_map/pallas_call | solution.py:384
  41.9 1.6 %collective-permute-start.22 = (f32[64,4096]{1,0:T(8,128)S(1)}, f32[64,4096]{1,0:T(8,128)S(1)}, u32[]{:S(2)}, u32[]{:S(2)}) collective-permute-start(f32[64,4096]{1,0:T(8,128)S(1)} %shard_map.77.refs_11_), channel_id=1, source_target_pairs={{0,2},{1,3},{2,0},{3,1},{4,6},{5,7},{6,4},{7,5},{8,10},{9,11},{10,... | collective-permute-start | bytes 3145736 | tf_op jit(solution)/shard_map/ppermute | solution.py:586
  43.5 6.3 %shard_map.78 = (f32[16,4096]{1,0:T(8,128)S(1)}, f32[16,4096]{1,0:T(8,128)S(1)}, f32[16,4096]{1,0:T(8,128)S(1)}, f32[16,4096]{1,0:T(8,128)S(1)}, f32[64,4096]{1,0:T(8,128)S(1)}) custom-call(s32[3]{0:T(128)S(1)} %add_add_fusion.1.place_ref, f32[2,128,128]{2,1,0:T(8,128)S(1)} %get-tuple-element.71.refs_0_, ...), custom_call_target="tpu_custom_call" | custom-call | flops 1 | bytes 1 | tf_op jit(solution)/shard_map/pallas_call | solution.py:384
  52.6 6.3 %shard_map.80 = (f32[16,4096]{1,0:T(8,128)S(1)}, f32[16,4096]{1,0:T(8,128)S(1)}, f32[16,4096]{1,0:T(8,128)S(1)}, f32[16,4096]{1,0:T(8,128)S(1)}, f32[64,4096]{1,0:T(8,128)S(1)}) custom-call(s32[3]{0:T(128)S(1)} %add_add_fusion.1.place_ref, f32[2,128,128]{2,1,0:T(8,128)S(1)} %get-tuple-element.71.refs_0_, ...), custom_call_target="tpu_custom_call" | custom-call | flops 1 | bytes 1 | tf_op jit(solution)/shard_map/pallas_call | solution.py:384
  61.7 6.3 %collective-permute-done.22.refs_4_.refs_0_ = f32[64,4096]{1,0:T(8,128)S(1)} collective-permute-done((f32[64,4096]{1,0:T(8,128)S(1)}, f32[64,4096]{1,0:T(8,128)S(1)}, u32[]{:S(2)}, u32[]{:S(2)}) %collective-permute-start.22) | collective-permute-done | bytes 1048608 | tf_op jit(solution)/shard_map/ppermute | solution.py:586
  69.0 1.5 %collective-permute-start.28 = (f32[64,4096]{1,0:T(8,128)S(1)}, f32[64,4096]{1,0:T(8,128)}, u32[]{:S(2)}, u32[]{:S(2)}) collective-permute-start(f32[64,4096]{1,0:T(8,128)S(1)} %shard_map.81.after_ref.refs_11_), channel_id=1, source_target_pairs={{0,2},{1,3},{2,0},{3,1},{4,6},{5,7},{6,4},{7,5},{8,10},{9,11},{10,... | collective-permute-start | bytes 3145736 | tf_op jit(solution)/shard_map/ppermute | solution.py:586
  70.5 5.5 %shard_map.82 = (f32[64,1024]{1,0:T(8,128)}, f32[64,8]{1,0:T(8,128)}, f32[64,1024]{1,0:T(8,128)}, f32[64,8]{1,0:T(8,128)}) custom-call(s32[3]{0:T(128)S(1)} %add_add_fusion.1.place_ref, f32[8,1024]{1,0:T(8,128)} %bitcast.9, bf16[1024,1024]{1,0:T(8,128)(2,1)} %refs_4_.9, bf16[1024,1024]{1,0:T(8,128)(2,1)} %key_hbm.9, bf16[1024,1024]{1,0:T(8,128)(2,1)} %value_hbm.9, ...), custom_call_target="tpu_custom_call" | custom-call | flops 1 | bytes 1 | tf_op jit(solution)/shard_map/pallas_call | solution.py:234
  76.0 7.1 %shard_map.83 = (f32[16,4096]{1,0:T(8,128)S(1)}, f32[16,4096]{1,0:T(8,128)}, f32[16,4096]{1,0:T(8,128)}, f32[16,4096]{1,0:T(8,128)}, f32[64,4096]{1,0:T(8,128)S(1)}) custom-call(s32[3]{0:T(128)S(1)} %add_add_fusion.1.place_ref, f32[2,128,128]{2,1,0:T(8,128)S(1)} %get-tuple-element.71.refs_0_, ...), custom_call_target="tpu_custom_call" | custom-call | flops 1 | bytes 1 | tf_op jit(solution)/shard_map/pallas_call | solution.py:384
  84.5 1.4 %collective-permute-done.23.refs_0_ = f32[16,4096]{1,0:T(8,128)S(1)} collective-permute-done((f32[16,4096]{1,0:T(8,128)S(1)}, f32[16,4096]{1,0:T(8,128)S(1)}, u32[]{:S(2)}, u32[]{:S(2)}) %collective-permute-start.23) | collective-permute-done | bytes 262176 | tf_op jit(solution)/shard_map/ppermute | solution.py:562
  86.5 1.3 collective-permute-done.26.refs_3_
  87.8 2.8 %collective-permute-done.27.refs_4_.refs_0_ = f32[64,4096]{1,0:T(8,128)} collective-permute-done((f32[64,4096]{1,0:T(8,128)S(1)}, f32[64,4096]{1,0:T(8,128)}, u32[]{:S(2)}, u32[]{:S(2)}) %collective-permute-start.27) | collective-permute-done | bytes 1048608 | tf_op jit(solution)/shard_map/ppermute | solution.py:586
  90.6 1.2 copy-done.3
  91.8 1.1 shard_map.84.after_ref.refs_11_
  92.9 6.7 %shard_map.85 = (f32[256,1024]{1,0:T(8,128)}, f32[256,8]{1,0:T(8,128)}, f32[256,1024]{1,0:T(8,128)}, f32[256,8]{1,0:T(8,128)}) custom-call(s32[3]{0:T(128)S(1)} %add_add_fusion.place_ref, f32[8,1024]{1,0:T(8,128)} %bitcast.10, bf16[1024,1024]{1,0:T(8,128)(2,1)} %refs_4_.9, bf16[1024,1024]{1,0:T(8,128)(2,1)} %key_hbm.9, bf16[1024,1024]{1,0:T(8,128)(2,1)} %value_hbm.9, ...), custom_call_target="tpu_custom_call" | custom-call | flops 1 | bytes 1 | tf_op jit(solution)/shard_map/pallas_call | solution.py:234
  99.6 7.2 %shard_map.87 = (f32[32,4096]{1,0:T(8,128)S(1)}, f32[32,4096]{1,0:T(8,128)S(1)}, f32[32,4096]{1,0:T(8,128)S(1)}, f32[32,4096]{1,0:T(8,128)S(1)}, f32[128,4096]{1,0:T(8,128)S(1)}) custom-call(s32[3]{0:T(128)S(1)} %add_add_fusion.place_ref, f32[2,128,128]{2,1,0:T(8,128)S(1)} %get-tuple-element.71.refs_0_, ...), custom_call_target="tpu_custom_call" | custom-call | flops 1 | bytes 1 | tf_op jit(solution)/shard_map/pallas_call | solution.py:384
  107.3 1.5 %collective-permute-start.29 = (f32[64,4096]{1,0:T(8,128)S(1)}, f32[64,4096]{1,0:T(8,128)S(1)}, u32[]{:S(2)}, u32[]{:S(2)}) collective-permute-start(f32[64,4096]{1,0:T(8,128)S(1)} %shard_map.84.after_ref.refs_11_), channel_id=1, source_target_pairs={{0,2},{1,3},{2,0},{3,1},{4,6},{5,7},{6,4},{7,5},{8,10},{9,11},{10,... | collective-permute-start | bytes 3145736 | tf_op jit(solution)/shard_map/ppermute | solution.py:586
  108.8 4.2 %collective-permute-done.28.refs_11_.refs_0_ = f32[64,4096]{1,0:T(8,128)} collective-permute-done((f32[64,4096]{1,0:T(8,128)S(1)}, f32[64,4096]{1,0:T(8,128)}, u32[]{:S(2)}, u32[]{:S(2)}) %collective-permute-start.28) | collective-permute-done | bytes 1048608 | tf_op jit(solution)/shard_map/ppermute | solution.py:586
  113.1 7.2 %shard_map.86 = (f32[32,4096]{1,0:T(8,128)S(1)}, f32[32,4096]{1,0:T(8,128)S(1)}, f32[32,4096]{1,0:T(8,128)S(1)}, f32[32,4096]{1,0:T(8,128)S(1)}, f32[128,4096]{1,0:T(8,128)S(1)}) custom-call(s32[3]{0:T(128)S(1)} %add_add_fusion.place_ref, f32[2,128,128]{2,1,0:T(8,128)S(1)} %get-tuple-element.71.refs_0_, ...), custom_call_target="tpu_custom_call" | custom-call | flops 1 | bytes 1 | tf_op jit(solution)/shard_map/pallas_call | solution.py:384
  122.4 2.2 %shard_map.89.refs_3_ = bf16[256,4096]{1,0:T(8,128)(2,1)} custom-call(f32[128,4096]{1,0:T(8,128)S(1)} %get-tuple-element.116.own_ref.refs_3_, f32[64,4096]{1,0:T(8,128)} %collective-permute-done.27.refs_4_.refs_0_, f32[32,4096]{1,0:T(8,128)S(1)} %collective-permute-done.34.refs_1_, ...), custom_call_target="tpu_custom_call", output_to_operand_aliasing={{}: (4, {})} | custom-call | flops 1 | bytes 1 | tf_op jit(solution)/shard_map/pallas_call | solution.py:438
  124.6 2.2 %shard_map.90.refs_3_ = bf16[256,4096]{1,0:T(8,128)(2,1)} custom-call(f32[128,4096]{1,0:T(8,128)S(1)} %get-tuple-element.111.own_ref, f32[64,4096]{1,0:T(8,128)} %collective-permute-done.28.refs_11_.refs_0_, f32[32,4096]{1,0:T(8,128)S(1)} %collective-permute-done.32.refs_1_, ...), custom_call_target="tpu_custom_call", output_to_operand_aliasing={{}: (4, {})} | custom-call | flops 1 | bytes 1 | tf_op jit(solution)/shard_map/pallas_call | solution.py:438
  126.8 7.8 %collective-permute-done.29.refs_0_ = f32[64,4096]{1,0:T(8,128)S(1)} collective-permute-done((f32[64,4096]{1,0:T(8,128)S(1)}, f32[64,4096]{1,0:T(8,128)S(1)}, u32[]{:S(2)}, u32[]{:S(2)}) %collective-permute-start.29) | collective-permute-done | bytes 1048608 | tf_op jit(solution)/shard_map/ppermute | solution.py:586
  (82 shorter events, 19.7 us)
Async XLA Ops:
  3.0 6.6 %collective-permute-start = (f32[2,136,128]{2,1,0:T(8,128)S(1)}, f32[2,136,128]{2,1,0:T(8,128)S(1)}, u32[]{:S(2)}, u32[]{:S(2)}) collective-permute-start(f32[2,136,128]{2,1,0:T(8,128)S(1)} %get-tuple-element.65), channel_id=1, source_target_pairs={{0,4},{4,0},{8,12},{12,8},{16,20},{20,16},{24,28},{28,24},{1,5},{5... | collective-permute-start | bytes 417800 | tf_op jit(solution)/shard_map/ppermute | solution.py:546
  4.5 6.9 %collective-permute-start.3 = (f32[2,136,128]{2,1,0:T(8,128)S(1)}, f32[2,136,128]{2,1,0:T(8,128)S(1)}, u32[]{:S(2)}, u32[]{:S(2)}) collective-permute-start(f32[2,136,128]{2,1,0:T(8,128)S(1)} %get-tuple-element.69), channel_id=1, source_target_pairs={{0,4},{4,0},{8,12},{12,8},{16,20},{20,16},{24,28},{28,24},{1,5},{5... | collective-permute-start | bytes 417800 | tf_op jit(solution)/shard_map/ppermute | solution.py:546
  9.6 2.5 %collective-permute-start.1 = (f32[2,128,128]{2,1,0:T(8,128)S(1)}, f32[2,128,128]{2,1,0:T(8,128)S(1)}, u32[]{:S(2)}, u32[]{:S(2)}) collective-permute-start(f32[2,128,128]{2,1,0:T(8,128)S(1)} %shard_map.66), channel_id=1, source_target_pairs={{0,8},{4,12},{1,9},{5,13},{2,10},{6,14},{3,11},{7,15}} | collective-permute-start | bytes 393224 | tf_op jit(solution)/shard_map/ppermute | solution.py:519
  12.2 7.8 %collective-permute-start.2 = (f32[2,128,128]{2,1,0:T(8,128)S(1)}, f32[2,128,128]{2,1,0:T(8,128)S(1)}, u32[]{:S(2)}, u32[]{:S(2)}) collective-permute-start(f32[2,128,128]{2,1,0:T(8,128)S(1)} %shard_map.67), channel_id=1, source_target_pairs={{8,16},{12,20},{9,17},{13,21},{10,18},{14,22},{11,19},{15,23}} | collective-permute-start | bytes 393224 | tf_op jit(solution)/shard_map/ppermute | solution.py:519
  12.9 8.4 %collective-permute-start.6 = (f32[2,128,128]{2,1,0:T(8,128)S(1)}, f32[2,128,128]{2,1,0:T(8,128)S(1)}, u32[]{:S(2)}, u32[]{:S(2)}) collective-permute-start(f32[2,128,128]{2,1,0:T(8,128)S(1)} %shard_map.69.after_ref), channel_id=1, source_target_pairs={{8,16},{12,20},{9,17},{13,21},{10,18},{14,22},{11,19},{15,23}} | collective-permute-start | bytes 393224 | tf_op jit(solution)/shard_map/ppermute | solution.py:519
  20.0 7.8 %collective-permute-start.5 = (f32[2,128,128]{2,1,0:T(8,128)S(1)}, f32[2,128,128]{2,1,0:T(8,128)S(1)}, u32[]{:S(2)}, u32[]{:S(2)}) collective-permute-start(f32[2,128,128]{2,1,0:T(8,128)S(1)} %shard_map.71), channel_id=1, source_target_pairs={{16,24},{20,28},{17,25},{21,29},{18,26},{22,30},{19,27},{23,31}} | collective-permute-start | bytes 393224 | tf_op jit(solution)/shard_map/ppermute | solution.py:519
  21.4 8.2 %collective-permute-start.7 = (f32[2,128,128]{2,1,0:T(8,128)S(1)}, f32[2,128,128]{2,1,0:T(8,128)S(1)}, u32[]{:S(2)}, u32[]{:S(2)}) collective-permute-start(f32[2,128,128]{2,1,0:T(8,128)S(1)} %shard_map.73), channel_id=1, source_target_pairs={{16,24},{20,28},{17,25},{21,29},{18,26},{22,30},{19,27},{23,31}} | collective-permute-start | bytes 393224 | tf_op jit(solution)/shard_map/ppermute | solution.py:519
  27.9 6.3 %collective-permute-start.8 = (f32[2,128,128]{2,1,0:T(8,128)S(1)}, f32[2,128,128]{2,1,0:T(8,128)S(1)}, u32[]{:S(2)}, u32[]{:S(2)}) collective-permute-start(f32[2,128,128]{2,1,0:T(8,128)S(1)} %get-tuple-element.73), channel_id=1, source_target_pairs={{0,4},{4,0},{8,12},{12,8},{16,20},{20,16},{24,28},{28,24},{1,5},{5... | collective-permute-start | bytes 393224 | tf_op jit(solution)/shard_map/ppermute | solution.py:527
  29.6 5.0 %collective-permute-start.9 = (f32[2,128,128]{2,1,0:T(8,128)S(1)}, f32[2,128,128]{2,1,0:T(8,128)S(1)}, u32[]{:S(2)}, u32[]{:S(2)}) collective-permute-start(f32[2,128,128]{2,1,0:T(8,128)S(1)} %get-tuple-element.74), channel_id=1, source_target_pairs={{0,4},{4,0},{8,12},{12,8},{16,20},{20,16},{24,28},{28,24},{1,5},{5... | collective-permute-start | bytes 393224 | tf_op jit(solution)/shard_map/ppermute | solution.py:527
  39.2 1.9 %collective-permute-start.11 = (f32[16,4096]{1,0:T(8,128)S(1)}, f32[16,4096]{1,0:T(8,128)S(1)}, u32[]{:S(2)}, u32[]{:S(2)}) collective-permute-start(f32[16,4096]{1,0:T(8,128)S(1)} %get-tuple-element.85), channel_id=1, source_target_pairs={{0,1},{1,0},{2,3},{3,2},{4,5},{5,4},{6,7},{7,6},{8,9},{9,8},{10,11... | collective-permute-start | bytes 786440 | tf_op jit(solution)/shard_map/ppermute | solution.py:562
  39.7 1.8 %collective-permute-start.12 = (f32[16,4096]{1,0:T(8,128)S(1)}, f32[16,4096]{1,0:T(8,128)S(1)}, u32[]{:S(2)}, u32[]{:S(2)}) collective-permute-start(f32[16,4096]{1,0:T(8,128)S(1)} %get-tuple-element.86), channel_id=1, source_target_pairs={{0,1},{1,0},{2,3},{3,2},{4,5},{5,4},{6,7},{7,6},{8,9},{9,8},{10,11... | collective-permute-start | bytes 786440 | tf_op jit(solution)/shard_map/ppermute | solution.py:562
  39.8 2.1 %collective-permute-start.13 = (f32[16,4096]{1,0:T(8,128)S(1)}, f32[16,4096]{1,0:T(8,128)S(1)}, u32[]{:S(2)}, u32[]{:S(2)}) collective-permute-start(f32[16,4096]{1,0:T(8,128)S(1)} %get-tuple-element.87), channel_id=1, source_target_pairs={{0,1},{1,0},{2,3},{3,2},{4,5},{5,4},{6,7},{7,6},{8,9},{9,8},{10,11... | collective-permute-start | bytes 786440 | tf_op jit(solution)/shard_map/ppermute | solution.py:562
  41.9 26.1 %collective-permute-start.22 = (f32[64,4096]{1,0:T(8,128)S(1)}, f32[64,4096]{1,0:T(8,128)S(1)}, u32[]{:S(2)}, u32[]{:S(2)}) collective-permute-start(f32[64,4096]{1,0:T(8,128)S(1)} %shard_map.77.refs_11_), channel_id=1, source_target_pairs={{0,2},{1,3},{2,0},{3,1},{4,6},{5,7},{6,4},{7,5},{8,10},{9,11},{10,... | collective-permute-start | bytes 3145736 | tf_op jit(solution)/shard_map/ppermute | solution.py:586
  49.9 1.9 %collective-permute-start.15 = (f32[16,4096]{1,0:T(8,128)S(1)}, f32[16,4096]{1,0:T(8,128)S(1)}, u32[]{:S(2)}, u32[]{:S(2)}) collective-permute-start(f32[16,4096]{1,0:T(8,128)S(1)} %get-tuple-element.90), channel_id=1, source_target_pairs={{0,1},{1,0},{2,3},{3,2},{4,5},{5,4},{6,7},{7,6},{8,9},{9,8},{10,11... | collective-permute-start | bytes 786440 | tf_op jit(solution)/shard_map/ppermute | solution.py:562
  50.5 2.1 %collective-permute-start.17 = (f32[16,4096]{1,0:T(8,128)S(1)}, f32[16,4096]{1,0:T(8,128)S(1)}, u32[]{:S(2)}, u32[]{:S(2)}) collective-permute-start(f32[16,4096]{1,0:T(8,128)S(1)} %get-tuple-element.92), channel_id=1, source_target_pairs={{0,1},{1,0},{2,3},{3,2},{4,5},{5,4},{6,7},{7,6},{8,9},{9,8},{10,11... | collective-permute-start | bytes 786440 | tf_op jit(solution)/shard_map/ppermute | solution.py:562
  59.2 1.9 %collective-permute-start.19 = (f32[16,4096]{1,0:T(8,128)S(1)}, f32[16,4096]{1,0:T(8,128)S(1)}, u32[]{:S(2)}, u32[]{:S(2)}) collective-permute-start(f32[16,4096]{1,0:T(8,128)S(1)} %get-tuple-element.95), channel_id=1, source_target_pairs={{0,1},{1,0},{2,3},{3,2},{4,5},{5,4},{6,7},{7,6},{8,9},{9,8},{10,11... | collective-permute-start | bytes 786440 | tf_op jit(solution)/shard_map/ppermute | solution.py:562
  59.7 2.0 %collective-permute-start.21 = (f32[16,4096]{1,0:T(8,128)S(1)}, f32[16,4096]{1,0:T(8,128)S(1)}, u32[]{:S(2)}, u32[]{:S(2)}) collective-permute-start(f32[16,4096]{1,0:T(8,128)S(1)} %get-tuple-element.97), channel_id=1, source_target_pairs={{0,1},{1,0},{2,3},{3,2},{4,5},{5,4},{6,7},{7,6},{8,9},{9,8},{10,11... | collective-permute-start | bytes 786440 | tf_op jit(solution)/shard_map/ppermute | solution.py:562
  60.6 30.0 %collective-permute-start.27 = (f32[64,4096]{1,0:T(8,128)S(1)}, f32[64,4096]{1,0:T(8,128)}, u32[]{:S(2)}, u32[]{:S(2)}) collective-permute-start(f32[64,4096]{1,0:T(8,128)S(1)} %shard_map.79.refs_11_), channel_id=1, source_target_pairs={{0,2},{1,3},{2,0},{3,1},{4,6},{5,7},{6,4},{7,5},{8,10},{9,11},{10,... | collective-permute-start | bytes 3145736 | tf_op jit(solution)/shard_map/ppermute | solution.py:586
  69.0 44.1 %collective-permute-start.28 = (f32[64,4096]{1,0:T(8,128)S(1)}, f32[64,4096]{1,0:T(8,128)}, u32[]{:S(2)}, u32[]{:S(2)}) collective-permute-start(f32[64,4096]{1,0:T(8,128)S(1)} %shard_map.81.after_ref.refs_11_), channel_id=1, source_target_pairs={{0,2},{1,3},{2,0},{3,1},{4,6},{5,7},{6,4},{7,5},{8,10},{9,11},{10,... | collective-permute-start | bytes 3145736 | tf_op jit(solution)/shard_map/ppermute | solution.py:586
  84.0 1.9 %collective-permute-start.23 = (f32[16,4096]{1,0:T(8,128)S(1)}, f32[16,4096]{1,0:T(8,128)S(1)}, u32[]{:S(2)}, u32[]{:S(2)}) collective-permute-start(f32[16,4096]{1,0:T(8,128)S(1)} %get-tuple-element.103), channel_id=1, source_target_pairs={{0,1},{1,0},{2,3},{3,2},{4,5},{5,4},{6,7},{7,6},{8,9},{9,8},{10,11... | collective-permute-start | bytes 786440 | tf_op jit(solution)/shard_map/ppermute | solution.py:562
  84.0 2.1 %collective-permute-start.24 = (f32[16,4096]{1,0:T(8,128)}, f32[16,4096]{1,0:T(8,128)S(1)}, u32[]{:S(2)}, u32[]{:S(2)}) collective-permute-start(f32[16,4096]{1,0:T(8,128)} %get-tuple-element.104), channel_id=1, source_target_pairs={{0,1},{1,0},{2,3},{3,2},{4,5},{5,4},{6,7},{7,6},{8,9},{9,8},{10,11... | collective-permute-start | bytes 786440 | tf_op jit(solution)/shard_map/ppermute | solution.py:562
  84.5 2.0 %collective-permute-start.25 = (f32[16,4096]{1,0:T(8,128)}, f32[16,4096]{1,0:T(8,128)S(1)}, u32[]{:S(2)}, u32[]{:S(2)}) collective-permute-start(f32[16,4096]{1,0:T(8,128)} %get-tuple-element.105), channel_id=1, source_target_pairs={{0,1},{1,0},{2,3},{3,2},{4,5},{5,4},{6,7},{7,6},{8,9},{9,8},{10,11... | collective-permute-start | bytes 786440 | tf_op jit(solution)/shard_map/ppermute | solution.py:562
  85.9 1.9 %collective-permute-start.26 = (f32[16,4096]{1,0:T(8,128)}, f32[16,4096]{1,0:T(8,128)}, u32[]{:S(2)}, u32[]{:S(2)}) collective-permute-start(f32[16,4096]{1,0:T(8,128)} %get-tuple-element.106), channel_id=1, source_target_pairs={{0,1},{1,0},{2,3},{3,2},{4,5},{5,4},{6,7},{7,6},{8,9},{9,8},{10,11... | collective-permute-start | bytes 786440 | tf_op jit(solution)/shard_map/ppermute | solution.py:562
  106.8 13.5 %collective-permute-start.34 = (f32[32,4096]{1,0:T(8,128)S(1)}, f32[32,4096]{1,0:T(8,128)S(1)}, u32[]{:S(2)}, u32[]{:S(2)}) collective-permute-start(f32[32,4096]{1,0:T(8,128)S(1)} %get-tuple-element.117), channel_id=1, source_target_pairs={{0,1},{1,0},{2,3},{3,2},{4,5},{5,4},{6,7},{7,6},{8,9},{9,8},{10,11... | collective-permute-start | bytes 1572872 | tf_op jit(solution)/shard_map/ppermute | solution.py:562
  106.9 14.0 %collective-permute-start.35 = (f32[32,4096]{1,0:T(8,128)S(1)}, f32[32,4096]{1,0:T(8,128)S(1)}, u32[]{:S(2)}, u32[]{:S(2)}) collective-permute-start(f32[32,4096]{1,0:T(8,128)S(1)} %get-tuple-element.118), channel_id=1, source_target_pairs={{0,1},{1,0},{2,3},{3,2},{4,5},{5,4},{6,7},{7,6},{8,9},{9,8},{10,11... | collective-permute-start | bytes 1572872 | tf_op jit(solution)/shard_map/ppermute | solution.py:562
  107.3 27.3 %collective-permute-start.29 = (f32[64,4096]{1,0:T(8,128)S(1)}, f32[64,4096]{1,0:T(8,128)S(1)}, u32[]{:S(2)}, u32[]{:S(2)}) collective-permute-start(f32[64,4096]{1,0:T(8,128)S(1)} %shard_map.84.after_ref.refs_11_), channel_id=1, source_target_pairs={{0,2},{1,3},{2,0},{3,1},{4,6},{5,7},{6,4},{7,5},{8,10},{9,11},{10,... | collective-permute-start | bytes 3145736 | tf_op jit(solution)/shard_map/ppermute | solution.py:586
  108.8 12.1 %collective-permute-start.36 = (f32[32,4096]{1,0:T(8,128)S(1)}, f32[32,4096]{1,0:T(8,128)S(1)}, u32[]{:S(2)}, u32[]{:S(2)}) collective-permute-start(f32[32,4096]{1,0:T(8,128)S(1)} %get-tuple-element.119), channel_id=1, source_target_pairs={{0,1},{1,0},{2,3},{3,2},{4,5},{5,4},{6,7},{7,6},{8,9},{9,8},{10,11... | collective-permute-start | bytes 1572872 | tf_op jit(solution)/shard_map/ppermute | solution.py:562
  113.1 8.3 %collective-permute-start.37 = (f32[32,4096]{1,0:T(8,128)S(1)}, f32[32,4096]{1,0:T(8,128)S(1)}, u32[]{:S(2)}, u32[]{:S(2)}) collective-permute-start(f32[32,4096]{1,0:T(8,128)S(1)} %get-tuple-element.120), channel_id=1, source_target_pairs={{0,1},{1,0},{2,3},{3,2},{4,5},{5,4},{6,7},{7,6},{8,9},{9,8},{10,11... | collective-permute-start | bytes 1572872 | tf_op jit(solution)/shard_map/ppermute | solution.py:562
  120.2 4.3 %collective-permute-start.32 = (f32[32,4096]{1,0:T(8,128)S(1)}, f32[32,4096]{1,0:T(8,128)S(1)}, u32[]{:S(2)}, u32[]{:S(2)}) collective-permute-start(f32[32,4096]{1,0:T(8,128)S(1)} %get-tuple-element.114), channel_id=1, source_target_pairs={{0,1},{1,0},{2,3},{3,2},{4,5},{5,4},{6,7},{7,6},{8,9},{9,8},{10,11... | collective-permute-start | bytes 1572872 | tf_op jit(solution)/shard_map/ppermute | solution.py:562
  120.8 3.8 %collective-permute-start.33 = (f32[32,4096]{1,0:T(8,128)S(1)}, f32[32,4096]{1,0:T(8,128)S(1)}, u32[]{:S(2)}, u32[]{:S(2)}) collective-permute-start(f32[32,4096]{1,0:T(8,128)S(1)} %get-tuple-element.115), channel_id=1, source_target_pairs={{0,1},{1,0},{2,3},{3,2},{4,5},{5,4},{6,7},{7,6},{8,9},{9,8},{10,11... | collective-permute-start | bytes 1572872 | tf_op jit(solution)/shard_map/ppermute | solution.py:562
  120.9 13.7 %collective-permute-start.30 = (f32[32,4096]{1,0:T(8,128)S(1)}, f32[32,4096]{1,0:T(8,128)S(1)}, u32[]{:S(2)}, u32[]{:S(2)}) collective-permute-start(f32[32,4096]{1,0:T(8,128)S(1)} %get-tuple-element.112), channel_id=1, source_target_pairs={{0,1},{1,0},{2,3},{3,2},{4,5},{5,4},{6,7},{7,6},{8,9},{9,8},{10,11... | collective-permute-start | bytes 1572872 | tf_op jit(solution)/shard_map/ppermute | solution.py:562
  121.3 13.3 %collective-permute-start.31 = (f32[32,4096]{1,0:T(8,128)S(1)}, f32[32,4096]{1,0:T(8,128)S(1)}, u32[]{:S(2)}, u32[]{:S(2)}) collective-permute-start(f32[32,4096]{1,0:T(8,128)S(1)} %get-tuple-element.113), channel_id=1, source_target_pairs={{0,1},{1,0},{2,3},{3,2},{4,5},{5,4},{6,7},{7,6},{8,9},{9,8},{10,11... | collective-permute-start | bytes 1572872 | tf_op jit(solution)/shard_map/ppermute | solution.py:562
  (10 other events, 21.3 us)

commit v6 on v5

--- a/solution.py
+++ b/solution.py
@@ -279,7 +279,7 @@
 
 def bring_rows(place, rows, first_row, part_row, block_len, queries, parts, gate_input, out_weight, after):
     features, width = out_weight.shape
-    shapes = row_shapes(rows, features) + [((features, width // TILE // 2 * TILE), BF16)]
+    shapes = row_shapes(rows, features) + [((features, width), BF16)]
     return pl.pallas_call(
         functools.partial(bring_kernel, first_row, part_row, block_len),
         in_specs=[pl.BlockSpec(memory_space=pltpu.SMEM)] + [pl.BlockSpec(memory_space=pl.ANY)] * 8,

time: 137 us -> 136 us (level)
  transfers between devices with their start and end apart: 38 -> 38, of which waited for: 22 -> 21; matrix products, arithmetic and copies ran while one was open for 0% -> 0% of each run, Pallas kernels for 49% -> 50%
where the time goes in v6:
time: 136 us; the launch traced here: 135 us
  Pallas kernels  75.4 us (55%)
  waiting for transfers between devices  35.2 us (26%)
  starting transfers between devices  21.2 us (16%)
  local copies, waits for them, and re-layouts  3.08 us (2%)
    pallas_call x6, Pallas kernels, project_rows(): pl.pallas_call(functools.partial(project_kernel, first_row, part_row, blo...  37.5 us
    ppermute x4, waiting for transfers between devices, per_device(): landed.append(lax.ppermute(last, 'head', across))  21.1 us
    pallas_call x3, Pallas kernels, inside_part(): pl.pallas_call(functools.partial(inside_kernel, begin, end), in_specs=[pl...  18.4 us
    ppermute x24, waiting for transfers between devices, project(): return (mine, [lax.ppermute(piece, 'head', cores) for piece in theirs])  7.43 us
    pallas_call x2, Pallas kernels, local_states(): pl.pallas_call(functools.partial(states_kernel, other is not None), in_sp...  7.01 us
    pallas_call x4, Pallas kernels, finish_rows(): pl.pallas_call(functools.partial(finish_kernel, len(arrived)), grid=(1,),...  6.31 us
    ppermute x24, starting transfers between devices, project(): return (mine, [lax.ppermute(piece, 'head', cores) for piece in theirs])  5.63 us
    ppermute x6, starting transfers between devices, incoming_states(): landed[i].append(lax.ppermute(value, 'seq', along))  5.44 us
  transfers between devices with their start and end apart: 38, of which 21 were waited for; matrix products, arithmetic and copies ran while one was open for 0% of the time, Pallas kernels for 50%

profile of v6, /device:TPU:24, one launch (start us, length us, event | category | flops | bytes accessed | tf_op | source)
XLA Modules:
  0.0 135.4 jit_solution(4779889124355347385)
XLA Ops:
  0.0 3.0 %shard_map.64 = (f32[2,136,128]{2,1,0:T(8,128)S(1)}, f32[2,136,128]{2,1,0:T(8,128)S(1)}, f32[4,4,128,128]{3,2,1,0:T(8,128)S(1)}) custom-call(s32[1]{0:T(128)S(6)} %sub.12.side_ref, f32[8,1024]{1,0:T(8,128)} %bitcast.6, bf16[1024,1024]{1,0:T(8,128)(2,1)} %key_hbm.9, bf16[1024,1024]{1,0:T(8,128)(2,1)} %value_hbm.9), custom_call_target="tpu_custom_call" | custom-call | flops 1 | bytes 1 | tf_op jit(solution)/shard_map/pallas_call | solution.py:153
  3.0 1.6 %collective-permute-start = (f32[2,136,128]{2,1,0:T(8,128)S(1)}, f32[2,136,128]{2,1,0:T(8,128)S(1)}, u32[]{:S(2)}, u32[]{:S(2)}) collective-permute-start(f32[2,136,128]{2,1,0:T(8,128)S(1)} %get-tuple-element.65), channel_id=1, source_target_pairs={{0,4},{4,0},{8,12},{12,8},{16,20},{20,16},{24,28},{28,24},{1,5},{5... | collective-permute-start | bytes 417800 | tf_op jit(solution)/shard_map/ppermute | solution.py:546
  5.1 4.0 %shard_map.65 = (f32[2,136,128]{2,1,0:T(8,128)S(1)}, f32[2,136,128]{2,1,0:T(8,128)S(1)}, f32[4,4,128,128]{3,2,1,0:T(8,128)}, f32[4,4,128,128]{3,2,1,0:T(8,128)}) custom-call(s32[1]{0:T(128)} %bitcast.2.side_ref.odd_ref, f32[8,1024]{1,0:T(8,128)} %bitcast.7, bf16[1024,1024]{1,0:T(8,128)(2,1)} %key_hbm.9, bf16[1024,1024]{1,0:T(8,128)(2,1)} %value_hbm.9, ...), custom_call_target="tpu_custom_call" | custom-call | flops 1 | bytes 1 | tf_op jit(solution)/shard_map/pallas_call | solution.py:153
  10.3 1.1 collective-permute-done.3.refs_1_.refs_2_.refs_3_.refs_4_
  13.7 6.2 %shard_map.70 = (f32[192,1024]{1,0:T(8,128)}, f32[192,8]{1,0:T(8,128)}, f32[192,1024]{1,0:T(8,128)}, f32[192,8]{1,0:T(8,128)}) custom-call(s32[3]{0:T(128)S(1)} %add_add_fusion.1.place_ref, f32[8,1024]{1,0:T(8,128)} %bitcast.8, bf16[1024,1024]{1,0:T(8,128)(2,1)} %refs_4_.9, bf16[1024,1024]{1,0:T(8,128)(2,1)} %key_hbm.9, bf16[1024,1024]{1,0:T(8,128)(2,1)} %value_hbm.9, ...), custom_call_target="tpu_custom_call" | custom-call | flops 1 | bytes 1 | tf_op jit(solution)/shard_map/pallas_call | solution.py:234
  20.0 1.3 collective-permute-start.5
  21.4 1.5 %collective-permute-start.7 = (f32[2,128,128]{2,1,0:T(8,128)S(1)}, f32[2,128,128]{2,1,0:T(8,128)S(1)}, u32[]{:S(2)}, u32[]{:S(2)}) collective-permute-start(f32[2,128,128]{2,1,0:T(8,128)S(1)} %shard_map.73), channel_id=1, source_target_pairs={{16,24},{20,28},{17,25},{21,29},{18,26},{22,30},{19,27},{23,31}} | collective-permute-start | bytes 393224 | tf_op jit(solution)/shard_map/ppermute | solution.py:519
  22.9 5.0 %collective-permute-done.5.refs_2_ = f32[2,128,128]{2,1,0:T(8,128)S(1)} collective-permute-done((f32[2,128,128]{2,1,0:T(8,128)S(1)}, f32[2,128,128]{2,1,0:T(8,128)S(1)}, u32[]{:S(2)}, u32[]{:S(2)}) %collective-permute-start.5) | collective-permute-done | bytes 131104 | tf_op jit(solution)/shard_map/ppermute | solution.py:519
  27.9 1.6 %collective-permute-start.8 = (f32[2,128,128]{2,1,0:T(8,128)S(1)}, f32[2,128,128]{2,1,0:T(8,128)S(1)}, u32[]{:S(2)}, u32[]{:S(2)}) collective-permute-start(f32[2,128,128]{2,1,0:T(8,128)S(1)} %get-tuple-element.73), channel_id=1, source_target_pairs={{0,4},{4,0},{8,12},{12,8},{16,20},{20,16},{24,28},{28,24},{1,5},{5... | collective-permute-start | bytes 393224 | tf_op jit(solution)/shard_map/ppermute | solution.py:527
  29.6 1.4 collective-permute-start.9
  31.0 4.4 %shard_map.75 = (bf16[128,1024]{1,0:T(8,128)(2,1)S(1)}, bf16[128,1024]{1,0:T(8,128)(2,1)S(1)}, f32[128,1024]{1,0:T(8,128)S(1)}, f32[128,8]{1,0:T(8,128)S(1)}, bf16[1024,4096]{1,0:T(8,128)(2,1)S(1)}) custom-call(s32[3]{0:T(128)S(1)} %add_add_fusion.1.place_ref, bf16[1024,1024]{1,0:T(8,128)(2,1)} %refs_4_.9, bf16[1024,1024]{1,0:T(8,128)(2,1)} %refs_5_.9, ...), custom_call_target="tpu_custom_call" | custom-call | flops 1 | bytes 1 | tf_op jit(solution)/shard_map/pallas_call | solution.py:283
  35.4 3.5 %shard_map.76 = (f32[16,4096]{1,0:T(8,128)S(1)}, f32[16,4096]{1,0:T(8,128)S(1)}, f32[16,4096]{1,0:T(8,128)S(1)}, f32[16,4096]{1,0:T(8,128)S(1)}, f32[64,4096]{1,0:T(8,128)S(1)}) custom-call(s32[3]{0:T(128)S(1)} %add_add_fusion.1.place_ref, f32[2,128,128]{2,1,0:T(8,128)S(1)} %get-tuple-element.71.refs_0_, ...), custom_call_target="tpu_custom_call" | custom-call | flops 1 | bytes 1 | tf_op jit(solution)/shard_map/pallas_call | solution.py:384
  41.8 1.6 %collective-permute-start.22 = (f32[64,4096]{1,0:T(8,128)S(1)}, f32[64,4096]{1,0:T(8,128)S(1)}, u32[]{:S(2)}, u32[]{:S(2)}) collective-permute-start(f32[64,4096]{1,0:T(8,128)S(1)} %shard_map.77.refs_11_), channel_id=1, source_target_pairs={{0,2},{1,3},{2,0},{3,1},{4,6},{5,7},{6,4},{7,5},{8,10},{9,11},{10,... | collective-permute-start | bytes 3145736 | tf_op jit(solution)/shard_map/ppermute | solution.py:586
  43.4 6.3 %shard_map.78 = (f32[16,4096]{1,0:T(8,128)S(1)}, f32[16,4096]{1,0:T(8,128)S(1)}, f32[16,4096]{1,0:T(8,128)S(1)}, f32[16,4096]{1,0:T(8,128)S(1)}, f32[64,4096]{1,0:T(8,128)S(1)}) custom-call(s32[3]{0:T(128)S(1)} %add_add_fusion.1.place_ref, f32[2,128,128]{2,1,0:T(8,128)S(1)} %get-tuple-element.71.refs_0_, ...), custom_call_target="tpu_custom_call" | custom-call | flops 1 | bytes 1 | tf_op jit(solution)/shard_map/pallas_call | solution.py:384
  52.5 6.3 %shard_map.80 = (f32[16,4096]{1,0:T(8,128)S(1)}, f32[16,4096]{1,0:T(8,128)S(1)}, f32[16,4096]{1,0:T(8,128)S(1)}, f32[16,4096]{1,0:T(8,128)S(1)}, f32[64,4096]{1,0:T(8,128)S(1)}) custom-call(s32[3]{0:T(128)S(1)} %add_add_fusion.1.place_ref, f32[2,128,128]{2,1,0:T(8,128)S(1)} %get-tuple-element.71.refs_0_, ...), custom_call_target="tpu_custom_call" | custom-call | flops 1 | bytes 1 | tf_op jit(solution)/shard_map/pallas_call | solution.py:384
  61.5 6.3 %collective-permute-done.22.refs_4_.refs_0_ = f32[64,4096]{1,0:T(8,128)S(1)} collective-permute-done((f32[64,4096]{1,0:T(8,128)S(1)}, f32[64,4096]{1,0:T(8,128)S(1)}, u32[]{:S(2)}, u32[]{:S(2)}) %collective-permute-start.22) | collective-permute-done | bytes 1048608 | tf_op jit(solution)/shard_map/ppermute | solution.py:586
  68.8 1.5 %collective-permute-start.28 = (f32[64,4096]{1,0:T(8,128)S(1)}, f32[64,4096]{1,0:T(8,128)}, u32[]{:S(2)}, u32[]{:S(2)}) collective-permute-start(f32[64,4096]{1,0:T(8,128)S(1)} %shard_map.81.after_ref.refs_11_), channel_id=1, source_target_pairs={{0,2},{1,3},{2,0},{3,1},{4,6},{5,7},{6,4},{7,5},{8,10},{9,11},{10,... | collective-permute-start | bytes 3145736 | tf_op jit(solution)/shard_map/ppermute | solution.py:586
  70.3 5.5 %shard_map.82 = (f32[64,1024]{1,0:T(8,128)}, f32[64,8]{1,0:T(8,128)}, f32[64,1024]{1,0:T(8,128)}, f32[64,8]{1,0:T(8,128)}) custom-call(s32[3]{0:T(128)S(1)} %add_add_fusion.1.place_ref, f32[8,1024]{1,0:T(8,128)} %bitcast.9, bf16[1024,1024]{1,0:T(8,128)(2,1)} %refs_4_.9, bf16[1024,1024]{1,0:T(8,128)(2,1)} %key_hbm.9, bf16[1024,1024]{1,0:T(8,128)(2,1)} %value_hbm.9, ...), custom_call_target="tpu_custom_call" | custom-call | flops 1 | bytes 1 | tf_op jit(solution)/shard_map/pallas_call | solution.py:234
  75.8 7.1 %shard_map.83 = (f32[16,4096]{1,0:T(8,128)S(1)}, f32[16,4096]{1,0:T(8,128)}, f32[16,4096]{1,0:T(8,128)}, f32[16,4096]{1,0:T(8,128)}, f32[64,4096]{1,0:T(8,128)S(1)}) custom-call(s32[3]{0:T(128)S(1)} %add_add_fusion.1.place_ref, f32[2,128,128]{2,1,0:T(8,128)S(1)} %get-tuple-element.71.refs_0_, ...), custom_call_target="tpu_custom_call" | custom-call | flops 1 | bytes 1 | tf_op jit(solution)/shard_map/pallas_call | solution.py:384
  84.4 1.4 %collective-permute-done.23.refs_0_ = f32[16,4096]{1,0:T(8,128)S(1)} collective-permute-done((f32[16,4096]{1,0:T(8,128)S(1)}, f32[16,4096]{1,0:T(8,128)S(1)}, u32[]{:S(2)}, u32[]{:S(2)}) %collective-permute-start.23) | collective-permute-done | bytes 262176 | tf_op jit(solution)/shard_map/ppermute | solution.py:562
  86.4 1.3 collective-permute-done.26.refs_3_
  87.6 2.8 %collective-permute-done.27.refs_4_.refs_0_ = f32[64,4096]{1,0:T(8,128)} collective-permute-done((f32[64,4096]{1,0:T(8,128)S(1)}, f32[64,4096]{1,0:T(8,128)}, u32[]{:S(2)}, u32[]{:S(2)}) %collective-permute-start.27) | collective-permute-done | bytes 1048608 | tf_op jit(solution)/shard_map/ppermute | solution.py:586
  90.4 1.2 copy-done.3
  91.7 1.1 shard_map.84.after_ref.refs_11_
  92.7 6.7 %shard_map.85 = (f32[256,1024]{1,0:T(8,128)}, f32[256,8]{1,0:T(8,128)}, f32[256,1024]{1,0:T(8,128)}, f32[256,8]{1,0:T(8,128)}) custom-call(s32[3]{0:T(128)S(1)} %add_add_fusion.place_ref, f32[8,1024]{1,0:T(8,128)} %bitcast.10, bf16[1024,1024]{1,0:T(8,128)(2,1)} %refs_4_.9, bf16[1024,1024]{1,0:T(8,128)(2,1)} %key_hbm.9, bf16[1024,1024]{1,0:T(8,128)(2,1)} %value_hbm.9, ...), custom_call_target="tpu_custom_call" | custom-call | flops 1 | bytes 1 | tf_op jit(solution)/shard_map/pallas_call | solution.py:234
  99.4 7.2 %shard_map.87 = (f32[32,4096]{1,0:T(8,128)S(1)}, f32[32,4096]{1,0:T(8,128)S(1)}, f32[32,4096]{1,0:T(8,128)S(1)}, f32[32,4096]{1,0:T(8,128)S(1)}, f32[128,4096]{1,0:T(8,128)S(1)}) custom-call(s32[3]{0:T(128)S(1)} %add_add_fusion.place_ref, f32[2,128,128]{2,1,0:T(8,128)S(1)} %get-tuple-element.71.refs_0_, ...), custom_call_target="tpu_custom_call" | custom-call | flops 1 | bytes 1 | tf_op jit(solution)/shard_map/pallas_call | solution.py:384
  107.2 1.5 %collective-permute-start.29 = (f32[64,4096]{1,0:T(8,128)S(1)}, f32[64,4096]{1,0:T(8,128)S(1)}, u32[]{:S(2)}, u32[]{:S(2)}) collective-permute-start(f32[64,4096]{1,0:T(8,128)S(1)} %shard_map.84.after_ref.refs_11_), channel_id=1, source_target_pairs={{0,2},{1,3},{2,0},{3,1},{4,6},{5,7},{6,4},{7,5},{8,10},{9,11},{10,... | collective-permute-start | bytes 3145736 | tf_op jit(solution)/shard_map/ppermute | solution.py:586
  108.7 4.2 %collective-permute-done.28.refs_11_.refs_0_ = f32[64,4096]{1,0:T(8,128)} collective-permute-done((f32[64,4096]{1,0:T(8,128)S(1)}, f32[64,4096]{1,0:T(8,128)}, u32[]{:S(2)}, u32[]{:S(2)}) %collective-permute-start.28) | collective-permute-done | bytes 1048608 | tf_op jit(solution)/shard_map/ppermute | solution.py:586
  112.9 7.2 %shard_map.86 = (f32[32,4096]{1,0:T(8,128)S(1)}, f32[32,4096]{1,0:T(8,128)S(1)}, f32[32,4096]{1,0:T(8,128)S(1)}, f32[32,4096]{1,0:T(8,128)S(1)}, f32[128,4096]{1,0:T(8,128)S(1)}) custom-call(s32[3]{0:T(128)S(1)} %add_add_fusion.place_ref, f32[2,128,128]{2,1,0:T(8,128)S(1)} %get-tuple-element.71.refs_0_, ...), custom_call_target="tpu_custom_call" | custom-call | flops 1 | bytes 1 | tf_op jit(solution)/shard_map/pallas_call | solution.py:384
  122.2 2.2 %shard_map.89.refs_3_ = bf16[256,4096]{1,0:T(8,128)(2,1)} custom-call(f32[128,4096]{1,0:T(8,128)S(1)} %get-tuple-element.116.own_ref.refs_3_, f32[64,4096]{1,0:T(8,128)} %collective-permute-done.27.refs_4_.refs_0_, f32[32,4096]{1,0:T(8,128)S(1)} %collective-permute-done.34.refs_1_, ...), custom_call_target="tpu_custom_call", output_to_operand_aliasing={{}: (4, {})} | custom-call | flops 1 | bytes 1 | tf_op jit(solution)/shard_map/pallas_call | solution.py:438
  124.4 2.2 %shard_map.90.refs_3_ = bf16[256,4096]{1,0:T(8,128)(2,1)} custom-call(f32[128,4096]{1,0:T(8,128)S(1)} %get-tuple-element.111.own_ref, f32[64,4096]{1,0:T(8,128)} %collective-permute-done.28.refs_11_.refs_0_, f32[32,4096]{1,0:T(8,128)S(1)} %collective-permute-done.32.refs_1_, ...), custom_call_target="tpu_custom_call", output_to_operand_aliasing={{}: (4, {})} | custom-call | flops 1 | bytes 1 | tf_op jit(solution)/shard_map/pallas_call | solution.py:438
  126.7 7.8 %collective-permute-done.29.refs_0_ = f32[64,4096]{1,0:T(8,128)S(1)} collective-permute-done((f32[64,4096]{1,0:T(8,128)S(1)}, f32[64,4096]{1,0:T(8,128)S(1)}, u32[]{:S(2)}, u32[]{:S(2)}) %collective-permute-start.29) | collective-permute-done | bytes 1048608 | tf_op jit(solution)/shard_map/ppermute | solution.py:586
  (82 shorter events, 19.2 us)
Async XLA Ops:
  3.0 6.6 %collective-permute-start = (f32[2,136,128]{2,1,0:T(8,128)S(1)}, f32[2,136,128]{2,1,0:T(8,128)S(1)}, u32[]{:S(2)}, u32[]{:S(2)}) collective-permute-start(f32[2,136,128]{2,1,0:T(8,128)S(1)} %get-tuple-element.65), channel_id=1, source_target_pairs={{0,4},{4,0},{8,12},{12,8},{16,20},{20,16},{24,28},{28,24},{1,5},{5... | collective-permute-start | bytes 417800 | tf_op jit(solution)/shard_map/ppermute | solution.py:546
  4.5 6.9 %collective-permute-start.3 = (f32[2,136,128]{2,1,0:T(8,128)S(1)}, f32[2,136,128]{2,1,0:T(8,128)S(1)}, u32[]{:S(2)}, u32[]{:S(2)}) collective-permute-start(f32[2,136,128]{2,1,0:T(8,128)S(1)} %get-tuple-element.69), channel_id=1, source_target_pairs={{0,4},{4,0},{8,12},{12,8},{16,20},{20,16},{24,28},{28,24},{1,5},{5... | collective-permute-start | bytes 417800 | tf_op jit(solution)/shard_map/ppermute | solution.py:546
  9.6 2.5 %collective-permute-start.1 = (f32[2,128,128]{2,1,0:T(8,128)S(1)}, f32[2,128,128]{2,1,0:T(8,128)S(1)}, u32[]{:S(2)}, u32[]{:S(2)}) collective-permute-start(f32[2,128,128]{2,1,0:T(8,128)S(1)} %shard_map.66), channel_id=1, source_target_pairs={{0,8},{4,12},{1,9},{5,13},{2,10},{6,14},{3,11},{7,15}} | collective-permute-start | bytes 393224 | tf_op jit(solution)/shard_map/ppermute | solution.py:519
  12.2 7.8 %collective-permute-start.2 = (f32[2,128,128]{2,1,0:T(8,128)S(1)}, f32[2,128,128]{2,1,0:T(8,128)S(1)}, u32[]{:S(2)}, u32[]{:S(2)}) collective-permute-start(f32[2,128,128]{2,1,0:T(8,128)S(1)} %shard_map.67), channel_id=1, source_target_pairs={{8,16},{12,20},{9,17},{13,21},{10,18},{14,22},{11,19},{15,23}} | collective-permute-start | bytes 393224 | tf_op jit(solution)/shard_map/ppermute | solution.py:519
  12.9 8.4 %collective-permute-start.6 = (f32[2,128,128]{2,1,0:T(8,128)S(1)}, f32[2,128,128]{2,1,0:T(8,128)S(1)}, u32[]{:S(2)}, u32[]{:S(2)}) collective-permute-start(f32[2,128,128]{2,1,0:T(8,128)S(1)} %shard_map.69.after_ref), channel_id=1, source_target_pairs={{8,16},{12,20},{9,17},{13,21},{10,18},{14,22},{11,19},{15,23}} | collective-permute-start | bytes 393224 | tf_op jit(solution)/shard_map/ppermute | solution.py:519
  20.0 7.8 %collective-permute-start.5 = (f32[2,128,128]{2,1,0:T(8,128)S(1)}, f32[2,128,128]{2,1,0:T(8,128)S(1)}, u32[]{:S(2)}, u32[]{:S(2)}) collective-permute-start(f32[2,128,128]{2,1,0:T(8,128)S(1)} %shard_map.71), channel_id=1, source_target_pairs={{16,24},{20,28},{17,25},{21,29},{18,26},{22,30},{19,27},{23,31}} | collective-permute-start | bytes 393224 | tf_op jit(solution)/shard_map/ppermute | solution.py:519
  21.4 8.2 %collective-permute-start.7 = (f32[2,128,128]{2,1,0:T(8,128)S(1)}, f32[2,128,128]{2,1,0:T(8,128)S(1)}, u32[]{:S(2)}, u32[]{:S(2)}) collective-permute-start(f32[2,128,128]{2,1,0:T(8,128)S(1)} %shard_map.73), channel_id=1, source_target_pairs={{16,24},{20,28},{17,25},{21,29},{18,26},{22,30},{19,27},{23,31}} | collective-permute-start | bytes 393224 | tf_op jit(solution)/shard_map/ppermute | solution.py:519
  27.9 7.5 %collective-permute-start.8 = (f32[2,128,128]{2,1,0:T(8,128)S(1)}, f32[2,128,128]{2,1,0:T(8,128)S(1)}, u32[]{:S(2)}, u32[]{:S(2)}) collective-permute-start(f32[2,128,128]{2,1,0:T(8,128)S(1)} %get-tuple-element.73), channel_id=1, source_target_pairs={{0,4},{4,0},{8,12},{12,8},{16,20},{20,16},{24,28},{28,24},{1,5},{5... | collective-permute-start | bytes 393224 | tf_op jit(solution)/shard_map/ppermute | solution.py:527
  29.6 5.8 %collective-permute-start.9 = (f32[2,128,128]{2,1,0:T(8,128)S(1)}, f32[2,128,128]{2,1,0:T(8,128)S(1)}, u32[]{:S(2)}, u32[]{:S(2)}) collective-permute-start(f32[2,128,128]{2,1,0:T(8,128)S(1)} %get-tuple-element.74), channel_id=1, source_target_pairs={{0,4},{4,0},{8,12},{12,8},{16,20},{20,16},{24,28},{28,24},{1,5},{5... | collective-permute-start | bytes 393224 | tf_op jit(solution)/shard_map/ppermute | solution.py:527
  39.0 1.9 %collective-permute-start.11 = (f32[16,4096]{1,0:T(8,128)S(1)}, f32[16,4096]{1,0:T(8,128)S(1)}, u32[]{:S(2)}, u32[]{:S(2)}) collective-permute-start(f32[16,4096]{1,0:T(8,128)S(1)} %get-tuple-element.85), channel_id=1, source_target_pairs={{0,1},{1,0},{2,3},{3,2},{4,5},{5,4},{6,7},{7,6},{8,9},{9,8},{10,11... | collective-permute-start | bytes 786440 | tf_op jit(solution)/shard_map/ppermute | solution.py:562
  39.5 1.8 %collective-permute-start.12 = (f32[16,4096]{1,0:T(8,128)S(1)}, f32[16,4096]{1,0:T(8,128)S(1)}, u32[]{:S(2)}, u32[]{:S(2)}) collective-permute-start(f32[16,4096]{1,0:T(8,128)S(1)} %get-tuple-element.86), channel_id=1, source_target_pairs={{0,1},{1,0},{2,3},{3,2},{4,5},{5,4},{6,7},{7,6},{8,9},{9,8},{10,11... | collective-permute-start | bytes 786440 | tf_op jit(solution)/shard_map/ppermute | solution.py:562
  39.6 2.1 %collective-permute-start.13 = (f32[16,4096]{1,0:T(8,128)S(1)}, f32[16,4096]{1,0:T(8,128)S(1)}, u32[]{:S(2)}, u32[]{:S(2)}) collective-permute-start(f32[16,4096]{1,0:T(8,128)S(1)} %get-tuple-element.87), channel_id=1, source_target_pairs={{0,1},{1,0},{2,3},{3,2},{4,5},{5,4},{6,7},{7,6},{8,9},{9,8},{10,11... | collective-permute-start | bytes 786440 | tf_op jit(solution)/shard_map/ppermute | solution.py:562
  41.8 26.1 %collective-permute-start.22 = (f32[64,4096]{1,0:T(8,128)S(1)}, f32[64,4096]{1,0:T(8,128)S(1)}, u32[]{:S(2)}, u32[]{:S(2)}) collective-permute-start(f32[64,4096]{1,0:T(8,128)S(1)} %shard_map.77.refs_11_), channel_id=1, source_target_pairs={{0,2},{1,3},{2,0},{3,1},{4,6},{5,7},{6,4},{7,5},{8,10},{9,11},{10,... | collective-permute-start | bytes 3145736 | tf_op jit(solution)/shard_map/ppermute | solution.py:586
  49.7 1.9 %collective-permute-start.15 = (f32[16,4096]{1,0:T(8,128)S(1)}, f32[16,4096]{1,0:T(8,128)S(1)}, u32[]{:S(2)}, u32[]{:S(2)}) collective-permute-start(f32[16,4096]{1,0:T(8,128)S(1)} %get-tuple-element.90), channel_id=1, source_target_pairs={{0,1},{1,0},{2,3},{3,2},{4,5},{5,4},{6,7},{7,6},{8,9},{9,8},{10,11... | collective-permute-start | bytes 786440 | tf_op jit(solution)/shard_map/ppermute | solution.py:562
  50.3 2.1 %collective-permute-start.17 = (f32[16,4096]{1,0:T(8,128)S(1)}, f32[16,4096]{1,0:T(8,128)S(1)}, u32[]{:S(2)}, u32[]{:S(2)}) collective-permute-start(f32[16,4096]{1,0:T(8,128)S(1)} %get-tuple-element.92), channel_id=1, source_target_pairs={{0,1},{1,0},{2,3},{3,2},{4,5},{5,4},{6,7},{7,6},{8,9},{9,8},{10,11... | collective-permute-start | bytes 786440 | tf_op jit(solution)/shard_map/ppermute | solution.py:562
  59.0 1.9 %collective-permute-start.19 = (f32[16,4096]{1,0:T(8,128)S(1)}, f32[16,4096]{1,0:T(8,128)S(1)}, u32[]{:S(2)}, u32[]{:S(2)}) collective-permute-start(f32[16,4096]{1,0:T(8,128)S(1)} %get-tuple-element.95), channel_id=1, source_target_pairs={{0,1},{1,0},{2,3},{3,2},{4,5},{5,4},{6,7},{7,6},{8,9},{9,8},{10,11... | collective-permute-start | bytes 786440 | tf_op jit(solution)/shard_map/ppermute | solution.py:562
  59.5 2.0 %collective-permute-start.21 = (f32[16,4096]{1,0:T(8,128)S(1)}, f32[16,4096]{1,0:T(8,128)S(1)}, u32[]{:S(2)}, u32[]{:S(2)}) collective-permute-start(f32[16,4096]{1,0:T(8,128)S(1)} %get-tuple-element.97), channel_id=1, source_target_pairs={{0,1},{1,0},{2,3},{3,2},{4,5},{5,4},{6,7},{7,6},{8,9},{9,8},{10,11... | collective-permute-start | bytes 786440 | tf_op jit(solution)/shard_map/ppermute | solution.py:562
  60.4 30.0 %collective-permute-start.27 = (f32[64,4096]{1,0:T(8,128)S(1)}, f32[64,4096]{1,0:T(8,128)}, u32[]{:S(2)}, u32[]{:S(2)}) collective-permute-start(f32[64,4096]{1,0:T(8,128)S(1)} %shard_map.79.refs_11_), channel_id=1, source_target_pairs={{0,2},{1,3},{2,0},{3,1},{4,6},{5,7},{6,4},{7,5},{8,10},{9,11},{10,... | collective-permute-start | bytes 3145736 | tf_op jit(solution)/shard_map/ppermute | solution.py:586
  68.8 44.1 %collective-permute-start.28 = (f32[64,4096]{1,0:T(8,128)S(1)}, f32[64,4096]{1,0:T(8,128)}, u32[]{:S(2)}, u32[]{:S(2)}) collective-permute-start(f32[64,4096]{1,0:T(8,128)S(1)} %shard_map.81.after_ref.refs_11_), channel_id=1, source_target_pairs={{0,2},{1,3},{2,0},{3,1},{4,6},{5,7},{6,4},{7,5},{8,10},{9,11},{10,... | collective-permute-start | bytes 3145736 | tf_op jit(solution)/shard_map/ppermute | solution.py:586
  83.9 1.9 %collective-permute-start.23 = (f32[16,4096]{1,0:T(8,128)S(1)}, f32[16,4096]{1,0:T(8,128)S(1)}, u32[]{:S(2)}, u32[]{:S(2)}) collective-permute-start(f32[16,4096]{1,0:T(8,128)S(1)} %get-tuple-element.103), channel_id=1, source_target_pairs={{0,1},{1,0},{2,3},{3,2},{4,5},{5,4},{6,7},{7,6},{8,9},{9,8},{10,11... | collective-permute-start | bytes 786440 | tf_op jit(solution)/shard_map/ppermute | solution.py:562
  83.9 2.1 %collective-permute-start.24 = (f32[16,4096]{1,0:T(8,128)}, f32[16,4096]{1,0:T(8,128)S(1)}, u32[]{:S(2)}, u32[]{:S(2)}) collective-permute-start(f32[16,4096]{1,0:T(8,128)} %get-tuple-element.104), channel_id=1, source_target_pairs={{0,1},{1,0},{2,3},{3,2},{4,5},{5,4},{6,7},{7,6},{8,9},{9,8},{10,11... | collective-permute-start | bytes 786440 | tf_op jit(solution)/shard_map/ppermute | solution.py:562
  84.4 2.0 %collective-permute-start.25 = (f32[16,4096]{1,0:T(8,128)}, f32[16,4096]{1,0:T(8,128)S(1)}, u32[]{:S(2)}, u32[]{:S(2)}) collective-permute-start(f32[16,4096]{1,0:T(8,128)} %get-tuple-element.105), channel_id=1, source_target_pairs={{0,1},{1,0},{2,3},{3,2},{4,5},{5,4},{6,7},{7,6},{8,9},{9,8},{10,11... | collective-permute-start | bytes 786440 | tf_op jit(solution)/shard_map/ppermute | solution.py:562
  85.8 1.9 %collective-permute-start.26 = (f32[16,4096]{1,0:T(8,128)}, f32[16,4096]{1,0:T(8,128)}, u32[]{:S(2)}, u32[]{:S(2)}) collective-permute-start(f32[16,4096]{1,0:T(8,128)} %get-tuple-element.106), channel_id=1, source_target_pairs={{0,1},{1,0},{2,3},{3,2},{4,5},{5,4},{6,7},{7,6},{8,9},{9,8},{10,11... | collective-permute-start | bytes 786440 | tf_op jit(solution)/shard_map/ppermute | solution.py:562
  106.6 13.5 %collective-permute-start.34 = (f32[32,4096]{1,0:T(8,128)S(1)}, f32[32,4096]{1,0:T(8,128)S(1)}, u32[]{:S(2)}, u32[]{:S(2)}) collective-permute-start(f32[32,4096]{1,0:T(8,128)S(1)} %get-tuple-element.117), channel_id=1, source_target_pairs={{0,1},{1,0},{2,3},{3,2},{4,5},{5,4},{6,7},{7,6},{8,9},{9,8},{10,11... | collective-permute-start | bytes 1572872 | tf_op jit(solution)/shard_map/ppermute | solution.py:562
  106.7 14.0 %collective-permute-start.35 = (f32[32,4096]{1,0:T(8,128)S(1)}, f32[32,4096]{1,0:T(8,128)S(1)}, u32[]{:S(2)}, u32[]{:S(2)}) collective-permute-start(f32[32,4096]{1,0:T(8,128)S(1)} %get-tuple-element.118), channel_id=1, source_target_pairs={{0,1},{1,0},{2,3},{3,2},{4,5},{5,4},{6,7},{7,6},{8,9},{9,8},{10,11... | collective-permute-start | bytes 1572872 | tf_op jit(solution)/shard_map/ppermute | solution.py:562
  107.2 27.3 %collective-permute-start.29 = (f32[64,4096]{1,0:T(8,128)S(1)}, f32[64,4096]{1,0:T(8,128)S(1)}, u32[]{:S(2)}, u32[]{:S(2)}) collective-permute-start(f32[64,4096]{1,0:T(8,128)S(1)} %shard_map.84.after_ref.refs_11_), channel_id=1, source_target_pairs={{0,2},{1,3},{2,0},{3,1},{4,6},{5,7},{6,4},{7,5},{8,10},{9,11},{10,... | collective-permute-start | bytes 3145736 | tf_op jit(solution)/shard_map/ppermute | solution.py:586
  108.7 12.1 %collective-permute-start.36 = (f32[32,4096]{1,0:T(8,128)S(1)}, f32[32,4096]{1,0:T(8,128)S(1)}, u32[]{:S(2)}, u32[]{:S(2)}) collective-permute-start(f32[32,4096]{1,0:T(8,128)S(1)} %get-tuple-element.119), channel_id=1, source_target_pairs={{0,1},{1,0},{2,3},{3,2},{4,5},{5,4},{6,7},{7,6},{8,9},{9,8},{10,11... | collective-permute-start | bytes 1572872 | tf_op jit(solution)/shard_map/ppermute | solution.py:562
  112.9 8.3 %collective-permute-start.37 = (f32[32,4096]{1,0:T(8,128)S(1)}, f32[32,4096]{1,0:T(8,128)S(1)}, u32[]{:S(2)}, u32[]{:S(2)}) collective-permute-start(f32[32,4096]{1,0:T(8,128)S(1)} %get-tuple-element.120), channel_id=1, source_target_pairs={{0,1},{1,0},{2,3},{3,2},{4,5},{5,4},{6,7},{7,6},{8,9},{9,8},{10,11... | collective-permute-start | bytes 1572872 | tf_op jit(solution)/shard_map/ppermute | solution.py:562
  120.1 4.3 %collective-permute-start.32 = (f32[32,4096]{1,0:T(8,128)S(1)}, f32[32,4096]{1,0:T(8,128)S(1)}, u32[]{:S(2)}, u32[]{:S(2)}) collective-permute-start(f32[32,4096]{1,0:T(8,128)S(1)} %get-tuple-element.114), channel_id=1, source_target_pairs={{0,1},{1,0},{2,3},{3,2},{4,5},{5,4},{6,7},{7,6},{8,9},{9,8},{10,11... | collective-permute-start | bytes 1572872 | tf_op jit(solution)/shard_map/ppermute | solution.py:562
  120.7 3.8 %collective-permute-start.33 = (f32[32,4096]{1,0:T(8,128)S(1)}, f32[32,4096]{1,0:T(8,128)S(1)}, u32[]{:S(2)}, u32[]{:S(2)}) collective-permute-start(f32[32,4096]{1,0:T(8,128)S(1)} %get-tuple-element.115), channel_id=1, source_target_pairs={{0,1},{1,0},{2,3},{3,2},{4,5},{5,4},{6,7},{7,6},{8,9},{9,8},{10,11... | collective-permute-start | bytes 1572872 | tf_op jit(solution)/shard_map/ppermute | solution.py:562
  120.7 13.7 %collective-permute-start.30 = (f32[32,4096]{1,0:T(8,128)S(1)}, f32[32,4096]{1,0:T(8,128)S(1)}, u32[]{:S(2)}, u32[]{:S(2)}) collective-permute-start(f32[32,4096]{1,0:T(8,128)S(1)} %get-tuple-element.112), channel_id=1, source_target_pairs={{0,1},{1,0},{2,3},{3,2},{4,5},{5,4},{6,7},{7,6},{8,9},{9,8},{10,11... | collective-permute-start | bytes 1572872 | tf_op jit(solution)/shard_map/ppermute | solution.py:562
  121.2 13.3 %collective-permute-start.31 = (f32[32,4096]{1,0:T(8,128)S(1)}, f32[32,4096]{1,0:T(8,128)S(1)}, u32[]{:S(2)}, u32[]{:S(2)}) collective-permute-start(f32[32,4096]{1,0:T(8,128)S(1)} %get-tuple-element.113), channel_id=1, source_target_pairs={{0,1},{1,0},{2,3},{3,2},{4,5},{5,4},{6,7},{7,6},{8,9},{9,8},{10,11... | collective-permute-start | bytes 1572872 | tf_op jit(solution)/shard_map/ppermute | solution.py:562
  (10 other events, 21.3 us)

commit v7 on v6

--- a/solution.py
+++ b/solution.py
@@ -294,7 +294,7 @@
 def project_kernel(first_row, part_row, block_len, pieces, brought, place_ref, *refs):
     states, refs = refs[:2 * CHAIN_PARTS], refs[2 * CHAIN_PARTS:]
     if brought:
-        queries, gates, parts, leads, early, weight_hbm, after_ref, *refs = refs
+        queries, gates, parts, leads, early, after_ref, *refs = refs
     else:
         query_hbm, gate_hbm, weight_hbm, part_0, lead_0, part_1, lead_1, after_ref, *refs = refs
     del after_ref
@@ -307,12 +307,11 @@
     columns = [slice(at, at + tile) for at in range(0, width, tile)]
     loads = [pltpu.make_async_copy(ref, incoming.at[i], state_sem.at[i])
              for i, ref in enumerate(states)]
-    skipped = early.shape[1] if brought else 0
-    weights = [
-        pltpu.make_async_copy(
-            weight_hbm.at[:, at], weight.at[:, at.start - skipped:at.stop - skipped], weight_sem.at[i])
-        for i, at in enumerate(columns) if at.start >= skipped
+    weights = [] if brought else [
+        pltpu.make_async_copy(weight_hbm.at[:, at], weight.at[:, at], weight_sem.at[i])
+        for i, at in enumerate(columns)
     ]
+    weight = early if brought else weight
     if not brought:
         queries, gates, parts, leads, row_sem = refs
         loads += row_loads(first_row, part_row, block_len, place_ref, query_hbm, gate_hbm,
@@ -340,12 +339,9 @@
         hidden[:, at] = (normed * (gate / (1.0 + jnp.exp(-gate)))).astype(BF16)
     stores = []
     for i, at in enumerate(columns):
-        if at.start < skipped:
-            tile_weight = early[:, at]
-        else:
-            weights[i - skipped // tile].wait()
-            tile_weight = weight[:, at.start - skipped:at.stop - skipped]
-        result[:, at] = jnp.dot(hidden[...], tile_weight, preferred_element_type=F32)
+        for load in weights[i:i + 1]:
+            load.wait()
+        result[:, at] = jnp.dot(hidden[...], weight[:, at], preferred_element_type=F32)
     begin = 0
     for j, out in enumerate(outs):
         size = out.shape[0]
@@ -369,13 +365,12 @@
         pltpu.VMEM((2 * CHAIN_PARTS, *kept[0].shape), F32),
         pltpu.VMEM((2 * rows, features), BF16),
         pltpu.VMEM((2 * rows, width), F32),
-        pltpu.VMEM((features, width if brought is None else width - brought[-1].shape[1]), BF16),
+        pltpu.VMEM((features, HEAD_DIM if brought is not None else width), BF16),
         dma((2 * CHAIN_PARTS,)), dma((len(sizes),)), dma((tiles,)),
     ]
     if brought is not None:
         operands = [pltpu.with_memory_space_constraint(value, pltpu.VMEM) for value in brought]
-        specs = [vmem] * len(operands) + [far]
-        operands += in_hbm(out_weight)
+        specs = [vmem] * len(operands)
     else:
         operands = in_hbm(queries, gate_input, out_weight, *parts[0], *parts[1])
         specs = [far] * len(operands)
@@ -517,7 +512,7 @@
         for i in parts:
             value = hop_states(odd, landed[i], kept[i], got[i], after)
             landed[i].append(lax.ppermute(value, "seq", along))
-        if hop == count // 2 - 3:
+        if hop == max(count // 2 - 3, 0):
             for work in meanwhile:
                 after = work(value)
     keep, back = [], []

time: 136 us -> 136 us (level)
  no operation moved by 1% of the time
where the time goes in v7:
time: 136 us; the launch traced here: 135 us
  Pallas kernels  75.4 us (55%)
  waiting for transfers between devices  35.3 us (26%)
  starting transfers between devices  21.1 us (16%)
  local copies, waits for them, and re-layouts  3.08 us (2%)
    pallas_call x6, Pallas kernels, project_rows(): pl.pallas_call(functools.partial(project_kernel, first_row, part_row, blo...  37.5 us
    ppermute x4, waiting for transfers between devices, per_device(): landed.append(lax.ppermute(last, 'head', across))  21.2 us
    pallas_call x3, Pallas kernels, inside_part(): pl.pallas_call(functools.partial(inside_kernel, begin, end), in_specs=[pl...  18.4 us
    ppermute x24, waiting for transfers between devices, project(): return (mine, [lax.ppermute(piece, 'head', cores) for piece in theirs])  7.4 us
    pallas_call x2, Pallas kernels, local_states(): pl.pallas_call(functools.partial(states_kernel, other is not None), in_sp...  7.01 us
    pallas_call x4, Pallas kernels, finish_rows(): pl.pallas_call(functools.partial(finish_kernel, len(arrived)), grid=(1,),...  6.31 us
    ppermute x24, starting transfers between devices, project(): return (mine, [lax.ppermute(piece, 'head', cores) for piece in theirs])  5.63 us
    ppermute x6, starting transfers between devices, incoming_states(): landed[i].append(lax.ppermute(value, 'seq', along))  5.44 us
  transfers between devices with their start and end apart: 38, of which 21 were waited for; matrix products, arithmetic and copies ran while one was open for 0% of the time, Pallas kernels for 50%

profile of v7, /device:TPU:24, one launch (start us, length us, event | category | flops | bytes accessed | tf_op | source)
XLA Modules:
  0.0 135.4 jit_solution(2308719909305359295)
XLA Ops:
  0.0 3.0 %shard_map.64 = (f32[2,136,128]{2,1,0:T(8,128)S(1)}, f32[2,136,128]{2,1,0:T(8,128)S(1)}, f32[4,4,128,128]{3,2,1,0:T(8,128)S(1)}) custom-call(s32[1]{0:T(128)S(6)} %sub.12.side_ref, f32[8,1024]{1,0:T(8,128)} %bitcast.6, bf16[1024,1024]{1,0:T(8,128)(2,1)} %key_hbm.9, bf16[1024,1024]{1,0:T(8,128)(2,1)} %value_hbm.9), custom_call_target="tpu_custom_call" | custom-call | flops 1 | bytes 1 | tf_op jit(solution)/shard_map/pallas_call | solution.py:153
  3.0 1.6 %collective-permute-start = (f32[2,136,128]{2,1,0:T(8,128)S(1)}, f32[2,136,128]{2,1,0:T(8,128)S(1)}, u32[]{:S(2)}, u32[]{:S(2)}) collective-permute-start(f32[2,136,128]{2,1,0:T(8,128)S(1)} %get-tuple-element.65), channel_id=1, source_target_pairs={{0,4},{4,0},{8,12},{12,8},{16,20},{20,16},{24,28},{28,24},{1,5},{5... | collective-permute-start | bytes 417800 | tf_op jit(solution)/shard_map/ppermute | solution.py:541
  5.1 4.0 %shard_map.65 = (f32[2,136,128]{2,1,0:T(8,128)S(1)}, f32[2,136,128]{2,1,0:T(8,128)S(1)}, f32[4,4,128,128]{3,2,1,0:T(8,128)}, f32[4,4,128,128]{3,2,1,0:T(8,128)}) custom-call(s32[1]{0:T(128)} %bitcast.2.side_ref.odd_ref, f32[8,1024]{1,0:T(8,128)} %bitcast.7, bf16[1024,1024]{1,0:T(8,128)(2,1)} %key_hbm.9, bf16[1024,1024]{1,0:T(8,128)(2,1)} %value_hbm.9, ...), custom_call_target="tpu_custom_call" | custom-call | flops 1 | bytes 1 | tf_op jit(solution)/shard_map/pallas_call | solution.py:153
  10.3 1.1 collective-permute-done.3.refs_1_.refs_2_.refs_3_.refs_4_
  13.7 6.2 %shard_map.70 = (f32[192,1024]{1,0:T(8,128)}, f32[192,8]{1,0:T(8,128)}, f32[192,1024]{1,0:T(8,128)}, f32[192,8]{1,0:T(8,128)}) custom-call(s32[3]{0:T(128)S(1)} %add_add_fusion.1.place_ref, f32[8,1024]{1,0:T(8,128)} %bitcast.8, bf16[1024,1024]{1,0:T(8,128)(2,1)} %refs_4_.9, bf16[1024,1024]{1,0:T(8,128)(2,1)} %key_hbm.9, bf16[1024,1024]{1,0:T(8,128)(2,1)} %value_hbm.9, ...), custom_call_target="tpu_custom_call" | custom-call | flops 1 | bytes 1 | tf_op jit(solution)/shard_map/pallas_call | solution.py:234
  20.0 1.3 collective-permute-start.5
  21.4 1.5 %collective-permute-start.7 = (f32[2,128,128]{2,1,0:T(8,128)S(1)}, f32[2,128,128]{2,1,0:T(8,128)S(1)}, u32[]{:S(2)}, u32[]{:S(2)}) collective-permute-start(f32[2,128,128]{2,1,0:T(8,128)S(1)} %shard_map.73), channel_id=1, source_target_pairs={{16,24},{20,28},{17,25},{21,29},{18,26},{22,30},{19,27},{23,31}} | collective-permute-start | bytes 393224 | tf_op jit(solution)/shard_map/ppermute | solution.py:514
  22.9 5.0 %collective-permute-done.5.refs_2_ = f32[2,128,128]{2,1,0:T(8,128)S(1)} collective-permute-done((f32[2,128,128]{2,1,0:T(8,128)S(1)}, f32[2,128,128]{2,1,0:T(8,128)S(1)}, u32[]{:S(2)}, u32[]{:S(2)}) %collective-permute-start.5) | collective-permute-done | bytes 131104 | tf_op jit(solution)/shard_map/ppermute | solution.py:514
  27.9 1.6 %collective-permute-start.8 = (f32[2,128,128]{2,1,0:T(8,128)S(1)}, f32[2,128,128]{2,1,0:T(8,128)S(1)}, u32[]{:S(2)}, u32[]{:S(2)}) collective-permute-start(f32[2,128,128]{2,1,0:T(8,128)S(1)} %get-tuple-element.73), channel_id=1, source_target_pairs={{0,4},{4,0},{8,12},{12,8},{16,20},{20,16},{24,28},{28,24},{1,5},{5... | collective-permute-start | bytes 393224 | tf_op jit(solution)/shard_map/ppermute | solution.py:522
  29.6 1.4 collective-permute-start.9
  31.0 4.4 %shard_map.75 = (bf16[128,1024]{1,0:T(8,128)(2,1)S(1)}, bf16[128,1024]{1,0:T(8,128)(2,1)S(1)}, f32[128,1024]{1,0:T(8,128)S(1)}, f32[128,8]{1,0:T(8,128)S(1)}, bf16[1024,4096]{1,0:T(8,128)(2,1)S(1)}) custom-call(s32[3]{0:T(128)S(1)} %add_add_fusion.1.place_ref, bf16[1024,1024]{1,0:T(8,128)(2,1)} %refs_4_.9, bf16[1024,1024]{1,0:T(8,128)(2,1)} %refs_5_.9, ...), custom_call_target="tpu_custom_call" | custom-call | flops 1 | bytes 1 | tf_op jit(solution)/shard_map/pallas_call | solution.py:283
  35.4 3.5 %shard_map.76 = (f32[16,4096]{1,0:T(8,128)S(1)}, f32[16,4096]{1,0:T(8,128)S(1)}, f32[16,4096]{1,0:T(8,128)S(1)}, f32[16,4096]{1,0:T(8,128)S(1)}, f32[64,4096]{1,0:T(8,128)S(1)}) custom-call(s32[3]{0:T(128)S(1)} %add_add_fusion.1.place_ref, f32[2,128,128]{2,1,0:T(8,128)S(1)} %get-tuple-element.71.refs_0_, ...), custom_call_target="tpu_custom_call" | custom-call | flops 1 | bytes 1 | tf_op jit(solution)/shard_map/pallas_call | solution.py:379
  41.8 1.5 %collective-permute-start.22 = (f32[64,4096]{1,0:T(8,128)S(1)}, f32[64,4096]{1,0:T(8,128)S(1)}, u32[]{:S(2)}, u32[]{:S(2)}) collective-permute-start(f32[64,4096]{1,0:T(8,128)S(1)} %shard_map.77.refs_11_), channel_id=1, source_target_pairs={{0,2},{1,3},{2,0},{3,1},{4,6},{5,7},{6,4},{7,5},{8,10},{9,11},{10,... | collective-permute-start | bytes 3145736 | tf_op jit(solution)/shard_map/ppermute | solution.py:581
  43.3 6.3 %shard_map.78 = (f32[16,4096]{1,0:T(8,128)S(1)}, f32[16,4096]{1,0:T(8,128)S(1)}, f32[16,4096]{1,0:T(8,128)S(1)}, f32[16,4096]{1,0:T(8,128)S(1)}, f32[64,4096]{1,0:T(8,128)S(1)}) custom-call(s32[3]{0:T(128)S(1)} %add_add_fusion.1.place_ref, f32[2,128,128]{2,1,0:T(8,128)S(1)} %get-tuple-element.71.refs_0_, ...), custom_call_target="tpu_custom_call" | custom-call | flops 1 | bytes 1 | tf_op jit(solution)/shard_map/pallas_call | solution.py:379
  52.5 6.3 %shard_map.80 = (f32[16,4096]{1,0:T(8,128)S(1)}, f32[16,4096]{1,0:T(8,128)S(1)}, f32[16,4096]{1,0:T(8,128)S(1)}, f32[16,4096]{1,0:T(8,128)S(1)}, f32[64,4096]{1,0:T(8,128)S(1)}) custom-call(s32[3]{0:T(128)S(1)} %add_add_fusion.1.place_ref, f32[2,128,128]{2,1,0:T(8,128)S(1)} %get-tuple-element.71.refs_0_, ...), custom_call_target="tpu_custom_call" | custom-call | flops 1 | bytes 1 | tf_op jit(solution)/shard_map/pallas_call | solution.py:379
  61.5 6.4 %collective-permute-done.22.refs_4_.refs_0_ = f32[64,4096]{1,0:T(8,128)S(1)} collective-permute-done((f32[64,4096]{1,0:T(8,128)S(1)}, f32[64,4096]{1,0:T(8,128)S(1)}, u32[]{:S(2)}, u32[]{:S(2)}) %collective-permute-start.22) | collective-permute-done | bytes 1048608 | tf_op jit(solution)/shard_map/ppermute | solution.py:581
  68.8 1.5 %collective-permute-start.28 = (f32[64,4096]{1,0:T(8,128)S(1)}, f32[64,4096]{1,0:T(8,128)}, u32[]{:S(2)}, u32[]{:S(2)}) collective-permute-start(f32[64,4096]{1,0:T(8,128)S(1)} %shard_map.81.after_ref.refs_11_), channel_id=1, source_target_pairs={{0,2},{1,3},{2,0},{3,1},{4,6},{5,7},{6,4},{7,5},{8,10},{9,11},{10,... | collective-permute-start | bytes 3145736 | tf_op jit(solution)/shard_map/ppermute | solution.py:581
  70.3 5.5 %shard_map.82 = (f32[64,1024]{1,0:T(8,128)}, f32[64,8]{1,0:T(8,128)}, f32[64,1024]{1,0:T(8,128)}, f32[64,8]{1,0:T(8,128)}) custom-call(s32[3]{0:T(128)S(1)} %add_add_fusion.1.place_ref, f32[8,1024]{1,0:T(8,128)} %bitcast.9, bf16[1024,1024]{1,0:T(8,128)(2,1)} %refs_4_.9, bf16[1024,1024]{1,0:T(8,128)(2,1)} %key_hbm.9, bf16[1024,1024]{1,0:T(8,128)(2,1)} %value_hbm.9, ...), custom_call_target="tpu_custom_call" | custom-call | flops 1 | bytes 1 | tf_op jit(solution)/shard_map/pallas_call | solution.py:234
  75.8 7.1 %shard_map.83 = (f32[16,4096]{1,0:T(8,128)S(1)}, f32[16,4096]{1,0:T(8,128)}, f32[16,4096]{1,0:T(8,128)}, f32[16,4096]{1,0:T(8,128)}, f32[64,4096]{1,0:T(8,128)S(1)}) custom-call(s32[3]{0:T(128)S(1)} %add_add_fusion.1.place_ref, f32[2,128,128]{2,1,0:T(8,128)S(1)} %get-tuple-element.71.refs_0_, ...), custom_call_target="tpu_custom_call" | custom-call | flops 1 | bytes 1 | tf_op jit(solution)/shard_map/pallas_call | solution.py:379
  84.4 1.4 %collective-permute-done.23.refs_0_ = f32[16,4096]{1,0:T(8,128)S(1)} collective-permute-done((f32[16,4096]{1,0:T(8,128)S(1)}, f32[16,4096]{1,0:T(8,128)S(1)}, u32[]{:S(2)}, u32[]{:S(2)}) %collective-permute-start.23) | collective-permute-done | bytes 262176 | tf_op jit(solution)/shard_map/ppermute | solution.py:557
  86.4 1.3 collective-permute-done.26.refs_3_
  87.6 2.8 %collective-permute-done.27.refs_4_.refs_0_ = f32[64,4096]{1,0:T(8,128)} collective-permute-done((f32[64,4096]{1,0:T(8,128)S(1)}, f32[64,4096]{1,0:T(8,128)}, u32[]{:S(2)}, u32[]{:S(2)}) %collective-permute-start.27) | collective-permute-done | bytes 1048608 | tf_op jit(solution)/shard_map/ppermute | solution.py:581
  90.4 1.2 copy-done.3
  91.7 1.1 shard_map.84.after_ref.refs_11_
  92.7 6.7 %shard_map.85 = (f32[256,1024]{1,0:T(8,128)}, f32[256,8]{1,0:T(8,128)}, f32[256,1024]{1,0:T(8,128)}, f32[256,8]{1,0:T(8,128)}) custom-call(s32[3]{0:T(128)S(1)} %add_add_fusion.place_ref, f32[8,1024]{1,0:T(8,128)} %bitcast.10, bf16[1024,1024]{1,0:T(8,128)(2,1)} %refs_4_.9, bf16[1024,1024]{1,0:T(8,128)(2,1)} %key_hbm.9, bf16[1024,1024]{1,0:T(8,128)(2,1)} %value_hbm.9, ...), custom_call_target="tpu_custom_call" | custom-call | flops 1 | bytes 1 | tf_op jit(solution)/shard_map/pallas_call | solution.py:234
  99.4 7.2 %shard_map.87 = (f32[32,4096]{1,0:T(8,128)S(1)}, f32[32,4096]{1,0:T(8,128)S(1)}, f32[32,4096]{1,0:T(8,128)S(1)}, f32[32,4096]{1,0:T(8,128)S(1)}, f32[128,4096]{1,0:T(8,128)S(1)}) custom-call(s32[3]{0:T(128)S(1)} %add_add_fusion.place_ref, f32[2,128,128]{2,1,0:T(8,128)S(1)} %get-tuple-element.71.refs_0_, ...), custom_call_target="tpu_custom_call" | custom-call | flops 1 | bytes 1 | tf_op jit(solution)/shard_map/pallas_call | solution.py:379
  107.2 1.5 %collective-permute-start.29 = (f32[64,4096]{1,0:T(8,128)S(1)}, f32[64,4096]{1,0:T(8,128)S(1)}, u32[]{:S(2)}, u32[]{:S(2)}) collective-permute-start(f32[64,4096]{1,0:T(8,128)S(1)} %shard_map.84.after_ref.refs_11_), channel_id=1, source_target_pairs={{0,2},{1,3},{2,0},{3,1},{4,6},{5,7},{6,4},{7,5},{8,10},{9,11},{10,... | collective-permute-start | bytes 3145736 | tf_op jit(solution)/shard_map/ppermute | solution.py:581
  108.7 4.2 %collective-permute-done.28.refs_11_.refs_0_ = f32[64,4096]{1,0:T(8,128)} collective-permute-done((f32[64,4096]{1,0:T(8,128)S(1)}, f32[64,4096]{1,0:T(8,128)}, u32[]{:S(2)}, u32[]{:S(2)}) %collective-permute-start.28) | collective-permute-done | bytes 1048608 | tf_op jit(solution)/shard_map/ppermute | solution.py:581
  112.9 7.2 %shard_map.86 = (f32[32,4096]{1,0:T(8,128)S(1)}, f32[32,4096]{1,0:T(8,128)S(1)}, f32[32,4096]{1,0:T(8,128)S(1)}, f32[32,4096]{1,0:T(8,128)S(1)}, f32[128,4096]{1,0:T(8,128)S(1)}) custom-call(s32[3]{0:T(128)S(1)} %add_add_fusion.place_ref, f32[2,128,128]{2,1,0:T(8,128)S(1)} %get-tuple-element.71.refs_0_, ...), custom_call_target="tpu_custom_call" | custom-call | flops 1 | bytes 1 | tf_op jit(solution)/shard_map/pallas_call | solution.py:379
  122.2 2.2 %shard_map.89.refs_3_ = bf16[256,4096]{1,0:T(8,128)(2,1)} custom-call(f32[128,4096]{1,0:T(8,128)S(1)} %get-tuple-element.116.own_ref.refs_3_, f32[64,4096]{1,0:T(8,128)} %collective-permute-done.27.refs_4_.refs_0_, f32[32,4096]{1,0:T(8,128)S(1)} %collective-permute-done.34.refs_1_, ...), custom_call_target="tpu_custom_call", output_to_operand_aliasing={{}: (4, {})} | custom-call | flops 1 | bytes 1 | tf_op jit(solution)/shard_map/pallas_call | solution.py:433
  124.4 2.2 %shard_map.90.refs_3_ = bf16[256,4096]{1,0:T(8,128)(2,1)} custom-call(f32[128,4096]{1,0:T(8,128)S(1)} %get-tuple-element.111.own_ref, f32[64,4096]{1,0:T(8,128)} %collective-permute-done.28.refs_11_.refs_0_, f32[32,4096]{1,0:T(8,128)S(1)} %collective-permute-done.32.refs_1_, ...), custom_call_target="tpu_custom_call", output_to_operand_aliasing={{}: (4, {})} | custom-call | flops 1 | bytes 1 | tf_op jit(solution)/shard_map/pallas_call | solution.py:433
  126.7 7.8 %collective-permute-done.29.refs_0_ = f32[64,4096]{1,0:T(8,128)S(1)} collective-permute-done((f32[64,4096]{1,0:T(8,128)S(1)}, f32[64,4096]{1,0:T(8,128)S(1)}, u32[]{:S(2)}, u32[]{:S(2)}) %collective-permute-start.29) | collective-permute-done | bytes 1048608 | tf_op jit(solution)/shard_map/ppermute | solution.py:581
  (82 shorter events, 19.2 us)
Async XLA Ops:
  3.0 6.6 %collective-permute-start = (f32[2,136,128]{2,1,0:T(8,128)S(1)}, f32[2,136,128]{2,1,0:T(8,128)S(1)}, u32[]{:S(2)}, u32[]{:S(2)}) collective-permute-start(f32[2,136,128]{2,1,0:T(8,128)S(1)} %get-tuple-element.65), channel_id=1, source_target_pairs={{0,4},{4,0},{8,12},{12,8},{16,20},{20,16},{24,28},{28,24},{1,5},{5... | collective-permute-start | bytes 417800 | tf_op jit(solution)/shard_map/ppermute | solution.py:541
  4.5 6.9 %collective-permute-start.3 = (f32[2,136,128]{2,1,0:T(8,128)S(1)}, f32[2,136,128]{2,1,0:T(8,128)S(1)}, u32[]{:S(2)}, u32[]{:S(2)}) collective-permute-start(f32[2,136,128]{2,1,0:T(8,128)S(1)} %get-tuple-element.69), channel_id=1, source_target_pairs={{0,4},{4,0},{8,12},{12,8},{16,20},{20,16},{24,28},{28,24},{1,5},{5... | collective-permute-start | bytes 417800 | tf_op jit(solution)/shard_map/ppermute | solution.py:541
  9.6 2.5 %collective-permute-start.1 = (f32[2,128,128]{2,1,0:T(8,128)S(1)}, f32[2,128,128]{2,1,0:T(8,128)S(1)}, u32[]{:S(2)}, u32[]{:S(2)}) collective-permute-start(f32[2,128,128]{2,1,0:T(8,128)S(1)} %shard_map.66), channel_id=1, source_target_pairs={{0,8},{4,12},{1,9},{5,13},{2,10},{6,14},{3,11},{7,15}} | collective-permute-start | bytes 393224 | tf_op jit(solution)/shard_map/ppermute | solution.py:514
  12.2 7.8 %collective-permute-start.2 = (f32[2,128,128]{2,1,0:T(8,128)S(1)}, f32[2,128,128]{2,1,0:T(8,128)S(1)}, u32[]{:S(2)}, u32[]{:S(2)}) collective-permute-start(f32[2,128,128]{2,1,0:T(8,128)S(1)} %shard_map.67), channel_id=1, source_target_pairs={{8,16},{12,20},{9,17},{13,21},{10,18},{14,22},{11,19},{15,23}} | collective-permute-start | bytes 393224 | tf_op jit(solution)/shard_map/ppermute | solution.py:514
  12.9 8.4 %collective-permute-start.6 = (f32[2,128,128]{2,1,0:T(8,128)S(1)}, f32[2,128,128]{2,1,0:T(8,128)S(1)}, u32[]{:S(2)}, u32[]{:S(2)}) collective-permute-start(f32[2,128,128]{2,1,0:T(8,128)S(1)} %shard_map.69.after_ref), channel_id=1, source_target_pairs={{8,16},{12,20},{9,17},{13,21},{10,18},{14,22},{11,19},{15,23}} | collective-permute-start | bytes 393224 | tf_op jit(solution)/shard_map/ppermute | solution.py:514
  20.0 7.8 %collective-permute-start.5 = (f32[2,128,128]{2,1,0:T(8,128)S(1)}, f32[2,128,128]{2,1,0:T(8,128)S(1)}, u32[]{:S(2)}, u32[]{:S(2)}) collective-permute-start(f32[2,128,128]{2,1,0:T(8,128)S(1)} %shard_map.71), channel_id=1, source_target_pairs={{16,24},{20,28},{17,25},{21,29},{18,26},{22,30},{19,27},{23,31}} | collective-permute-start | bytes 393224 | tf_op jit(solution)/shard_map/ppermute | solution.py:514
  21.4 8.2 %collective-permute-start.7 = (f32[2,128,128]{2,1,0:T(8,128)S(1)}, f32[2,128,128]{2,1,0:T(8,128)S(1)}, u32[]{:S(2)}, u32[]{:S(2)}) collective-permute-start(f32[2,128,128]{2,1,0:T(8,128)S(1)} %shard_map.73), channel_id=1, source_target_pairs={{16,24},{20,28},{17,25},{21,29},{18,26},{22,30},{19,27},{23,31}} | collective-permute-start | bytes 393224 | tf_op jit(solution)/shard_map/ppermute | solution.py:514
  27.9 7.5 %collective-permute-start.8 = (f32[2,128,128]{2,1,0:T(8,128)S(1)}, f32[2,128,128]{2,1,0:T(8,128)S(1)}, u32[]{:S(2)}, u32[]{:S(2)}) collective-permute-start(f32[2,128,128]{2,1,0:T(8,128)S(1)} %get-tuple-element.73), channel_id=1, source_target_pairs={{0,4},{4,0},{8,12},{12,8},{16,20},{20,16},{24,28},{28,24},{1,5},{5... | collective-permute-start | bytes 393224 | tf_op jit(solution)/shard_map/ppermute | solution.py:522
  29.6 5.8 %collective-permute-start.9 = (f32[2,128,128]{2,1,0:T(8,128)S(1)}, f32[2,128,128]{2,1,0:T(8,128)S(1)}, u32[]{:S(2)}, u32[]{:S(2)}) collective-permute-start(f32[2,128,128]{2,1,0:T(8,128)S(1)} %get-tuple-element.74), channel_id=1, source_target_pairs={{0,4},{4,0},{8,12},{12,8},{16,20},{20,16},{24,28},{28,24},{1,5},{5... | collective-permute-start | bytes 393224 | tf_op jit(solution)/shard_map/ppermute | solution.py:522
  39.0 1.9 %collective-permute-start.11 = (f32[16,4096]{1,0:T(8,128)S(1)}, f32[16,4096]{1,0:T(8,128)S(1)}, u32[]{:S(2)}, u32[]{:S(2)}) collective-permute-start(f32[16,4096]{1,0:T(8,128)S(1)} %get-tuple-element.85), channel_id=1, source_target_pairs={{0,1},{1,0},{2,3},{3,2},{4,5},{5,4},{6,7},{7,6},{8,9},{9,8},{10,11... | collective-permute-start | bytes 786440 | tf_op jit(solution)/shard_map/ppermute | solution.py:557
  39.5 1.8 %collective-permute-start.12 = (f32[16,4096]{1,0:T(8,128)S(1)}, f32[16,4096]{1,0:T(8,128)S(1)}, u32[]{:S(2)}, u32[]{:S(2)}) collective-permute-start(f32[16,4096]{1,0:T(8,128)S(1)} %get-tuple-element.86), channel_id=1, source_target_pairs={{0,1},{1,0},{2,3},{3,2},{4,5},{5,4},{6,7},{7,6},{8,9},{9,8},{10,11... | collective-permute-start | bytes 786440 | tf_op jit(solution)/shard_map/ppermute | solution.py:557
  39.6 2.1 %collective-permute-start.13 = (f32[16,4096]{1,0:T(8,128)S(1)}, f32[16,4096]{1,0:T(8,128)S(1)}, u32[]{:S(2)}, u32[]{:S(2)}) collective-permute-start(f32[16,4096]{1,0:T(8,128)S(1)} %get-tuple-element.87), channel_id=1, source_target_pairs={{0,1},{1,0},{2,3},{3,2},{4,5},{5,4},{6,7},{7,6},{8,9},{9,8},{10,11... | collective-permute-start | bytes 786440 | tf_op jit(solution)/shard_map/ppermute | solution.py:557
  41.8 26.1 %collective-permute-start.22 = (f32[64,4096]{1,0:T(8,128)S(1)}, f32[64,4096]{1,0:T(8,128)S(1)}, u32[]{:S(2)}, u32[]{:S(2)}) collective-permute-start(f32[64,4096]{1,0:T(8,128)S(1)} %shard_map.77.refs_11_), channel_id=1, source_target_pairs={{0,2},{1,3},{2,0},{3,1},{4,6},{5,7},{6,4},{7,5},{8,10},{9,11},{10,... | collective-permute-start | bytes 3145736 | tf_op jit(solution)/shard_map/ppermute | solution.py:581
  49.7 1.9 %collective-permute-start.15 = (f32[16,4096]{1,0:T(8,128)S(1)}, f32[16,4096]{1,0:T(8,128)S(1)}, u32[]{:S(2)}, u32[]{:S(2)}) collective-permute-start(f32[16,4096]{1,0:T(8,128)S(1)} %get-tuple-element.90), channel_id=1, source_target_pairs={{0,1},{1,0},{2,3},{3,2},{4,5},{5,4},{6,7},{7,6},{8,9},{9,8},{10,11... | collective-permute-start | bytes 786440 | tf_op jit(solution)/shard_map/ppermute | solution.py:557
  50.3 2.1 %collective-permute-start.17 = (f32[16,4096]{1,0:T(8,128)S(1)}, f32[16,4096]{1,0:T(8,128)S(1)}, u32[]{:S(2)}, u32[]{:S(2)}) collective-permute-start(f32[16,4096]{1,0:T(8,128)S(1)} %get-tuple-element.92), channel_id=1, source_target_pairs={{0,1},{1,0},{2,3},{3,2},{4,5},{5,4},{6,7},{7,6},{8,9},{9,8},{10,11... | collective-permute-start | bytes 786440 | tf_op jit(solution)/shard_map/ppermute | solution.py:557
  59.0 2.0 %collective-permute-start.19 = (f32[16,4096]{1,0:T(8,128)S(1)}, f32[16,4096]{1,0:T(8,128)S(1)}, u32[]{:S(2)}, u32[]{:S(2)}) collective-permute-start(f32[16,4096]{1,0:T(8,128)S(1)} %get-tuple-element.95), channel_id=1, source_target_pairs={{0,1},{1,0},{2,3},{3,2},{4,5},{5,4},{6,7},{7,6},{8,9},{9,8},{10,11... | collective-permute-start | bytes 786440 | tf_op jit(solution)/shard_map/ppermute | solution.py:557
  59.5 2.0 %collective-permute-start.21 = (f32[16,4096]{1,0:T(8,128)S(1)}, f32[16,4096]{1,0:T(8,128)S(1)}, u32[]{:S(2)}, u32[]{:S(2)}) collective-permute-start(f32[16,4096]{1,0:T(8,128)S(1)} %get-tuple-element.97), channel_id=1, source_target_pairs={{0,1},{1,0},{2,3},{3,2},{4,5},{5,4},{6,7},{7,6},{8,9},{9,8},{10,11... | collective-permute-start | bytes 786440 | tf_op jit(solution)/shard_map/ppermute | solution.py:557
  60.4 30.1 %collective-permute-start.27 = (f32[64,4096]{1,0:T(8,128)S(1)}, f32[64,4096]{1,0:T(8,128)}, u32[]{:S(2)}, u32[]{:S(2)}) collective-permute-start(f32[64,4096]{1,0:T(8,128)S(1)} %shard_map.79.refs_11_), channel_id=1, source_target_pairs={{0,2},{1,3},{2,0},{3,1},{4,6},{5,7},{6,4},{7,5},{8,10},{9,11},{10,... | collective-permute-start | bytes 3145736 | tf_op jit(solution)/shard_map/ppermute | solution.py:581
  68.8 44.1 %collective-permute-start.28 = (f32[64,4096]{1,0:T(8,128)S(1)}, f32[64,4096]{1,0:T(8,128)}, u32[]{:S(2)}, u32[]{:S(2)}) collective-permute-start(f32[64,4096]{1,0:T(8,128)S(1)} %shard_map.81.after_ref.refs_11_), channel_id=1, source_target_pairs={{0,2},{1,3},{2,0},{3,1},{4,6},{5,7},{6,4},{7,5},{8,10},{9,11},{10,... | collective-permute-start | bytes 3145736 | tf_op jit(solution)/shard_map/ppermute | solution.py:581
  83.9 1.9 %collective-permute-start.23 = (f32[16,4096]{1,0:T(8,128)S(1)}, f32[16,4096]{1,0:T(8,128)S(1)}, u32[]{:S(2)}, u32[]{:S(2)}) collective-permute-start(f32[16,4096]{1,0:T(8,128)S(1)} %get-tuple-element.103), channel_id=1, source_target_pairs={{0,1},{1,0},{2,3},{3,2},{4,5},{5,4},{6,7},{7,6},{8,9},{9,8},{10,11... | collective-permute-start | bytes 786440 | tf_op jit(solution)/shard_map/ppermute | solution.py:557
  83.9 2.1 %collective-permute-start.24 = (f32[16,4096]{1,0:T(8,128)}, f32[16,4096]{1,0:T(8,128)S(1)}, u32[]{:S(2)}, u32[]{:S(2)}) collective-permute-start(f32[16,4096]{1,0:T(8,128)} %get-tuple-element.104), channel_id=1, source_target_pairs={{0,1},{1,0},{2,3},{3,2},{4,5},{5,4},{6,7},{7,6},{8,9},{9,8},{10,11... | collective-permute-start | bytes 786440 | tf_op jit(solution)/shard_map/ppermute | solution.py:557
  84.4 2.0 %collective-permute-start.25 = (f32[16,4096]{1,0:T(8,128)}, f32[16,4096]{1,0:T(8,128)S(1)}, u32[]{:S(2)}, u32[]{:S(2)}) collective-permute-start(f32[16,4096]{1,0:T(8,128)} %get-tuple-element.105), channel_id=1, source_target_pairs={{0,1},{1,0},{2,3},{3,2},{4,5},{5,4},{6,7},{7,6},{8,9},{9,8},{10,11... | collective-permute-start | bytes 786440 | tf_op jit(solution)/shard_map/ppermute | solution.py:557
  85.7 1.9 %collective-permute-start.26 = (f32[16,4096]{1,0:T(8,128)}, f32[16,4096]{1,0:T(8,128)}, u32[]{:S(2)}, u32[]{:S(2)}) collective-permute-start(f32[16,4096]{1,0:T(8,128)} %get-tuple-element.106), channel_id=1, source_target_pairs={{0,1},{1,0},{2,3},{3,2},{4,5},{5,4},{6,7},{7,6},{8,9},{9,8},{10,11... | collective-permute-start | bytes 786440 | tf_op jit(solution)/shard_map/ppermute | solution.py:557
  106.6 13.5 %collective-permute-start.34 = (f32[32,4096]{1,0:T(8,128)S(1)}, f32[32,4096]{1,0:T(8,128)S(1)}, u32[]{:S(2)}, u32[]{:S(2)}) collective-permute-start(f32[32,4096]{1,0:T(8,128)S(1)} %get-tuple-element.117), channel_id=1, source_target_pairs={{0,1},{1,0},{2,3},{3,2},{4,5},{5,4},{6,7},{7,6},{8,9},{9,8},{10,11... | collective-permute-start | bytes 1572872 | tf_op jit(solution)/shard_map/ppermute | solution.py:557
  106.7 14.0 %collective-permute-start.35 = (f32[32,4096]{1,0:T(8,128)S(1)}, f32[32,4096]{1,0:T(8,128)S(1)}, u32[]{:S(2)}, u32[]{:S(2)}) collective-permute-start(f32[32,4096]{1,0:T(8,128)S(1)} %get-tuple-element.118), channel_id=1, source_target_pairs={{0,1},{1,0},{2,3},{3,2},{4,5},{5,4},{6,7},{7,6},{8,9},{9,8},{10,11... | collective-permute-start | bytes 1572872 | tf_op jit(solution)/shard_map/ppermute | solution.py:557
  107.2 27.3 %collective-permute-start.29 = (f32[64,4096]{1,0:T(8,128)S(1)}, f32[64,4096]{1,0:T(8,128)S(1)}, u32[]{:S(2)}, u32[]{:S(2)}) collective-permute-start(f32[64,4096]{1,0:T(8,128)S(1)} %shard_map.84.after_ref.refs_11_), channel_id=1, source_target_pairs={{0,2},{1,3},{2,0},{3,1},{4,6},{5,7},{6,4},{7,5},{8,10},{9,11},{10,... | collective-permute-start | bytes 3145736 | tf_op jit(solution)/shard_map/ppermute | solution.py:581
  108.7 12.1 %collective-permute-start.36 = (f32[32,4096]{1,0:T(8,128)S(1)}, f32[32,4096]{1,0:T(8,128)S(1)}, u32[]{:S(2)}, u32[]{:S(2)}) collective-permute-start(f32[32,4096]{1,0:T(8,128)S(1)} %get-tuple-element.119), channel_id=1, source_target_pairs={{0,1},{1,0},{2,3},{3,2},{4,5},{5,4},{6,7},{7,6},{8,9},{9,8},{10,11... | collective-permute-start | bytes 1572872 | tf_op jit(solution)/shard_map/ppermute | solution.py:557
  112.9 8.3 %collective-permute-start.37 = (f32[32,4096]{1,0:T(8,128)S(1)}, f32[32,4096]{1,0:T(8,128)S(1)}, u32[]{:S(2)}, u32[]{:S(2)}) collective-permute-start(f32[32,4096]{1,0:T(8,128)S(1)} %get-tuple-element.120), channel_id=1, source_target_pairs={{0,1},{1,0},{2,3},{3,2},{4,5},{5,4},{6,7},{7,6},{8,9},{9,8},{10,11... | collective-permute-start | bytes 1572872 | tf_op jit(solution)/shard_map/ppermute | solution.py:557
  120.1 4.3 %collective-permute-start.32 = (f32[32,4096]{1,0:T(8,128)S(1)}, f32[32,4096]{1,0:T(8,128)S(1)}, u32[]{:S(2)}, u32[]{:S(2)}) collective-permute-start(f32[32,4096]{1,0:T(8,128)S(1)} %get-tuple-element.114), channel_id=1, source_target_pairs={{0,1},{1,0},{2,3},{3,2},{4,5},{5,4},{6,7},{7,6},{8,9},{9,8},{10,11... | collective-permute-start | bytes 1572872 | tf_op jit(solution)/shard_map/ppermute | solution.py:557
  120.7 3.8 %collective-permute-start.33 = (f32[32,4096]{1,0:T(8,128)S(1)}, f32[32,4096]{1,0:T(8,128)S(1)}, u32[]{:S(2)}, u32[]{:S(2)}) collective-permute-start(f32[32,4096]{1,0:T(8,128)S(1)} %get-tuple-element.115), channel_id=1, source_target_pairs={{0,1},{1,0},{2,3},{3,2},{4,5},{5,4},{6,7},{7,6},{8,9},{9,8},{10,11... | collective-permute-start | bytes 1572872 | tf_op jit(solution)/shard_map/ppermute | solution.py:557
  120.8 13.7 %collective-permute-start.30 = (f32[32,4096]{1,0:T(8,128)S(1)}, f32[32,4096]{1,0:T(8,128)S(1)}, u32[]{:S(2)}, u32[]{:S(2)}) collective-permute-start(f32[32,4096]{1,0:T(8,128)S(1)} %get-tuple-element.112), channel_id=1, source_target_pairs={{0,1},{1,0},{2,3},{3,2},{4,5},{5,4},{6,7},{7,6},{8,9},{9,8},{10,11... | collective-permute-start | bytes 1572872 | tf_op jit(solution)/shard_map/ppermute | solution.py:557
  121.2 13.3 %collective-permute-start.31 = (f32[32,4096]{1,0:T(8,128)S(1)}, f32[32,4096]{1,0:T(8,128)S(1)}, u32[]{:S(2)}, u32[]{:S(2)}) collective-permute-start(f32[32,4096]{1,0:T(8,128)S(1)} %get-tuple-element.113), channel_id=1, source_target_pairs={{0,1},{1,0},{2,3},{3,2},{4,5},{5,4},{6,7},{7,6},{8,9},{9,8},{10,11... | collective-permute-start | bytes 1572872 | tf_op jit(solution)/shard_map/ppermute | solution.py:557
  (10 other events, 21.3 us)

commit v8 on v7

--- a/solution.py
+++ b/solution.py
@@ -566,7 +566,7 @@
 
     keep, got = incoming_states(
         odd, kept, met, starts[0], [functools.partial(inside_of, target) for target in targets])
-    last = keep[-1]
+    last = keep[0]
     brought = bring_rows(place_of(targets[0]), sizes[0], 0, 0, block_len, queries, parts[0],
                          gate_input, out_weight, last)
     landed, own, result = [last, last], [], None

time: 136 us -> 136 us (level)
  no operation moved by 1% of the time
where the time goes in v8:
time: 136 us; the launch traced here: 135 us
  Pallas kernels  75.4 us (55%)
  waiting for transfers between devices  35.3 us (26%)
  starting transfers between devices  21.1 us (16%)
  local copies, waits for them, and re-layouts  3.08 us (2%)
    pallas_call x6, Pallas kernels, project_rows(): pl.pallas_call(functools.partial(project_kernel, first_row, part_row, blo...  37.5 us
    ppermute x4, waiting for transfers between devices, per_device(): landed.append(lax.ppermute(last, 'head', across))  21.2 us
    pallas_call x3, Pallas kernels, inside_part(): pl.pallas_call(functools.partial(inside_kernel, begin, end), in_specs=[pl...  18.4 us
    ppermute x24, waiting for transfers between devices, project(): return (mine, [lax.ppermute(piece, 'head', cores) for piece in theirs])  7.4 us
    pallas_call x2, Pallas kernels, local_states(): pl.pallas_call(functools.partial(states_kernel, other is not None), in_sp...  7.01 us
    pallas_call x4, Pallas kernels, finish_rows(): pl.pallas_call(functools.partial(finish_kernel, len(arrived)), grid=(1,),...  6.31 us
    ppermute x24, starting transfers between devices, project(): return (mine, [lax.ppermute(piece, 'head', cores) for piece in theirs])  5.63 us
    ppermute x6, starting transfers between devices, incoming_states(): landed[i].append(lax.ppermute(value, 'seq', along))  5.44 us
  transfers between devices with their start and end apart: 38, of which 21 were waited for; matrix products, arithmetic and copies ran while one was open for 0% of the time, Pallas kernels for 50%

profile of v8, /device:TPU:24, one launch (start us, length us, event | category | flops | bytes accessed | tf_op | source)
XLA Modules:
  0.0 135.4 jit_solution(2148269376987596834)
XLA Ops:
  0.0 3.0 %shard_map.64 = (f32[2,136,128]{2,1,0:T(8,128)S(1)}, f32[2,136,128]{2,1,0:T(8,128)S(1)}, f32[4,4,128,128]{3,2,1,0:T(8,128)S(1)}) custom-call(s32[1]{0:T(128)S(6)} %sub.12.side_ref, f32[8,1024]{1,0:T(8,128)} %bitcast.6, bf16[1024,1024]{1,0:T(8,128)(2,1)} %key_hbm.9, bf16[1024,1024]{1,0:T(8,128)(2,1)} %value_hbm.9), custom_call_target="tpu_custom_call" | custom-call | flops 1 | bytes 1 | tf_op jit(solution)/shard_map/pallas_call | solution.py:153
  3.0 1.6 %collective-permute-start = (f32[2,136,128]{2,1,0:T(8,128)S(1)}, f32[2,136,128]{2,1,0:T(8,128)S(1)}, u32[]{:S(2)}, u32[]{:S(2)}) collective-permute-start(f32[2,136,128]{2,1,0:T(8,128)S(1)} %get-tuple-element.65), channel_id=1, source_target_pairs={{0,4},{4,0},{8,12},{12,8},{16,20},{20,16},{24,28},{28,24},{1,5},{5... | collective-permute-start | bytes 417800 | tf_op jit(solution)/shard_map/ppermute | solution.py:541
  5.1 4.0 %shard_map.65 = (f32[2,136,128]{2,1,0:T(8,128)S(1)}, f32[2,136,128]{2,1,0:T(8,128)S(1)}, f32[4,4,128,128]{3,2,1,0:T(8,128)}, f32[4,4,128,128]{3,2,1,0:T(8,128)}) custom-call(s32[1]{0:T(128)} %bitcast.2.side_ref.odd_ref, f32[8,1024]{1,0:T(8,128)} %bitcast.7, bf16[1024,1024]{1,0:T(8,128)(2,1)} %key_hbm.9, bf16[1024,1024]{1,0:T(8,128)(2,1)} %value_hbm.9, ...), custom_call_target="tpu_custom_call" | custom-call | flops 1 | bytes 1 | tf_op jit(solution)/shard_map/pallas_call | solution.py:153
  10.3 1.1 collective-permute-done.3.refs_1_.refs_2_.refs_3_.refs_4_
  13.7 6.2 %shard_map.70 = (f32[192,1024]{1,0:T(8,128)}, f32[192,8]{1,0:T(8,128)}, f32[192,1024]{1,0:T(8,128)}, f32[192,8]{1,0:T(8,128)}) custom-call(s32[3]{0:T(128)S(1)} %add_add_fusion.1.place_ref, f32[8,1024]{1,0:T(8,128)} %bitcast.8, bf16[1024,1024]{1,0:T(8,128)(2,1)} %refs_4_.9, bf16[1024,1024]{1,0:T(8,128)(2,1)} %key_hbm.9, bf16[1024,1024]{1,0:T(8,128)(2,1)} %value_hbm.9, ...), custom_call_target="tpu_custom_call" | custom-call | flops 1 | bytes 1 | tf_op jit(solution)/shard_map/pallas_call | solution.py:234
  20.0 1.3 collective-permute-start.5
  21.4 1.5 %collective-permute-start.7 = (f32[2,128,128]{2,1,0:T(8,128)S(1)}, f32[2,128,128]{2,1,0:T(8,128)S(1)}, u32[]{:S(2)}, u32[]{:S(2)}) collective-permute-start(f32[2,128,128]{2,1,0:T(8,128)S(1)} %shard_map.73), channel_id=1, source_target_pairs={{16,24},{20,28},{17,25},{21,29},{18,26},{22,30},{19,27},{23,31}} | collective-permute-start | bytes 393224 | tf_op jit(solution)/shard_map/ppermute | solution.py:514
  22.9 5.0 %collective-permute-done.5.refs_2_ = f32[2,128,128]{2,1,0:T(8,128)S(1)} collective-permute-done((f32[2,128,128]{2,1,0:T(8,128)S(1)}, f32[2,128,128]{2,1,0:T(8,128)S(1)}, u32[]{:S(2)}, u32[]{:S(2)}) %collective-permute-start.5) | collective-permute-done | bytes 131104 | tf_op jit(solution)/shard_map/ppermute | solution.py:514
  27.9 1.6 %collective-permute-start.8 = (f32[2,128,128]{2,1,0:T(8,128)S(1)}, f32[2,128,128]{2,1,0:T(8,128)S(1)}, u32[]{:S(2)}, u32[]{:S(2)}) collective-permute-start(f32[2,128,128]{2,1,0:T(8,128)S(1)} %get-tuple-element.73), channel_id=1, source_target_pairs={{0,4},{4,0},{8,12},{12,8},{16,20},{20,16},{24,28},{28,24},{1,5},{5... | collective-permute-start | bytes 393224 | tf_op jit(solution)/shard_map/ppermute | solution.py:522
  29.6 1.4 collective-permute-start.9
  31.0 4.4 %shard_map.75 = (bf16[128,1024]{1,0:T(8,128)(2,1)S(1)}, bf16[128,1024]{1,0:T(8,128)(2,1)S(1)}, f32[128,1024]{1,0:T(8,128)S(1)}, f32[128,8]{1,0:T(8,128)S(1)}, bf16[1024,4096]{1,0:T(8,128)(2,1)S(1)}) custom-call(s32[3]{0:T(128)S(1)} %add_add_fusion.1.place_ref, bf16[1024,1024]{1,0:T(8,128)(2,1)} %refs_4_.9, bf16[1024,1024]{1,0:T(8,128)(2,1)} %refs_5_.9, ...), custom_call_target="tpu_custom_call" | custom-call | flops 1 | bytes 1 | tf_op jit(solution)/shard_map/pallas_call | solution.py:283
  35.4 3.5 %shard_map.76 = (f32[16,4096]{1,0:T(8,128)S(1)}, f32[16,4096]{1,0:T(8,128)S(1)}, f32[16,4096]{1,0:T(8,128)S(1)}, f32[16,4096]{1,0:T(8,128)S(1)}, f32[64,4096]{1,0:T(8,128)S(1)}) custom-call(s32[3]{0:T(128)S(1)} %add_add_fusion.1.place_ref, f32[2,128,128]{2,1,0:T(8,128)S(1)} %get-tuple-element.71.after_ref.refs_0_.refs_9_.refs_4_, ...), custom_call_target="tpu_custom_call" | custom-call | flops 1 | bytes 1 | tf_op jit(solution)/shard_map/pallas_call | solution.py:379
  41.8 1.5 %collective-permute-start.22 = (f32[64,4096]{1,0:T(8,128)S(1)}, f32[64,4096]{1,0:T(8,128)S(1)}, u32[]{:S(2)}, u32[]{:S(2)}) collective-permute-start(f32[64,4096]{1,0:T(8,128)S(1)} %shard_map.77.refs_11_), channel_id=1, source_target_pairs={{0,2},{1,3},{2,0},{3,1},{4,6},{5,7},{6,4},{7,5},{8,10},{9,11},{10,... | collective-permute-start | bytes 3145736 | tf_op jit(solution)/shard_map/ppermute | solution.py:581
  43.3 6.3 %shard_map.78 = (f32[16,4096]{1,0:T(8,128)S(1)}, f32[16,4096]{1,0:T(8,128)S(1)}, f32[16,4096]{1,0:T(8,128)S(1)}, f32[16,4096]{1,0:T(8,128)S(1)}, f32[64,4096]{1,0:T(8,128)S(1)}) custom-call(s32[3]{0:T(128)S(1)} %add_add_fusion.1.place_ref, f32[2,128,128]{2,1,0:T(8,128)S(1)} %get-tuple-element.71.after_ref.refs_0_.refs_9_.refs_4_, ...), custom_call_target="tpu_custom_call" | custom-call | flops 1 | bytes 1 | tf_op jit(solution)/shard_map/pallas_call | solution.py:379
  52.5 6.3 %shard_map.80 = (f32[16,4096]{1,0:T(8,128)S(1)}, f32[16,4096]{1,0:T(8,128)S(1)}, f32[16,4096]{1,0:T(8,128)S(1)}, f32[16,4096]{1,0:T(8,128)S(1)}, f32[64,4096]{1,0:T(8,128)S(1)}) custom-call(s32[3]{0:T(128)S(1)} %add_add_fusion.1.place_ref, f32[2,128,128]{2,1,0:T(8,128)S(1)} %get-tuple-element.71.after_ref.refs_0_.refs_9_.refs_4_, ...), custom_call_target="tpu_custom_call" | custom-call | flops 1 | bytes 1 | tf_op jit(solution)/shard_map/pallas_call | solution.py:379
  61.5 6.4 %collective-permute-done.22.refs_4_.refs_0_ = f32[64,4096]{1,0:T(8,128)S(1)} collective-permute-done((f32[64,4096]{1,0:T(8,128)S(1)}, f32[64,4096]{1,0:T(8,128)S(1)}, u32[]{:S(2)}, u32[]{:S(2)}) %collective-permute-start.22) | collective-permute-done | bytes 1048608 | tf_op jit(solution)/shard_map/ppermute | solution.py:581
  68.8 1.5 %collective-permute-start.28 = (f32[64,4096]{1,0:T(8,128)S(1)}, f32[64,4096]{1,0:T(8,128)}, u32[]{:S(2)}, u32[]{:S(2)}) collective-permute-start(f32[64,4096]{1,0:T(8,128)S(1)} %shard_map.81.after_ref.refs_11_), channel_id=1, source_target_pairs={{0,2},{1,3},{2,0},{3,1},{4,6},{5,7},{6,4},{7,5},{8,10},{9,11},{10,... | collective-permute-start | bytes 3145736 | tf_op jit(solution)/shard_map/ppermute | solution.py:581
  70.3 5.5 %shard_map.82 = (f32[64,1024]{1,0:T(8,128)}, f32[64,8]{1,0:T(8,128)}, f32[64,1024]{1,0:T(8,128)}, f32[64,8]{1,0:T(8,128)}) custom-call(s32[3]{0:T(128)S(1)} %add_add_fusion.1.place_ref, f32[8,1024]{1,0:T(8,128)} %bitcast.9, bf16[1024,1024]{1,0:T(8,128)(2,1)} %refs_4_.9, bf16[1024,1024]{1,0:T(8,128)(2,1)} %key_hbm.9, bf16[1024,1024]{1,0:T(8,128)(2,1)} %value_hbm.9, ...), custom_call_target="tpu_custom_call" | custom-call | flops 1 | bytes 1 | tf_op jit(solution)/shard_map/pallas_call | solution.py:234
  75.8 7.1 %shard_map.83 = (f32[16,4096]{1,0:T(8,128)S(1)}, f32[16,4096]{1,0:T(8,128)}, f32[16,4096]{1,0:T(8,128)}, f32[16,4096]{1,0:T(8,128)}, f32[64,4096]{1,0:T(8,128)S(1)}) custom-call(s32[3]{0:T(128)S(1)} %add_add_fusion.1.place_ref, f32[2,128,128]{2,1,0:T(8,128)S(1)} %get-tuple-element.71.after_ref.refs_0_.refs_9_.refs_4_, ...), custom_call_target="tpu_custom_call" | custom-call | flops 1 | bytes 1 | tf_op jit(solution)/shard_map/pallas_call | solution.py:379
  84.4 1.4 %collective-permute-done.23.refs_0_ = f32[16,4096]{1,0:T(8,128)S(1)} collective-permute-done((f32[16,4096]{1,0:T(8,128)S(1)}, f32[16,4096]{1,0:T(8,128)S(1)}, u32[]{:S(2)}, u32[]{:S(2)}) %collective-permute-start.23) | collective-permute-done | bytes 262176 | tf_op jit(solution)/shard_map/ppermute | solution.py:557
  86.4 1.3 collective-permute-done.26.refs_3_
  87.6 2.8 %collective-permute-done.27.refs_4_.refs_0_ = f32[64,4096]{1,0:T(8,128)} collective-permute-done((f32[64,4096]{1,0:T(8,128)S(1)}, f32[64,4096]{1,0:T(8,128)}, u32[]{:S(2)}, u32[]{:S(2)}) %collective-permute-start.27) | collective-permute-done | bytes 1048608 | tf_op jit(solution)/shard_map/ppermute | solution.py:581
  90.4 1.2 copy-done.3
  91.7 1.1 shard_map.84.after_ref.refs_11_
  92.7 6.7 %shard_map.85 = (f32[256,1024]{1,0:T(8,128)}, f32[256,8]{1,0:T(8,128)}, f32[256,1024]{1,0:T(8,128)}, f32[256,8]{1,0:T(8,128)}) custom-call(s32[3]{0:T(128)S(1)} %add_add_fusion.place_ref, f32[8,1024]{1,0:T(8,128)} %bitcast.10, bf16[1024,1024]{1,0:T(8,128)(2,1)} %refs_4_.9, bf16[1024,1024]{1,0:T(8,128)(2,1)} %key_hbm.9, bf16[1024,1024]{1,0:T(8,128)(2,1)} %value_hbm.9, ...), custom_call_target="tpu_custom_call" | custom-call | flops 1 | bytes 1 | tf_op jit(solution)/shard_map/pallas_call | solution.py:234
  99.4 7.2 %shard_map.87 = (f32[32,4096]{1,0:T(8,128)S(1)}, f32[32,4096]{1,0:T(8,128)S(1)}, f32[32,4096]{1,0:T(8,128)S(1)}, f32[32,4096]{1,0:T(8,128)S(1)}, f32[128,4096]{1,0:T(8,128)S(1)}) custom-call(s32[3]{0:T(128)S(1)} %add_add_fusion.place_ref, f32[2,128,128]{2,1,0:T(8,128)S(1)} %get-tuple-element.71.after_ref.refs_0_.refs_9_.refs_4_, ...), custom_call_target="tpu_custom_call" | custom-call | flops 1 | bytes 1 | tf_op jit(solution)/shard_map/pallas_call | solution.py:379
  107.2 1.5 %collective-permute-start.29 = (f32[64,4096]{1,0:T(8,128)S(1)}, f32[64,4096]{1,0:T(8,128)S(1)}, u32[]{:S(2)}, u32[]{:S(2)}) collective-permute-start(f32[64,4096]{1,0:T(8,128)S(1)} %shard_map.84.after_ref.refs_11_), channel_id=1, source_target_pairs={{0,2},{1,3},{2,0},{3,1},{4,6},{5,7},{6,4},{7,5},{8,10},{9,11},{10,... | collective-permute-start | bytes 3145736 | tf_op jit(solution)/shard_map/ppermute | solution.py:581
  108.7 4.2 %collective-permute-done.28.refs_11_.refs_0_ = f32[64,4096]{1,0:T(8,128)} collective-permute-done((f32[64,4096]{1,0:T(8,128)S(1)}, f32[64,4096]{1,0:T(8,128)}, u32[]{:S(2)}, u32[]{:S(2)}) %collective-permute-start.28) | collective-permute-done | bytes 1048608 | tf_op jit(solution)/shard_map/ppermute | solution.py:581
  112.9 7.2 %shard_map.86 = (f32[32,4096]{1,0:T(8,128)S(1)}, f32[32,4096]{1,0:T(8,128)S(1)}, f32[32,4096]{1,0:T(8,128)S(1)}, f32[32,4096]{1,0:T(8,128)S(1)}, f32[128,4096]{1,0:T(8,128)S(1)}) custom-call(s32[3]{0:T(128)S(1)} %add_add_fusion.place_ref, f32[2,128,128]{2,1,0:T(8,128)S(1)} %get-tuple-element.71.after_ref.refs_0_.refs_9_.refs_4_, ...), custom_call_target="tpu_custom_call" | custom-call | flops 1 | bytes 1 | tf_op jit(solution)/shard_map/pallas_call | solution.py:379
  122.2 2.2 %shard_map.89.refs_3_ = bf16[256,4096]{1,0:T(8,128)(2,1)} custom-call(f32[128,4096]{1,0:T(8,128)S(1)} %get-tuple-element.116.own_ref.refs_3_, f32[64,4096]{1,0:T(8,128)} %collective-permute-done.27.refs_4_.refs_0_, f32[32,4096]{1,0:T(8,128)S(1)} %collective-permute-done.34.refs_1_, ...), custom_call_target="tpu_custom_call", output_to_operand_aliasing={{}: (4, {})} | custom-call | flops 1 | bytes 1 | tf_op jit(solution)/shard_map/pallas_call | solution.py:433
  124.4 2.2 %shard_map.90.refs_3_ = bf16[256,4096]{1,0:T(8,128)(2,1)} custom-call(f32[128,4096]{1,0:T(8,128)S(1)} %get-tuple-element.111.own_ref, f32[64,4096]{1,0:T(8,128)} %collective-permute-done.28.refs_11_.refs_0_, f32[32,4096]{1,0:T(8,128)S(1)} %collective-permute-done.32.refs_1_, ...), custom_call_target="tpu_custom_call", output_to_operand_aliasing={{}: (4, {})} | custom-call | flops 1 | bytes 1 | tf_op jit(solution)/shard_map/pallas_call | solution.py:433
  126.7 7.8 %collective-permute-done.29.refs_0_ = f32[64,4096]{1,0:T(8,128)S(1)} collective-permute-done((f32[64,4096]{1,0:T(8,128)S(1)}, f32[64,4096]{1,0:T(8,128)S(1)}, u32[]{:S(2)}, u32[]{:S(2)}) %collective-permute-start.29) | collective-permute-done | bytes 1048608 | tf_op jit(solution)/shard_map/ppermute | solution.py:581
  (82 shorter events, 19.2 us)
Async XLA Ops:
  3.0 6.6 %collective-permute-start = (f32[2,136,128]{2,1,0:T(8,128)S(1)}, f32[2,136,128]{2,1,0:T(8,128)S(1)}, u32[]{:S(2)}, u32[]{:S(2)}) collective-permute-start(f32[2,136,128]{2,1,0:T(8,128)S(1)} %get-tuple-element.65), channel_id=1, source_target_pairs={{0,4},{4,0},{8,12},{12,8},{16,20},{20,16},{24,28},{28,24},{1,5},{5... | collective-permute-start | bytes 417800 | tf_op jit(solution)/shard_map/ppermute | solution.py:541
  4.5 6.9 %collective-permute-start.3 = (f32[2,136,128]{2,1,0:T(8,128)S(1)}, f32[2,136,128]{2,1,0:T(8,128)S(1)}, u32[]{:S(2)}, u32[]{:S(2)}) collective-permute-start(f32[2,136,128]{2,1,0:T(8,128)S(1)} %get-tuple-element.69), channel_id=1, source_target_pairs={{0,4},{4,0},{8,12},{12,8},{16,20},{20,16},{24,28},{28,24},{1,5},{5... | collective-permute-start | bytes 417800 | tf_op jit(solution)/shard_map/ppermute | solution.py:541
  9.6 2.5 %collective-permute-start.1 = (f32[2,128,128]{2,1,0:T(8,128)S(1)}, f32[2,128,128]{2,1,0:T(8,128)S(1)}, u32[]{:S(2)}, u32[]{:S(2)}) collective-permute-start(f32[2,128,128]{2,1,0:T(8,128)S(1)} %shard_map.66), channel_id=1, source_target_pairs={{0,8},{4,12},{1,9},{5,13},{2,10},{6,14},{3,11},{7,15}} | collective-permute-start | bytes 393224 | tf_op jit(solution)/shard_map/ppermute | solution.py:514
  12.2 7.8 %collective-permute-start.2 = (f32[2,128,128]{2,1,0:T(8,128)S(1)}, f32[2,128,128]{2,1,0:T(8,128)S(1)}, u32[]{:S(2)}, u32[]{:S(2)}) collective-permute-start(f32[2,128,128]{2,1,0:T(8,128)S(1)} %shard_map.67), channel_id=1, source_target_pairs={{8,16},{12,20},{9,17},{13,21},{10,18},{14,22},{11,19},{15,23}} | collective-permute-start | bytes 393224 | tf_op jit(solution)/shard_map/ppermute | solution.py:514
  12.9 8.4 %collective-permute-start.6 = (f32[2,128,128]{2,1,0:T(8,128)S(1)}, f32[2,128,128]{2,1,0:T(8,128)S(1)}, u32[]{:S(2)}, u32[]{:S(2)}) collective-permute-start(f32[2,128,128]{2,1,0:T(8,128)S(1)} %shard_map.69.after_ref), channel_id=1, source_target_pairs={{8,16},{12,20},{9,17},{13,21},{10,18},{14,22},{11,19},{15,23}} | collective-permute-start | bytes 393224 | tf_op jit(solution)/shard_map/ppermute | solution.py:514
  20.0 7.8 %collective-permute-start.5 = (f32[2,128,128]{2,1,0:T(8,128)S(1)}, f32[2,128,128]{2,1,0:T(8,128)S(1)}, u32[]{:S(2)}, u32[]{:S(2)}) collective-permute-start(f32[2,128,128]{2,1,0:T(8,128)S(1)} %shard_map.71), channel_id=1, source_target_pairs={{16,24},{20,28},{17,25},{21,29},{18,26},{22,30},{19,27},{23,31}} | collective-permute-start | bytes 393224 | tf_op jit(solution)/shard_map/ppermute | solution.py:514
  21.4 8.2 %collective-permute-start.7 = (f32[2,128,128]{2,1,0:T(8,128)S(1)}, f32[2,128,128]{2,1,0:T(8,128)S(1)}, u32[]{:S(2)}, u32[]{:S(2)}) collective-permute-start(f32[2,128,128]{2,1,0:T(8,128)S(1)} %shard_map.73), channel_id=1, source_target_pairs={{16,24},{20,28},{17,25},{21,29},{18,26},{22,30},{19,27},{23,31}} | collective-permute-start | bytes 393224 | tf_op jit(solution)/shard_map/ppermute | solution.py:514
  27.9 7.5 %collective-permute-start.8 = (f32[2,128,128]{2,1,0:T(8,128)S(1)}, f32[2,128,128]{2,1,0:T(8,128)S(1)}, u32[]{:S(2)}, u32[]{:S(2)}) collective-permute-start(f32[2,128,128]{2,1,0:T(8,128)S(1)} %get-tuple-element.73), channel_id=1, source_target_pairs={{0,4},{4,0},{8,12},{12,8},{16,20},{20,16},{24,28},{28,24},{1,5},{5... | collective-permute-start | bytes 393224 | tf_op jit(solution)/shard_map/ppermute | solution.py:522
  29.6 5.8 %collective-permute-start.9 = (f32[2,128,128]{2,1,0:T(8,128)S(1)}, f32[2,128,128]{2,1,0:T(8,128)S(1)}, u32[]{:S(2)}, u32[]{:S(2)}) collective-permute-start(f32[2,128,128]{2,1,0:T(8,128)S(1)} %get-tuple-element.74), channel_id=1, source_target_pairs={{0,4},{4,0},{8,12},{12,8},{16,20},{20,16},{24,28},{28,24},{1,5},{5... | collective-permute-start | bytes 393224 | tf_op jit(solution)/shard_map/ppermute | solution.py:522
  39.0 1.9 %collective-permute-start.11 = (f32[16,4096]{1,0:T(8,128)S(1)}, f32[16,4096]{1,0:T(8,128)S(1)}, u32[]{:S(2)}, u32[]{:S(2)}) collective-permute-start(f32[16,4096]{1,0:T(8,128)S(1)} %get-tuple-element.85), channel_id=1, source_target_pairs={{0,1},{1,0},{2,3},{3,2},{4,5},{5,4},{6,7},{7,6},{8,9},{9,8},{10,11... | collective-permute-start | bytes 786440 | tf_op jit(solution)/shard_map/ppermute | solution.py:557
  39.5 1.8 %collective-permute-start.12 = (f32[16,4096]{1,0:T(8,128)S(1)}, f32[16,4096]{1,0:T(8,128)S(1)}, u32[]{:S(2)}, u32[]{:S(2)}) collective-permute-start(f32[16,4096]{1,0:T(8,128)S(1)} %get-tuple-element.86), channel_id=1, source_target_pairs={{0,1},{1,0},{2,3},{3,2},{4,5},{5,4},{6,7},{7,6},{8,9},{9,8},{10,11... | collective-permute-start | bytes 786440 | tf_op jit(solution)/shard_map/ppermute | solution.py:557
  39.6 2.1 %collective-permute-start.13 = (f32[16,4096]{1,0:T(8,128)S(1)}, f32[16,4096]{1,0:T(8,128)S(1)}, u32[]{:S(2)}, u32[]{:S(2)}) collective-permute-start(f32[16,4096]{1,0:T(8,128)S(1)} %get-tuple-element.87), channel_id=1, source_target_pairs={{0,1},{1,0},{2,3},{3,2},{4,5},{5,4},{6,7},{7,6},{8,9},{9,8},{10,11... | collective-permute-start | bytes 786440 | tf_op jit(solution)/shard_map/ppermute | solution.py:557
  41.8 26.1 %collective-permute-start.22 = (f32[64,4096]{1,0:T(8,128)S(1)}, f32[64,4096]{1,0:T(8,128)S(1)}, u32[]{:S(2)}, u32[]{:S(2)}) collective-permute-start(f32[64,4096]{1,0:T(8,128)S(1)} %shard_map.77.refs_11_), channel_id=1, source_target_pairs={{0,2},{1,3},{2,0},{3,1},{4,6},{5,7},{6,4},{7,5},{8,10},{9,11},{10,... | collective-permute-start | bytes 3145736 | tf_op jit(solution)/shard_map/ppermute | solution.py:581
  49.7 1.9 %collective-permute-start.15 = (f32[16,4096]{1,0:T(8,128)S(1)}, f32[16,4096]{1,0:T(8,128)S(1)}, u32[]{:S(2)}, u32[]{:S(2)}) collective-permute-start(f32[16,4096]{1,0:T(8,128)S(1)} %get-tuple-element.90), channel_id=1, source_target_pairs={{0,1},{1,0},{2,3},{3,2},{4,5},{5,4},{6,7},{7,6},{8,9},{9,8},{10,11... | collective-permute-start | bytes 786440 | tf_op jit(solution)/shard_map/ppermute | solution.py:557
  50.3 2.1 %collective-permute-start.17 = (f32[16,4096]{1,0:T(8,128)S(1)}, f32[16,4096]{1,0:T(8,128)S(1)}, u32[]{:S(2)}, u32[]{:S(2)}) collective-permute-start(f32[16,4096]{1,0:T(8,128)S(1)} %get-tuple-element.92), channel_id=1, source_target_pairs={{0,1},{1,0},{2,3},{3,2},{4,5},{5,4},{6,7},{7,6},{8,9},{9,8},{10,11... | collective-permute-start | bytes 786440 | tf_op jit(solution)/shard_map/ppermute | solution.py:557
  59.0 2.0 %collective-permute-start.19 = (f32[16,4096]{1,0:T(8,128)S(1)}, f32[16,4096]{1,0:T(8,128)S(1)}, u32[]{:S(2)}, u32[]{:S(2)}) collective-permute-start(f32[16,4096]{1,0:T(8,128)S(1)} %get-tuple-element.95), channel_id=1, source_target_pairs={{0,1},{1,0},{2,3},{3,2},{4,5},{5,4},{6,7},{7,6},{8,9},{9,8},{10,11... | collective-permute-start | bytes 786440 | tf_op jit(solution)/shard_map/ppermute | solution.py:557
  59.5 2.0 %collective-permute-start.21 = (f32[16,4096]{1,0:T(8,128)S(1)}, f32[16,4096]{1,0:T(8,128)S(1)}, u32[]{:S(2)}, u32[]{:S(2)}) collective-permute-start(f32[16,4096]{1,0:T(8,128)S(1)} %get-tuple-element.97), channel_id=1, source_target_pairs={{0,1},{1,0},{2,3},{3,2},{4,5},{5,4},{6,7},{7,6},{8,9},{9,8},{10,11... | collective-permute-start | bytes 786440 | tf_op jit(solution)/shard_map/ppermute | solution.py:557
  60.4 30.1 %collective-permute-start.27 = (f32[64,4096]{1,0:T(8,128)S(1)}, f32[64,4096]{1,0:T(8,128)}, u32[]{:S(2)}, u32[]{:S(2)}) collective-permute-start(f32[64,4096]{1,0:T(8,128)S(1)} %shard_map.79.refs_11_), channel_id=1, source_target_pairs={{0,2},{1,3},{2,0},{3,1},{4,6},{5,7},{6,4},{7,5},{8,10},{9,11},{10,... | collective-permute-start | bytes 3145736 | tf_op jit(solution)/shard_map/ppermute | solution.py:581
  68.8 44.1 %collective-permute-start.28 = (f32[64,4096]{1,0:T(8,128)S(1)}, f32[64,4096]{1,0:T(8,128)}, u32[]{:S(2)}, u32[]{:S(2)}) collective-permute-start(f32[64,4096]{1,0:T(8,128)S(1)} %shard_map.81.after_ref.refs_11_), channel_id=1, source_target_pairs={{0,2},{1,3},{2,0},{3,1},{4,6},{5,7},{6,4},{7,5},{8,10},{9,11},{10,... | collective-permute-start | bytes 3145736 | tf_op jit(solution)/shard_map/ppermute | solution.py:581
  83.9 1.9 %collective-permute-start.23 = (f32[16,4096]{1,0:T(8,128)S(1)}, f32[16,4096]{1,0:T(8,128)S(1)}, u32[]{:S(2)}, u32[]{:S(2)}) collective-permute-start(f32[16,4096]{1,0:T(8,128)S(1)} %get-tuple-element.103), channel_id=1, source_target_pairs={{0,1},{1,0},{2,3},{3,2},{4,5},{5,4},{6,7},{7,6},{8,9},{9,8},{10,11... | collective-permute-start | bytes 786440 | tf_op jit(solution)/shard_map/ppermute | solution.py:557
  83.9 2.1 %collective-permute-start.24 = (f32[16,4096]{1,0:T(8,128)}, f32[16,4096]{1,0:T(8,128)S(1)}, u32[]{:S(2)}, u32[]{:S(2)}) collective-permute-start(f32[16,4096]{1,0:T(8,128)} %get-tuple-element.104), channel_id=1, source_target_pairs={{0,1},{1,0},{2,3},{3,2},{4,5},{5,4},{6,7},{7,6},{8,9},{9,8},{10,11... | collective-permute-start | bytes 786440 | tf_op jit(solution)/shard_map/ppermute | solution.py:557
  84.4 2.0 %collective-permute-start.25 = (f32[16,4096]{1,0:T(8,128)}, f32[16,4096]{1,0:T(8,128)S(1)}, u32[]{:S(2)}, u32[]{:S(2)}) collective-permute-start(f32[16,4096]{1,0:T(8,128)} %get-tuple-element.105), channel_id=1, source_target_pairs={{0,1},{1,0},{2,3},{3,2},{4,5},{5,4},{6,7},{7,6},{8,9},{9,8},{10,11... | collective-permute-start | bytes 786440 | tf_op jit(solution)/shard_map/ppermute | solution.py:557
  85.7 1.9 %collective-permute-start.26 = (f32[16,4096]{1,0:T(8,128)}, f32[16,4096]{1,0:T(8,128)}, u32[]{:S(2)}, u32[]{:S(2)}) collective-permute-start(f32[16,4096]{1,0:T(8,128)} %get-tuple-element.106), channel_id=1, source_target_pairs={{0,1},{1,0},{2,3},{3,2},{4,5},{5,4},{6,7},{7,6},{8,9},{9,8},{10,11... | collective-permute-start | bytes 786440 | tf_op jit(solution)/shard_map/ppermute | solution.py:557
  106.6 13.5 %collective-permute-start.34 = (f32[32,4096]{1,0:T(8,128)S(1)}, f32[32,4096]{1,0:T(8,128)S(1)}, u32[]{:S(2)}, u32[]{:S(2)}) collective-permute-start(f32[32,4096]{1,0:T(8,128)S(1)} %get-tuple-element.117), channel_id=1, source_target_pairs={{0,1},{1,0},{2,3},{3,2},{4,5},{5,4},{6,7},{7,6},{8,9},{9,8},{10,11... | collective-permute-start | bytes 1572872 | tf_op jit(solution)/shard_map/ppermute | solution.py:557
  106.7 14.0 %collective-permute-start.35 = (f32[32,4096]{1,0:T(8,128)S(1)}, f32[32,4096]{1,0:T(8,128)S(1)}, u32[]{:S(2)}, u32[]{:S(2)}) collective-permute-start(f32[32,4096]{1,0:T(8,128)S(1)} %get-tuple-element.118), channel_id=1, source_target_pairs={{0,1},{1,0},{2,3},{3,2},{4,5},{5,4},{6,7},{7,6},{8,9},{9,8},{10,11... | collective-permute-start | bytes 1572872 | tf_op jit(solution)/shard_map/ppermute | solution.py:557
  107.2 27.3 %collective-permute-start.29 = (f32[64,4096]{1,0:T(8,128)S(1)}, f32[64,4096]{1,0:T(8,128)S(1)}, u32[]{:S(2)}, u32[]{:S(2)}) collective-permute-start(f32[64,4096]{1,0:T(8,128)S(1)} %shard_map.84.after_ref.refs_11_), channel_id=1, source_target_pairs={{0,2},{1,3},{2,0},{3,1},{4,6},{5,7},{6,4},{7,5},{8,10},{9,11},{10,... | collective-permute-start | bytes 3145736 | tf_op jit(solution)/shard_map/ppermute | solution.py:581
  108.7 12.1 %collective-permute-start.36 = (f32[32,4096]{1,0:T(8,128)S(1)}, f32[32,4096]{1,0:T(8,128)S(1)}, u32[]{:S(2)}, u32[]{:S(2)}) collective-permute-start(f32[32,4096]{1,0:T(8,128)S(1)} %get-tuple-element.119), channel_id=1, source_target_pairs={{0,1},{1,0},{2,3},{3,2},{4,5},{5,4},{6,7},{7,6},{8,9},{9,8},{10,11... | collective-permute-start | bytes 1572872 | tf_op jit(solution)/shard_map/ppermute | solution.py:557
  112.9 8.3 %collective-permute-start.37 = (f32[32,4096]{1,0:T(8,128)S(1)}, f32[32,4096]{1,0:T(8,128)S(1)}, u32[]{:S(2)}, u32[]{:S(2)}) collective-permute-start(f32[32,4096]{1,0:T(8,128)S(1)} %get-tuple-element.120), channel_id=1, source_target_pairs={{0,1},{1,0},{2,3},{3,2},{4,5},{5,4},{6,7},{7,6},{8,9},{9,8},{10,11... | collective-permute-start | bytes 1572872 | tf_op jit(solution)/shard_map/ppermute | solution.py:557
  120.1 4.3 %collective-permute-start.32 = (f32[32,4096]{1,0:T(8,128)S(1)}, f32[32,4096]{1,0:T(8,128)S(1)}, u32[]{:S(2)}, u32[]{:S(2)}) collective-permute-start(f32[32,4096]{1,0:T(8,128)S(1)} %get-tuple-element.114), channel_id=1, source_target_pairs={{0,1},{1,0},{2,3},{3,2},{4,5},{5,4},{6,7},{7,6},{8,9},{9,8},{10,11... | collective-permute-start | bytes 1572872 | tf_op jit(solution)/shard_map/ppermute | solution.py:557
  120.7 3.8 %collective-permute-start.33 = (f32[32,4096]{1,0:T(8,128)S(1)}, f32[32,4096]{1,0:T(8,128)S(1)}, u32[]{:S(2)}, u32[]{:S(2)}) collective-permute-start(f32[32,4096]{1,0:T(8,128)S(1)} %get-tuple-element.115), channel_id=1, source_target_pairs={{0,1},{1,0},{2,3},{3,2},{4,5},{5,4},{6,7},{7,6},{8,9},{9,8},{10,11... | collective-permute-start | bytes 1572872 | tf_op jit(solution)/shard_map/ppermute | solution.py:557
  120.8 13.7 %collective-permute-start.30 = (f32[32,4096]{1,0:T(8,128)S(1)}, f32[32,4096]{1,0:T(8,128)S(1)}, u32[]{:S(2)}, u32[]{:S(2)}) collective-permute-start(f32[32,4096]{1,0:T(8,128)S(1)} %get-tuple-element.112), channel_id=1, source_target_pairs={{0,1},{1,0},{2,3},{3,2},{4,5},{5,4},{6,7},{7,6},{8,9},{9,8},{10,11... | collective-permute-start | bytes 1572872 | tf_op jit(solution)/shard_map/ppermute | solution.py:557
  121.2 13.3 %collective-permute-start.31 = (f32[32,4096]{1,0:T(8,128)S(1)}, f32[32,4096]{1,0:T(8,128)S(1)}, u32[]{:S(2)}, u32[]{:S(2)}) collective-permute-start(f32[32,4096]{1,0:T(8,128)S(1)} %get-tuple-element.113), channel_id=1, source_target_pairs={{0,1},{1,0},{2,3},{3,2},{4,5},{5,4},{6,7},{7,6},{8,9},{9,8},{10,11... | collective-permute-start | bytes 1572872 | tf_op jit(solution)/shard_map/ppermute | solution.py:557
  (10 other events, 21.3 us)
